TPU v7x, 32 devices: a whole 2x2x4 slice. The times are simulated.
32 devices in a mesh: section: 2 (over x), dp: 16 (over z, y, core).
Axes of the slice: x: 2, y: 2, z: 4, core: 2. Of those that a mesh axis runs over, the one named last changes fastest.
Arguments:
- inputs: bfloat16 [2, 4096, 1024], P(None, 'dp'), may hold values from -6 to 6
- teacher: float32 [2, 4096, 1024], P(None, 'dp'), may hold values from -6 to 6
- lengths: int32 [2, 16, 4], P(None, 'dp'), may hold values from 1 to 128, 256 in all within a row
- attn_query: bfloat16 [2, 1024, 2048], P('section', 'dp'), may hold values from -0.1875 to 0.1875
- attn_key: bfloat16 [2, 1024, 1024], P('section', 'dp'), may hold values from -0.1875 to 0.1875
- attn_value: bfloat16 [2, 1024, 1024], P('section', 'dp'), may hold values from -0.1875 to 0.1875
- attn_out: bfloat16 [2, 2048, 1024], P('section', 'dp'), may hold values from -0.75 to 0.75
- ffn_gate: bfloat16 [2, 1024, 3072], P('section', 'dp'), may hold values from -0.1875 to 0.1875
- ffn_up: bfloat16 [2, 1024, 3072], P('section', 'dp'), may hold values from -0.1875 to 0.1875
- ffn_down: bfloat16 [2, 3072, 1024], P('section', 'dp'), may hold values from -0.109375 to 0.109375
- norm_attn: bfloat16 [2, 1024], P('section', 'dp'), may hold values from 0.5 to 1.5
- norm_ffn: bfloat16 [2, 1024], P('section', 'dp'), may hold values from 0.5 to 1.5
- norm_query: bfloat16 [2, 128], P('section', 'dp'), may hold values from 0.5 to 1.5
- norm_key: bfloat16 [2, 128], P('section', 'dp'), may hold values from 0.5 to 1.5
Outputs:
- output: bfloat16 [2, 4096, 1024], P('section', 'dp')
- loss: float32 [], replicated
- input_grad: bfloat16 [2, 4096, 1024], P('section', 'dp')
- grad_query: float32 [2, 1024, 2048], P('section', 'dp')
- grad_key: float32 [2, 1024, 1024], P('section', 'dp')
- grad_value: float32 [2, 1024, 1024], P('section', 'dp')
- grad_out: float32 [2, 2048, 1024], P('section', 'dp')
- grad_gate: float32 [2, 1024, 3072], P('section', 'dp')
- grad_up: float32 [2, 1024, 3072], P('section', 'dp')
- grad_down: float32 [2, 3072, 1024], P('section', 'dp')
- grad_norm_attn: float32 [2, 1024], P('section', 'dp')
- grad_norm_ffn: float32 [2, 1024], P('section', 'dp')
- grad_norm_query: float32 [2, 128], P('section', 'dp')
- grad_norm_key: float32 [2, 128], P('section', 'dp')
Inputs may be any that keep to these rules, and one draw needn't show every extreme that they name: In each micro-batch the 4 lengths of one index of dp sum to 256, and the largest of them is 128.
All inputs are finite; a program needn't handle non-finite values.
Results may differ from a plain program's by a relative error of at most 0.017.
Values may be sent and summed in bfloat16 or wider, within the bound.
No kernel may reach another device: no remote copies, remote signals or barrier semaphores. Data moves between devices by JAX's collectives and lax.ppermute only.
A program may use at most 256 MiB of HBM per device.

v0:
```python
import jax
import jax.numpy as jnp
from jax import lax
from jax.sharding import PartitionSpec as P

QUERY_HEADS = 16
KEY_VALUE_HEADS = 8
HEAD_SIZE = 128
TOKENS_PER_SHARD = 256


EPS = 1e-06
THETA = 1000000.0
NEGATIVE = -1e30
CONTRACT_ROWS = (((0,), (0,)), ((), ()))
CONTRACT_COLS = (((1,), (1,)), ((), ()))


def from_behind(value, axis, steps):
    count = lax.axis_size(axis)
    leading, last = (max(0, -steps), min(count, count - steps))
    return lax.ppermute(value, axis, [(source, source + steps) for source in range(leading, last)])


def partner(block, axis, bit):
    count = lax.axis_size(axis)
    route = []
    for low in range(count):
        high = low | 1 << bit
        if high != low and high < count:
            route += [(low, high), (high, low)]
    return lax.ppermute(block, axis, route)


def layout(lengths_row):
    ends = jnp.cumsum(lengths_row)
    places = jnp.arange(TOKENS_PER_SHARD, dtype=jnp.int32)
    passed = (ends[None, :] <= places[:, None]).astype(jnp.int32)
    segment_index = jnp.sum(passed, axis=1)
    start = jnp.sum(passed * lengths_row[None, :], axis=1)
    return (segment_index, places - start)


def rotary_tables(place):
    half = HEAD_SIZE // 2
    freqs = THETA ** (-(jnp.arange(half, dtype=jnp.float32) * 2.0 / HEAD_SIZE))
    angles = place.astype(jnp.float32)[:, None] * freqs[None, :]
    return (jnp.cos(angles), jnp.sin(angles))


def squared_partial_sums(values):
    factor = lax.rsqrt(jnp.mean(values * values, axis=-1, keepdims=True) + EPS)
    return (values * factor, factor)


def norm_back(grad, scaled, factor, gain):
    pulled = grad * gain
    return factor * (pulled - scaled * jnp.mean(pulled * scaled, axis=-1, keepdims=True))


def rotate(values, cosine_table, sine_table):
    half = values.shape[-1] // 2
    first = values[..., :half]
    second = values[..., half:]
    turn_cos = cosine_table[:, None, :]
    turn_sin = sine_table[:, None, :]
    return jnp.concatenate(
        [first * turn_cos - second * turn_sin, second * turn_cos + first * turn_sin], axis=-1
    )


def inverse_rotation(grad, cosine_table, sine_table):
    half = grad.shape[-1] // 2
    first = grad[..., :half]
    second = grad[..., half:]
    turn_cos = cosine_table[:, None, :]
    turn_sin = sine_table[:, None, :]
    return jnp.concatenate(
        [first * turn_cos + second * turn_sin, second * turn_cos - first * turn_sin], axis=-1
    )


def product(left, right):
    return jnp.dot(left, right, preferred_element_type=jnp.float32)


def outer_rows(left, right):
    return lax.dot_general(left, right, CONTRACT_ROWS, preferred_element_type=jnp.float32)


def times_transpose(left, right):
    return lax.dot_general(left, right, CONTRACT_COLS, preferred_element_type=jnp.float32)


def block_scores(grouped_heads, key, allowed):
    scores = jnp.einsum(
        "qhgd,khd->hgqk", grouped_heads, key, preferred_element_type=jnp.float32
    ) * HEAD_SIZE ** (-0.5)
    return jnp.where(allowed[None, None], scores, NEGATIVE)


def attend(parts):
    grouped_heads, key, value_rows, allowed = parts
    scores = block_scores(grouped_heads, key, allowed)
    top = jnp.max(scores, axis=-1, keepdims=True)
    raised = jnp.exp(scores - top)
    total = jnp.sum(raised, axis=-1, keepdims=True)
    weights = (raised / total).astype(jnp.bfloat16)
    mixed_output = jnp.einsum(
        "hgqk,khd->qhgd", weights, value_rows, preferred_element_type=jnp.float32
    )
    return (mixed_output, top + jnp.log(total))


def attend_back(parts):
    grouped_heads, key, value_rows, allowed, log_total, mixed_gradient = parts
    weights = jnp.exp(block_scores(grouped_heads, key, allowed) - log_total)
    value_gradient = jnp.einsum(
        "hgqk,qhgd->khd",
        weights.astype(jnp.bfloat16),
        mixed_gradient,
        preferred_element_type=jnp.float32,
    )
    d_weights = jnp.einsum(
        "qhgd,khd->hgqk", mixed_gradient, value_rows, preferred_element_type=jnp.float32
    )
    d_scores = (
        weights * (d_weights - jnp.sum(d_weights * weights, axis=-1, keepdims=True))
    ).astype(jnp.bfloat16)
    scale = HEAD_SIZE ** (-0.5)
    d_query = (
        jnp.einsum("hgqk,khd->qhgd", d_scores, key, preferred_element_type=jnp.float32) * scale
    )
    key_gradient = (
        jnp.einsum("hgqk,qhgd->khd", d_scores, grouped_heads, preferred_element_type=jnp.float32)
        * scale
    )
    return (d_query, key_gradient, value_gradient)


def forward_layer(
    hidden_in,
    cosine_table,
    sine_table,
    allowed,
    attn_query,
    attn_key,
    attn_value,
    attn_out,
    norm_attn,
    norm_query,
    norm_key,
    ffn_gate,
    ffn_up,
    ffn_down,
    norm_ffn,
):
    token_rows = hidden_in.shape[0]
    group_count = QUERY_HEADS // KEY_VALUE_HEADS
    block_list = token_rows // TOKENS_PER_SHARD
    full_query, full_key, full_value, full_out, gain_attn, gain_query, key_norm_scale = (
        lax.all_gather(attn_query, "dp", axis=1, tiled=True),
        lax.all_gather(attn_key, "dp", axis=1, tiled=True),
        lax.all_gather(attn_value, "dp", axis=1, tiled=True),
        lax.all_gather(attn_out, "dp", axis=1, tiled=True),
        lax.all_gather(norm_attn, "dp", axis=1, tiled=True),
        lax.all_gather(norm_query, "dp", axis=1, tiled=True),
        lax.all_gather(norm_key, "dp", axis=1, tiled=True),
    )
    hidden = hidden_in.astype(jnp.float32)
    scaled, factor = squared_partial_sums(hidden)
    normalized_rows = (scaled * gain_attn[0].astype(jnp.float32)).astype(jnp.bfloat16)
    query_pre = product(normalized_rows, full_query[0])
    unrotated_key = product(normalized_rows, full_key[0])
    reduced_value = product(normalized_rows, full_value[0]).astype(jnp.bfloat16)
    reduced_query = rotate(
        squared_partial_sums(query_pre.reshape(token_rows, QUERY_HEADS, HEAD_SIZE))[0]
        * gain_query[0].astype(jnp.float32),
        cosine_table,
        sine_table,
    ).astype(jnp.bfloat16)
    reduced_key = rotate(
        squared_partial_sums(unrotated_key.reshape(token_rows, KEY_VALUE_HEADS, HEAD_SIZE))[0]
        * key_norm_scale[0].astype(jnp.float32),
        cosine_table,
        sine_table,
    ).astype(jnp.bfloat16)
    mixed_output, log_total = lax.map(
        attend,
        (
            reduced_query.reshape(
                block_list, TOKENS_PER_SHARD, KEY_VALUE_HEADS, group_count, HEAD_SIZE
            ),
            reduced_key.reshape(block_list, TOKENS_PER_SHARD, KEY_VALUE_HEADS, HEAD_SIZE),
            reduced_value.reshape(block_list, TOKENS_PER_SHARD, KEY_VALUE_HEADS, HEAD_SIZE),
            allowed,
        ),
    )
    mixed_low = mixed_output.reshape(token_rows, QUERY_HEADS * HEAD_SIZE).astype(jnp.bfloat16)
    middle = hidden + product(mixed_low, full_out[0])
    full_gate, full_up, full_down, gain_ffn = (
        lax.all_gather(ffn_gate, "dp", axis=1, tiled=True),
        lax.all_gather(ffn_up, "dp", axis=1, tiled=True),
        lax.all_gather(ffn_down, "dp", axis=1, tiled=True),
        lax.all_gather(norm_ffn, "dp", axis=1, tiled=True),
    )
    scaled_ffn, factor_ffn = squared_partial_sums(middle)
    normed_ffn = (scaled_ffn * gain_ffn[0].astype(jnp.float32)).astype(jnp.bfloat16)
    gate = product(normed_ffn, full_gate[0])
    up_part = product(normed_ffn, full_up[0])
    inner = (jax.nn.silu(gate) * up_part).astype(jnp.bfloat16)
    result = middle + product(inner, full_down[0])
    kept = (
        hidden,
        normalized_rows,
        query_pre,
        unrotated_key,
        reduced_query,
        reduced_key,
        reduced_value,
        log_total,
        mixed_low,
        middle,
        normed_ffn,
        gate,
        up_part,
        inner,
    )
    return (result, kept)


def backward_layer(
    kept,
    d_result,
    cosine_table,
    sine_table,
    allowed,
    attn_query,
    attn_key,
    attn_value,
    attn_out,
    norm_attn,
    norm_query,
    norm_key,
    ffn_gate,
    ffn_up,
    ffn_down,
    norm_ffn,
):
    (
        hidden,
        normalized_rows,
        query_pre,
        unrotated_key,
        reduced_query,
        reduced_key,
        reduced_value,
        log_total,
        mixed_low,
        middle,
        normed_ffn,
        gate,
        up_part,
        inner,
    ) = kept
    token_rows = hidden.shape[0]
    group_count = QUERY_HEADS // KEY_VALUE_HEADS
    block_list = token_rows // TOKENS_PER_SHARD
    full_gate, full_up, full_down, gain_ffn = (
        lax.all_gather(ffn_gate, "dp", axis=1, tiled=True),
        lax.all_gather(ffn_up, "dp", axis=1, tiled=True),
        lax.all_gather(ffn_down, "dp", axis=1, tiled=True),
        lax.all_gather(norm_ffn, "dp", axis=1, tiled=True),
    )
    d_branch = d_result.astype(jnp.bfloat16)
    grad_down = outer_rows(inner, d_branch)
    d_inner = times_transpose(d_branch, full_down[0])
    sigma = jax.nn.sigmoid(gate)
    d_gate = (d_inner * up_part * sigma * (1.0 + gate * (1.0 - sigma))).astype(jnp.bfloat16)
    d_up = (d_inner * gate * sigma).astype(jnp.bfloat16)
    grad_gate = outer_rows(normed_ffn, d_gate)
    grad_up = outer_rows(normed_ffn, d_up)
    d_normed_ffn = times_transpose(d_gate, full_gate[0]) + times_transpose(d_up, full_up[0])
    scaled_ffn, factor_ffn = squared_partial_sums(middle)
    grad_gain_ffn = jnp.sum(d_normed_ffn * scaled_ffn, axis=0)
    d_middle = d_result + norm_back(
        d_normed_ffn, scaled_ffn, factor_ffn, gain_ffn[0].astype(jnp.float32)
    )
    ffn_terms = (grad_gate, grad_up, grad_down, grad_gain_ffn)
    full_query, full_key, full_value, full_out, gain_attn, gain_query, key_norm_scale = (
        lax.all_gather(attn_query, "dp", axis=1, tiled=True),
        lax.all_gather(attn_key, "dp", axis=1, tiled=True),
        lax.all_gather(attn_value, "dp", axis=1, tiled=True),
        lax.all_gather(attn_out, "dp", axis=1, tiled=True),
        lax.all_gather(norm_attn, "dp", axis=1, tiled=True),
        lax.all_gather(norm_query, "dp", axis=1, tiled=True),
        lax.all_gather(norm_key, "dp", axis=1, tiled=True),
    )
    d_attn = d_middle.astype(jnp.bfloat16)
    grad_out = outer_rows(mixed_low, d_attn)
    mixed_gradient = times_transpose(d_attn, full_out[0]).astype(jnp.bfloat16)
    d_query, key_gradient, value_gradient = lax.map(
        attend_back,
        (
            reduced_query.reshape(
                block_list, TOKENS_PER_SHARD, KEY_VALUE_HEADS, group_count, HEAD_SIZE
            ),
            reduced_key.reshape(block_list, TOKENS_PER_SHARD, KEY_VALUE_HEADS, HEAD_SIZE),
            reduced_value.reshape(block_list, TOKENS_PER_SHARD, KEY_VALUE_HEADS, HEAD_SIZE),
            allowed,
            log_total,
            mixed_gradient.reshape(
                block_list, TOKENS_PER_SHARD, KEY_VALUE_HEADS, group_count, HEAD_SIZE
            ),
        ),
    )
    reduced_value_gradient = value_gradient.reshape(token_rows, KEY_VALUE_HEADS * HEAD_SIZE).astype(
        jnp.bfloat16
    )
    query_scaled, query_factor = squared_partial_sums(
        query_pre.reshape(token_rows, QUERY_HEADS, HEAD_SIZE)
    )
    d_query_normed = inverse_rotation(
        d_query.reshape(token_rows, QUERY_HEADS, HEAD_SIZE), cosine_table, sine_table
    )
    grad_gain_query = jnp.sum(d_query_normed * query_scaled, axis=(0, 1))
    d_query_pre = (
        norm_back(d_query_normed, query_scaled, query_factor, gain_query[0].astype(jnp.float32))
        .reshape(token_rows, QUERY_HEADS * HEAD_SIZE)
        .astype(jnp.bfloat16)
    )
    scaled_key_rows, key_multiplier = squared_partial_sums(
        unrotated_key.reshape(token_rows, KEY_VALUE_HEADS, HEAD_SIZE)
    )
    normed_key_gradient = inverse_rotation(
        key_gradient.reshape(token_rows, KEY_VALUE_HEADS, HEAD_SIZE), cosine_table, sine_table
    )
    grad_gain_key = jnp.sum(normed_key_gradient * scaled_key_rows, axis=(0, 1))
    d_key_pre = (
        norm_back(
            normed_key_gradient,
            scaled_key_rows,
            key_multiplier,
            key_norm_scale[0].astype(jnp.float32),
        )
        .reshape(token_rows, KEY_VALUE_HEADS * HEAD_SIZE)
        .astype(jnp.bfloat16)
    )
    grad_query = outer_rows(normalized_rows, d_query_pre)
    grad_key = outer_rows(normalized_rows, d_key_pre)
    grad_value = outer_rows(normalized_rows, reduced_value_gradient)
    d_normed = (
        times_transpose(d_query_pre, full_query[0])
        + times_transpose(d_key_pre, full_key[0])
        + times_transpose(reduced_value_gradient, full_value[0])
    )
    scaled, factor = squared_partial_sums(hidden)
    grad_gain_attn = jnp.sum(d_normed * scaled, axis=0)
    d_hidden = d_middle + norm_back(d_normed, scaled, factor, gain_attn[0].astype(jnp.float32))
    attn_terms = (
        grad_query,
        grad_key,
        grad_value,
        grad_out,
        grad_gain_attn,
        grad_gain_query,
        grad_gain_key,
    )
    return (d_hidden, ffn_terms, attn_terms)


def add_tuples(total, extra):
    if total is None:
        return extra
    return tuple((left + right for left, right in zip(total, extra)))


def local(
    inputs,
    teacher,
    lengths,
    attn_query,
    attn_key,
    attn_value,
    attn_out,
    ffn_gate,
    ffn_up,
    ffn_down,
    norm_attn,
    norm_ffn,
    norm_query,
    norm_key,
):
    section = lax.axis_index("section")
    batches = inputs.shape[0]
    model = inputs.shape[2]
    slots = lengths.shape[2]
    group = 1
    steps = batches // group + 1
    token_rows = group * TOKENS_PER_SHARD
    segments_all, places_all = jax.vmap(layout)(lengths[:, 0, :])
    valid_all = (segments_all < slots - 1).astype(jnp.float32)
    order = jnp.arange(TOKENS_PER_SHARD, dtype=jnp.int32)
    causal = order[:, None] >= order[None, :]
    weights_set = (
        attn_query,
        attn_key,
        attn_value,
        attn_out,
        norm_attn,
        norm_query,
        norm_key,
        ffn_gate,
        ffn_up,
        ffn_down,
        norm_ffn,
    )
    carried = jnp.zeros((token_rows, model), jnp.bfloat16)
    kept_steps = []
    tables = []
    cotangents = []
    finals = []
    squares = jnp.zeros((), jnp.float32)
    for step in range(steps):
        own = min(step, steps - 2)
        other = max(step - 1, 0)
        first = inputs[own * group : (own + 1) * group].reshape(token_rows, model)
        hidden_in = jnp.where(section == 0, first, carried)
        index = jnp.where(section == 0, own, other).astype(jnp.int32)
        segment_index = lax.dynamic_slice_in_dim(segments_all, index * group, group, 0)
        place = lax.dynamic_slice_in_dim(places_all, index * group, group, 0)
        allowed = (segment_index[:, :, None] == segment_index[:, None, :]) & causal[None]
        cosine_table, sine_table = rotary_tables(place.reshape(token_rows))
        cosine_table, sine_table, allowed = (cosine_table, sine_table, allowed)
        result, kept = forward_layer(hidden_in, cosine_table, sine_table, allowed, *weights_set)
        result_low = result.astype(jnp.bfloat16)
        kept_steps.append(kept)
        tables.append((cosine_table, sine_table, allowed))
        if step + 1 < steps:
            carried = from_behind(result_low, "section", 1)
        if step >= 1:
            target = teacher[(step - 1) * group : step * group].reshape(token_rows, model)
            keep = valid_all[(step - 1) * group : step * group].reshape(token_rows)
            diff = result_low.astype(jnp.float32) - target
            cotangent = keep[:, None] * diff
            squares = squares + jnp.sum(cotangent * diff)
            cotangents.append(cotangent)
            finals.append(result_low.reshape(group, TOKENS_PER_SHARD, model))
        else:
            cotangents.append(jnp.zeros((token_rows, model), jnp.float32))
    on_last = (section == 1).astype(jnp.float32)
    totals = lax.psum((squares * on_last, jnp.sum(valid_all) * on_last), ("section", "dp"))
    loss = totals[0] / (totals[1] * model)
    incoming = jnp.zeros((token_rows, model), jnp.bfloat16)
    ffn_total = None
    attn_total = None
    input_parts = [None] * (steps - 1)
    for back in range(steps):
        forward_step = steps - 1 - back
        cosine_table, sine_table, allowed = tables[forward_step]
        d_result = jnp.where(section == 1, cotangents[forward_step], incoming.astype(jnp.float32))
        d_hidden, ffn_terms, attn_terms = backward_layer(
            kept_steps[forward_step], d_result, cosine_table, sine_table, allowed, *weights_set
        )
        d_low = d_hidden.astype(jnp.bfloat16)
        if back + 1 < steps:
            incoming = from_behind(d_low, "section", -1)
        if forward_step <= steps - 2:
            input_parts[forward_step] = d_low.reshape(group, TOKENS_PER_SHARD, model)
        ffn_total = add_tuples(ffn_total, ffn_terms)
        attn_total = add_tuples(attn_total, attn_terms)
    ffn_total = (
        lax.psum_scatter(ffn_total[0], "dp", scatter_dimension=0, tiled=True),
        lax.psum_scatter(ffn_total[1], "dp", scatter_dimension=0, tiled=True),
        lax.psum_scatter(ffn_total[2], "dp", scatter_dimension=0, tiled=True),
        lax.psum_scatter(ffn_total[3], "dp", scatter_dimension=0, tiled=True),
    )
    attn_total = (
        lax.psum_scatter(attn_total[0], "dp", scatter_dimension=0, tiled=True),
        lax.psum_scatter(attn_total[1], "dp", scatter_dimension=0, tiled=True),
        lax.psum_scatter(attn_total[2], "dp", scatter_dimension=0, tiled=True),
        lax.psum_scatter(attn_total[3], "dp", scatter_dimension=0, tiled=True),
        lax.psum_scatter(attn_total[4], "dp", scatter_dimension=0, tiled=True),
        lax.psum_scatter(attn_total[5], "dp", scatter_dimension=0, tiled=True),
        lax.psum_scatter(attn_total[6], "dp", scatter_dimension=0, tiled=True),
    )
    out_stack = jnp.concatenate(finals, axis=0)
    grad_stack = jnp.concatenate(input_parts, axis=0)
    half = batches // 2
    sending = jnp.where(section == 0, grad_stack[half:], out_stack[:half])
    received = partner(sending, "section", 0)
    output = jnp.where(section == 0, received, out_stack[half:])
    input_grad = jnp.where(section == 0, grad_stack[:half], received)
    grad_gate, grad_up, grad_down, grad_gain_ffn = ffn_total
    grad_query, grad_key, grad_value, grad_out, grad_gain_attn, grad_gain_query, grad_gain_key = (
        attn_total
    )
    return (
        output,
        loss,
        input_grad,
        grad_query[None],
        grad_key[None],
        grad_value[None],
        grad_out[None],
        grad_gate[None],
        grad_up[None],
        grad_down[None],
        grad_gain_attn[None],
        grad_gain_ffn[None],
        grad_gain_query[None],
        grad_gain_key[None],
    )


def solution(mesh):
    placed = (
        P(None, "dp", None),
        P(None, "dp", None),
        P(None, "dp", None),
        P("section", "dp", None),
        P("section", "dp", None),
        P("section", "dp", None),
        P("section", "dp", None),
        P("section", "dp", None),
        P("section", "dp", None),
        P("section", "dp", None),
        P("section", "dp"),
        P("section", "dp"),
        P("section", "dp"),
        P("section", "dp"),
    )
    return jax.shard_map(
        local,
        mesh=mesh,
        in_specs=placed,
        out_specs=(
            P("section", "dp", None),
            P(),
            P("section", "dp", None),
            P("section", "dp", None),
            P("section", "dp", None),
            P("section", "dp", None),
            P("section", "dp", None),
            P("section", "dp", None),
            P("section", "dp", None),
            P("section", "dp", None),
            P("section", "dp"),
            P("section", "dp"),
            P("section", "dp"),
            P("section", "dp"),
        ),
        check_vma=False,
    )
```

profile of v0, /device:TPU:0, one launch (start us, length us, event | category | flops | bytes accessed | tf_op | source)
XLA Modules:
  0.0 1408.0 jit_solution(1722116352831567412)
XLA Ops:
  18.8 35.7 %all-reduce.10 = (bf16[1024]{0:T(1024)(128)(2,1)S(1)}, bf16[128]{0:T(256)(128)(2,1)S(1)}, bf16[128]{0:T(256)(128)(2,1)S(1)}, bf16[1024]{0:T(1024)(128)(2,1)S(1)}) all-reduce(bf16[1024]{0:T(1024)(128)(2,1)S(1)} %dynamic-update-slice, bf16[128]{0:T(256)(128)(2,1)S(1)} %dynamic-update-slice.1, ...), channel_id=1, replica_groups=mesh['section'=2,'dp'=16] {'dp'}, use_global_device_ids=true, to_apply=%add | all-reduce | flops 2304 | bytes 9216
  62.9 34.2 %all-gather.10.cloned.1.call-done = bf16[1,1024,1024]{2,1,0:T(8,128)(2,1)} async-done(((bf16[1,64,1024]{2,1,0:T(8,128)(2,1)}), bf16[1,1024,1024]{2,1,0:T(8,128)(2,1)}) %all-gather.10.cloned.1.call-update) | async-done | bytes 2097168 | tf_op jit(solution)/shard_map/all_gather | solution.py:163
  102.9 45.9 %all-gather.12.cloned.1.call-done = bf16[1,1024,2048]{2,1,0:T(8,128)(2,1)} async-done(((bf16[1,64,2048]{2,1,0:T(8,128)(2,1)}), bf16[1,1024,2048]{2,1,0:T(8,128)(2,1)}) %all-gather.12.cloned.1.call-update) | async-done | bytes 4194320 | tf_op jit(solution)/shard_map/all_gather | solution.py:162
  148.7 6.7 copy.105
  169.6 30.4 %all-gather.14.cloned.1.call-done = bf16[1,2048,1024]{2,1,0:T(8,128)(2,1)} async-done(((bf16[1,128,1024]{2,1,0:T(8,128)(2,1)}), bf16[1,2048,1024]{2,1,0:T(8,128)(2,1)}) %all-gather.14.cloned.1.call-update) | async-done | bytes 4194320 | tf_op jit(solution)/shard_map/all_gather | solution.py:165
  204.1 58.4 %all-gather.16.cloned.1.call-done = bf16[1,1024,3072]{2,1,0:T(8,128)(2,1)} async-done(((bf16[1,64,3072]{2,1,0:T(8,128)(2,1)}), bf16[1,1024,3072]{2,1,0:T(8,128)(2,1)}) %all-gather.16.cloned.1.call-update) | async-done | bytes 6291472 | tf_op jit(solution)/shard_map/all_gather | solution.py:202
  262.5 6.2 fusion.34
  268.7 56.4 %all-gather.18.cloned.1.call-done = bf16[1,1024,3072]{2,1,0:T(8,128)(2,1)} async-done(((bf16[1,64,3072]{2,1,0:T(8,128)(2,1)}), bf16[1,1024,3072]{2,1,0:T(8,128)(2,1)}) %all-gather.18.cloned.1.call-update) | async-done | bytes 6291472 | tf_op jit(solution)/shard_map/all_gather | solution.py:203
  325.1 8.0 multiply_convert_fusion.8
  333.1 54.8 %all-gather.20.cloned.1.call-done = bf16[1,3072,1024]{2,1,0:T(8,128)(2,1)} async-done(((bf16[1,192,1024]{2,1,0:T(8,128)(2,1)}), bf16[1,3072,1024]{2,1,0:T(8,128)(2,1)}) %all-gather.20.cloned.1.call-update) | async-done | bytes 6291472 | tf_op jit(solution)/shard_map/all_gather | solution.py:204
  387.9 5.2 fusion.197
  398.1 10.2 collective-permute-done
  444.7 9.4 collective-permute-done.1
  487.5 7.7 multiply_convert_fusion.5
  531.0 11.7 collective-permute-done.2
  544.0 7.0 multiply_convert_fusion.3
  590.9 6.2 collective-permute-done.4
  597.1 5.7 multiply_convert_fusion.1
  614.2 5.2 add_add_fusion.5
  656.4 7.9 fusion.337
  666.2 12.3 add_add_fusion
  682.9 6.5 fusion.334
  689.4 12.0 add_add_fusion.2
  704.9 6.7 fusion.336
  711.6 12.3 add_add_fusion.1
  728.1 43.2 %all-reduce.8 = (f32[]{:T(128)}, f32[]{:T(128)}) all-reduce(f32[]{:T(128)S(6)} %mul.1398, f32[]{:T(128)S(6)} %mul.1399), channel_id=1, replica_groups=mesh['section'=2,'dp'=16] {'section','dp'}, use_global_device_ids=true, to_apply=%region_33.34 | all-reduce | flops 2 | bytes 16 | tf_op jit(solution)/shard_map/psum | solution.py:452
  779.9 33.2 %all-reduce.9 = (f32[1024]{0:T(1024)S(1)}, f32[1024]{0:T(1024)S(1)}, f32[128]{0:T(128)S(1)}, f32[128]{0:T(128)S(1)}) all-reduce(f32[1024]{0:T(1024)S(1)} %add_add_fusion.8, f32[1024]{0:T(1024)S(1)} %add_add_fusion.7, f32[128]{0:T(128)S(1)} %add_add_fusion.10, ...), channel_id=9, replica_groups=mesh['section'=2,'dp'=16] {'dp'}, use_global_device_ids=true, to_apply=%region_51.52.clone | all-reduce | flops 2304 | bytes 18432
  818.4 57.0 %reduce-scatter.14.cloned.1.call-done = f32[128,1024]{1,0:T(8,128)} async-done(((f32[2048,1024]{1,0:T(8,128)}), f32[128,1024]{1,0:T(8,128)}) %reduce-scatter.14.cloned.1.call-update) | async-done | bytes 524304 | tf_op jit(solution)/shard_map/reduce_scatter | solution.py:482
  875.4 109.1 %reduce-scatter.8.cloned.1.call-done = f32[64,2048]{1,0:T(8,128)} async-done(((f32[1024,2048]{1,0:T(8,128)}), f32[64,2048]{1,0:T(8,128)}) %reduce-scatter.8.cloned.1.call-update) | async-done | bytes 524304 | tf_op jit(solution)/shard_map/reduce_scatter | solution.py:479
  984.4 138.9 %reduce-scatter.20.cloned.1.call-done = f32[192,1024]{1,0:T(8,128)} async-done(((f32[3072,1024]{1,0:T(8,128)}), f32[192,1024]{1,0:T(8,128)}) %reduce-scatter.20.cloned.1.call-update) | async-done | bytes 786448 | tf_op jit(solution)/shard_map/reduce_scatter | solution.py:475
  1123.3 138.5 %reduce-scatter.16.cloned.1.call-done = f32[64,3072]{1,0:T(8,128)} async-done(((f32[1024,3072]{1,0:T(8,128)}), f32[64,3072]{1,0:T(8,128)}) %reduce-scatter.16.cloned.1.call-update) | async-done | bytes 786448 | tf_op jit(solution)/shard_map/reduce_scatter | solution.py:473
  1261.8 138.4 %reduce-scatter.18.cloned.1.call-done = f32[64,3072]{1,0:T(8,128)} async-done(((f32[1024,3072]{1,0:T(8,128)}), f32[64,3072]{1,0:T(8,128)}) %reduce-scatter.18.cloned.1.call-update) | async-done | bytes 786448 | tf_op jit(solution)/shard_map/reduce_scatter | solution.py:474
  (680 shorter events, 262.9 us)
Async XLA Ops:
  7.2 52.2 %all-gather.8.cloned.1.call-start = ((), (), s32[]{:S(2)}) async-start(), calls=%async_computation.7 | async-start | bytes 2228224 | tf_op jit(solution)/shard_map/all_gather | solution.py:164
  7.9 89.1 %all-gather.10.cloned.1.call-start = ((), (), s32[]{:S(2)}) async-start(), calls=%async_computation.8 | async-start | bytes 2228224 | tf_op jit(solution)/shard_map/all_gather | solution.py:163
  8.7 140.1 %all-gather.12.cloned.1.call-start = ((), (), s32[]{:S(2)}) async-start(), calls=%async_computation.9 | async-start | bytes 4456448 | tf_op jit(solution)/shard_map/all_gather | solution.py:162
  9.4 190.6 %all-gather.14.cloned.1.call-start = ((), (), s32[]{:S(2)}) async-start(), calls=%async_computation.10 | async-start | bytes 4456448 | tf_op jit(solution)/shard_map/all_gather | solution.py:165
  10.0 252.5 %all-gather.16.cloned.1.call-start = ((), (), s32[]{:S(2)}) async-start(), calls=%async_computation.11 | async-start | bytes 6684672 | tf_op jit(solution)/shard_map/all_gather | solution.py:202
  10.6 314.6 %all-gather.18.cloned.1.call-start = ((), (), s32[]{:S(2)}) async-start(), calls=%async_computation.12 | async-start | bytes 6684672 | tf_op jit(solution)/shard_map/all_gather | solution.py:203
  11.1 376.8 %all-gather.20.cloned.1.call-start = ((), (), s32[]{:S(2)}) async-start(), calls=%async_computation.13 | async-start | bytes 6684672 | tf_op jit(solution)/shard_map/all_gather | solution.py:204
  11.9 806.5 %reduce-scatter.12.cloned.1.call-start = ((), (), s32[]{:S(2)}) async-start(), calls=%async_computation.16 | async-start | bytes 4456448 | tf_op jit(solution)/shard_map/reduce_scatter | solution.py:481
  54.5 104.7 %copy-start.162 = (f32[128]{0:T(128)}, f32[128]{0:T(128)S(1)}, u32[]{:S(2)}) copy-start(f32[128]{0:T(128)S(1)} %convert_element_type.472) | copy-start | bytes 1540
  56.6 98.8 %copy-start.172 = (f32[256]{0:T(256)}, f32[256]{0:T(256)S(1)}, u32[]{:S(2)}) copy-start(f32[256]{0:T(256)S(1)} %add_rsqrt_fusion.11) | copy-start | bytes 3076
  59.4 100.3 %copy-start.109 = (f32[256,64]{0,1:T(8,128)}, f32[256,64]{0,1:T(8,128)S(1)}, u32[]{:S(2)}) copy-start(f32[256,64]{0,1:T(8,128)S(1)} %get-tuple-element.262) | copy-start | bytes 196612
  59.4 100.3 %copy-start.111 = (f32[256,64]{0,1:T(8,128)}, f32[256,64]{0,1:T(8,128)S(1)}, u32[]{:S(2)}) copy-start(f32[256,64]{0,1:T(8,128)S(1)} %get-tuple-element.263) | copy-start | bytes 196612
  102.9 60.4 %copy-start.80 = (bf16[256,8,64]{0,2,1:T(8,128)(2,1)}, bf16[256,8,64]{0,2,1:T(8,128)(2,1)S(1)}, u32[]{:S(2)}) copy-start(bf16[256,8,64]{0,2,1:T(8,128)(2,1)S(1)} %get-tuple-element.240) | copy-start | bytes 786436
  203.9 184.0 %copy-start.78 = (f32[256,1024]{1,0:T(8,128)}, f32[256,1024]{1,0:T(8,128)S(1)}, u32[]{:S(2)}) copy-start(f32[256,1024]{1,0:T(8,128)S(1)} %get-tuple-element.271) | copy-start | bytes 3145732
  203.9 64.8 %copy-start.182 = (f32[256]{0:T(256)}, f32[256]{0:T(256)S(1)}, u32[]{:S(2)}) copy-start(f32[256]{0:T(256)S(1)} %add_rsqrt_fusion.10) | copy-start | bytes 3076
  204.1 121.1 %copy-start.53 = (bf16[256,1024]{1,0:T(8,128)(2,1)}, bf16[256,1024]{1,0:T(8,128)(2,1)S(1)}, u32[]{:S(2)}) copy-start(bf16[256,1024]{1,0:T(8,128)(2,1)S(1)} %multiply_convert_fusion.17) | copy-start | bytes 1572868
  393.1 15.2 %collective-permute-start = (bf16[256,1024]{1,0:T(8,128)(2,1)S(1)}, bf16[256,1024]{1,0:T(8,128)(2,1)S(1)}, u32[]{:S(2)}, u32[]{:S(2)}) collective-permute-start(bf16[256,1024]{1,0:T(8,128)(2,1)S(1)} %fusion.197), channel_id=1, source_target_pairs={{0,16},{1,17},{2,18},{3,19},{4,20},{5,21},{6,22},{7,23},{8,24},{9,... | collective-permute-start | bytes 1572872 | tf_op jit(solution)/shard_map/ppermute | solution.py:22
  438.9 15.2 %collective-permute-start.1 = (bf16[256,1024]{1,0:T(8,128)(2,1)S(1)}, bf16[256,1024]{1,0:T(8,128)(2,1)S(1)}, u32[]{:S(2)}, u32[]{:S(2)}) collective-permute-start(bf16[256,1024]{1,0:T(8,128)(2,1)S(1)} %fusion.194), channel_id=1, source_target_pairs={{0,16},{1,17},{2,18},{3,19},{4,20},{5,21},{6,22},{7,23},{8,24},{9,... | collective-permute-start | bytes 1572872 | tf_op jit(solution)/shard_map/ppermute | solution.py:22
  528.0 14.7 %collective-permute-start.2 = (bf16[256,1024]{1,0:T(8,128)(2,1)S(1)}, bf16[256,1024]{1,0:T(8,128)(2,1)S(1)}, u32[]{:S(2)}, u32[]{:S(2)}) collective-permute-start(bf16[256,1024]{1,0:T(8,128)(2,1)S(1)} %fusion.242), channel_id=1, source_target_pairs={{16,0},{17,1},{18,2},{19,3},{20,4},{21,5},{22,6},{23,7},{24,8},{25... | collective-permute-start | bytes 1572872 | tf_op jit(solution)/shard_map/ppermute | solution.py:22
  583.4 13.6 collective-permute-start.4
  619.5 198.9 %reduce-scatter.10.cloned.1.call-start = ((), (), s32[]{:S(2)}) async-start(), calls=%async_computation.15 | async-start | bytes 4456448 | tf_op jit(solution)/shard_map/reduce_scatter | solution.py:480
  632.3 243.1 %reduce-scatter.14.cloned.1.call-start = ((), (), s32[]{:S(2)}) async-start(), calls=%async_computation.17 | async-start | bytes 8912896 | tf_op jit(solution)/shard_map/reduce_scatter | solution.py:482
  641.7 342.8 %reduce-scatter.8.cloned.1.call-start = ((), (), s32[]{:S(2)}) async-start(), calls=%async_computation.14 | async-start | bytes 8912896 | tf_op jit(solution)/shard_map/reduce_scatter | solution.py:479
  655.4 468.0 %reduce-scatter.20.cloned.1.call-start = ((), (), s32[]{:S(2)}) async-start(), calls=%async_computation.20 | async-start | bytes 13369344 | tf_op jit(solution)/shard_map/reduce_scatter | solution.py:475
  678.5 583.3 %reduce-scatter.16.cloned.1.call-start = ((), (), s32[]{:S(2)}) async-start(), calls=%async_computation.18 | async-start | bytes 13369344 | tf_op jit(solution)/shard_map/reduce_scatter | solution.py:473
  701.4 698.7 %reduce-scatter.18.cloned.1.call-start = ((), (), s32[]{:S(2)}) async-start(), calls=%async_computation.19 | async-start | bytes 13369344 | tf_op jit(solution)/shard_map/reduce_scatter | solution.py:474
  724.0 48.6 %copy-start.187 = (f32[128]{0:T(128)S(1)}, f32[128]{0:T(128)}, u32[]{:S(2)}) copy-start(f32[128]{0:T(128)} %get-tuple-element.129) | copy-start | bytes 1540
  724.0 48.6 %copy-start.188 = (f32[128]{0:T(128)S(1)}, f32[128]{0:T(128)}, u32[]{:S(2)}) copy-start(f32[128]{0:T(128)} %get-tuple-element.127) | copy-start | bytes 1540
  724.0 48.6 %copy-start.185 = (f32[1024]{0:T(1024)S(1)}, f32[1024]{0:T(1024)}, u32[]{:S(2)}) copy-start(f32[1024]{0:T(1024)} %get-tuple-element.151) | copy-start | bytes 12292
  724.0 48.6 %copy-start.186 = (f32[1024]{0:T(1024)S(1)}, f32[1024]{0:T(1024)}, u32[]{:S(2)}) copy-start(f32[1024]{0:T(1024)} %get-tuple-element.149) | copy-start | bytes 12292
  724.0 48.6 %copy-start.77 = (bf16[256,16,128]{0,2,1:T(8,128)(2,1)S(1)}, bf16[256,16,128]{0,2,1:T(8,128)(2,1)}, u32[]{:S(2)}) copy-start(bf16[256,16,128]{0,2,1:T(8,128)(2,1)} %copy-done.76) | copy-start | bytes 3145732
  728.0 87.5 %collective-permute-start.3 = (bf16[1,256,1024]{2,1,0:T(8,128)(2,1)}, bf16[1,256,1024]{2,1,0:T(8,128)(2,1)}, u32[]{:S(2)}, u32[]{:S(2)}) collective-permute-start(bf16[1,256,1024]{2,1,0:T(8,128)(2,1)} %get-tuple-element.205), channel_id=1, source_target_pairs={{0,16},{16,0},{1,17},{17,1},{2,18},{18,2},{3,19},{19,3},{4,20},{20... | collective-permute-start | bytes 1572872 | tf_op jit(solution)/shard_map/ppermute | solution.py:32
  (208 other events, 1089.2 us)
Sparse Core Ops, SparseCore 0:
  10.2 44.2 all-gather.7
  56.7 40.3 all-gather.9
  99.2 49.4 all-gather.11
  150.8 49.1 all-gather.13
  202.1 60.3 all-gather.15
  264.6 60.4 all-gather.17
  327.4 60.4 all-gather.19
  619.6 70.0 reduce-scatter.11
  694.6 72.2 reduce-scatter.9
  771.4 103.8 reduce-scatter.13
  880.0 104.3 reduce-scatter.7
  988.9 134.3 reduce-scatter.19
  1127.9 133.8 reduce-scatter.15
  1266.3 133.8 reduce-scatter.17
where the time goes:
time: 1410 us
  waiting for transfers between devices  904 us (64%)
  matrix products  240 us (17%)
  blocking collectives  112 us (8%)
  local copies, waits for them, and re-layouts  75 us (5%)
  other arithmetic  39.2 us (3%)
  between operations  24.2 us (2%)
    reduce_scatter x1, waiting for transfers between devices, local(): lax.psum_scatter(ffn_total[2], 'dp', scatter_dimension=0, tiled=True)  139 us
    reduce_scatter x1, waiting for transfers between devices, local(): lax.psum_scatter(ffn_total[0], 'dp', scatter_dimension=0, tiled=True)  138 us
    reduce_scatter x1, waiting for transfers between devices, local(): lax.psum_scatter(ffn_total[1], 'dp', scatter_dimension=0, tiled=True)  138 us
    reduce_scatter x1, waiting for transfers between devices, local(): lax.psum_scatter(attn_total[0], 'dp', scatter_dimension=0, tiled=True)  109 us
    dot_general x21, matrix products, outer_rows(): lax.dot_general(left, right, CONTRACT_ROWS, preferred_element_type=jnp.fl...  99.9 us
    unnamed x2, blocking collectives  68.9 us
    all_gather x1, waiting for transfers between devices, forward_layer(): lax.all_gather(ffn_gate, 'dp', axis=1, tiled=True)  58.4 us
    dot_general x21, matrix products, product(): return jnp.dot(left, right, preferred_element_type=jnp.float32)  57.5 us
  transfers between devices with their start and end apart: 19, of which 15 were waited for; matrix products, arithmetic and copies ran while one was open for 12% of the time, Pallas kernels for 0%

commit v1 on v0

v1 whole, which is shorter than its diff:
```python
import jax
import jax.numpy as jnp
from jax import lax
from jax.sharding import PartitionSpec as P

QUERY_HEADS = 16
KEY_VALUE_HEADS = 8
HEAD_SIZE = 128
TOKENS_PER_SHARD = 256


EPS = 1e-06
THETA = 1000000.0
NEGATIVE = -1e30
CONTRACT_ROWS = (((0,), (0,)), ((), ()))
CONTRACT_COLS = (((1,), (1,)), ((), ()))


def one_way(value, source):
    return lax.ppermute(value, "section", [(source, 1 - source)])


def chip_at(place, chips):
    place = lax.rem(place + 2 * chips, chips)
    return jnp.where(place < chips // 2, 2 * place, 2 * (chips - 1 - place) + 1)


def ring_place(chip, chips):
    return jnp.where(chip % 2 == 0, chip // 2, chips - 1 - chip // 2)


def ring_routes(devices):
    chips = devices // 2
    order = list(range(0, chips, 2)) + list(range(chips - 1, 0, -2))
    right, left = [], []
    for place in range(chips):
        here, there = order[place], order[(place + 1) % chips]
        for core in range(2):
            right.append((2 * here + core, 2 * there + core))
            left.append((2 * there + core, 2 * here + core))
    return right, left, [(device, device ^ 1) for device in range(devices)]


def gather_ring(shard, after=None):
    devices = lax.axis_size("dp")
    chips = devices // 2
    right, left, pair = ring_routes(devices)
    index = lax.axis_index("dp")
    core = index % 2
    place = ring_place(index // 2, chips)
    rows = shard.shape[0]
    half = rows // 2
    if after is not None:
        shard, after = lax.optimization_barrier((shard, after))
    whole = jnp.zeros((devices,) + shard.shape, shard.dtype)

    def put(whole, piece, owner, offset):
        return lax.dynamic_update_slice(whole, piece[None], (owner, offset, 0))

    whole = put(whole, shard, index, 0)
    whole = put(whole, lax.ppermute(shard, "dp", pair), index + 1 - 2 * core, 0)
    forward, behind = shard[:half], shard[half:]
    marks = []
    for step in range(1, chips):
        forward = lax.ppermute(forward, "dp", right)
        behind = lax.ppermute(behind, "dp", left)
        marks.append((forward, behind))
        forward_pair = lax.ppermute(forward, "dp", pair)
        behind_pair = lax.ppermute(behind, "dp", pair)
        owner = 2 * chip_at(place - step, chips)
        whole = put(whole, forward, owner + core, 0)
        whole = put(whole, forward_pair, owner + 1 - core, 0)
        owner = 2 * chip_at(place + step, chips)
        whole = put(whole, behind, owner + core, half)
        whole = put(whole, behind_pair, owner + 1 - core, half)
    return whole, marks


def scatter_ring(parts):
    devices = lax.axis_size("dp")
    chips = devices // 2
    right, left, pair = ring_routes(devices)
    index = lax.axis_index("dp")
    core = index % 2
    place = ring_place(index // 2, chips)
    half = parts.shape[1] // 2
    grouped = parts.reshape((chips, 2) + parts.shape[1:])
    mine = lax.dynamic_index_in_dim(grouped, core, 1, keepdims=False)
    theirs = lax.dynamic_index_in_dim(grouped, 1 - core, 1, keepdims=False)
    sums = []
    for low, high in ((0, half), (half, 2 * half)):
        got = lax.ppermute(theirs[:, low:high], "dp", pair)
        sums.append(
            (mine[:, low:high].astype(jnp.float32) + got.astype(jnp.float32)).astype(jnp.bfloat16)
        )

    def own(total, where):
        return lax.dynamic_index_in_dim(total, chip_at(where, chips), 0, keepdims=False)

    forward = own(sums[0], place - 1)
    behind = own(sums[1], place + 1)
    for step in range(1, chips):
        forward = lax.ppermute(forward, "dp", right).astype(jnp.float32)
        behind = lax.ppermute(behind, "dp", left).astype(jnp.float32)
        forward = forward + own(sums[0], place - step - 1).astype(jnp.float32)
        behind = behind + own(sums[1], place + step + 1).astype(jnp.float32)
        if step + 1 < chips:
            forward = forward.astype(jnp.bfloat16)
            behind = behind.astype(jnp.bfloat16)
    return jnp.concatenate([forward, behind], axis=0)


def packed(shard, width):
    pieces = shard.shape[-1] // width
    return [shard[:, width * i : width * (i + 1)] for i in range(pieces)]


def packed_grad(grad, devices, width):
    rows, columns = grad.shape
    pieces = columns // width
    grad = grad.astype(jnp.bfloat16).reshape(devices, rows // devices, pieces, width)
    return grad.transpose(0, 2, 1, 3).reshape(devices, pieces * rows // devices, width)


def unpacked(whole, low, pieces, rows):
    devices, width = whole.shape[0], whole.shape[-1]
    part = whole[:, low : low + pieces * rows].reshape(devices, pieces, rows, width)
    return part.transpose(0, 2, 1, 3).reshape(devices * rows, pieces * width)


def beside(grad, low, pieces, rows):
    return jnp.concatenate(
        [grad[low + rows * i : low + rows * (i + 1)] for i in range(pieces)], axis=1
    )


def layout(lengths_row):
    ends = jnp.cumsum(lengths_row)
    places = jnp.arange(TOKENS_PER_SHARD, dtype=jnp.int32)
    passed = (ends[None, :] <= places[:, None]).astype(jnp.int32)
    segment_index = jnp.sum(passed, axis=1)
    start = jnp.sum(passed * lengths_row[None, :], axis=1)
    return (segment_index, places - start)


def rotary_tables(place):
    half = HEAD_SIZE // 2
    freqs = THETA ** (-(jnp.arange(half, dtype=jnp.float32) * 2.0 / HEAD_SIZE))
    angles = place.astype(jnp.float32)[:, None] * freqs[None, :]
    return (jnp.cos(angles), jnp.sin(angles))


def squared_partial_sums(values):
    factor = lax.rsqrt(jnp.mean(values * values, axis=-1, keepdims=True) + EPS)
    return (values * factor, factor)


def norm_back(grad, scaled, factor, gain):
    pulled = grad * gain
    return factor * (pulled - scaled * jnp.mean(pulled * scaled, axis=-1, keepdims=True))


def rotate(values, cosine_table, sine_table):
    half = values.shape[-1] // 2
    first = values[..., :half]
    second = values[..., half:]
    turn_cos = cosine_table[:, None, :]
    turn_sin = sine_table[:, None, :]
    return jnp.concatenate(
        [first * turn_cos - second * turn_sin, second * turn_cos + first * turn_sin], axis=-1
    )


def inverse_rotation(grad, cosine_table, sine_table):
    half = grad.shape[-1] // 2
    first = grad[..., :half]
    second = grad[..., half:]
    turn_cos = cosine_table[:, None, :]
    turn_sin = sine_table[:, None, :]
    return jnp.concatenate(
        [first * turn_cos + second * turn_sin, second * turn_cos - first * turn_sin], axis=-1
    )


def product(left, right):
    return jnp.dot(left, right, preferred_element_type=jnp.float32)


def outer_rows(left, right):
    return lax.dot_general(left, right, CONTRACT_ROWS, preferred_element_type=jnp.float32)


def times_transpose(left, right):
    return lax.dot_general(left, right, CONTRACT_COLS, preferred_element_type=jnp.float32)


def block_scores(grouped_heads, key, allowed):
    scores = jnp.einsum(
        "bqhgd,bkhd->bhgqk", grouped_heads, key, preferred_element_type=jnp.float32
    ) * HEAD_SIZE ** (-0.5)
    return jnp.where(allowed[:, None, None], scores, NEGATIVE)


def attend(grouped_heads, key, value_rows, allowed):
    scores = block_scores(grouped_heads, key, allowed)
    top = jnp.max(scores, axis=-1, keepdims=True)
    raised = jnp.exp(scores - top)
    total = jnp.sum(raised, axis=-1, keepdims=True)
    weights = (raised / total).astype(jnp.bfloat16)
    mixed_output = jnp.einsum(
        "bhgqk,bkhd->bqhgd", weights, value_rows, preferred_element_type=jnp.float32
    )
    return (mixed_output, top + jnp.log(total))


def attend_back(grouped_heads, key, value_rows, allowed, log_total, mixed_gradient):
    weights = jnp.exp(block_scores(grouped_heads, key, allowed) - log_total)
    value_gradient = jnp.einsum(
        "bhgqk,bqhgd->bkhd",
        weights.astype(jnp.bfloat16),
        mixed_gradient,
        preferred_element_type=jnp.float32,
    )
    d_weights = jnp.einsum(
        "bqhgd,bkhd->bhgqk", mixed_gradient, value_rows, preferred_element_type=jnp.float32
    )
    d_scores = (
        weights * (d_weights - jnp.sum(d_weights * weights, axis=-1, keepdims=True))
    ).astype(jnp.bfloat16)
    scale = HEAD_SIZE ** (-0.5)
    d_query = (
        jnp.einsum("bhgqk,bkhd->bqhgd", d_scores, key, preferred_element_type=jnp.float32) * scale
    )
    key_gradient = (
        jnp.einsum("bhgqk,bqhgd->bkhd", d_scores, grouped_heads, preferred_element_type=jnp.float32)
        * scale
    )
    return (d_query, key_gradient, value_gradient)


def attention_rows(hidden_in, tables, attn_weights, gains):
    cosine_table, sine_table, allowed = tables
    full_query, full_key, full_value, full_out = attn_weights
    gain_attn, gain_query, key_norm_scale, _ = gains
    token_rows = hidden_in.shape[0]
    group_count = QUERY_HEADS // KEY_VALUE_HEADS
    block_list = token_rows // TOKENS_PER_SHARD
    hidden = hidden_in.astype(jnp.float32)
    scaled, factor = squared_partial_sums(hidden)
    normalized_rows = (scaled * gain_attn).astype(jnp.bfloat16)
    query_pre = product(normalized_rows, full_query)
    unrotated_key = product(normalized_rows, full_key)
    reduced_value = product(normalized_rows, full_value).astype(jnp.bfloat16)
    reduced_query = rotate(
        squared_partial_sums(query_pre.reshape(token_rows, QUERY_HEADS, HEAD_SIZE))[0] * gain_query,
        cosine_table,
        sine_table,
    ).astype(jnp.bfloat16)
    reduced_key = rotate(
        squared_partial_sums(unrotated_key.reshape(token_rows, KEY_VALUE_HEADS, HEAD_SIZE))[0]
        * key_norm_scale,
        cosine_table,
        sine_table,
    ).astype(jnp.bfloat16)
    reduced_query = reduced_query.reshape(
        block_list, TOKENS_PER_SHARD, KEY_VALUE_HEADS, group_count, HEAD_SIZE
    )
    reduced_key = reduced_key.reshape(block_list, TOKENS_PER_SHARD, KEY_VALUE_HEADS, HEAD_SIZE)
    reduced_value = reduced_value.reshape(block_list, TOKENS_PER_SHARD, KEY_VALUE_HEADS, HEAD_SIZE)
    mixed_output, log_total = attend(reduced_query, reduced_key, reduced_value, allowed)
    mixed_low = mixed_output.reshape(token_rows, QUERY_HEADS * HEAD_SIZE).astype(jnp.bfloat16)
    middle = hidden + product(mixed_low, full_out)
    kept = (
        hidden,
        normalized_rows,
        query_pre,
        unrotated_key,
        reduced_query,
        reduced_key,
        reduced_value,
        log_total,
        mixed_low,
    )
    return middle, kept


def feed_forward(middle, ffn_weights, gains):
    full_gate, full_up, full_down = ffn_weights
    gain_ffn = gains[3]
    scaled_ffn, factor_ffn = squared_partial_sums(middle)
    normed_ffn = (scaled_ffn * gain_ffn).astype(jnp.bfloat16)
    gate = product(normed_ffn, full_gate)
    up_part = product(normed_ffn, full_up)
    inner = (jax.nn.silu(gate) * up_part).astype(jnp.bfloat16)
    result = middle + product(inner, full_down)
    return result, (middle, normed_ffn, gate, up_part, inner)


def feed_forward_back(kept, d_result, ffn_weights, gains):
    middle, normed_ffn, gate, up_part, inner = kept
    full_gate, full_up, full_down = ffn_weights
    gain_ffn = gains[3]
    d_branch = d_result.astype(jnp.bfloat16)
    d_inner = times_transpose(d_branch, full_down)
    sigma = jax.nn.sigmoid(gate)
    d_gate = (d_inner * up_part * sigma * (1.0 + gate * (1.0 - sigma))).astype(jnp.bfloat16)
    d_up = (d_inner * gate * sigma).astype(jnp.bfloat16)
    d_normed_ffn = times_transpose(d_gate, full_gate) + times_transpose(d_up, full_up)
    scaled_ffn, factor_ffn = squared_partial_sums(middle)
    grad_gain_ffn = jnp.sum(d_normed_ffn * scaled_ffn, axis=0)
    d_middle = d_result + norm_back(d_normed_ffn, scaled_ffn, factor_ffn, gain_ffn)
    return d_middle, (d_branch, d_gate, d_up, grad_gain_ffn)


def attention_back(kept, d_middle, tables, attn_weights, gains):
    (
        hidden,
        normalized_rows,
        query_pre,
        unrotated_key,
        reduced_query,
        reduced_key,
        reduced_value,
        log_total,
        mixed_low,
    ) = kept
    cosine_table, sine_table, allowed = tables
    full_query, full_key, full_value, full_out = attn_weights
    gain_attn, gain_query, key_norm_scale, _ = gains
    token_rows = hidden.shape[0]
    d_attn = d_middle.astype(jnp.bfloat16)
    mixed_gradient = times_transpose(d_attn, full_out).astype(jnp.bfloat16)
    d_query, key_gradient, value_gradient = attend_back(
        reduced_query,
        reduced_key,
        reduced_value,
        allowed,
        log_total,
        mixed_gradient.reshape(reduced_query.shape),
    )
    reduced_value_gradient = value_gradient.reshape(token_rows, KEY_VALUE_HEADS * HEAD_SIZE).astype(
        jnp.bfloat16
    )
    query_scaled, query_factor = squared_partial_sums(
        query_pre.reshape(token_rows, QUERY_HEADS, HEAD_SIZE)
    )
    d_query_normed = inverse_rotation(
        d_query.reshape(token_rows, QUERY_HEADS, HEAD_SIZE), cosine_table, sine_table
    )
    grad_gain_query = jnp.sum(d_query_normed * query_scaled, axis=(0, 1))
    d_query_pre = (
        norm_back(d_query_normed, query_scaled, query_factor, gain_query)
        .reshape(token_rows, QUERY_HEADS * HEAD_SIZE)
        .astype(jnp.bfloat16)
    )
    scaled_key_rows, key_multiplier = squared_partial_sums(
        unrotated_key.reshape(token_rows, KEY_VALUE_HEADS, HEAD_SIZE)
    )
    normed_key_gradient = inverse_rotation(
        key_gradient.reshape(token_rows, KEY_VALUE_HEADS, HEAD_SIZE), cosine_table, sine_table
    )
    grad_gain_key = jnp.sum(normed_key_gradient * scaled_key_rows, axis=(0, 1))
    d_key_pre = (
        norm_back(normed_key_gradient, scaled_key_rows, key_multiplier, key_norm_scale)
        .reshape(token_rows, KEY_VALUE_HEADS * HEAD_SIZE)
        .astype(jnp.bfloat16)
    )
    d_normed = (
        times_transpose(d_query_pre, full_query)
        + times_transpose(d_key_pre, full_key)
        + times_transpose(reduced_value_gradient, full_value)
    )
    scaled, factor = squared_partial_sums(hidden)
    grad_gain_attn = jnp.sum(d_normed * scaled, axis=0)
    d_hidden = d_middle + norm_back(d_normed, scaled, factor, gain_attn)
    return d_hidden, (
        d_attn,
        d_query_pre,
        d_key_pre,
        reduced_value_gradient,
        grad_gain_attn,
        grad_gain_query,
        grad_gain_key,
    )


def local(
    inputs,
    teacher,
    lengths,
    attn_query,
    attn_key,
    attn_value,
    attn_out,
    ffn_gate,
    ffn_up,
    ffn_down,
    norm_attn,
    norm_ffn,
    norm_query,
    norm_key,
):
    section = lax.axis_index("section")
    index = lax.axis_index("dp")
    devices = lax.axis_size("dp")
    batches, _, model = inputs.shape
    slots = lengths.shape[2]
    token_rows = batches * TOKENS_PER_SHARD
    rows = attn_query.shape[1]
    forward_rows = ffn_down.shape[1]

    gain_sizes = (norm_attn.shape[1], norm_query.shape[1], norm_key.shape[1], norm_ffn.shape[1])
    gain_shard = jnp.concatenate([norm_attn[0], norm_query[0], norm_key[0], norm_ffn[0]])
    gain_whole = lax.all_gather(gain_shard.astype(jnp.float32), "dp", axis=0)
    gains, low = [], 0
    for size in gain_sizes:
        gains.append(gain_whole[:, low : low + size].reshape(devices * size))
        low += size

    half_down = forward_rows // 2
    half_out = attn_out.shape[1] // 2
    attn_shard = jnp.concatenate(
        packed(attn_query[0], model)
        + [attn_out[0]]
        + packed(attn_key[0], model)
        + packed(attn_value[0], model),
        axis=0,
    )
    ffn_shard = jnp.concatenate(
        packed(ffn_gate[0], model) + [ffn_down[0]] + packed(ffn_up[0], model), axis=0
    )
    attn_whole, marks = gather_ring(attn_shard)
    ffn_whole, _ = gather_ring(ffn_shard, marks[-2])
    attn_weights = (
        unpacked(attn_whole, 0, 2, rows),
        unpacked(attn_whole, 4 * rows, 1, rows),
        unpacked(attn_whole, 5 * rows, 1, rows),
        unpacked(attn_whole, 2 * rows, 1, 2 * rows),
    )
    ffn_weights = (
        unpacked(ffn_whole, 0, 3, rows),
        unpacked(ffn_whole, 3 * rows + forward_rows, 3, rows),
        unpacked(ffn_whole, 3 * rows, 1, forward_rows),
    )

    segments, places = jax.vmap(layout)(lengths[:, 0, :])
    keep = (segments < slots - 1).astype(jnp.float32).reshape(token_rows)
    order = jnp.arange(TOKENS_PER_SHARD, dtype=jnp.int32)
    causal = order[:, None] >= order[None, :]
    allowed = (segments[:, :, None] == segments[:, None, :]) & causal[None]
    cosine_table, sine_table = rotary_tables(places.reshape(token_rows))
    tables = (cosine_table, sine_table, allowed)

    first = inputs.reshape(token_rows, model)
    middle, _ = attention_rows(first, tables, attn_weights, gains)
    result, _ = feed_forward(middle, ffn_weights, gains)
    carried = one_way(result.astype(jnp.bfloat16), 0)
    hidden_in = jnp.where(section == 0, first, carried)
    middle, attn_kept = attention_rows(hidden_in, tables, attn_weights, gains)
    result, ffn_kept = feed_forward(middle, ffn_weights, gains)
    result_low = result.astype(jnp.bfloat16)

    diff = result_low.astype(jnp.float32) - teacher.reshape(token_rows, model)
    cotangent = keep[:, None] * diff
    squares = jnp.sum(cotangent * diff)

    d_middle, _ = feed_forward_back(ffn_kept, cotangent, ffn_weights, gains)
    d_hidden, _ = attention_back(attn_kept, d_middle, tables, attn_weights, gains)
    incoming = one_way(d_hidden.astype(jnp.bfloat16), 1)
    d_result = jnp.where(section == 1, cotangent, incoming.astype(jnp.float32))
    d_middle, ffn_terms = feed_forward_back(ffn_kept, d_result, ffn_weights, gains)
    d_branch, d_gate, d_up, grad_gain_ffn = ffn_terms
    _, normed_ffn, _, _, inner = ffn_kept
    ffn_parts = jnp.concatenate(
        [
            packed_grad(outer_rows(normed_ffn, d_gate), devices, model),
            packed_grad(outer_rows(inner, d_branch), devices, model),
            packed_grad(outer_rows(normed_ffn, d_up), devices, model),
        ],
        axis=1,
    )
    ffn_grad = scatter_ring(ffn_parts)
    d_hidden, attn_terms = attention_back(attn_kept, d_middle, tables, attn_weights, gains)
    d_attn, d_query, d_key, d_value, grad_gain_attn, grad_gain_query, grad_gain_key = attn_terms
    normalized_rows, mixed_low = attn_kept[1], attn_kept[8]
    attn_parts = jnp.concatenate(
        [
            packed_grad(outer_rows(normalized_rows, d_query), devices, model),
            packed_grad(outer_rows(mixed_low, d_attn), devices, model),
            packed_grad(outer_rows(normalized_rows, d_key), devices, model),
            packed_grad(outer_rows(normalized_rows, d_value), devices, model),
        ],
        axis=1,
    )
    attn_grad = scatter_ring(attn_parts)

    grad_gate = beside(ffn_grad, 0, 3, rows)
    grad_down = ffn_grad[3 * rows : 3 * rows + forward_rows]
    grad_up = beside(ffn_grad, 3 * rows + forward_rows, 3, rows)
    grad_query = beside(attn_grad, 0, 2, rows)
    grad_out = attn_grad[2 * rows : 4 * rows]
    grad_key = attn_grad[4 * rows : 5 * rows]
    grad_value = attn_grad[5 * rows :]

    small = jnp.concatenate(
        [
            grad_gain_attn,
            grad_gain_query,
            grad_gain_key,
            grad_gain_ffn,
            jnp.stack([squares, jnp.sum(keep)]),
        ]
    )
    small_sum = jnp.sum(lax.all_gather(small, "dp", axis=0), axis=0)
    totals = small_sum[-2:]
    totals = jnp.where(section == 1, totals, one_way(totals, 1))
    loss = totals[0] / (totals[1] * model)
    gain_grads, low = [], 0
    for size in gain_sizes:
        gain_grads.append(lax.dynamic_slice(small_sum, (low + index * size,), (size,))[None])
        low += devices * size
    grad_gain_attn, grad_gain_query, grad_gain_key, grad_gain_ffn = gain_grads

    half = batches // 2
    finals = result_low.reshape(batches, TOKENS_PER_SHARD, model)
    grads = d_hidden.astype(jnp.bfloat16).reshape(batches, TOKENS_PER_SHARD, model)
    output = jnp.where(section == 0, one_way(finals[:half], 1), finals[half:])
    input_grad = jnp.where(section == 0, grads[:half], one_way(grads[half:], 0))
    return (
        output,
        loss,
        input_grad,
        grad_query[None],
        grad_key[None],
        grad_value[None],
        grad_out[None],
        grad_gate[None],
        grad_up[None],
        grad_down[None],
        grad_gain_attn,
        grad_gain_ffn,
        grad_gain_query,
        grad_gain_key,
    )


def solution(mesh):
    placed = (
        P(None, "dp", None),
        P(None, "dp", None),
        P(None, "dp", None),
        P("section", "dp", None),
        P("section", "dp", None),
        P("section", "dp", None),
        P("section", "dp", None),
        P("section", "dp", None),
        P("section", "dp", None),
        P("section", "dp", None),
        P("section", "dp"),
        P("section", "dp"),
        P("section", "dp"),
        P("section", "dp"),
    )
    return jax.shard_map(
        local,
        mesh=mesh,
        in_specs=placed,
        out_specs=(
            P("section", "dp", None),
            P(),
            P("section", "dp", None),
            P("section", "dp", None),
            P("section", "dp", None),
            P("section", "dp", None),
            P("section", "dp", None),
            P("section", "dp", None),
            P("section", "dp", None),
            P("section", "dp", None),
            P("section", "dp"),
            P("section", "dp"),
            P("section", "dp"),
            P("section", "dp"),
        ),
        check_vma=False,
    )
```

time: 1410 us -> 1200 us (0.85)
  waiting for transfers between devices: 904 us -> 335 us
  local copies, waits for them, and re-layouts: 75 us -> 410 us
  blocking collectives: 112 us -> 24.2 us
  other arithmetic: 39.2 us -> 103 us
  starting transfers between devices: 13.4 us -> 66.1 us
    reduce_scatter x7 -> x0, waiting for transfers between devices: 582 us -> none  [the longest x1 139 us: local(): lax.psum_scatter(ffn_total[2], 'dp', scatter_dimension=0, tiled=True)]
    all_gather x7 -> x0, waiting for transfers between devices: 280 us -> none  [the longest x1 58.4 us: forward_layer(): lax.all_gather(ffn_gate, 'dp', axis=1, tiled=True)]
    ppermute x5 -> x95, waiting for transfers between devices: 37.5 us -> 253 us  [the longest x14 108 us: scatter_ring(): forward = lax.ppermute(forward, 'dp', right).astype(jnp.float32)]
    reshape x0 -> x14, local copies, waits for them, and re-layouts: none -> 84.6 us  [the longest x4 49.3 us: packed_grad(): grad.astype(jnp.bfloat16).reshape(devices, rows // devices, pieces, width)]
    unnamed x14 -> x2, waiting for transfers between devices: 4.45 us -> 82.6 us
    dot_general x21 -> x7, matrix products: 99.9 us -> 29.6 us  [outer_rows(): lax.dot_general(left, right, CONTRACT_ROWS, preferred_element_type=jnp.fl...]
    unnamed x2 -> x0, blocking collectives: 68.9 us -> none
    dynamic_update_slice x0 -> x60, local copies, waits for them, and re-layouts: none -> 55.7 us  [put(): return lax.dynamic_update_slice(whole, piece[None], (owner, offset, 0))]
  transfers between devices with their start and end apart: 19 -> 96, of which waited for: 15 -> 41; matrix products, arithmetic and copies ran while one was open for 12% -> 25% of each run, Pallas kernels for 0% -> 0%
where the time goes in v1:
time: 1200 us; the launch traced here: 1190 us
  local copies, waits for them, and re-layouts  410 us (34%)
  waiting for transfers between devices  335 us (28%)
  matrix products  229 us (19%)
  other arithmetic  103 us (9%)
  starting transfers between devices  66.1 us (6%)
  blocking collectives  24.2 us (2%)
  between operations  20.5 us (2%)
    ppermute x14, waiting for transfers between devices, scatter_ring(): forward = lax.ppermute(forward, 'dp', right).astype(jnp.float32)  108 us
    unnamed x2, waiting for transfers between devices  82.6 us
    dot_general x14, matrix products, times_transpose(): lax.dot_general(left, right, CONTRACT_COLS, preferred_element_type=jnp.fl...  72.9 us
    dot_general x13, matrix products, product(): return jnp.dot(left, right, preferred_element_type=jnp.float32)  72 us
    dynamic_update_slice x60, local copies, waits for them, and re-layouts, put(): return lax.dynamic_update_slice(whole, piece[None], (owner, offset, 0))  55.7 us
    unnamed x266, local copies, waits for them, and re-layouts  54.2 us
    ppermute x5, waiting for transfers between devices, one_way(): return lax.ppermute(value, 'section', [(source, 1 - source)])  54.1 us
    reshape x4, local copies, waits for them, and re-layouts, packed_grad(): grad.astype(jnp.bfloat16).reshape(devices, rows // devices, pieces, width)  49.3 us
  transfers between devices with their start and end apart: 96, of which 41 were waited for; matrix products, arithmetic and copies ran while one was open for 25% of the time, Pallas kernels for 0%

profile of v1, /device:TPU:0, one launch (start us, length us, event | category | flops | bytes accessed | tf_op | source)
XLA Modules:
  0.0 1187.7 jit_solution(10819224974631258164)
XLA Ops:
  18.0 24.2 %all-gather.1 = f32[16,1,144]{2,1,0:T(1,128)S(1)} all-gather(f32[1,1,144]{2,1,0:T(1,128)S(1)} %fusion.122), channel_id=1, replica_groups=mesh['section'=2,'dp'=16] {'dp'}, dimensions={0}, use_global_device_ids=true | all-gather | bytes 9792 | tf_op jit(solution)/shard_map/all_gather | solution.py:414
  131.5 9.4 broadcast_in_dim.336
  164.0 9.3 copy.199
  341.1 15.5 %fusion.138 = (bf16[16,192,1024]{2,1,0:T(8,128)(2,1)}, bf16[16,192,1024]{2,1,0:T(8,128)(2,1)}, bf16[16,192,1024]{2,1,0:T(8,128)(2,1)}) fusion(bf16[16,576,1024]{2,1,0:T(8,128)(2,1)} %bitcast_dynamic-update-slice_fusion.4), kind=kLoop, calls=%fused_computation.393 | loop fusion | bytes 37748736 | tf_op jit(solution)/shard_map/slice | solution.py:127
  356.6 11.7 copy.206
  368.3 10.2 copy.280
  378.5 12.0 %copy.207 = bf16[16,64,3,1024]{3,2,1,0:T(4,128)(2,1)} copy(bf16[16,64,3,1024]{3,1,2,0:T(8,128)(2,1)} %bitcast.593) | data formatting | bytes 12582912 | tf_op jit(solution)/shard_map/transpose | solution.py:128
  390.5 10.3 copy.281
  406.9 15.4 %add_convert_fusion.6 = bf16[512,1024]{1,0:T(8,128)(2,1)} fusion(f32[512,1024]{1,0:T(8,128)} %get-tuple-element.103, bf16[3072,1024]{1,0:T(8,128)(2,1)} %bitcast.623, f32[512,3072]{1,0:T(8,128)} %fusion.91, bf16[1024,3072]{1,0:T(8,128)(2,1)} %bitcast.615, f32[1024]{0:T(1024)S(1)} %mul.528, f32[512]{0:T(512)S(1)} %add_rsqrt_fusion.6), kind=kOutput, calls=%fused_computation.141 | convolution fusion | flops 6454509568 | bytes 22026240 | tf_op jit(solution)/shard_map/dot_general | solution.py:186
  426.4 22.7 %collective-permute-done.58 = bf16[512,1024]{1,0:T(8,128)(2,1)S(1)} collective-permute-done((bf16[512,1024]{1,0:T(8,128)(2,1)}, bf16[512,1024]{1,0:T(8,128)(2,1)S(1)}, u32[]{:S(2)}, u32[]{:S(2)}) %collective-permute-start.58) | collective-permute-done | bytes 1048608 | tf_op jit(solution)/shard_map/ppermute | solution.py:20
  542.2 11.0 fusion.15
  553.2 9.0 multiply_reduce_fusion.10
  641.8 31.4 %collective-permute-done.59 = bf16[1,256,1024]{2,1,0:T(8,128)(2,1)} collective-permute-done((bf16[1,256,1024]{2,1,0:T(8,128)(2,1)}, bf16[1,256,1024]{2,1,0:T(8,128)(2,1)}, u32[]{:S(2)}, u32[]{:S(2)}) %collective-permute-start.59) | collective-permute-done | bytes 524320 | tf_op jit(solution)/shard_map/ppermute | solution.py:20
  679.2 12.0 %multiply_convert_fusion = (bf16[512,3072]{1,0:T(8,128)(2,1)S(1)}, bf16[512,3072]{1,0:T(8,128)(2,1)}) fusion(f32[512,3072]{1,0:T(8,128)} %copy-done.98, f32[512,3072]{1,0:T(8,128)} %get-tuple-element.113, bf16[512,1024]{1,0:T(8,128)(2,1)S(1)} %get-tuple-element.58, bf16[3072,1024]{1,0:T(8,128)(2,1)} %bitcast.624), kind=kOutput, calls=%fused_computation.30 | convolution fusion | flops 3241672704 | bytes 26214400 | tf_op jit(solution)/shard_map/dot_general | solution.py:194
  691.3 7.8 fusion.155
  800.3 8.2 reshape.533
  812.6 14.1 %pad_maximum_fusion.1 = bf16[8,2,384,1024]{3,2,1,0:T(8,128)(2,1)} fusion(bf16[8,2,64,1024]{3,2,1,0:T(8,128)(2,1)S(1)} %bitcast.650, bf16[8,2,64,1024]{3,2,1,0:T(8,128)(2,1)S(1)} %bitcast.651, bf16[8,2,128,1024]{3,2,1,0:T(8,128)(2,1)S(1)} %bitcast.647, bf16[8,2,128,1024]{3,2,1,0:T(8,128)(2,1)S(1)} %bitcast.608), kind=kLoop, calls=%fused_computation.2 | loop fusion | flops 50331648 | bytes 25165824 | tf_op jit(solution)/shard_map/concatenate | solution.py:486
  826.6 11.2 dynamic-slice_bitcast_fusion.3
  844.8 18.6 %reshape.535 = bf16[16,64,3,1024]{3,2,1,0:T(4,128)(2,1)} reshape(bf16[1024,3072]{1,0:T(8,128)(2,1)} %convolution_convert_fusion) | data formatting | bytes 12582912 | tf_op jit(solution)/shard_map/reshape | solution.py:121
  863.4 9.0 copy.239
  872.4 18.7 %reshape.534 = bf16[16,64,3,1024]{3,2,1,0:T(4,128)(2,1)} reshape(bf16[1024,3072]{1,0:T(8,128)(2,1)} %convolution_convert_fusion.2) | data formatting | bytes 12582912 | tf_op jit(solution)/shard_map/reshape | solution.py:121
  930.1 82.6 %all-reduce.3.cloned.1.call-done = f32[36896]{0:T(1024)} async-done(((f32[36896]{0:T(1024)}), f32[36896]{0:T(1024)}) %all-reduce.3.cloned.1.call-update) | async-done | bytes 147600
  1057.4 11.7 collective-permute-done.80
  1069.8 7.8 collective-permute-done.67
  1080.9 9.3 collective-permute-done.81
  1090.8 7.8 collective-permute-done.68
  1102.0 9.3 collective-permute-done.82
  1111.9 7.8 collective-permute-done.69
  1123.0 9.3 collective-permute-done.83
  1133.0 7.8 collective-permute-done.70
  1141.9 8.5 collective-permute-done.84
  1154.2 9.7 collective-permute-done.85
  (725 shorter events, 703.7 us)
Async XLA Ops:
  7.2 1005.4 %all-reduce.3.cloned.1.call-start = ((), (), s32[]{:S(2)}) async-start(), calls=%async_computation | async-start | bytes 303104
  12.1 63.1 %collective-permute-start = (bf16[384,1024]{1,0:T(8,128)(2,1)S(1)}, bf16[384,1024]{1,0:T(8,128)(2,1)S(1)}, u32[]{:S(2)}, u32[]{:S(2)}) collective-permute-start(bf16[384,1024]{1,0:T(8,128)(2,1)S(1)} %constant_dynamic-update-slice_fusion), channel_id=1, source_target_pairs={{0,1},{1,0},{2,3},{3,2},{4,5},{5,4},{6,7},{7,6},{8,9},{9,8},{10,11... | collective-permute-start | bytes 2359304 | tf_op jit(solution)/shard_map/ppermute | solution.py:61
  14.6 49.0 %collective-permute-start.1 = (bf16[192,1024]{1,0:T(8,128)(2,1)}, bf16[192,1024]{1,0:T(8,128)(2,1)}, u32[]{:S(2)}, u32[]{:S(2)}) collective-permute-start(bf16[192,1024]{1,0:T(8,128)(2,1)} %get-tuple-element.80), channel_id=1, source_target_pairs={{0,4},{1,5},{4,8},{5,9},{8,12},{9,13},{12,14},{13,15},{14,10},{15,... | collective-permute-start | bytes 1179656 | tf_op jit(solution)/shard_map/ppermute | solution.py:65
  17.2 46.4 %collective-permute-start.3 = (bf16[192,1024]{1,0:T(8,128)(2,1)}, bf16[192,1024]{1,0:T(8,128)(2,1)S(1)}, u32[]{:S(2)}, u32[]{:S(2)}) collective-permute-start(bf16[192,1024]{1,0:T(8,128)(2,1)} %get-tuple-element.79), channel_id=1, source_target_pairs={{4,0},{5,1},{8,4},{9,5},{12,8},{13,9},{14,12},{15,13},{10,14},{11,... | collective-permute-start | bytes 1179656 | tf_op jit(solution)/shard_map/ppermute | solution.py:66
  125.6 29.2 %collective-permute-start.30 = (bf16[288,1024]{1,0:T(8,128)(2,1)S(1)}, bf16[288,1024]{1,0:T(8,128)(2,1)}, u32[]{:S(2)}, u32[]{:S(2)}) collective-permute-start(bf16[288,1024]{1,0:T(8,128)(2,1)S(1)} %get-tuple-element.74), channel_id=1, source_target_pairs={{0,4},{1,5},{4,8},{5,9},{8,12},{9,13},{12,14},{13,15},{14,10},{15,... | collective-permute-start | bytes 1769480 | tf_op jit(solution)/shard_map/ppermute | solution.py:65
  125.8 29.6 %collective-permute-start.32 = (bf16[288,1024]{1,0:T(8,128)(2,1)S(1)}, bf16[288,1024]{1,0:T(8,128)(2,1)}, u32[]{:S(2)}, u32[]{:S(2)}) collective-permute-start(bf16[288,1024]{1,0:T(8,128)(2,1)S(1)} %get-tuple-element.73), channel_id=1, source_target_pairs={{4,0},{5,1},{8,4},{9,5},{12,8},{13,9},{14,12},{15,13},{10,14},{11,... | collective-permute-start | bytes 1769480 | tf_op jit(solution)/shard_map/ppermute | solution.py:66
  145.9 107.2 %collective-permute-start.29 = (bf16[576,1024]{1,0:T(8,128)(2,1)}, bf16[576,1024]{1,0:T(8,128)(2,1)}, u32[]{:S(2)}, u32[]{:S(2)}) collective-permute-start(bf16[576,1024]{1,0:T(8,128)(2,1)} %slice_dynamic-update-slice_fusion), channel_id=1, source_target_pairs={{0,1},{1,0},{2,3},{3,2},{4,5},{5,4},{6,7},{7,6},{8,9},{9,8},{10,11... | collective-permute-start | bytes 3538952 | tf_op jit(solution)/shard_map/ppermute | solution.py:61
  154.8 103.1 %collective-permute-start.31 = (bf16[288,1024]{1,0:T(8,128)(2,1)}, bf16[288,1024]{1,0:T(8,128)(2,1)}, u32[]{:S(2)}, u32[]{:S(2)}) collective-permute-start(bf16[288,1024]{1,0:T(8,128)(2,1)} %collective-permute-done.30), channel_id=1, source_target_pairs={{0,1},{1,0},{2,3},{3,2},{4,5},{5,4},{6,7},{7,6},{8,9},{9,8},{10,11... | collective-permute-start | bytes 1769480 | tf_op jit(solution)/shard_map/ppermute | solution.py:68
  155.4 97.6 %collective-permute-start.34 = (bf16[288,1024]{1,0:T(8,128)(2,1)}, bf16[288,1024]{1,0:T(8,128)(2,1)}, u32[]{:S(2)}, u32[]{:S(2)}) collective-permute-start(bf16[288,1024]{1,0:T(8,128)(2,1)} %collective-permute-done.30), channel_id=1, source_target_pairs={{0,4},{1,5},{4,8},{5,9},{8,12},{9,13},{12,14},{13,15},{14,10},{15,... | collective-permute-start | bytes 1769480 | tf_op jit(solution)/shard_map/ppermute | solution.py:65
  155.8 107.7 %collective-permute-start.33 = (bf16[288,1024]{1,0:T(8,128)(2,1)}, bf16[288,1024]{1,0:T(8,128)(2,1)}, u32[]{:S(2)}, u32[]{:S(2)}) collective-permute-start(bf16[288,1024]{1,0:T(8,128)(2,1)} %collective-permute-done.32), channel_id=1, source_target_pairs={{0,1},{1,0},{2,3},{3,2},{4,5},{5,4},{6,7},{7,6},{8,9},{9,8},{10,11... | collective-permute-start | bytes 1769480 | tf_op jit(solution)/shard_map/ppermute | solution.py:69
  156.5 101.3 %collective-permute-start.36 = (bf16[288,1024]{1,0:T(8,128)(2,1)}, bf16[288,1024]{1,0:T(8,128)(2,1)}, u32[]{:S(2)}, u32[]{:S(2)}) collective-permute-start(bf16[288,1024]{1,0:T(8,128)(2,1)} %collective-permute-done.32), channel_id=1, source_target_pairs={{4,0},{5,1},{8,4},{9,5},{12,8},{13,9},{14,12},{15,13},{10,14},{11,... | collective-permute-start | bytes 1769480 | tf_op jit(solution)/shard_map/ppermute | solution.py:66
  422.3 26.8 %collective-permute-start.58 = (bf16[512,1024]{1,0:T(8,128)(2,1)}, bf16[512,1024]{1,0:T(8,128)(2,1)S(1)}, u32[]{:S(2)}, u32[]{:S(2)}) collective-permute-start(bf16[512,1024]{1,0:T(8,128)(2,1)} %add_convert_fusion.6), channel_id=1, source_target_pairs={{0,16},{1,17},{2,18},{3,19},{4,20},{5,21},{6,22},{7,23},{8,24},{9,... | collective-permute-start | bytes 3145736 | tf_op jit(solution)/shard_map/ppermute | solution.py:20
  635.0 40.3 %collective-permute-start.60 = (bf16[512,1024]{1,0:T(8,128)(2,1)}, bf16[512,1024]{1,0:T(8,128)(2,1)}, u32[]{:S(2)}, u32[]{:S(2)}) collective-permute-start(bf16[512,1024]{1,0:T(8,128)(2,1)} %fusion.34), channel_id=1, source_target_pairs={{16,0},{17,1},{18,2},{19,3},{20,4},{21,5},{22,6},{23,7},{24,8},{25... | collective-permute-start | bytes 3145736 | tf_op jit(solution)/shard_map/ppermute | solution.py:20
  637.1 36.1 %collective-permute-start.59 = (bf16[1,256,1024]{2,1,0:T(8,128)(2,1)}, bf16[1,256,1024]{2,1,0:T(8,128)(2,1)}, u32[]{:S(2)}, u32[]{:S(2)}) collective-permute-start(bf16[1,256,1024]{2,1,0:T(8,128)(2,1)} %slice_bitcast_fusion.3), channel_id=1, source_target_pairs={{16,0},{17,1},{18,2},{19,3},{20,4},{21,5},{22,6},{23,7},{24,8},{25... | collective-permute-start | bytes 1572872 | tf_op jit(solution)/shard_map/ppermute | solution.py:20
  844.3 170.7 %collective-permute-start.71 = (bf16[8,192,1024]{2,1,0:T(8,128)(2,1)}, bf16[8,192,1024]{2,1,0:T(8,128)(2,1)}, u32[]{:S(2)}, u32[]{:S(2)}) collective-permute-start(bf16[8,192,1024]{2,1,0:T(8,128)(2,1)} %get-tuple-element.47), channel_id=1, source_target_pairs={{0,1},{1,0},{2,3},{3,2},{4,5},{5,4},{6,7},{7,6},{8,9},{9,8},{10,11... | collective-permute-start | bytes 9437192 | tf_op jit(solution)/shard_map/ppermute | solution.py:92
  844.3 172.0 %collective-permute-start.63 = (bf16[8,192,1024]{2,1,0:T(8,128)(2,1)}, bf16[8,192,1024]{2,1,0:T(8,128)(2,1)}, u32[]{:S(2)}, u32[]{:S(2)}) collective-permute-start(bf16[8,192,1024]{2,1,0:T(8,128)(2,1)} %get-tuple-element.48), channel_id=1, source_target_pairs={{0,1},{1,0},{2,3},{3,2},{4,5},{5,4},{6,7},{7,6},{8,9},{9,8},{10,11... | collective-permute-start | bytes 9437192 | tf_op jit(solution)/shard_map/ppermute | solution.py:92
  913.7 132.2 %collective-permute-start.87 = (bf16[8,288,1024]{2,1,0:T(8,128)(2,1)}, bf16[8,288,1024]{2,1,0:T(8,128)(2,1)}, u32[]{:S(2)}, u32[]{:S(2)}) collective-permute-start(bf16[8,288,1024]{2,1,0:T(8,128)(2,1)} %get-tuple-element.43), channel_id=1, source_target_pairs={{0,1},{1,0},{2,3},{3,2},{4,5},{5,4},{6,7},{7,6},{8,9},{9,8},{10,11... | collective-permute-start | bytes 14155784 | tf_op jit(solution)/shard_map/ppermute | solution.py:92
  913.7 132.2 %collective-permute-start.79 = (bf16[8,288,1024]{2,1,0:T(8,128)(2,1)}, bf16[8,288,1024]{2,1,0:T(8,128)(2,1)}, u32[]{:S(2)}, u32[]{:S(2)}) collective-permute-start(bf16[8,288,1024]{2,1,0:T(8,128)(2,1)} %get-tuple-element.44), channel_id=1, source_target_pairs={{0,1},{1,0},{2,3},{3,2},{4,5},{5,4},{6,7},{7,6},{8,9},{9,8},{10,11... | collective-permute-start | bytes 14155784 | tf_op jit(solution)/shard_map/ppermute | solution.py:92
  928.7 107.3 %collective-permute-start.62 = (bf16[1,256,1024]{2,1,0:T(8,128)(2,1)S(1)}, bf16[1,256,1024]{2,1,0:T(8,128)(2,1)S(1)}, u32[]{:S(2)}, u32[]{:S(2)}) collective-permute-start(bf16[1,256,1024]{2,1,0:T(8,128)(2,1)S(1)} %slice_bitcast_fusion), channel_id=1, source_target_pairs={{0,16},{1,17},{2,18},{3,19},{4,20},{5,21},{6,22},{7,23},{8,24},{9,... | collective-permute-start | bytes 1572872 | tf_op jit(solution)/shard_map/ppermute | solution.py:20
  1053.4 24.2 %collective-permute-start.67 = (bf16[192,1024]{1,0:T(8,128)(2,1)S(1)}, bf16[192,1024]{1,0:T(8,128)(2,1)S(1)}, u32[]{:S(2)}, u32[]{:S(2)}) collective-permute-start(bf16[192,1024]{1,0:T(8,128)(2,1)S(1)} %fusion.112), channel_id=1, source_target_pairs={{0,4},{1,5},{4,8},{5,9},{8,12},{9,13},{12,14},{13,15},{14,10},{15,... | collective-permute-start | bytes 1179656 | tf_op jit(solution)/shard_map/ppermute | solution.py:103
  1055.0 23.1 %collective-permute-start.88 = (bf16[288,1024]{1,0:T(8,128)(2,1)S(1)}, bf16[288,1024]{1,0:T(8,128)(2,1)S(1)}, u32[]{:S(2)}, u32[]{:S(2)}) collective-permute-start(bf16[288,1024]{1,0:T(8,128)(2,1)S(1)} %dynamic-slice_bitcast_fusion.4), channel_id=1, source_target_pairs={{4,0},{5,1},{8,4},{9,5},{12,8},{13,9},{14,12},{15,13},{10,14},{11,... | collective-permute-start | bytes 1769480 | tf_op jit(solution)/shard_map/ppermute | solution.py:104
  1055.7 24.4 %collective-permute-start.75 = (bf16[192,1024]{1,0:T(8,128)(2,1)S(1)}, bf16[192,1024]{1,0:T(8,128)(2,1)S(1)}, u32[]{:S(2)}, u32[]{:S(2)}) collective-permute-start(bf16[192,1024]{1,0:T(8,128)(2,1)S(1)} %fusion.106), channel_id=1, source_target_pairs={{4,0},{5,1},{8,4},{9,5},{12,8},{13,9},{14,12},{15,13},{10,14},{11,... | collective-permute-start | bytes 1179656 | tf_op jit(solution)/shard_map/ppermute | solution.py:104
  1069.4 20.8 %collective-permute-start.81 = (bf16[288,1024]{1,0:T(8,128)(2,1)S(1)}, bf16[288,1024]{1,0:T(8,128)(2,1)S(1)}, u32[]{:S(2)}, u32[]{:S(2)}) collective-permute-start(bf16[288,1024]{1,0:T(8,128)(2,1)S(1)} %fusion.76), channel_id=1, source_target_pairs={{0,4},{1,5},{4,8},{5,9},{8,12},{9,13},{12,14},{13,15},{14,10},{15,... | collective-permute-start | bytes 1769480 | tf_op jit(solution)/shard_map/ppermute | solution.py:103
  1077.7 20.9 %collective-permute-start.68 = (bf16[192,1024]{1,0:T(8,128)(2,1)S(1)}, bf16[192,1024]{1,0:T(8,128)(2,1)S(1)}, u32[]{:S(2)}, u32[]{:S(2)}) collective-permute-start(bf16[192,1024]{1,0:T(8,128)(2,1)S(1)} %fusion.111), channel_id=1, source_target_pairs={{0,4},{1,5},{4,8},{5,9},{8,12},{9,13},{12,14},{13,15},{14,10},{15,... | collective-permute-start | bytes 1179656 | tf_op jit(solution)/shard_map/ppermute | solution.py:103
  1078.4 20.8 %collective-permute-start.89 = (bf16[288,1024]{1,0:T(8,128)(2,1)S(1)}, bf16[288,1024]{1,0:T(8,128)(2,1)S(1)}, u32[]{:S(2)}, u32[]{:S(2)}) collective-permute-start(bf16[288,1024]{1,0:T(8,128)(2,1)S(1)} %fusion.70), channel_id=1, source_target_pairs={{4,0},{5,1},{8,4},{9,5},{12,8},{13,9},{14,12},{15,13},{10,14},{11,... | collective-permute-start | bytes 1769480 | tf_op jit(solution)/shard_map/ppermute | solution.py:104
  1080.2 20.9 %collective-permute-start.76 = (bf16[192,1024]{1,0:T(8,128)(2,1)S(1)}, bf16[192,1024]{1,0:T(8,128)(2,1)S(1)}, u32[]{:S(2)}, u32[]{:S(2)}) collective-permute-start(bf16[192,1024]{1,0:T(8,128)(2,1)S(1)} %fusion.105), channel_id=1, source_target_pairs={{4,0},{5,1},{8,4},{9,5},{12,8},{13,9},{14,12},{15,13},{10,14},{11,... | collective-permute-start | bytes 1179656 | tf_op jit(solution)/shard_map/ppermute | solution.py:104
  1090.5 20.8 %collective-permute-start.82 = (bf16[288,1024]{1,0:T(8,128)(2,1)S(1)}, bf16[288,1024]{1,0:T(8,128)(2,1)S(1)}, u32[]{:S(2)}, u32[]{:S(2)}) collective-permute-start(bf16[288,1024]{1,0:T(8,128)(2,1)S(1)} %fusion.75), channel_id=1, source_target_pairs={{0,4},{1,5},{4,8},{5,9},{8,12},{9,13},{12,14},{13,15},{14,10},{15,... | collective-permute-start | bytes 1769480 | tf_op jit(solution)/shard_map/ppermute | solution.py:103
  1098.8 20.9 %collective-permute-start.69 = (bf16[192,1024]{1,0:T(8,128)(2,1)S(1)}, bf16[192,1024]{1,0:T(8,128)(2,1)S(1)}, u32[]{:S(2)}, u32[]{:S(2)}) collective-permute-start(bf16[192,1024]{1,0:T(8,128)(2,1)S(1)} %fusion.110), channel_id=1, source_target_pairs={{0,4},{1,5},{4,8},{5,9},{8,12},{9,13},{12,14},{13,15},{14,10},{15,... | collective-permute-start | bytes 1179656 | tf_op jit(solution)/shard_map/ppermute | solution.py:103
  1099.4 20.8 %collective-permute-start.90 = (bf16[288,1024]{1,0:T(8,128)(2,1)S(1)}, bf16[288,1024]{1,0:T(8,128)(2,1)S(1)}, u32[]{:S(2)}, u32[]{:S(2)}) collective-permute-start(bf16[288,1024]{1,0:T(8,128)(2,1)S(1)} %fusion.69), channel_id=1, source_target_pairs={{4,0},{5,1},{8,4},{9,5},{12,8},{13,9},{14,12},{15,13},{10,14},{11,... | collective-permute-start | bytes 1769480 | tf_op jit(solution)/shard_map/ppermute | solution.py:104
  1101.3 20.9 %collective-permute-start.77 = (bf16[192,1024]{1,0:T(8,128)(2,1)S(1)}, bf16[192,1024]{1,0:T(8,128)(2,1)S(1)}, u32[]{:S(2)}, u32[]{:S(2)}) collective-permute-start(bf16[192,1024]{1,0:T(8,128)(2,1)S(1)} %fusion.104), channel_id=1, source_target_pairs={{4,0},{5,1},{8,4},{9,5},{12,8},{13,9},{14,12},{15,13},{10,14},{11,... | collective-permute-start | bytes 1179656 | tf_op jit(solution)/shard_map/ppermute | solution.py:104
  1111.5 20.8 %collective-permute-start.83 = (bf16[288,1024]{1,0:T(8,128)(2,1)S(1)}, bf16[288,1024]{1,0:T(8,128)(2,1)S(1)}, u32[]{:S(2)}, u32[]{:S(2)}) collective-permute-start(bf16[288,1024]{1,0:T(8,128)(2,1)S(1)} %fusion.74), channel_id=1, source_target_pairs={{0,4},{1,5},{4,8},{5,9},{8,12},{9,13},{12,14},{13,15},{14,10},{15,... | collective-permute-start | bytes 1769480 | tf_op jit(solution)/shard_map/ppermute | solution.py:103
  1119.9 20.9 %collective-permute-start.70 = (bf16[192,1024]{1,0:T(8,128)(2,1)S(1)}, bf16[192,1024]{1,0:T(8,128)(2,1)S(1)}, u32[]{:S(2)}, u32[]{:S(2)}) collective-permute-start(bf16[192,1024]{1,0:T(8,128)(2,1)S(1)} %fusion.109), channel_id=1, source_target_pairs={{0,4},{1,5},{4,8},{5,9},{8,12},{9,13},{12,14},{13,15},{14,10},{15,... | collective-permute-start | bytes 1179656 | tf_op jit(solution)/shard_map/ppermute | solution.py:103
  (187 other events, 3509.2 us)
Sparse Core Ops, SparseCore 0:
  925.7 86.9 all-reduce.2

commit v2 on v1

v2 whole, which is shorter than its diff:
```python
import functools

import jax
import jax.numpy as jnp
from jax import lax
from jax.experimental import pallas as pl
from jax.experimental.pallas import tpu as pltpu
from jax.sharding import PartitionSpec as P

QUERY_HEADS = 16
KEY_VALUE_HEADS = 8
HEAD_SIZE = 128
TOKENS_PER_SHARD = 256


EPS = 1e-06
THETA = 1000000.0
NEGATIVE = -1e30
CONTRACT_ROWS = (((0,), (0,)), ((), ()))
CONTRACT_COLS = (((1,), (1,)), ((), ()))
RING_LEAD = 1


def one_way(value, source):
    return lax.ppermute(value, "section", [(source, 1 - source)])


def chip_at(place, chips):
    place = lax.rem(place + 2 * chips, chips)
    return jnp.where(place < chips // 2, 2 * place, 2 * (chips - 1 - place) + 1)


def ring_place(chip, chips):
    return jnp.where(chip % 2 == 0, chip // 2, chips - 1 - chip // 2)


def ring_routes(devices):
    chips = devices // 2
    order = list(range(0, chips, 2)) + list(range(chips - 1, 0, -2))
    right, left = [], []
    for place in range(chips):
        here, there = order[place], order[(place + 1) % chips]
        for core in range(2):
            right.append((2 * here + core, 2 * there + core))
            left.append((2 * there + core, 2 * here + core))
    return right, left, [(device, device ^ 1) for device in range(devices)]


def spread(value):
    devices = lax.axis_size("dp")
    index = lax.axis_index("dp")
    step = 1
    while step < devices:
        other = lax.ppermute(value, "dp", [(low, low ^ step) for low in range(devices)])
        later = (index // step) % 2 == 1
        value = jnp.where(
            later,
            jnp.concatenate([other, value], axis=0),
            jnp.concatenate([value, other], axis=0),
        )
        step *= 2
    return value


def summed(value):
    devices = lax.axis_size("dp")
    step = 1
    while step < devices:
        value = value + lax.ppermute(value, "dp", [(low, low ^ step) for low in range(devices)])
        step *= 2
    return value


def blank(shape, dtype):
    return pl.pallas_call(
        lambda ref: None,
        out_specs=pl.BlockSpec(memory_space=pl.ANY),
        out_shape=jax.ShapeDtypeStruct(shape, dtype),
    )()


def gather_ring(shard, after=None):
    devices = lax.axis_size("dp")
    chips = devices // 2
    right, left, pair = ring_routes(devices)
    index = lax.axis_index("dp")
    core = index % 2
    place = ring_place(index // 2, chips)
    half = shard.shape[0] // 2
    if after is not None:
        shard, after = lax.optimization_barrier((shard, after))
    whole = blank((devices,) + shard.shape, shard.dtype)

    def put(whole, piece, owner, offset):
        return lax.dynamic_update_slice(whole, piece[None], (owner, offset, 0))

    forward, behind = shard[:half], shard[half:]
    marks = []
    other = lax.ppermute(shard, "dp", pair)
    whole = put(whole, shard, index, 0)
    whole = put(whole, other, index + 1 - 2 * core, 0)
    for step in range(1, chips):
        forward = lax.ppermute(forward, "dp", right)
        behind = lax.ppermute(behind, "dp", left)
        marks.append((forward, behind))
        forward_pair = lax.ppermute(forward, "dp", pair)
        behind_pair = lax.ppermute(behind, "dp", pair)
        owner = 2 * chip_at(place - step, chips)
        whole = put(whole, forward, owner + core, 0)
        whole = put(whole, forward_pair, owner + 1 - core, 0)
        owner = 2 * chip_at(place + step, chips)
        whole = put(whole, behind, owner + core, half)
        whole = put(whole, behind_pair, owner + 1 - core, half)
    return whole, marks


def scatter_ring(forward_parts, behind_parts):
    devices = lax.axis_size("dp")
    chips = devices // 2
    right, left, pair = ring_routes(devices)
    sums = []
    for mine, theirs in (forward_parts, behind_parts):
        got = lax.ppermute(theirs, "dp", pair)
        sums.append((mine, got))

    def own(which, place):
        mine, got = sums[which]
        return mine[place].astype(jnp.float32) + got[place].astype(jnp.float32)

    forward = own(0, chips - 1)
    behind = own(1, 1)
    for step in range(1, chips):
        forward = lax.ppermute(forward.astype(jnp.bfloat16), "dp", right).astype(jnp.float32)
        behind = lax.ppermute(behind.astype(jnp.bfloat16), "dp", left).astype(jnp.float32)
        forward = forward + own(0, chips - 1 - step)
        behind = behind + own(1, (step + 1) % chips)
    return jnp.concatenate([forward, behind], axis=0)


def packed(shard, width):
    pieces = shard.shape[-1] // width
    return [shard[:, width * i : width * (i + 1)] for i in range(pieces)]


def beside(grad, low, pieces, rows):
    return jnp.concatenate(
        [grad[low + rows * i : low + rows * (i + 1)] for i in range(pieces)], axis=1
    )


def layout(lengths_row):
    ends = jnp.cumsum(lengths_row)
    places = jnp.arange(TOKENS_PER_SHARD, dtype=jnp.int32)
    passed = (ends[None, :] <= places[:, None]).astype(jnp.int32)
    segment_index = jnp.sum(passed, axis=1)
    start = jnp.sum(passed * lengths_row[None, :], axis=1)
    return (segment_index, places - start)


def rotary_tables(place):
    half = HEAD_SIZE // 2
    freqs = THETA ** (-(jnp.arange(half, dtype=jnp.float32) * 2.0 / HEAD_SIZE))
    angles = place.astype(jnp.float32)[:, None] * freqs[None, :]
    return (jnp.cos(angles), jnp.sin(angles))


def wide_call(body, grid, in_specs, out_specs, out_shape, scratch=(), flops=0, moved=0, prefetch=0, vmem=48):
    return pl.pallas_call(
        body,
        grid_spec=pltpu.PrefetchScalarGridSpec(
            num_scalar_prefetch=prefetch,
            grid=grid,
            in_specs=in_specs,
            out_specs=out_specs,
            scratch_shapes=list(scratch),
        ),
        out_shape=out_shape,
        compiler_params=pltpu.CompilerParams(vmem_limit_bytes=vmem << 20),
        cost_estimate=pl.CostEstimate(
            flops=int(flops), bytes_accessed=int(moved), transcendentals=0
        ),
    )


def whole_spec(shape):
    return pl.BlockSpec(shape, lambda *_: (0,) * len(shape))


def dot_plain(left, right):
    return jnp.dot(left, right, preferred_element_type=jnp.float32)


def dot_columns(left, right):
    return lax.dot_general(left, right, CONTRACT_COLS, preferred_element_type=jnp.float32)


def dot_rows(left, right):
    return lax.dot_general(left, right, CONTRACT_ROWS, preferred_element_type=jnp.float32)


def unit_rows(values):
    factor = lax.rsqrt(jnp.mean(values * values, axis=-1, keepdims=True) + EPS)
    return values * factor, factor


def norm_pull(grad, scaled, factor, gain):
    pulled = grad * gain
    return factor * (pulled - scaled * jnp.mean(pulled * scaled, axis=-1, keepdims=True))


def square(ref):
    value = ref[...]
    return value.reshape(value.shape[0] * value.shape[1], value.shape[2])


def qkv_kernel(h_ref, gain_ref, gain_q_ref, gain_k_ref, cos_ref, sin_ref, w_ref, xa_ref, qkv_ref, pre_ref):
    step = pl.program_id(0)

    @pl.when(step == 0)
    def _():
        scaled, _ = unit_rows(h_ref[...].astype(jnp.float32))
        xa_ref[...] = (scaled * gain_ref[...]).astype(jnp.bfloat16)

    pre = dot_plain(xa_ref[...], square(w_ref))

    @pl.when(step < 3)
    def _():
        pre_ref[...] = pre.astype(jnp.bfloat16)
        gain = jnp.where(step < 2, gain_q_ref[...], gain_k_ref[...])
        cosine, sine = cos_ref[...], sin_ref[...]
        for head in range(pre.shape[1] // HEAD_SIZE):
            part = slice(head * HEAD_SIZE, (head + 1) * HEAD_SIZE)
            scaled, _ = unit_rows(pre[:, part])
            scaled = scaled * gain
            turned = scaled * cosine + pltpu.roll(scaled, HEAD_SIZE // 2, 1) * sine
            qkv_ref[:, part] = turned.astype(jnp.bfloat16)

    @pl.when(step == 3)
    def _():
        qkv_ref[...] = pre.astype(jnp.bfloat16)


def project_qkv(hidden, gains, tables, whole):
    devices, rows, model = whole.shape
    rows = rows // 6
    tokens = hidden.shape[0]
    cosine, sine = tables[:2]
    return wide_call(
        qkv_kernel,
        (4,),
        [
            whole_spec((tokens, model)),
            whole_spec((1, model)),
            whole_spec((1, HEAD_SIZE)),
            whole_spec((1, HEAD_SIZE)),
            whole_spec((tokens, HEAD_SIZE)),
            whole_spec((tokens, HEAD_SIZE)),
            pl.BlockSpec((devices, rows, model), lambda j: (0, j + 2 * (j // 2), 0)),
        ],
        [
            whole_spec((tokens, model)),
            pl.BlockSpec((tokens, model), lambda j: (0, j)),
            pl.BlockSpec((tokens, model), lambda j: (0, jnp.minimum(j, 2))),
        ],
        [
            jax.ShapeDtypeStruct((tokens, model), jnp.bfloat16),
            jax.ShapeDtypeStruct((tokens, 4 * model), jnp.bfloat16),
            jax.ShapeDtypeStruct((tokens, 3 * model), jnp.bfloat16),
        ],
        flops=2 * tokens * model * 4 * model,
        moved=8 * model * model + 18 * tokens * model,
    )(hidden, gains[0], gains[1], gains[2], cosine, sine, whole)


HEADS_PER_STEP = 4


def attend_kernel(q_ref, k_ref, v_ref, row_ref, column_ref, o_ref):
    tokens = k_ref.shape[0]
    causal = lax.broadcasted_iota(jnp.int32, (tokens, tokens), 0) >= lax.broadcasted_iota(
        jnp.int32, (tokens, tokens), 1
    )
    allowed = (row_ref[...] == column_ref[0]) & causal
    for head in range(2 * HEADS_PER_STEP):
        part = slice(head * HEAD_SIZE, (head + 1) * HEAD_SIZE)
        shared = slice(head // 2 * HEAD_SIZE, (head // 2 + 1) * HEAD_SIZE)
        scores = dot_columns(q_ref[:, part], k_ref[:, shared]) * HEAD_SIZE ** (-0.5)
        scores = jnp.where(allowed, scores, NEGATIVE)
        raised = jnp.exp(scores - jnp.max(scores, axis=-1, keepdims=True))
        weights = raised * (1.0 / jnp.sum(raised, axis=-1, keepdims=True))
        mixed = dot_plain(weights.astype(jnp.bfloat16), v_ref[:, shared])
        o_ref[:, part] = mixed.astype(jnp.bfloat16)


def attend(qkv, tables):
    row_segments, column_segments = tables[2:]
    tokens = qkv.shape[0]
    blocks = tokens // TOKENS_PER_SHARD
    groups = KEY_VALUE_HEADS // HEADS_PER_STEP
    wide = HEADS_PER_STEP * HEAD_SIZE
    return wide_call(
        attend_kernel,
        (blocks, groups),
        [
            pl.BlockSpec((TOKENS_PER_SHARD, 2 * wide), lambda b, g: (b, g)),
            pl.BlockSpec((TOKENS_PER_SHARD, wide), lambda b, g: (b, 2 * groups + g)),
            pl.BlockSpec((TOKENS_PER_SHARD, wide), lambda b, g: (b, 3 * groups + g)),
            pl.BlockSpec((TOKENS_PER_SHARD, 1), lambda b, g: (b, 0)),
            pl.BlockSpec((1, 1, TOKENS_PER_SHARD), lambda b, g: (b, 0, 0)),
        ],
        pl.BlockSpec((TOKENS_PER_SHARD, 2 * wide), lambda b, g: (b, g)),
        jax.ShapeDtypeStruct((tokens, QUERY_HEADS * HEAD_SIZE), jnp.bfloat16),
        flops=16 * tokens * TOKENS_PER_SHARD * QUERY_HEADS * HEAD_SIZE,
        moved=12 * tokens * 1024,
    )(qkv, qkv, qkv, row_segments, column_segments)


def out_kernel(o_ref, w_ref, h_ref, gain_ref, hm_ref, xf_ref, total):
    step = pl.program_id(0)
    term = dot_plain(o_ref[...], square(w_ref))

    @pl.when(step == 0)
    def _():
        total[...] = h_ref[...].astype(jnp.float32) + term

    @pl.when(step > 0)
    def _():
        total[...] += term

    @pl.when(step == pl.num_programs(0) - 1)
    def _():
        middle = total[...]
        hm_ref[...] = middle
        scaled, _ = unit_rows(middle)
        xf_ref[...] = (scaled * gain_ref[...]).astype(jnp.bfloat16)


def project_out(mixed, whole, hidden, gains):
    devices, rows, model = whole.shape
    rows = rows // 6
    tokens, wide = mixed.shape
    return wide_call(
        out_kernel,
        (4,),
        [
            pl.BlockSpec((tokens, wide // 4), lambda c: (0, c)),
            pl.BlockSpec((devices // 4, 2 * rows, model), lambda c: (c, 1, 0)),
            whole_spec((tokens, model)),
            whole_spec((1, model)),
        ],
        [whole_spec((tokens, model)), whole_spec((tokens, model))],
        [
            jax.ShapeDtypeStruct((tokens, model), jnp.float32),
            jax.ShapeDtypeStruct((tokens, model), jnp.bfloat16),
        ],
        scratch=[pltpu.VMEM((tokens, model), jnp.float32)],
        flops=2 * tokens * wide * model,
        moved=2 * wide * model + 12 * tokens * model,
    )(mixed, whole, hidden, gains[3])


def ffn_kernel(chunk, xf_ref, hm_ref, gate_ref, up_ref, down_ref, *rest):
    outs, (inner, total) = rest[:-2], rest[-2:]
    step = pl.program_id(0)
    model = xf_ref.shape[1]

    @pl.when(step < 3)
    def _():
        xf = xf_ref[...]
        gate = dot_plain(xf, square(gate_ref))
        up = dot_plain(xf, square(up_ref))
        mixed = (gate * jax.nn.sigmoid(gate) * up).astype(jnp.bfloat16)
        inner[:, pl.ds(pl.multiple_of(step * model, model), model)] = mixed
        if len(outs) > 1:
            outs[1][...] = gate.astype(jnp.bfloat16)
            outs[2][...] = up.astype(jnp.bfloat16)
            outs[3][...] = mixed

    @pl.when(step >= 3)
    def _():
        place = pl.multiple_of((step - 3) * chunk, 128)
        term = dot_plain(inner[:, pl.ds(place, chunk)], square(down_ref))

        @pl.when(step == 3)
        def _():
            total[...] = hm_ref[...] + term

        @pl.when(step > 3)
        def _():
            total[...] += term

        @pl.when(step == pl.num_programs(0) - 1)
        def _():
            outs[0][...] = total[...].astype(jnp.bfloat16)


def feed_forward(normed, middle, whole, keep):
    devices, rows, model = whole.shape
    rows = rows // 9
    tokens = normed.shape[0]
    width = 3 * model
    chunk = width // 4
    column = pl.BlockSpec((tokens, model), lambda i: (0, jnp.minimum(i, 2)))
    shapes = [jax.ShapeDtypeStruct((tokens, model), jnp.bfloat16)]
    specs = [whole_spec((tokens, model))]
    if keep:
        shapes += [jax.ShapeDtypeStruct((tokens, width), jnp.bfloat16)] * 3
        specs += [column] * 3
    return wide_call(
        functools.partial(ffn_kernel, chunk),
        (7,),
        [
            whole_spec((tokens, model)),
            whole_spec((tokens, model)),
            pl.BlockSpec((devices, rows, model), lambda i: (0, jnp.minimum(i, 2), 0)),
            pl.BlockSpec((devices, rows, model), lambda i: (0, 6 + jnp.minimum(i, 2), 0)),
            pl.BlockSpec(
                (devices // 4, 3 * rows, model), lambda i: (jnp.maximum(i - 3, 0), 1, 0)
            ),
        ],
        specs,
        shapes,
        scratch=[
            pltpu.VMEM((tokens, width), jnp.bfloat16),
            pltpu.VMEM((tokens, model), jnp.float32),
        ],
        flops=6 * tokens * width * model,
        moved=6 * width * model + 8 * tokens * model + (6 * tokens * width if keep else 0),
    )(normed, middle, whole, whole, whole)


def ffn_back_kernel(
    chunk, dy_ref, hm_ref, gain_ref, g_ref, u_ref, gate_ref, up_ref, down_ref,
    dh_ref, low_ref, dg_ref, du_ref, dgain_ref, dg_all, du_all, low_dy, total,
):
    step = pl.program_id(0)
    model = hm_ref.shape[1]

    @pl.when(step == 0)
    def _():
        low_dy[...] = dy_ref[...].astype(jnp.bfloat16)

    @pl.when(step < 4)
    def _():
        d_inner = dot_columns(low_dy[...], square(down_ref))
        gate = g_ref[...].astype(jnp.float32)
        sigma = jax.nn.sigmoid(gate)
        silu = gate * sigma
        d_gate = (
            d_inner * u_ref[...].astype(jnp.float32) * (sigma + silu * (1.0 - sigma))
        ).astype(jnp.bfloat16)
        d_up = (d_inner * silu).astype(jnp.bfloat16)
        place = pl.multiple_of(step * chunk, 128)
        dg_all[:, pl.ds(place, chunk)] = d_gate
        du_all[:, pl.ds(place, chunk)] = d_up
        dg_ref[...] = d_gate
        du_ref[...] = d_up

    @pl.when(step >= 4)
    def _():
        place = pl.ds(pl.multiple_of((step - 4) * model, 128), model)
        term = dot_columns(dg_all[:, place], square(gate_ref)) + dot_columns(
            du_all[:, place], square(up_ref)
        )

        @pl.when(step == 4)
        def _():
            total[...] = term

        @pl.when(step > 4)
        def _():
            total[...] += term

        @pl.when(step == pl.num_programs(0) - 1)
        def _():
            grad = total[...]
            scaled, factor = unit_rows(hm_ref[...])
            dgain_ref[...] = jnp.sum(grad * scaled, axis=0, keepdims=True)
            d_hidden = dy_ref[...] + norm_pull(grad, scaled, factor, gain_ref[...])
            dh_ref[...] = d_hidden
            low_ref[...] = d_hidden.astype(jnp.bfloat16)


def feed_forward_back(d_result, middle, gains, gate, up, whole):
    devices, rows, model = whole.shape
    rows = rows // 9
    tokens = middle.shape[0]
    width = 3 * model
    chunk = width // 4
    column = pl.BlockSpec((tokens, chunk), lambda i: (0, jnp.minimum(i, 3)))
    full = whole_spec((tokens, model))
    return wide_call(
        functools.partial(ffn_back_kernel, chunk),
        (7,),
        [
            full,
            full,
            whole_spec((1, model)),
            column,
            column,
            pl.BlockSpec((devices, rows, model), lambda i: (0, jnp.maximum(i - 4, 0), 0)),
            pl.BlockSpec((devices, rows, model), lambda i: (0, 6 + jnp.maximum(i - 4, 0), 0)),
            pl.BlockSpec((devices // 4, 3 * rows, model), lambda i: (jnp.minimum(i, 3), 1, 0)),
        ],
        [full, full, column, column, whole_spec((1, model))],
        [
            jax.ShapeDtypeStruct((tokens, model), jnp.float32),
            jax.ShapeDtypeStruct((tokens, model), jnp.bfloat16),
            jax.ShapeDtypeStruct((tokens, width), jnp.bfloat16),
            jax.ShapeDtypeStruct((tokens, width), jnp.bfloat16),
            jax.ShapeDtypeStruct((1, model), jnp.float32),
        ],
        scratch=[
            pltpu.VMEM((tokens, width), jnp.bfloat16),
            pltpu.VMEM((tokens, width), jnp.bfloat16),
            pltpu.VMEM((tokens, model), jnp.bfloat16),
            pltpu.VMEM((tokens, model), jnp.float32),
        ],
        flops=6 * tokens * width * model,
        moved=6 * width * model + 14 * tokens * model + 8 * tokens * width,
        vmem=56,
    )(d_result, middle, gains[3], gate, up, whole, whole, whole)


def out_back_kernel(d_ref, w_ref, o_ref):
    o_ref[...] = dot_columns(d_ref[...], square(w_ref)).astype(jnp.bfloat16)


def project_out_back(low, whole):
    devices, rows, model = whole.shape
    rows = rows // 6
    tokens = low.shape[0]
    wide = QUERY_HEADS * HEAD_SIZE
    return wide_call(
        out_back_kernel,
        (4,),
        [
            whole_spec((tokens, model)),
            pl.BlockSpec((devices // 4, 2 * rows, model), lambda c: (c, 1, 0)),
        ],
        pl.BlockSpec((tokens, wide // 4), lambda c: (0, c)),
        jax.ShapeDtypeStruct((tokens, wide), jnp.bfloat16),
        flops=2 * tokens * wide * model,
        moved=2 * wide * model + 6 * tokens * model,
    )(low, whole)


BACK_HEADS = 4


def attend_back_kernel(
    q_ref, k_ref, v_ref, do_ref, pre_q_ref, pre_k_ref, row_ref, column_ref, cos_ref, sin_ref,
    gain_q_ref, gain_k_ref, dq_ref, dk_ref, dv_ref, dgain_q_ref, dgain_k_ref,
):
    tokens = k_ref.shape[0]
    first = (pl.program_id(0) == 0) & (pl.program_id(1) == 0)

    @pl.when(first)
    def _():
        dgain_q_ref[...] = jnp.zeros_like(dgain_q_ref)
        dgain_k_ref[...] = jnp.zeros_like(dgain_k_ref)

    causal = lax.broadcasted_iota(jnp.int32, (tokens, tokens), 0) <= lax.broadcasted_iota(
        jnp.int32, (tokens, tokens), 1
    )
    allowed = (row_ref[...] == column_ref[0]) & causal
    cosine, sine = cos_ref[...], sin_ref[...]
    scale = HEAD_SIZE ** (-0.5)

    def through_norm(grad, pre, gain, dgain_ref):
        grad = grad * cosine - pltpu.roll(grad, HEAD_SIZE // 2, 1) * sine
        scaled, factor = unit_rows(pre.astype(jnp.float32))
        dgain_ref[...] += jnp.sum(grad * scaled, axis=0, keepdims=True)
        return norm_pull(grad, scaled, factor, gain).astype(jnp.bfloat16)

    for shared in range(BACK_HEADS):
        lone = slice(shared * HEAD_SIZE, (shared + 1) * HEAD_SIZE)
        key, value = k_ref[:, lone], v_ref[:, lone]
        d_key = d_value = None
        for head in range(2 * shared, 2 * shared + 2):
            part = slice(head * HEAD_SIZE, (head + 1) * HEAD_SIZE)
            query, d_mixed = q_ref[:, part], do_ref[:, part]
            scores = dot_columns(key, query) * scale
            scores = jnp.where(allowed, scores, NEGATIVE)
            raised = jnp.exp(scores - jnp.max(scores, axis=0, keepdims=True))
            weights = raised * (1.0 / jnp.sum(raised, axis=0, keepdims=True))
            value_term = dot_plain(weights.astype(jnp.bfloat16), d_mixed)
            d_weights = dot_columns(value, d_mixed)
            pulled = jnp.sum(d_weights * weights, axis=0, keepdims=True)
            d_scores = (weights * (d_weights - pulled)).astype(jnp.bfloat16)
            d_query = dot_rows(d_scores, key) * scale
            key_term = dot_plain(d_scores, query)
            d_key = key_term if d_key is None else d_key + key_term
            d_value = value_term if d_value is None else d_value + value_term
            dq_ref[:, part] = through_norm(d_query, pre_q_ref[:, part], gain_q_ref[...], dgain_q_ref)
        dk_ref[:, lone] = through_norm(
            d_key * scale, pre_k_ref[:, lone], gain_k_ref[...], dgain_k_ref
        )
        dv_ref[:, lone] = d_value.astype(jnp.bfloat16)


def attend_back(qkv, pre, d_mixed, tables, gains):
    cosine, sine, row_segments, column_segments = tables
    tokens = qkv.shape[0]
    blocks = tokens // TOKENS_PER_SHARD
    groups = KEY_VALUE_HEADS // BACK_HEADS
    wide = BACK_HEADS * HEAD_SIZE
    model = KEY_VALUE_HEADS * HEAD_SIZE
    pair = pl.BlockSpec((TOKENS_PER_SHARD, 2 * wide), lambda b, g: (b, g))
    lone = pl.BlockSpec((TOKENS_PER_SHARD, wide), lambda b, g: (b, g))
    table = pl.BlockSpec((TOKENS_PER_SHARD, HEAD_SIZE), lambda b, g: (b, 0))
    return wide_call(
        attend_back_kernel,
        (blocks, groups),
        [
            pair,
            pl.BlockSpec((TOKENS_PER_SHARD, wide), lambda b, g: (b, 2 * groups + g)),
            pl.BlockSpec((TOKENS_PER_SHARD, wide), lambda b, g: (b, 3 * groups + g)),
            pair,
            pair,
            pl.BlockSpec((TOKENS_PER_SHARD, wide), lambda b, g: (b, 2 * groups + g)),
            pl.BlockSpec((TOKENS_PER_SHARD, 1), lambda b, g: (b, 0)),
            pl.BlockSpec((1, 1, TOKENS_PER_SHARD), lambda b, g: (b, 0, 0)),
            table,
            table,
            whole_spec((1, HEAD_SIZE)),
            whole_spec((1, HEAD_SIZE)),
        ],
        [pair, lone, lone, whole_spec((1, HEAD_SIZE)), whole_spec((1, HEAD_SIZE))],
        [
            jax.ShapeDtypeStruct((tokens, 2 * model), jnp.bfloat16),
            jax.ShapeDtypeStruct((tokens, model), jnp.bfloat16),
            jax.ShapeDtypeStruct((tokens, model), jnp.bfloat16),
            jax.ShapeDtypeStruct((1, HEAD_SIZE), jnp.float32),
            jax.ShapeDtypeStruct((1, HEAD_SIZE), jnp.float32),
        ],
        flops=32 * tokens * TOKENS_PER_SHARD * QUERY_HEADS * HEAD_SIZE,
        moved=30 * tokens * 1024,
    )(
        qkv, qkv, qkv, d_mixed, pre, pre, row_segments, column_segments, cosine, sine,
        gains[1], gains[2],
    )


def qkv_back_kernel(dq_ref, dk_ref, dv_ref, w_ref, h_ref, dh_ref, gain_ref, dx_ref, dgain_ref, total):
    step = pl.program_id(0)
    model = h_ref.shape[1]

    def add(part):
        term = dot_columns(part, square(w_ref))

        @pl.when(step == 0)
        def _():
            total[...] = term

        @pl.when(step > 0)
        def _():
            total[...] += term

    @pl.when(step < 2)
    def _():
        add(dq_ref[:, pl.ds(pl.multiple_of(step * model, 128), model)])

    @pl.when(step == 2)
    def _():
        add(dk_ref[...])

    @pl.when(step == 3)
    def _():
        add(dv_ref[...])
        grad = total[...]
        scaled, factor = unit_rows(h_ref[...].astype(jnp.float32))
        dgain_ref[...] = jnp.sum(grad * scaled, axis=0, keepdims=True)
        d_hidden = dh_ref[...] + norm_pull(grad, scaled, factor, gain_ref[...])
        dx_ref[...] = d_hidden.astype(jnp.bfloat16)


def project_qkv_back(d_query, d_key, d_value, whole, hidden, d_middle, gains):
    devices, rows, model = whole.shape
    rows = rows // 6
    tokens = hidden.shape[0]
    full = whole_spec((tokens, model))
    return wide_call(
        qkv_back_kernel,
        (4,),
        [
            whole_spec((tokens, 2 * model)),
            full,
            full,
            pl.BlockSpec((devices, rows, model), lambda j: (0, j + 2 * (j // 2), 0)),
            full,
            full,
            whole_spec((1, model)),
        ],
        [full, whole_spec((1, model))],
        [
            jax.ShapeDtypeStruct((tokens, model), jnp.bfloat16),
            jax.ShapeDtypeStruct((1, model), jnp.float32),
        ],
        scratch=[pltpu.VMEM((tokens, model), jnp.float32)],
        flops=8 * tokens * model * model,
        moved=8 * model * model + 16 * tokens * model,
    )(d_query, d_key, d_value, whole, hidden, d_middle, gains[0])


def grad_kernel(plan, chips, order_ref, *refs):
    count = len(plan)
    lefts, rights = refs[:count], refs[count : 2 * count]
    mine_ref, theirs_ref = refs[2 * count : 2 * count + 2]
    stores = refs[2 * count + 2 :]
    step = pl.program_id(0)
    core = order_ref[chips]

    @pl.when(step == 0)
    def _():
        for index, (rows, low, size, unit, start, blocks) in enumerate(plan):
            turned, mine, theirs = stores[3 * index : 3 * index + 3]
            turned[...] = jnp.transpose(lefts[index][...])

            def place(t, _, rows=rows, low=low, size=size, turned=turned, mine=mine, theirs=theirs):
                here = (2 * order_ref[t] + core) * rows + low
                there = (2 * order_ref[t] + 1 - core) * rows + low
                mine[t] = turned[pl.ds(pl.multiple_of(here, 16), size), :]
                theirs[t] = turned[pl.ds(pl.multiple_of(there, 16), size), :]
                return 0

            lax.fori_loop(0, chips, place, 0)

    for index, (rows, low, size, unit, start, blocks) in enumerate(plan):
        turned, mine, theirs = stores[3 * index : 3 * index + 3]
        split = size // unit

        @pl.when((step >= start) & (step < start + split * blocks))
        def _(index=index, unit=unit, start=start, split=split, mine=mine, theirs=theirs):
            part = pl.ds(pl.multiple_of(lax.rem(step - start, split) * unit, 16), unit)
            right = rights[index][...]
            for source, target in ((theirs, theirs_ref), (mine, mine_ref)):
                left = source[:, part, :]
                left = left.reshape(chips * unit, left.shape[2])
                value = dot_plain(left, right).astype(jnp.bfloat16)
                target[...] = value.reshape(target.shape)


def weight_grads(order, parts, unit):
    tokens = parts[0][0].shape[0]
    model = parts[0][4]
    chips = order.shape[0] - 1
    plan, specs_left, specs_right, scratch, start, flops = [], [], [], [], 0, 0
    for left, right, low, size, width in parts:
        rows = left.shape[1] // (2 * chips)
        blocks = right.shape[1] // width
        split = size // unit
        plan.append((rows, low, size, unit, start, blocks))
        specs_left.append(whole_spec(left.shape))

        def column(i, _, start=start, split=split, blocks=blocks):
            return (0, jnp.clip((i - start) // split, 0, blocks - 1))

        specs_right.append(pl.BlockSpec((tokens, width), column))
        scratch += [
            pltpu.VMEM((left.shape[1], tokens), jnp.bfloat16),
            pltpu.VMEM((chips, size, tokens), jnp.bfloat16),
            pltpu.VMEM((chips, size, tokens), jnp.bfloat16),
        ]
        start += split * blocks
        flops += 4 * chips * size * blocks * width * tokens
    out = pl.BlockSpec((chips, unit, model), lambda i, _: (0, i, 0))
    shape = jax.ShapeDtypeStruct((chips, start * unit, model), jnp.bfloat16)
    return wide_call(
        functools.partial(grad_kernel, tuple(plan), chips),
        (start,),
        specs_left + specs_right,
        [out, out],
        [shape, shape],
        scratch=scratch,
        flops=flops,
        moved=flops // tokens * 2,
        prefetch=1,
        vmem=56,
    )(order, *[part[0] for part in parts], *[part[1] for part in parts])


def local(
    inputs,
    teacher,
    lengths,
    attn_query,
    attn_key,
    attn_value,
    attn_out,
    ffn_gate,
    ffn_up,
    ffn_down,
    norm_attn,
    norm_ffn,
    norm_query,
    norm_key,
):
    section = lax.axis_index("section")
    index = lax.axis_index("dp")
    devices = lax.axis_size("dp")
    chips = devices // 2
    batches, _, model = inputs.shape
    slots = lengths.shape[2]
    tokens = batches * TOKENS_PER_SHARD
    rows = attn_query.shape[1]
    forward_rows = ffn_down.shape[1]

    attn_shard = jnp.concatenate(
        packed(attn_query[0], model)
        + [attn_out[0]]
        + packed(attn_key[0], model)
        + packed(attn_value[0], model),
        axis=0,
    )
    ffn_shard = jnp.concatenate(
        packed(ffn_gate[0], model) + [ffn_down[0]] + packed(ffn_up[0], model), axis=0
    )
    attn_whole, marks = gather_ring(attn_shard)
    ffn_whole, _ = gather_ring(ffn_shard, marks[RING_LEAD])

    gain_sizes = (norm_attn.shape[1], norm_query.shape[1], norm_key.shape[1], norm_ffn.shape[1])
    gain_shard = jnp.concatenate([norm_attn, norm_query, norm_key, norm_ffn], axis=1)
    gain_whole = spread(gain_shard.astype(jnp.float32))
    gains, low = [], 0
    for size in gain_sizes:
        gains.append(gain_whole[:, low : low + size].reshape(1, devices * size))
        low += size

    segments, places = jax.vmap(layout)(lengths[:, 0, :])
    keep = (segments < slots - 1).astype(jnp.float32).reshape(tokens)
    cosine_table, sine_table = rotary_tables(places.reshape(tokens))
    tables = (
        jnp.concatenate([cosine_table, cosine_table], axis=1),
        jnp.concatenate([-sine_table, sine_table], axis=1),
        segments.reshape(tokens, 1),
        segments.reshape(batches, 1, TOKENS_PER_SHARD),
    )

    first = inputs.reshape(tokens, model)
    _, qkv, _ = project_qkv(first, gains, tables, attn_whole)
    mixed = attend(qkv, tables)
    middle, normed = project_out(mixed, attn_whole, first, gains)
    (result,) = feed_forward(normed, middle, ffn_whole, False)
    carried = one_way(result, 0)

    hidden = jnp.where(section == 0, first, carried)
    normalized, qkv, pre = project_qkv(hidden, gains, tables, attn_whole)
    mixed = attend(qkv, tables)
    middle, normed = project_out(mixed, attn_whole, hidden, gains)
    result, gate, up, inner = feed_forward(normed, middle, ffn_whole, True)

    diff = result.astype(jnp.float32) - teacher.reshape(tokens, model)
    cotangent = keep[:, None] * diff
    squares = jnp.sum(cotangent * diff)

    def backward(d_result):
        d_middle, d_attn, d_gate, d_up, gain_ffn = feed_forward_back(
            d_result, middle, gains, gate, up, ffn_whole
        )
        d_mixed = project_out_back(d_attn, attn_whole)
        d_query, d_key, d_value, gain_query, gain_key = attend_back(
            qkv, pre, d_mixed, tables, gains
        )
        d_hidden, gain_attn = project_qkv_back(
            d_query, d_key, d_value, attn_whole, hidden, d_middle, gains
        )
        gain_grads = (gain_attn, gain_query, gain_key, gain_ffn)
        return d_hidden, d_attn, d_gate, d_up, d_query, d_key, d_value, gain_grads

    d_hidden = backward(cotangent)[0]
    incoming = one_way(d_hidden, 1)
    d_result = jnp.where(section == 1, cotangent, incoming.astype(jnp.float32))
    d_hidden, d_attn, d_gate, d_up, d_query, d_key, d_value, gain_grads = backward(d_result)

    core = index % 2
    place = ring_place(index // 2, chips)
    order = jnp.concatenate(
        [chip_at(place + jnp.arange(chips, dtype=jnp.int32), chips), core[None]]
    ).astype(jnp.int32)
    d_branch = d_result.astype(jnp.bfloat16)
    unit = rows // 2 if rows % 32 == 0 else rows
    cut = forward_rows // 2 if forward_rows // 2 % unit == 0 else 2 * unit
    ffn_grad = scatter_ring(
        weight_grads(
            order, [(normed, d_gate, 0, rows, model), (inner, d_branch, 0, cut, model)], unit
        ),
        weight_grads(
            order,
            [
                (inner, d_branch, cut, forward_rows - cut, model),
                (normed, d_up, 0, rows, model),
            ],
            unit,
        ),
    )
    attn_grad = scatter_ring(
        weight_grads(
            order, [(normalized, d_query, 0, rows, model), (mixed, d_attn, 0, rows, model)], rows
        ),
        weight_grads(
            order,
            [
                (mixed, d_attn, rows, rows, model),
                (normalized, d_key, 0, rows, model),
                (normalized, d_value, 0, rows, model),
            ],
            rows,
        ),
    )

    grad_gate = beside(ffn_grad, 0, 3, rows)
    grad_down = ffn_grad[3 * rows : 3 * rows + forward_rows]
    grad_up = beside(ffn_grad, 3 * rows + forward_rows, 3, rows)
    grad_query = beside(attn_grad, 0, 2, rows)
    grad_out = attn_grad[2 * rows : 4 * rows]
    grad_key = attn_grad[4 * rows : 5 * rows]
    grad_value = attn_grad[5 * rows :]

    small = jnp.concatenate(
        [*gain_grads, jnp.stack([squares, jnp.sum(keep)])[None]], axis=1
    )
    small_sum = summed(small)
    totals = small_sum[:, -2:]
    totals = jnp.where(section == 1, totals, one_way(totals, 1))[0]
    loss = totals[0] / (totals[1] * model)
    gain_grads, low = [], 0
    for size in gain_sizes:
        gain_grads.append(lax.dynamic_slice(small_sum, (0, low + index * size), (1, size)))
        low += devices * size
    grad_gain_attn, grad_gain_query, grad_gain_key, grad_gain_ffn = gain_grads

    half = batches // 2
    finals = result.reshape(batches, TOKENS_PER_SHARD, model)
    grads = d_hidden.reshape(batches, TOKENS_PER_SHARD, model)
    output = jnp.where(section == 0, one_way(finals[:half], 1), finals[half:])
    input_grad = jnp.where(section == 0, grads[:half], one_way(grads[half:], 0))
    return (
        output,
        loss,
        input_grad,
        grad_query[None],
        grad_key[None],
        grad_value[None],
        grad_out[None],
        grad_gate[None],
        grad_up[None],
        grad_down[None],
        grad_gain_attn,
        grad_gain_ffn,
        grad_gain_query,
        grad_gain_key,
    )


def solution(mesh):
    placed = (
        P(None, "dp", None),
        P(None, "dp", None),
        P(None, "dp", None),
        P("section", "dp", None),
        P("section", "dp", None),
        P("section", "dp", None),
        P("section", "dp", None),
        P("section", "dp", None),
        P("section", "dp", None),
        P("section", "dp", None),
        P("section", "dp"),
        P("section", "dp"),
        P("section", "dp"),
        P("section", "dp"),
    )
    return jax.shard_map(
        local,
        mesh=mesh,
        in_specs=placed,
        out_specs=(
            P("section", "dp", None),
            P(),
            P("section", "dp", None),
            P("section", "dp", None),
            P("section", "dp", None),
            P("section", "dp", None),
            P("section", "dp", None),
            P("section", "dp", None),
            P("section", "dp", None),
            P("section", "dp", None),
            P("section", "dp"),
            P("section", "dp"),
            P("section", "dp"),
            P("section", "dp"),
        ),
        check_vma=False,
    )
```

time: 1200 us -> 750 us (0.62)
  local copies, waits for them, and re-layouts: 410 us -> 79 us
  Pallas kernels: 0 us -> 260 us
  matrix products: 229 us -> 0 us
  waiting for transfers between devices: 335 us -> 260 us
  other arithmetic: 103 us -> 61.1 us
  blocking collectives: 24.2 us -> 0 us
  between operations: 20.5 us -> 5.08 us
    pallas_call x0 -> x22, Pallas kernels: none -> 260 us  [the longest x4 49.8 us: weight_grads(): wide_call(functools.partial(grad_kernel, tuple(plan), chips), (start,), s...]
    dot_general x46 -> x0, matrix products: 229 us -> none  [the longest x14 72.9 us: times_transpose(): lax.dot_general(left, right, CONTRACT_COLS, preferred_element_type=jnp.fl...]
    reshape x14 -> x5, local copies, waits for them, and re-layouts: 84.6 us -> 0.33 us  [the longest x4 0.33 us: local(): gains.append(gain_whole[:, low:low + size].reshape(1, devices * size))]
    unnamed x2 -> x0, waiting for transfers between devices: 82.6 us -> none
    transpose x5 -> x0, local copies, waits for them, and re-layouts: 48.5 us -> none  [the longest x3 33 us: unpacked(): return part.transpose(0, 2, 1, 3).reshape(devices * rows, pieces * width)]
    concatenate x17 -> x0, local copies, waits for them, and re-layouts: 42.7 us -> none  [the longest x16 41.4 us: rotate(): jnp.concatenate([first * turn_cos - second * turn_sin, second * turn_cos...]
    unnamed x266 -> x93, local copies, waits for them, and re-layouts: 54.2 us -> 19.2 us
    slice x8 -> x3, local copies, waits for them, and re-layouts: 32.5 us -> 0.15 us  [the longest x2 0.14 us: local(): gains.append(gain_whole[:, low:low + size].reshape(1, devices * size))]
  transfers between devices with their start and end apart: 96 -> 103, of which waited for: 41 -> 52; matrix products, arithmetic and copies ran while one was open for 25% -> 15% of each run, Pallas kernels for 0% -> 10%
where the time goes in v2:
time: 750 us; the launch traced here: 741 us
  Pallas kernels  260 us (35%)
  waiting for transfers between devices  260 us (35%)
  local copies, waits for them, and re-layouts  79 us (11%)
  starting transfers between devices  75.2 us (10%)
  other arithmetic  61.1 us (8%)
    ppermute x14, waiting for transfers between devices, gather_ring(): forward = lax.ppermute(forward, 'dp', right)  73.2 us
    ppermute x14, waiting for transfers between devices, scatter_ring(): lax.ppermute(forward.astype(jnp.bfloat16), 'dp', right).astype(jnp.float32)  67.1 us
    ppermute x5, waiting for transfers between devices, one_way(): return lax.ppermute(value, 'section', [(source, 1 - source)])  60.6 us
    dynamic_update_slice x60, local copies, waits for them, and re-layouts, put(): return lax.dynamic_update_slice(whole, piece[None], (owner, offset, 0))  54.5 us
    pallas_call x4, Pallas kernels, weight_grads(): wide_call(functools.partial(grad_kernel, tuple(plan), chips), (start,), s...  49.8 us
    pallas_call x2, Pallas kernels, feed_forward_back(): wide_call(functools.partial(ffn_back_kernel, chunk), (7,), [full, full, w...  45.8 us
    pallas_call x2, Pallas kernels, attend_back(): wide_call(attend_back_kernel, (blocks, groups), [pair, pl.BlockSpec((TOKE...  44.2 us
    pallas_call x2, Pallas kernels, feed_forward(): wide_call(functools.partial(ffn_kernel, chunk), (7,), [whole_spec((tokens...  34.4 us
  transfers between devices with their start and end apart: 103, of which 52 were waited for; matrix products, arithmetic and copies ran while one was open for 15% of the time, Pallas kernels for 10%

profile of v2, /device:TPU:0, one launch (start us, length us, event | category | flops | bytes accessed | tf_op | source)
XLA Modules:
  0.0 740.7 jit_solution(1604480539919814416)
XLA Ops:
  57.0 7.7 %collective-permute-done.13 = bf16[192,1024]{1,0:T(8,128)(2,1)S(1)} collective-permute-done((bf16[192,1024]{1,0:T(8,128)(2,1)}, bf16[192,1024]{1,0:T(8,128)(2,1)S(1)}, u32[]{:S(2)}, u32[]{:S(2)}) %collective-permute-start.13) | collective-permute-done | bytes 393248 | tf_op jit(solution)/shard_map/ppermute | solution.py:103
  87.7 11.2 %collective-permute-done.21 = bf16[192,1024]{1,0:T(8,128)(2,1)S(1)} collective-permute-done((bf16[192,1024]{1,0:T(8,128)(2,1)S(1)}, bf16[192,1024]{1,0:T(8,128)(2,1)S(1)}, u32[]{:S(2)}, u32[]{:S(2)}) %collective-permute-start.21) | collective-permute-done | bytes 393248 | tf_op jit(solution)/shard_map/ppermute | solution.py:103
  100.5 9.1 %collective-permute-done.23 = bf16[192,1024]{1,0:T(8,128)(2,1)S(1)} collective-permute-done((bf16[192,1024]{1,0:T(8,128)(2,1)S(1)}, bf16[192,1024]{1,0:T(8,128)(2,1)S(1)}, u32[]{:S(2)}, u32[]{:S(2)}) %collective-permute-start.23) | collective-permute-done | bytes 393248 | tf_op jit(solution)/shard_map/ppermute | solution.py:104
  125.6 7.0 collective-permute-done.42
  147.8 13.6 %shard_map.246 = (bf16[512,1024]{1,0:T(8,128)(2,1)}, bf16[512,4096]{1,0:T(8,128)(2,1)}, bf16[512,3072]{1,0:T(8,128)(2,1)}) custom-call(bf16[512,1024]{1,0:T(8,128)(2,1)S(1)} %bitcast.297, f32[1,1024]{1,0:T(1,128)S(1)} %reshape.254.gain_ref, f32[1,128]{1,0:T(1,128)S(1)} %reshape.255.gain_q_ref, f32[1,128]{1,0:T(1,128)S(1)} %reshape.256.gain_k_ref, ...), custom_call_target="tpu_custom_call" | custom-call | flops 4294967296 | bytes 17825792 | tf_op jit(solution)/shard_map/pallas_call | solution.py:248
  161.4 7.6 %shard_map.247.o_ref = bf16[512,2048]{1,0:T(8,128)(2,1)S(1)} custom-call(bf16[512,4096]{1,0:T(8,128)(2,1)} %get-tuple-element.53.q_ref.k_ref.v_ref, bf16[512,4096]{1,0:T(8,128)(2,1)} %get-tuple-element.53.q_ref.k_ref.v_ref, bf16[512,4096]{1,0:T(8,128)(2,1)} %get-tuple-element.53.q_ref.k_ref.v_ref, s32[512,1]{1,0:T(8,128)S(1)} %bitcast.299, ...), custom_call_target="tpu_custom_call" | custom-call | flops 4294967296 | bytes 6291456 | tf_op jit(solution)/shard_map/pallas_call | solution.py:301
  170.3 6.1 shard_map.248
  182.3 9.9 %collective-permute-done.50 = bf16[288,1024]{1,0:T(8,128)(2,1)S(1)} collective-permute-done((bf16[288,1024]{1,0:T(8,128)(2,1)S(1)}, bf16[288,1024]{1,0:T(8,128)(2,1)S(1)}, u32[]{:S(2)}, u32[]{:S(2)}) %collective-permute-start.50) | collective-permute-done | bytes 589856 | tf_op jit(solution)/shard_map/ppermute | solution.py:103
  198.0 9.9 %collective-permute-done.54 = bf16[288,1024]{1,0:T(8,128)(2,1)S(1)} collective-permute-done((bf16[288,1024]{1,0:T(8,128)(2,1)S(1)}, bf16[288,1024]{1,0:T(8,128)(2,1)S(1)}, u32[]{:S(2)}, u32[]{:S(2)}) %collective-permute-start.54) | collective-permute-done | bytes 589856 | tf_op jit(solution)/shard_map/ppermute | solution.py:103
  213.8 9.9 %collective-permute-done.58 = bf16[288,1024]{1,0:T(8,128)(2,1)S(1)} collective-permute-done((bf16[288,1024]{1,0:T(8,128)(2,1)S(1)}, bf16[288,1024]{1,0:T(8,128)(2,1)S(1)}, u32[]{:S(2)}, u32[]{:S(2)}) %collective-permute-start.58) | collective-permute-done | bytes 589856 | tf_op jit(solution)/shard_map/ppermute | solution.py:103
  230.2 15.2 %shard_map.250 = bf16[512,1024]{1,0:T(8,128)(2,1)S(1)} custom-call(bf16[512,1024]{1,0:T(8,128)(2,1)S(1)} %get-tuple-element.54.xf_ref, f32[512,1024]{1,0:T(8,128)S(1)} %get-tuple-element.55.hm_ref, bf16[16,576,1024]{2,1,0:T(8,128)(2,1)} %bitcast_dynamic-update-slice_fusion.4.gate_ref.up_ref.down_ref, ...), custom_call_target="tpu_custom_call" | custom-call | flops 9663676416 | bytes 23068672 | tf_op jit(solution)/shard_map/pallas_call | solution.py:409
  250.3 21.3 %collective-permute-done.62 = bf16[512,1024]{1,0:T(8,128)(2,1)} collective-permute-done((bf16[512,1024]{1,0:T(8,128)(2,1)S(1)}, bf16[512,1024]{1,0:T(8,128)(2,1)}, u32[]{:S(2)}, u32[]{:S(2)}) %collective-permute-start.62) | collective-permute-done | bytes 1048608 | tf_op jit(solution)/shard_map/ppermute | solution.py:25
  272.7 13.2 %shard_map.251 = (bf16[512,1024]{1,0:T(8,128)(2,1)S(1)}, bf16[512,4096]{1,0:T(8,128)(2,1)}, bf16[512,3072]{1,0:T(8,128)(2,1)S(1)}) custom-call(bf16[512,1024]{1,0:T(8,128)(2,1)S(1)} %broadcast_select_fusion.h_ref, f32[1,1024]{1,0:T(1,128)S(1)} %reshape.254.gain_ref, f32[1,128]{1,0:T(1,128)S(1)} %reshape.255.gain_q_ref, f32[1,128]{1,0:T(1,128)S(1)} %reshape.256.gain_k_ref, ...), custom_call_target="tpu_custom_call" | custom-call | flops 4294967296 | bytes 17825792 | tf_op jit(solution)/shard_map/pallas_call | solution.py:248
  287.0 8.3 %shard_map.252.o_ref.refs_1_.refs_0_ = bf16[512,2048]{1,0:T(8,128)(2,1)S(1)} custom-call(bf16[512,4096]{1,0:T(8,128)(2,1)} %get-tuple-element.57.q_ref.k_ref.v_ref, bf16[512,4096]{1,0:T(8,128)(2,1)} %get-tuple-element.57.q_ref.k_ref.v_ref, bf16[512,4096]{1,0:T(8,128)(2,1)} %get-tuple-element.57.q_ref.k_ref.v_ref, s32[512,1]{1,0:T(8,128)S(1)} %bitcast.300, ...), custom_call_target="tpu_custom_call" | custom-call | flops 4294967296 | bytes 6291456 | tf_op jit(solution)/shard_map/pallas_call | solution.py:301
  296.7 6.1 shard_map.253
  302.8 19.2 %shard_map.254 = (bf16[512,1024]{1,0:T(8,128)(2,1)S(1)}, bf16[512,3072]{1,0:T(8,128)(2,1)}, bf16[512,3072]{1,0:T(8,128)(2,1)}, bf16[512,3072]{1,0:T(8,128)(2,1)}) custom-call(bf16[512,1024]{1,0:T(8,128)(2,1)S(1)} %get-tuple-element.58.xf_ref.refs_0_.refs_1_, f32[512,1024]{1,0:T(8,128)S(1)} %get-tuple-element.59.hm_ref, ...), custom_call_target="tpu_custom_call" | custom-call | flops 9663676416 | bytes 32505856 | tf_op jit(solution)/shard_map/pallas_call | solution.py:409
  324.5 22.9 %shard_map.255 = (f32[512,1024]{1,0:T(8,128)}, bf16[512,1024]{1,0:T(8,128)(2,1)}, bf16[512,3072]{1,0:T(8,128)(2,1)}, bf16[512,3072]{1,0:T(8,128)(2,1)}, f32[1,1024]{1,0:T(1,128)}) custom-call(f32[512,1024]{1,0:T(8,128)} %fusion.dy_ref, f32[512,1024]{1,0:T(8,128)} %copy-done, f32[1,1024]{1,0:T(1,128)} %copy-done.24, ...), custom_call_target="tpu_custom_call" | custom-call | flops 9663676416 | bytes 38797312 | tf_op jit(solution)/shard_map/pallas_call | solution.py:492
  354.9 22.3 %shard_map.257 = (bf16[512,2048]{1,0:T(8,128)(2,1)S(1)}, bf16[512,1024]{1,0:T(8,128)(2,1)S(1)}, bf16[512,1024]{1,0:T(8,128)(2,1)S(1)}, f32[1,128]{1,0:T(1,128)}, f32[1,128]{1,0:T(1,128)}) custom-call(bf16[512,4096]{1,0:T(8,128)(2,1)} %get-tuple-element.57.q_ref.k_ref.v_ref, bf16[512,4096]{1,0:T(8,128)(2,1)} %get-tuple-element.57.q_ref.k_ref.v_ref, ...), custom_call_target="tpu_custom_call" | custom-call | flops 8589934592 | bytes 15728640 | tf_op jit(solution)/shard_map/pallas_call | solution.py:612
  378.6 11.3 %shard_map.258 = (bf16[512,1024]{1,0:T(8,128)(2,1)}, f32[1,1024]{1,0:T(1,128)}) custom-call(bf16[512,2048]{1,0:T(8,128)(2,1)} %copy-done.9, bf16[512,1024]{1,0:T(8,128)(2,1)S(1)} %get-tuple-element.66.dk_ref, bf16[512,1024]{1,0:T(8,128)(2,1)S(1)} %get-tuple-element.67.dv_ref, bf16[16,384,1024]{2,1,0:T(8,128)(2,1)} %bitcast_dynamic-update-slice_fusion.33.w_ref, ...), custom_call_target="tpu_custom_call" | custom-call | flops 4294967296 | bytes 16777216 | tf_op jit(solution)/shard_map/pallas_call | solution.py:683
  392.4 25.3 %collective-permute-done.64 = bf16[512,1024]{1,0:T(8,128)(2,1)S(1)} collective-permute-done((bf16[512,1024]{1,0:T(8,128)(2,1)}, bf16[512,1024]{1,0:T(8,128)(2,1)S(1)}, u32[]{:S(2)}, u32[]{:S(2)}) %collective-permute-start.64) | collective-permute-done | bytes 1048608 | tf_op jit(solution)/shard_map/ppermute | solution.py:25
  422.2 23.0 %shard_map.259 = (f32[512,1024]{1,0:T(8,128)}, bf16[512,1024]{1,0:T(8,128)(2,1)}, bf16[512,3072]{1,0:T(8,128)(2,1)}, bf16[512,3072]{1,0:T(8,128)(2,1)}, f32[1,1024]{1,0:T(1,128)}) custom-call(f32[512,1024]{1,0:T(8,128)} %get-tuple-element.95.dy_ref, f32[512,1024]{1,0:T(8,128)} %copy-done, f32[1,1024]{1,0:T(1,128)} %copy-done.24, ...), custom_call_target="tpu_custom_call" | custom-call | flops 9663676416 | bytes 38797312 | tf_op jit(solution)/shard_map/pallas_call | solution.py:492
  452.7 21.9 %shard_map.261 = (bf16[512,2048]{1,0:T(8,128)(2,1)S(1)}, bf16[512,1024]{1,0:T(8,128)(2,1)S(1)}, bf16[512,1024]{1,0:T(8,128)(2,1)S(1)}, f32[1,128]{1,0:T(1,128)S(1)}, f32[1,128]{1,0:T(1,128)S(1)}) custom-call(bf16[512,4096]{1,0:T(8,128)(2,1)} %get-tuple-element.57.q_ref.k_ref.v_ref, bf16[512,4096]{1,0:T(8,128)(2,1)} %get-tuple-element.57.q_ref.k_ref.v_ref, ...), custom_call_target="tpu_custom_call" | custom-call | flops 8589934592 | bytes 15728640 | tf_op jit(solution)/shard_map/pallas_call | solution.py:612
  477.9 9.8 %shard_map.263 = (bf16[8,192,1024]{2,1,0:T(8,128)(2,1)}, bf16[8,192,1024]{2,1,0:T(8,128)(2,1)}) custom-call(s32[9]{0:T(128)} %pad_add_fusion.order_ref, bf16[512,1024]{1,0:T(8,128)(2,1)} %copy-done.26, bf16[512,2048]{1,0:T(8,128)(2,1)} %copy-done.4, bf16[512,2048]{1,0:T(8,128)(2,1)} %copy-done.8, bf16[512,1024]{1,0:T(8,128)(2,1)} %get-tuple-element.70.d_ref.refs_3_), custom_call_target="tpu_custom_call" | custom-call | flops 3221225472 | bytes 12582912 | tf_op jit(solution)/shard_map/pallas_call | solution.py:769
  487.6 10.6 %shard_map.264 = (bf16[8,192,1024]{2,1,0:T(8,128)(2,1)}, bf16[8,192,1024]{2,1,0:T(8,128)(2,1)}) custom-call(s32[9]{0:T(128)} %pad_add_fusion.order_ref, bf16[512,2048]{1,0:T(8,128)(2,1)} %copy-done.4, bf16[512,1024]{1,0:T(8,128)(2,1)} %copy-done.26, bf16[512,1024]{1,0:T(8,128)(2,1)} %copy-done.26, bf16[512,1024]{1,0:T(8,128)(2,1)} %get-tuple-element.70.d_ref.refs_3_, ...), custom_call_target="tpu_custom_call" | custom-call | flops 3221225472 | bytes 12582912 | tf_op jit(solution)/shard_map/pallas_call | solution.py:769
  498.7 14.8 %shard_map.265 = (bf16[8,288,1024]{2,1,0:T(8,128)(2,1)}, bf16[8,288,1024]{2,1,0:T(8,128)(2,1)}) custom-call(s32[9]{0:T(128)} %pad_add_fusion.order_ref, bf16[512,1024]{1,0:T(8,128)(2,1)} %copy-done.10, bf16[512,3072]{1,0:T(8,128)(2,1)} %get-tuple-element.85.refs_1_.refs_0_, bf16[512,3072]{1,0:T(8,128)(2,1)} %get-tuple-element.86.refs_2_, ...), custom_call_target="tpu_custom_call" | custom-call | flops 4831838208 | bytes 18874368 | tf_op jit(solution)/shard_map/pallas_call | solution.py:769
  513.5 14.7 %shard_map.266 = (bf16[8,288,1024]{2,1,0:T(8,128)(2,1)}, bf16[8,288,1024]{2,1,0:T(8,128)(2,1)}) custom-call(s32[9]{0:T(128)} %pad_add_fusion.order_ref, bf16[512,3072]{1,0:T(8,128)(2,1)} %get-tuple-element.85.refs_1_.refs_0_, bf16[512,1024]{1,0:T(8,128)(2,1)} %copy-done.10, bf16[512,1024]{1,0:T(8,128)(2,1)} %get-tuple-element.94.refs_3_.refs_2_, ...), custom_call_target="tpu_custom_call" | custom-call | flops 4831838208 | bytes 18874368 | tf_op jit(solution)/shard_map/pallas_call | solution.py:769
  528.7 10.2 %shard_map.262 = (bf16[512,1024]{1,0:T(8,128)(2,1)S(1)}, f32[1,1024]{1,0:T(1,128)S(1)}) custom-call(bf16[512,2048]{1,0:T(8,128)(2,1)} %copy-done.8, bf16[512,1024]{1,0:T(8,128)(2,1)S(1)} %copy-done.12, bf16[512,1024]{1,0:T(8,128)(2,1)S(1)} %copy-done.14, bf16[16,384,1024]{2,1,0:T(8,128)(2,1)} %bitcast_dynamic-update-slice_fusion.33.w_ref, ...), custom_call_target="tpu_custom_call" | custom-call | flops 4294967296 | bytes 16777216 | tf_op jit(solution)/shard_map/pallas_call | solution.py:683
  546.6 13.4 %collective-permute-done.63 = bf16[1,256,1024]{2,1,0:T(8,128)(2,1)S(1)} collective-permute-done((bf16[1,256,1024]{2,1,0:T(8,128)(2,1)S(1)}, bf16[1,256,1024]{2,1,0:T(8,128)(2,1)S(1)}, u32[]{:S(2)}, u32[]{:S(2)}) %collective-permute-start.63) | collective-permute-done | bytes 524320 | tf_op jit(solution)/shard_map/ppermute | solution.py:25
  622.5 6.5 collective-permute-done.75
  643.6 6.5 collective-permute-done.76
  664.6 6.5 collective-permute-done.77
  728.6 6.3 collective-permute-done.102
  (435 shorter events, 334.3 us)
Async XLA Ops:
  6.6 35.5 %collective-permute-start.4 = (bf16[384,1024]{1,0:T(8,128)(2,1)S(1)}, bf16[384,1024]{1,0:T(8,128)(2,1)}, u32[]{:S(2)}, u32[]{:S(2)}) collective-permute-start(bf16[384,1024]{1,0:T(8,128)(2,1)S(1)} %constant_dynamic-update-slice_fusion), channel_id=1, source_target_pairs={{0,1},{1,0},{2,3},{3,2},{4,5},{5,4},{6,7},{7,6},{8,9},{9,8},{10,11... | collective-permute-start | bytes 2359304 | tf_op jit(solution)/shard_map/ppermute | solution.py:99
  8.8 21.6 %collective-permute-start.5 = (bf16[192,1024]{1,0:T(8,128)(2,1)}, bf16[192,1024]{1,0:T(8,128)(2,1)}, u32[]{:S(2)}, u32[]{:S(2)}) collective-permute-start(bf16[192,1024]{1,0:T(8,128)(2,1)} %get-tuple-element.110), channel_id=1, source_target_pairs={{0,4},{1,5},{4,8},{5,9},{8,12},{9,13},{12,14},{13,15},{14,10},{15,... | collective-permute-start | bytes 1179656 | tf_op jit(solution)/shard_map/ppermute | solution.py:103
  11.8 20.7 %collective-permute-start.7 = (bf16[192,1024]{1,0:T(8,128)(2,1)}, bf16[192,1024]{1,0:T(8,128)(2,1)}, u32[]{:S(2)}, u32[]{:S(2)}) collective-permute-start(bf16[192,1024]{1,0:T(8,128)(2,1)} %get-tuple-element.109), channel_id=1, source_target_pairs={{4,0},{5,1},{8,4},{9,5},{12,8},{13,9},{14,12},{15,13},{10,14},{11,... | collective-permute-start | bytes 1179656 | tf_op jit(solution)/shard_map/ppermute | solution.py:104
  40.4 39.8 %collective-permute-start.33 = (bf16[576,1024]{1,0:T(8,128)(2,1)S(1)}, bf16[576,1024]{1,0:T(8,128)(2,1)S(1)}, u32[]{:S(2)}, u32[]{:S(2)}) collective-permute-start(bf16[576,1024]{1,0:T(8,128)(2,1)S(1)} %slice_dynamic-update-slice_fusion), channel_id=1, source_target_pairs={{0,1},{1,0},{2,3},{3,2},{4,5},{5,4},{6,7},{7,6},{8,9},{9,8},{10,11... | collective-permute-start | bytes 3538952 | tf_op jit(solution)/shard_map/ppermute | solution.py:99
  40.5 30.2 %collective-permute-start.34 = (bf16[288,1024]{1,0:T(8,128)(2,1)S(1)}, bf16[288,1024]{1,0:T(8,128)(2,1)S(1)}, u32[]{:S(2)}, u32[]{:S(2)}) collective-permute-start(bf16[288,1024]{1,0:T(8,128)(2,1)S(1)} %get-tuple-element.104), channel_id=1, source_target_pairs={{0,4},{1,5},{4,8},{5,9},{8,12},{9,13},{12,14},{13,15},{14,10},{15,... | collective-permute-start | bytes 1769480 | tf_op jit(solution)/shard_map/ppermute | solution.py:103
  42.2 29.9 %collective-permute-start.36 = (bf16[288,1024]{1,0:T(8,128)(2,1)S(1)}, bf16[288,1024]{1,0:T(8,128)(2,1)S(1)}, u32[]{:S(2)}, u32[]{:S(2)}) collective-permute-start(bf16[288,1024]{1,0:T(8,128)(2,1)S(1)} %get-tuple-element.103), channel_id=1, source_target_pairs={{4,0},{5,1},{8,4},{9,5},{12,8},{13,9},{14,12},{15,13},{10,14},{11,... | collective-permute-start | bytes 1769480 | tf_op jit(solution)/shard_map/ppermute | solution.py:104
  72.1 38.2 %collective-permute-start.38 = (bf16[288,1024]{1,0:T(8,128)(2,1)S(1)}, bf16[288,1024]{1,0:T(8,128)(2,1)S(1)}, u32[]{:S(2)}, u32[]{:S(2)}) collective-permute-start(bf16[288,1024]{1,0:T(8,128)(2,1)S(1)} %collective-permute-done.34), channel_id=1, source_target_pairs={{0,4},{1,5},{4,8},{5,9},{8,12},{9,13},{12,14},{13,15},{14,10},{15,... | collective-permute-start | bytes 1769480 | tf_op jit(solution)/shard_map/ppermute | solution.py:103
  86.3 29.6 %collective-permute-start.40 = (bf16[288,1024]{1,0:T(8,128)(2,1)S(1)}, bf16[288,1024]{1,0:T(8,128)(2,1)S(1)}, u32[]{:S(2)}, u32[]{:S(2)}) collective-permute-start(bf16[288,1024]{1,0:T(8,128)(2,1)S(1)} %collective-permute-done.36), channel_id=1, source_target_pairs={{4,0},{5,1},{8,4},{9,5},{12,8},{13,9},{14,12},{15,13},{10,14},{11,... | collective-permute-start | bytes 1769480 | tf_op jit(solution)/shard_map/ppermute | solution.py:104
  86.5 24.6 %collective-permute-start.20 = (bf16[192,1024]{1,0:T(8,128)(2,1)S(1)}, bf16[192,1024]{1,0:T(8,128)(2,1)S(1)}, u32[]{:S(2)}, u32[]{:S(2)}) collective-permute-start(bf16[192,1024]{1,0:T(8,128)(2,1)S(1)} %collective-permute-done.19), channel_id=1, source_target_pairs={{0,1},{1,0},{2,3},{3,2},{4,5},{5,4},{6,7},{7,6},{8,9},{9,8},{10,11... | collective-permute-start | bytes 1179656 | tf_op jit(solution)/shard_map/ppermute | solution.py:107
  87.4 22.2 %collective-permute-start.23 = (bf16[192,1024]{1,0:T(8,128)(2,1)S(1)}, bf16[192,1024]{1,0:T(8,128)(2,1)S(1)}, u32[]{:S(2)}, u32[]{:S(2)}) collective-permute-start(bf16[192,1024]{1,0:T(8,128)(2,1)S(1)} %collective-permute-done.19), channel_id=1, source_target_pairs={{4,0},{5,1},{8,4},{9,5},{12,8},{13,9},{14,12},{15,13},{10,14},{11,... | collective-permute-start | bytes 1179656 | tf_op jit(solution)/shard_map/ppermute | solution.py:104
  133.9 43.6 %collective-permute-start.43 = (bf16[288,1024]{1,0:T(8,128)(2,1)S(1)}, bf16[288,1024]{1,0:T(8,128)(2,1)S(1)}, u32[]{:S(2)}, u32[]{:S(2)}) collective-permute-start(bf16[288,1024]{1,0:T(8,128)(2,1)S(1)} %collective-permute-done.42), channel_id=1, source_target_pairs={{0,1},{1,0},{2,3},{3,2},{4,5},{5,4},{6,7},{7,6},{8,9},{9,8},{10,11... | collective-permute-start | bytes 1769480 | tf_op jit(solution)/shard_map/ppermute | solution.py:106
  136.3 40.1 %collective-permute-start.46 = (bf16[288,1024]{1,0:T(8,128)(2,1)S(1)}, bf16[288,1024]{1,0:T(8,128)(2,1)S(1)}, u32[]{:S(2)}, u32[]{:S(2)}) collective-permute-start(bf16[288,1024]{1,0:T(8,128)(2,1)S(1)} %collective-permute-done.42), channel_id=1, source_target_pairs={{0,4},{1,5},{4,8},{5,9},{8,12},{9,13},{12,14},{13,15},{14,10},{15,... | collective-permute-start | bytes 1769480 | tf_op jit(solution)/shard_map/ppermute | solution.py:103
  137.1 43.5 %collective-permute-start.45 = (bf16[288,1024]{1,0:T(8,128)(2,1)S(1)}, bf16[288,1024]{1,0:T(8,128)(2,1)S(1)}, u32[]{:S(2)}, u32[]{:S(2)}) collective-permute-start(bf16[288,1024]{1,0:T(8,128)(2,1)S(1)} %collective-permute-done.44), channel_id=1, source_target_pairs={{0,1},{1,0},{2,3},{3,2},{4,5},{5,4},{6,7},{7,6},{8,9},{9,8},{10,11... | collective-permute-start | bytes 1769480 | tf_op jit(solution)/shard_map/ppermute | solution.py:107
  143.8 33.7 %collective-permute-start.48 = (bf16[288,1024]{1,0:T(8,128)(2,1)S(1)}, bf16[288,1024]{1,0:T(8,128)(2,1)S(1)}, u32[]{:S(2)}, u32[]{:S(2)}) collective-permute-start(bf16[288,1024]{1,0:T(8,128)(2,1)S(1)} %collective-permute-done.44), channel_id=1, source_target_pairs={{4,0},{5,1},{8,4},{9,5},{12,8},{13,9},{14,12},{15,13},{10,14},{11,... | collective-permute-start | bytes 1769480 | tf_op jit(solution)/shard_map/ppermute | solution.py:104
  245.5 26.1 %collective-permute-start.62 = (bf16[512,1024]{1,0:T(8,128)(2,1)S(1)}, bf16[512,1024]{1,0:T(8,128)(2,1)}, u32[]{:S(2)}, u32[]{:S(2)}) collective-permute-start(bf16[512,1024]{1,0:T(8,128)(2,1)S(1)} %shard_map.250), channel_id=1, source_target_pairs={{0,16},{1,17},{2,18},{3,19},{4,20},{5,21},{6,22},{7,23},{8,24},{9,... | collective-permute-start | bytes 3145736 | tf_op jit(solution)/shard_map/ppermute | solution.py:25
  389.9 27.8 %collective-permute-start.64 = (bf16[512,1024]{1,0:T(8,128)(2,1)}, bf16[512,1024]{1,0:T(8,128)(2,1)S(1)}, u32[]{:S(2)}, u32[]{:S(2)}) collective-permute-start(bf16[512,1024]{1,0:T(8,128)(2,1)} %get-tuple-element.69), channel_id=1, source_target_pairs={{16,0},{17,1},{18,2},{19,3},{20,4},{21,5},{22,6},{23,7},{24,8},{25... | collective-permute-start | bytes 3145736 | tf_op jit(solution)/shard_map/ppermute | solution.py:25
  487.6 83.5 %collective-permute-start.71 = (bf16[8,192,1024]{2,1,0:T(8,128)(2,1)}, bf16[8,192,1024]{2,1,0:T(8,128)(2,1)}, u32[]{:S(2)}, u32[]{:S(2)}) collective-permute-start(bf16[8,192,1024]{2,1,0:T(8,128)(2,1)} %get-tuple-element.82), channel_id=1, source_target_pairs={{0,1},{1,0},{2,3},{3,2},{4,5},{5,4},{6,7},{7,6},{8,9},{9,8},{10,11... | collective-permute-start | bytes 9437192 | tf_op jit(solution)/shard_map/ppermute | solution.py:123
  498.2 75.6 %collective-permute-start.79 = (bf16[8,192,1024]{2,1,0:T(8,128)(2,1)}, bf16[8,192,1024]{2,1,0:T(8,128)(2,1)}, u32[]{:S(2)}, u32[]{:S(2)}) collective-permute-start(bf16[8,192,1024]{2,1,0:T(8,128)(2,1)} %get-tuple-element.84), channel_id=1, source_target_pairs={{0,1},{1,0},{2,3},{3,2},{4,5},{5,4},{6,7},{7,6},{8,9},{9,8},{10,11... | collective-permute-start | bytes 9437192 | tf_op jit(solution)/shard_map/ppermute | solution.py:123
  513.5 86.4 %collective-permute-start.87 = (bf16[8,288,1024]{2,1,0:T(8,128)(2,1)}, bf16[8,288,1024]{2,1,0:T(8,128)(2,1)}, u32[]{:S(2)}, u32[]{:S(2)}) collective-permute-start(bf16[8,288,1024]{2,1,0:T(8,128)(2,1)} %get-tuple-element.88), channel_id=1, source_target_pairs={{0,1},{1,0},{2,3},{3,2},{4,5},{5,4},{6,7},{7,6},{8,9},{9,8},{10,11... | collective-permute-start | bytes 14155784 | tf_op jit(solution)/shard_map/ppermute | solution.py:123
  528.2 81.6 %collective-permute-start.95 = (bf16[8,288,1024]{2,1,0:T(8,128)(2,1)}, bf16[8,288,1024]{2,1,0:T(8,128)(2,1)}, u32[]{:S(2)}, u32[]{:S(2)}) collective-permute-start(bf16[8,288,1024]{2,1,0:T(8,128)(2,1)} %get-tuple-element.91), channel_id=1, source_target_pairs={{0,1},{1,0},{2,3},{3,2},{4,5},{5,4},{6,7},{7,6},{8,9},{9,8},{10,11... | collective-permute-start | bytes 14155784 | tf_op jit(solution)/shard_map/ppermute | solution.py:123
  609.3 19.7 %collective-permute-start.75 = (bf16[192,1024]{1,0:T(8,128)(2,1)S(1)}, bf16[192,1024]{1,0:T(8,128)(2,1)S(1)}, u32[]{:S(2)}, u32[]{:S(2)}) collective-permute-start(bf16[192,1024]{1,0:T(8,128)(2,1)S(1)} %fusion.23), channel_id=1, source_target_pairs={{0,4},{1,5},{4,8},{5,9},{8,12},{9,13},{12,14},{13,15},{14,10},{15,... | collective-permute-start | bytes 1179656 | tf_op jit(solution)/shard_map/ppermute | solution.py:133
  611.1 19.6 %collective-permute-start.96 = (bf16[288,1024]{1,0:T(8,128)(2,1)S(1)}, bf16[288,1024]{1,0:T(8,128)(2,1)S(1)}, u32[]{:S(2)}, u32[]{:S(2)}) collective-permute-start(bf16[288,1024]{1,0:T(8,128)(2,1)S(1)} %fusion.27), channel_id=1, source_target_pairs={{4,0},{5,1},{8,4},{9,5},{12,8},{13,9},{14,12},{15,13},{10,14},{11,... | collective-permute-start | bytes 1769480 | tf_op jit(solution)/shard_map/ppermute | solution.py:134
  613.9 20.7 %collective-permute-start.83 = (bf16[192,1024]{1,0:T(8,128)(2,1)S(1)}, bf16[192,1024]{1,0:T(8,128)(2,1)S(1)}, u32[]{:S(2)}, u32[]{:S(2)}) collective-permute-start(bf16[192,1024]{1,0:T(8,128)(2,1)S(1)} %fusion.17), channel_id=1, source_target_pairs={{4,0},{5,1},{8,4},{9,5},{12,8},{13,9},{14,12},{15,13},{10,14},{11,... | collective-permute-start | bytes 1179656 | tf_op jit(solution)/shard_map/ppermute | solution.py:134
  622.0 19.7 %collective-permute-start.89 = (bf16[288,1024]{1,0:T(8,128)(2,1)S(1)}, bf16[288,1024]{1,0:T(8,128)(2,1)S(1)}, u32[]{:S(2)}, u32[]{:S(2)}) collective-permute-start(bf16[288,1024]{1,0:T(8,128)(2,1)S(1)} %fusion.12), channel_id=1, source_target_pairs={{0,4},{1,5},{4,8},{5,9},{8,12},{9,13},{12,14},{13,15},{14,10},{15,... | collective-permute-start | bytes 1769480 | tf_op jit(solution)/shard_map/ppermute | solution.py:133
  630.2 19.9 %collective-permute-start.76 = (bf16[192,1024]{1,0:T(8,128)(2,1)S(1)}, bf16[192,1024]{1,0:T(8,128)(2,1)S(1)}, u32[]{:S(2)}, u32[]{:S(2)}) collective-permute-start(bf16[192,1024]{1,0:T(8,128)(2,1)S(1)} %fusion.22), channel_id=1, source_target_pairs={{0,4},{1,5},{4,8},{5,9},{8,12},{9,13},{12,14},{13,15},{14,10},{15,... | collective-permute-start | bytes 1179656 | tf_op jit(solution)/shard_map/ppermute | solution.py:133
  632.1 19.7 %collective-permute-start.97 = (bf16[288,1024]{1,0:T(8,128)(2,1)S(1)}, bf16[288,1024]{1,0:T(8,128)(2,1)S(1)}, u32[]{:S(2)}, u32[]{:S(2)}) collective-permute-start(bf16[288,1024]{1,0:T(8,128)(2,1)S(1)} %fusion.6), channel_id=1, source_target_pairs={{4,0},{5,1},{8,4},{9,5},{12,8},{13,9},{14,12},{15,13},{10,14},{11,... | collective-permute-start | bytes 1769480 | tf_op jit(solution)/shard_map/ppermute | solution.py:134
  635.9 19.6 %collective-permute-start.84 = (bf16[192,1024]{1,0:T(8,128)(2,1)S(1)}, bf16[192,1024]{1,0:T(8,128)(2,1)S(1)}, u32[]{:S(2)}, u32[]{:S(2)}) collective-permute-start(bf16[192,1024]{1,0:T(8,128)(2,1)S(1)} %fusion.16), channel_id=1, source_target_pairs={{4,0},{5,1},{8,4},{9,5},{12,8},{13,9},{14,12},{15,13},{10,14},{11,... | collective-permute-start | bytes 1179656 | tf_op jit(solution)/shard_map/ppermute | solution.py:134
  643.0 19.7 %collective-permute-start.90 = (bf16[288,1024]{1,0:T(8,128)(2,1)S(1)}, bf16[288,1024]{1,0:T(8,128)(2,1)S(1)}, u32[]{:S(2)}, u32[]{:S(2)}) collective-permute-start(bf16[288,1024]{1,0:T(8,128)(2,1)S(1)} %fusion.11), channel_id=1, source_target_pairs={{0,4},{1,5},{4,8},{5,9},{8,12},{9,13},{12,14},{13,15},{14,10},{15,... | collective-permute-start | bytes 1769480 | tf_op jit(solution)/shard_map/ppermute | solution.py:133
  651.3 19.9 %collective-permute-start.77 = (bf16[192,1024]{1,0:T(8,128)(2,1)S(1)}, bf16[192,1024]{1,0:T(8,128)(2,1)S(1)}, u32[]{:S(2)}, u32[]{:S(2)}) collective-permute-start(bf16[192,1024]{1,0:T(8,128)(2,1)S(1)} %fusion.21), channel_id=1, source_target_pairs={{0,4},{1,5},{4,8},{5,9},{8,12},{9,13},{12,14},{13,15},{14,10},{15,... | collective-permute-start | bytes 1179656 | tf_op jit(solution)/shard_map/ppermute | solution.py:133
  653.2 19.7 %collective-permute-start.98 = (bf16[288,1024]{1,0:T(8,128)(2,1)S(1)}, bf16[288,1024]{1,0:T(8,128)(2,1)S(1)}, u32[]{:S(2)}, u32[]{:S(2)}) collective-permute-start(bf16[288,1024]{1,0:T(8,128)(2,1)S(1)} %fusion.5), channel_id=1, source_target_pairs={{4,0},{5,1},{8,4},{9,5},{12,8},{13,9},{14,12},{15,13},{10,14},{11,... | collective-permute-start | bytes 1769480 | tf_op jit(solution)/shard_map/ppermute | solution.py:134
  656.7 20.1 %collective-permute-start.85 = (bf16[192,1024]{1,0:T(8,128)(2,1)S(1)}, bf16[192,1024]{1,0:T(8,128)(2,1)S(1)}, u32[]{:S(2)}, u32[]{:S(2)}) collective-permute-start(bf16[192,1024]{1,0:T(8,128)(2,1)S(1)} %fusion.15), channel_id=1, source_target_pairs={{4,0},{5,1},{8,4},{9,5},{12,8},{13,9},{14,12},{15,13},{10,14},{11,... | collective-permute-start | bytes 1179656 | tf_op jit(solution)/shard_map/ppermute | solution.py:134
  664.1 19.7 %collective-permute-start.91 = (bf16[288,1024]{1,0:T(8,128)(2,1)S(1)}, bf16[288,1024]{1,0:T(8,128)(2,1)S(1)}, u32[]{:S(2)}, u32[]{:S(2)}) collective-permute-start(bf16[288,1024]{1,0:T(8,128)(2,1)S(1)} %fusion.10), channel_id=1, source_target_pairs={{0,4},{1,5},{4,8},{5,9},{8,12},{9,13},{12,14},{13,15},{14,10},{15,... | collective-permute-start | bytes 1769480 | tf_op jit(solution)/shard_map/ppermute | solution.py:133
  (109 other events, 1724.6 us)

commit v3 on v1

v3 whole, which is shorter than its diff:
```python
import functools

import jax
import jax.numpy as jnp
from jax import lax
from jax.experimental import pallas as pl
from jax.experimental.pallas import tpu as pltpu
from jax.sharding import PartitionSpec as P

QUERY_HEADS = 16
KEY_VALUE_HEADS = 8
HEAD_SIZE = 128
TOKENS_PER_SHARD = 256


EPS = 1e-06
THETA = 1000000.0
NEGATIVE = -1e30
CONTRACT_ROWS = (((0,), (0,)), ((), ()))
CONTRACT_COLS = (((1,), (1,)), ((), ()))
RING_LEAD = 1
FIRST_WAIT = 3


def one_way(value, source):
    return lax.ppermute(value, "section", [(source, 1 - source)])


def chip_at(place, chips):
    place = lax.rem(place + 2 * chips, chips)
    return jnp.where(place < chips // 2, 2 * place, 2 * (chips - 1 - place) + 1)


def ring_place(chip, chips):
    return jnp.where(chip % 2 == 0, chip // 2, chips - 1 - chip // 2)


def ring_routes(devices):
    chips = devices // 2
    order = list(range(0, chips, 2)) + list(range(chips - 1, 0, -2))
    right, left = [], []
    for place in range(chips):
        here, there = order[place], order[(place + 1) % chips]
        for core in range(2):
            right.append((2 * here + core, 2 * there + core))
            left.append((2 * there + core, 2 * here + core))
    return right, left, [(device, device ^ 1) for device in range(devices)]


def tie(*values):
    return lax.optimization_barrier(values)


def spread(value):
    devices = lax.axis_size("dp")
    index = lax.axis_index("dp")
    step = 1
    while step < devices:
        other = lax.ppermute(value, "dp", [(low, low ^ step) for low in range(devices)])
        later = (index // step) % 2 == 1
        value = jnp.where(
            later,
            jnp.concatenate([other, value], axis=0),
            jnp.concatenate([value, other], axis=0),
        )
        step *= 2
    return value


def summed(value):
    devices = lax.axis_size("dp")
    step = 1
    while step < devices:
        value = value + lax.ppermute(value, "dp", [(low, low ^ step) for low in range(devices)])
        step *= 2
    return value


def blank(shape, dtype):
    return pl.pallas_call(
        lambda ref: None,
        out_specs=pl.BlockSpec(memory_space=pl.ANY),
        out_shape=jax.ShapeDtypeStruct(shape, dtype),
    )()


def gather_ring(shard, after=None):
    devices = lax.axis_size("dp")
    chips = devices // 2
    right, left, pair = ring_routes(devices)
    index = lax.axis_index("dp")
    core = index % 2
    place = ring_place(index // 2, chips)
    half = shard.shape[0] // 2
    if after is not None:
        shard, after = tie(shard, after)
    whole = blank((devices,) + shard.shape, shard.dtype)

    def put(whole, piece, owner, offset):
        return lax.dynamic_update_slice(whole, piece[None], (owner, offset, 0))

    forward, behind = shard[:half], shard[half:]
    marks = []
    other = None
    for step in range(1, chips):
        forward = lax.ppermute(forward, "dp", right)
        behind = lax.ppermute(behind, "dp", left)
        if other is None:
            other = lax.ppermute(shard, "dp", pair)
            whole = put(whole, shard, index, 0)
            whole = put(whole, other, index + 1 - 2 * core, 0)
        marks.append((forward, behind))
        forward_pair = lax.ppermute(forward, "dp", pair)
        behind_pair = lax.ppermute(behind, "dp", pair)
        owner = 2 * chip_at(place - step, chips)
        whole = put(whole, forward, owner + core, 0)
        whole = put(whole, forward_pair, owner + 1 - core, 0)
        owner = 2 * chip_at(place + step, chips)
        whole = put(whole, behind, owner + core, half)
        whole = put(whole, behind_pair, owner + 1 - core, half)
    return whole, marks


def scatter_ring(forward_parts, behind_parts):
    devices = lax.axis_size("dp")
    chips = devices // 2
    right, left, pair = ring_routes(devices)
    sums = []
    for mine, theirs in (forward_parts, behind_parts):
        got = lax.ppermute(theirs, "dp", pair)
        sums.append((mine, got))

    def own(which, place):
        mine, got = sums[which]
        return mine[place].astype(jnp.float32) + got[place].astype(jnp.float32)

    forward = own(0, chips - 1).astype(jnp.bfloat16)
    behind = own(1, 1).astype(jnp.bfloat16)
    marks = [(forward, behind)]
    for step in range(1, chips):
        forward = lax.ppermute(forward, "dp", right).astype(jnp.float32)
        behind = lax.ppermute(behind, "dp", left).astype(jnp.float32)
        forward = forward + own(0, chips - 1 - step)
        behind = behind + own(1, (step + 1) % chips)
        if step + 1 < chips:
            forward = forward.astype(jnp.bfloat16)
            behind = behind.astype(jnp.bfloat16)
            marks.append((forward, behind))
    return jnp.concatenate([forward, behind], axis=0), marks


def packed(shard, width):
    pieces = shard.shape[-1] // width
    return [shard[:, width * i : width * (i + 1)] for i in range(pieces)]


def beside(grad, low, pieces, rows):
    return jnp.concatenate(
        [grad[low + rows * i : low + rows * (i + 1)] for i in range(pieces)], axis=1
    )


def layout(lengths_row):
    ends = jnp.cumsum(lengths_row)
    places = jnp.arange(TOKENS_PER_SHARD, dtype=jnp.int32)
    passed = (ends[None, :] <= places[:, None]).astype(jnp.int32)
    segment_index = jnp.sum(passed, axis=1)
    start = jnp.sum(passed * lengths_row[None, :], axis=1)
    return (segment_index, places - start)


def rotary_tables(place):
    half = HEAD_SIZE // 2
    freqs = THETA ** (-(jnp.arange(half, dtype=jnp.float32) * 2.0 / HEAD_SIZE))
    angles = place.astype(jnp.float32)[:, None] * freqs[None, :]
    return (jnp.cos(angles), jnp.sin(angles))


LOCAL = pl.BlockSpec(memory_space=pltpu.VMEM)
SCALARS = pl.BlockSpec(memory_space=pltpu.SMEM)


def flat_call(body, arguments, out_shape, scratch=(), flops=0, moved=0, vmem=24, scalars=False):
    specs = [LOCAL] * len(arguments)
    if scalars:
        specs[0] = SCALARS
    return pl.pallas_call(
        body,
        in_specs=specs,
        out_specs=[LOCAL] * len(out_shape),
        out_shape=out_shape,
        scratch_shapes=list(scratch),
        compiler_params=pltpu.CompilerParams(vmem_limit_bytes=vmem << 20),
        cost_estimate=pl.CostEstimate(
            flops=int(flops), bytes_accessed=int(moved), transcendentals=0
        ),
    )(*arguments)


def low_shape(*shape):
    return jax.ShapeDtypeStruct(shape, jnp.bfloat16)


def full_shape(*shape):
    return jax.ShapeDtypeStruct(shape, jnp.float32)


def dot_plain(left, right):
    return jnp.dot(left, right, preferred_element_type=jnp.float32)


def dot_columns(left, right):
    return lax.dot_general(left, right, CONTRACT_COLS, preferred_element_type=jnp.float32)


def dot_rows(left, right):
    return lax.dot_general(left, right, CONTRACT_ROWS, preferred_element_type=jnp.float32)


def unit_rows(values):
    factor = lax.rsqrt(jnp.mean(values * values, axis=-1, keepdims=True) + EPS)
    return values * factor, factor


def norm_pull(grad, scaled, factor, gain):
    pulled = grad * gain
    return factor * (pulled - scaled * jnp.mean(pulled * scaled, axis=-1, keepdims=True))


def head_mean(values):
    average = jnp.full((HEAD_SIZE, HEAD_SIZE), 1.0 / HEAD_SIZE, jnp.bfloat16)
    return dot_plain(values.astype(jnp.bfloat16), average)


def slab(ref, low, rows):
    value = ref[:, low : low + rows, :]
    return value.reshape(value.shape[0] * rows, value.shape[2])


def part_of(index, width=HEAD_SIZE):
    return slice(index * width, (index + 1) * width)


def attention_kernel(
    keep, h_ref, gain_ref, gain_q_ref, gain_k_ref, gain_ffn_ref, cos_ref, sin_ref, row_ref,
    column_ref, w_ref, hm_ref, xf_ref, *rest,
):
    if keep:
        xf_t_ref, xa_t_ref, o_t_ref, qkv_ref, pre_ref, o_ref = rest
    else:
        qkv_ref, o_ref = rest
    tokens, model = h_ref.shape
    rows = w_ref.shape[1] // 6
    hidden = h_ref[...].astype(jnp.float32)
    scaled, _ = unit_rows(hidden)
    xa = (scaled * gain_ref[...]).astype(jnp.bfloat16)
    cosine, sine = cos_ref[...], sin_ref[...]
    for block, low in enumerate((0, rows, 4 * rows, 5 * rows)):
        pre = dot_plain(xa, slab(w_ref, low, rows))
        if block == 3:
            qkv_ref[:, part_of(block, model)] = pre.astype(jnp.bfloat16)
            continue
        if keep:
            pre_ref[:, part_of(block, model)] = pre.astype(jnp.bfloat16)
        gain = gain_q_ref[...] if block < 2 else gain_k_ref[...]
        for head in range(model // HEAD_SIZE):
            value = pre[:, part_of(head)]
            value = value * lax.rsqrt(head_mean(value * value) + EPS) * gain
            value = value * cosine + pltpu.roll(value, HEAD_SIZE // 2, 1) * sine
            qkv_ref[:, part_of(block * (model // HEAD_SIZE) + head)] = value.astype(jnp.bfloat16)
    causal = lax.broadcasted_iota(jnp.int32, (tokens, tokens), 0) >= lax.broadcasted_iota(
        jnp.int32, (tokens, tokens), 1
    )
    allowed = (row_ref[...] == column_ref[0]) & causal
    ones = jnp.ones((tokens, HEAD_SIZE), jnp.bfloat16)
    for shared in range(KEY_VALUE_HEADS):
        key = qkv_ref[:, part_of(QUERY_HEADS + shared)]
        value = qkv_ref[:, part_of(QUERY_HEADS + KEY_VALUE_HEADS + shared)]
        value = jnp.concatenate([value, ones], axis=1)
        for head in range(2 * shared, 2 * shared + 2):
            scores = dot_columns(qkv_ref[:, part_of(head)], key) * HEAD_SIZE ** (-0.5)
            raised = jnp.where(allowed, jnp.exp(scores), 0.0).astype(jnp.bfloat16)
            mixed = dot_plain(raised, value)
            mixed = mixed[:, :HEAD_SIZE] / mixed[:, HEAD_SIZE:]
            o_ref[:, part_of(head)] = mixed.astype(jnp.bfloat16)
    middle = hidden + dot_plain(o_ref[...], slab(w_ref, 2 * rows, 2 * rows))
    hm_ref[...] = middle
    scaled, _ = unit_rows(middle)
    xf = (scaled * gain_ffn_ref[...]).astype(jnp.bfloat16)
    xf_ref[...] = xf
    if keep:
        xf_t_ref[...] = jnp.transpose(xf)
        xa_t_ref[...] = jnp.transpose(xa)
        o_t_ref[...] = jnp.transpose(o_ref[...])


def attention(hidden, gains, tables, whole, keep):
    tokens, model = hidden.shape
    wide = QUERY_HEADS * HEAD_SIZE
    shapes = [full_shape(tokens, model), low_shape(tokens, model)]
    scratch = [pltpu.VMEM((tokens, wide), jnp.bfloat16)]
    if keep:
        shapes += [
            low_shape(model, tokens),
            low_shape(model, tokens),
            low_shape(wide, tokens),
            low_shape(tokens, 4 * model),
            low_shape(tokens, 3 * model),
        ]
    else:
        scratch = [pltpu.VMEM((tokens, 4 * model), jnp.bfloat16)] + scratch
    return flat_call(
        functools.partial(attention_kernel, keep),
        (hidden, *gains, *tables, whole),
        shapes,
        scratch=scratch,
        flops=2 * tokens * model * 6 * model + 8 * tokens * tokens * wide,
        moved=12 * model * model + 20 * tokens * model,
    )


def ffn_kernel(keep, xf_ref, hm_ref, w_ref, y_ref, *rest):
    if keep:
        g_ref, u_ref, z_t_ref, inner = rest
    else:
        (inner,) = rest
    tokens, model = xf_ref.shape
    rows = w_ref.shape[1] // 9
    xf = xf_ref[...]
    for block in range(3):
        gate = dot_plain(xf, slab(w_ref, block * rows, rows))
        up = dot_plain(xf, slab(w_ref, (6 + block) * rows, rows))
        mixed = (gate * jax.nn.sigmoid(gate) * up).astype(jnp.bfloat16)
        inner[:, part_of(block, model)] = mixed
        if keep:
            g_ref[:, part_of(block, model)] = gate.astype(jnp.bfloat16)
            u_ref[:, part_of(block, model)] = up.astype(jnp.bfloat16)
            z_t_ref[part_of(block, model), :] = jnp.transpose(mixed)
    total = hm_ref[...] + dot_plain(inner[...], slab(w_ref, 3 * rows, 3 * rows))
    y_ref[...] = total.astype(jnp.bfloat16)


def feed_forward(normed, middle, whole, keep):
    tokens, model = normed.shape
    width = 3 * model
    shapes = [low_shape(tokens, model)]
    if keep:
        shapes += [low_shape(tokens, width), low_shape(tokens, width), low_shape(width, tokens)]
    return flat_call(
        functools.partial(ffn_kernel, keep),
        (normed, middle, whole),
        shapes,
        scratch=[pltpu.VMEM((tokens, width), jnp.bfloat16)],
        flops=6 * tokens * width * model,
        moved=6 * width * model + 8 * tokens * model,
    )


def ffn_back_kernel(
    dy_ref, hm_ref, gain_ref, g_ref, u_ref, w_ref, dh_ref, low_ref, dg_ref, du_ref, dgain_ref
):
    devices, rows, model = w_ref.shape
    rows = rows // 9
    low_dy = dy_ref[...].astype(jnp.bfloat16)
    chunks = 4
    owners = devices // chunks
    chunk = 3 * model // chunks
    for block in range(chunks):
        part = part_of(block, chunk)
        down = w_ref[block * owners : (block + 1) * owners, 3 * rows : 6 * rows, :]
        d_inner = dot_columns(low_dy, down.reshape(chunk, model))
        gate = g_ref[:, part].astype(jnp.float32)
        sigma = jax.nn.sigmoid(gate)
        silu = gate * sigma
        d_gate = d_inner * u_ref[:, part].astype(jnp.float32) * (sigma + silu * (1.0 - sigma))
        dg_ref[:, part] = d_gate.astype(jnp.bfloat16)
        du_ref[:, part] = (d_inner * silu).astype(jnp.bfloat16)
    grad = None
    for block in range(3):
        part = part_of(block, model)
        term = dot_columns(dg_ref[:, part], slab(w_ref, block * rows, rows))
        term = term + dot_columns(du_ref[:, part], slab(w_ref, (6 + block) * rows, rows))
        grad = term if grad is None else grad + term
    scaled, factor = unit_rows(hm_ref[...])
    dgain_ref[...] = jnp.sum(grad * scaled, axis=0, keepdims=True)
    d_hidden = dy_ref[...] + norm_pull(grad, scaled, factor, gain_ref[...])
    dh_ref[...] = d_hidden
    low_ref[...] = d_hidden.astype(jnp.bfloat16)


def feed_forward_back(d_result, middle, gains, gate, up, whole):
    tokens, model = middle.shape
    width = 3 * model
    return flat_call(
        ffn_back_kernel,
        (d_result, middle, gains[3], gate, up, whole),
        [
            full_shape(tokens, model),
            low_shape(tokens, model),
            low_shape(tokens, width),
            low_shape(tokens, width),
            full_shape(1, model),
        ],
        flops=6 * tokens * width * model,
        moved=6 * width * model + 14 * tokens * model + 8 * tokens * width,
    )


def attention_back_kernel(
    low_ref, dh_ref, h_ref, qkv_ref, pre_ref, gain_ref, gain_q_ref, gain_k_ref, cos_ref, sin_ref,
    row_ref, column_ref, w_ref, dq_ref, dk_ref, dv_ref, dx_ref, dgain_ref, dgain_q_ref,
    dgain_k_ref, do_ref,
):
    tokens, model = h_ref.shape
    rows = w_ref.shape[1] // 6
    do_ref[...] = dot_columns(low_ref[...], slab(w_ref, 2 * rows, 2 * rows)).astype(jnp.bfloat16)
    causal = lax.broadcasted_iota(jnp.int32, (tokens, tokens), 0) <= lax.broadcasted_iota(
        jnp.int32, (tokens, tokens), 1
    )
    allowed = (row_ref[...] == column_ref[0]) & causal
    cosine, sine = cos_ref[...], sin_ref[...]
    scale = HEAD_SIZE ** (-0.5)
    gain_grads = [jnp.zeros((1, HEAD_SIZE), jnp.float32)] * 2

    def through_norm(grad, pre, gain_ref, which):
        gain = gain_ref[...]
        grad = grad * cosine - pltpu.roll(grad, HEAD_SIZE // 2, 1) * sine
        pre = pre.astype(jnp.float32)
        factor = lax.rsqrt(head_mean(pre * pre) + EPS)
        scaled = pre * factor
        gain_grads[which] = gain_grads[which] + jnp.sum(grad * scaled, axis=0, keepdims=True)
        pulled = grad * gain
        return (factor * (pulled - scaled * head_mean(pulled * scaled))).astype(jnp.bfloat16)

    for shared in range(KEY_VALUE_HEADS):
        lone = part_of(shared)
        key = qkv_ref[:, part_of(QUERY_HEADS + shared)]
        value = qkv_ref[:, part_of(QUERY_HEADS + KEY_VALUE_HEADS + shared)]
        d_key = d_value = None
        for head in range(2 * shared, 2 * shared + 2):
            part = part_of(head)
            query, d_mixed = qkv_ref[:, part], do_ref[:, part]
            scores = dot_columns(key, query) * scale
            raised = jnp.where(allowed, jnp.exp(scores), 0.0)
            weights = raised * (1.0 / jnp.sum(raised, axis=0, keepdims=True))
            value_term = dot_plain(weights.astype(jnp.bfloat16), d_mixed)
            d_weights = dot_columns(value, d_mixed)
            pulled = jnp.sum(d_weights * weights, axis=0, keepdims=True)
            d_scores = (weights * (d_weights - pulled)).astype(jnp.bfloat16)
            d_query = dot_rows(d_scores, key) * scale
            key_term = dot_plain(d_scores, query)
            d_key = key_term if d_key is None else d_key + key_term
            d_value = value_term if d_value is None else d_value + value_term
            dq_ref[:, part] = through_norm(d_query, pre_ref[:, part], gain_q_ref, 0)
        dk_ref[:, lone] = through_norm(
            d_key * scale, pre_ref[:, part_of(QUERY_HEADS + shared)], gain_k_ref, 1
        )
        dv_ref[:, lone] = d_value.astype(jnp.bfloat16)
    dgain_q_ref[...], dgain_k_ref[...] = gain_grads
    grad = dot_columns(dq_ref[:, part_of(0, model)], slab(w_ref, 0, rows))
    grad = grad + dot_columns(dq_ref[:, part_of(1, model)], slab(w_ref, rows, rows))
    grad = grad + dot_columns(dk_ref[...], slab(w_ref, 4 * rows, rows))
    grad = grad + dot_columns(dv_ref[...], slab(w_ref, 5 * rows, rows))
    scaled, factor = unit_rows(h_ref[...].astype(jnp.float32))
    dgain_ref[...] = jnp.sum(grad * scaled, axis=0, keepdims=True)
    d_hidden = dh_ref[...] + norm_pull(grad, scaled, factor, gain_ref[...])
    dx_ref[...] = d_hidden.astype(jnp.bfloat16)


def attention_back(low, d_middle, hidden, qkv, pre, gains, tables, whole):
    tokens, model = hidden.shape
    wide = QUERY_HEADS * HEAD_SIZE
    return flat_call(
        attention_back_kernel,
        (low, d_middle, hidden, qkv, pre, *gains[:3], *tables, whole),
        [
            low_shape(tokens, wide),
            low_shape(tokens, model),
            low_shape(tokens, model),
            low_shape(tokens, model),
            full_shape(1, model),
            full_shape(1, HEAD_SIZE),
            full_shape(1, HEAD_SIZE),
        ],
        scratch=[pltpu.VMEM((tokens, wide), jnp.bfloat16)],
        flops=2 * tokens * model * 6 * model + 20 * tokens * tokens * wide,
        moved=12 * model * model + 40 * tokens * model,
    )


def grad_kernel(plan, chips, batches, order_ref, *refs):
    count = len(plan) * batches
    lefts, rights = refs[:count], refs[count : 2 * count]
    mine_ref, theirs_ref = refs[2 * count : 2 * count + 2]
    stores = refs[2 * count + 2 :]
    core = order_ref[chips]
    model = mine_ref.shape[2]
    for index, (rows, low, size, blocks, start) in enumerate(plan):
        left, right = lefts[index * batches :][:batches], rights[index * batches :][:batches]
        for target, side, store in (
            (theirs_ref, 1 - core, stores[2 * index]),
            (mine_ref, core, stores[2 * index + 1]),
        ):
            for t in range(chips):
                place = pl.multiple_of((2 * order_ref[t] + side) * rows + low, 16)
                for batch in range(batches):
                    store[batch, t * size : (t + 1) * size, :] = left[batch][pl.ds(place, size), :]
            for block in range(blocks):
                value = None
                for batch in range(batches):
                    term = dot_plain(store[batch], right[batch][:, part_of(block, model)])
                    value = term if value is None else value + term
                value = value.astype(jnp.bfloat16).reshape(chips, size, model)
                target[:, start + block * size : start + (block + 1) * size, :] = value


def weight_grads(order, parts, model):
    batches = len(parts[0][0])
    tokens = parts[0][0][0].shape[1]
    chips = order.shape[0] - 1
    plan, scratch, start = [], [], 0
    for left, right, low, size in parts:
        rows = left[0].shape[0] // (2 * chips)
        blocks = right[0].shape[1] // model
        plan.append((rows, low, size, blocks, start))
        scratch += [pltpu.VMEM((batches, chips * size, tokens), jnp.bfloat16)] * 2
        start += size * blocks
    shape = low_shape(chips, start, model)
    lefts = [array for part in parts for array in part[0]]
    rights = [array for part in parts for array in part[1]]
    flops = 4 * chips * start * model * tokens * batches
    return flat_call(
        functools.partial(grad_kernel, tuple(plan), chips, batches),
        (order, *lefts, *rights),
        [shape, shape],
        scratch=scratch,
        flops=flops,
        moved=4 * chips * start * model + 8 * tokens * batches * model,
        scalars=True,
    )


def local(
    inputs,
    teacher,
    lengths,
    attn_query,
    attn_key,
    attn_value,
    attn_out,
    ffn_gate,
    ffn_up,
    ffn_down,
    norm_attn,
    norm_ffn,
    norm_query,
    norm_key,
):
    section = lax.axis_index("section")
    index = lax.axis_index("dp")
    devices = lax.axis_size("dp")
    chips = devices // 2
    batches, _, model = inputs.shape
    slots = lengths.shape[2]
    rows = attn_query.shape[1]
    forward_rows = ffn_down.shape[1]

    attn_shard = jnp.concatenate(
        packed(attn_query[0], model)
        + [attn_out[0]]
        + packed(attn_key[0], model)
        + packed(attn_value[0], model),
        axis=0,
    )
    ffn_shard = jnp.concatenate(
        packed(ffn_gate[0], model) + [ffn_down[0]] + packed(ffn_up[0], model), axis=0
    )
    attn_whole, attn_marks = gather_ring(attn_shard)
    ffn_whole, ffn_marks = gather_ring(ffn_shard, attn_marks[min(RING_LEAD, chips - 2)])

    gain_sizes = (norm_attn.shape[1], norm_query.shape[1], norm_key.shape[1], norm_ffn.shape[1])
    gain_shard = jnp.concatenate([norm_attn, norm_query, norm_key, norm_ffn], axis=1)
    gain_shard, _ = tie(gain_shard.astype(jnp.float32), attn_marks[min(2, chips - 2)])
    gain_whole = spread(gain_shard)
    gains, low = [], 0
    for size in gain_sizes:
        gains.append(gain_whole[:, low : low + size].reshape(1, devices * size))
        low += size

    segments, places = jax.vmap(layout)(lengths[:, 0, :])
    keep = (segments < slots - 1).astype(jnp.float32)
    tables = []
    for batch in range(batches):
        cosine_table, sine_table = rotary_tables(places[batch])
        tables.append(
            (
                jnp.concatenate([cosine_table, cosine_table], axis=1),
                jnp.concatenate([-sine_table, sine_table], axis=1),
                segments[batch].reshape(TOKENS_PER_SHARD, 1),
                segments[batch].reshape(1, 1, TOKENS_PER_SHARD),
            )
        )
    both = range(batches)

    def waiting(value, marks, step):
        return tie(value, marks[min(step, chips - 2)])[0]

    first = [inputs[batch] for batch in both]
    carried, seen = [], []
    for batch in both:
        start = waiting(first[batch], ffn_marks, FIRST_WAIT + batch)
        seen.append(attention(start, gains, tables[batch], attn_whole, False))
    for batch in both:
        (result,) = feed_forward(seen[batch][1], seen[batch][0], ffn_whole, False)
        carried.append(one_way(result, 0))

    kept = []
    for batch in both:
        hidden = jnp.where(section == 0, first[batch], carried[batch])
        mid, norm, norm_t, normalized_t, mix_t, qkv, pre = attention(
            hidden, gains, tables[batch], attn_whole, True
        )
        result, gate, up, inner_t = feed_forward(norm, mid, ffn_whole, True)
        kept.append((hidden, normalized_t, qkv, pre, mix_t, mid, norm_t, result, gate, up, inner_t))
    hidden, normalized_t, qkv, pre, mixed_t, middle, normed_t, result, gate, up, inner_t = (
        list(column) for column in zip(*kept)
    )

    cotangent, squares = [], 0.0
    for batch in both:
        diff = result[batch].astype(jnp.float32) - teacher[batch]
        cotangent.append(keep[batch][:, None] * diff)
        squares = squares + jnp.sum(cotangent[batch] * diff)

    core = index % 2
    place = ring_place(index // 2, chips)
    order = jnp.concatenate(
        [chip_at(place + jnp.arange(chips, dtype=jnp.int32), chips), core[None]]
    ).astype(jnp.int32)
    cut = forward_rows // 2 if forward_rows % 32 == 0 else 2 * rows

    incoming = []
    for batch in both:
        d_middle, d_attn, _, _, _ = feed_forward_back(
            cotangent[batch], middle[batch], gains, gate[batch], up[batch], ffn_whole
        )
        d_hidden = attention_back(
            d_attn, d_middle, hidden[batch], qkv[batch], pre[batch], gains, tables[batch], attn_whole
        )[3]
        incoming.append(one_way(d_hidden, 1))

    d_middle, d_attn, d_gate, d_up, d_branch, gain_ffn = [], [], [], [], [], 0.0
    for batch in both:
        d_result = jnp.where(
            section == 1, cotangent[batch], incoming[batch].astype(jnp.float32)
        )
        d_branch.append(d_result.astype(jnp.bfloat16))
        m, a, g, u, gain = feed_forward_back(
            d_result, middle[batch], gains, gate[batch], up[batch], ffn_whole
        )
        d_middle.append(m)
        d_attn.append(a)
        d_gate.append(g)
        d_up.append(u)
        gain_ffn = gain_ffn + gain
    forward_parts = weight_grads(
        order, [(normed_t, d_gate, 0, rows), (inner_t, d_branch, 0, cut)], model
    )
    behind_parts = weight_grads(
        order, [(inner_t, d_branch, cut, forward_rows - cut), (normed_t, d_up, 0, rows)], model
    )
    ffn_grad, marks = scatter_ring(forward_parts, behind_parts)
    d_query, d_key, d_value, d_hidden = [], [], [], []
    gain_attn, gain_query, gain_key = 0.0, 0.0, 0.0
    for batch in both:
        if batch == 0:
            value, _ = tie(d_attn[batch], (forward_parts, behind_parts))
        else:
            value = waiting(d_attn[batch], marks, batch - 1)
        q, k, v, x, gain_a, gain_q, gain_k = attention_back(
            value, d_middle[batch], hidden[batch], qkv[batch], pre[batch], gains, tables[batch],
            attn_whole,
        )
        d_query.append(q)
        d_key.append(k)
        d_value.append(v)
        d_hidden.append(x)
        gain_attn = gain_attn + gain_a
        gain_query = gain_query + gain_q
        gain_key = gain_key + gain_k
    gain_grads = (gain_attn, gain_query, gain_key, gain_ffn)
    attn_grad, attn_marks = scatter_ring(
        weight_grads(
            waiting(order, marks, 1),
            [(normalized_t, d_query, 0, rows), (mixed_t, d_attn, 0, rows)],
            model,
        ),
        weight_grads(
            waiting(order, marks, 2),
            [
                (mixed_t, d_attn, rows, rows),
                (normalized_t, d_key, 0, rows),
                (normalized_t, d_value, 0, rows),
            ],
            model,
        ),
    )

    grad_gate = beside(ffn_grad, 0, 3, rows)
    grad_down = ffn_grad[3 * rows : 3 * rows + forward_rows]
    grad_up = beside(ffn_grad, 3 * rows + forward_rows, 3, rows)
    grad_query = beside(attn_grad, 0, 2, rows)
    grad_out = attn_grad[2 * rows : 4 * rows]
    grad_key = attn_grad[4 * rows : 5 * rows]
    grad_value = attn_grad[5 * rows :]

    small = jnp.concatenate(
        [*gain_grads, jnp.stack([squares, jnp.sum(keep)])[None]], axis=1
    )
    small_sum = summed(waiting(small, attn_marks, 2))
    totals = small_sum[:, -2:]
    totals = jnp.where(section == 1, totals, one_way(totals, 1))[0]
    loss = totals[0] / (totals[1] * model)
    gain_grads, low = [], 0
    for size in gain_sizes:
        gain_grads.append(lax.dynamic_slice(small_sum, (0, low + index * size), (1, size)))
        low += devices * size
    grad_gain_attn, grad_gain_query, grad_gain_key, grad_gain_ffn = gain_grads

    half = batches // 2
    finals = jnp.stack(result)
    grads = jnp.stack(d_hidden)
    output = jnp.where(section == 0, one_way(finals[:half], 1), finals[half:])
    input_grad = jnp.where(section == 0, grads[:half], one_way(grads[half:], 0))
    return (
        output,
        loss,
        input_grad,
        grad_query[None],
        grad_key[None],
        grad_value[None],
        grad_out[None],
        grad_gate[None],
        grad_up[None],
        grad_down[None],
        grad_gain_attn,
        grad_gain_ffn,
        grad_gain_query,
        grad_gain_key,
    )


def solution(mesh):
    placed = (
        P(None, "dp", None),
        P(None, "dp", None),
        P(None, "dp", None),
        P("section", "dp", None),
        P("section", "dp", None),
        P("section", "dp", None),
        P("section", "dp", None),
        P("section", "dp", None),
        P("section", "dp", None),
        P("section", "dp", None),
        P("section", "dp"),
        P("section", "dp"),
        P("section", "dp"),
        P("section", "dp"),
    )
    return jax.shard_map(
        local,
        mesh=mesh,
        in_specs=placed,
        out_specs=(
            P("section", "dp", None),
            P(),
            P("section", "dp", None),
            P("section", "dp", None),
            P("section", "dp", None),
            P("section", "dp", None),
            P("section", "dp", None),
            P("section", "dp", None),
            P("section", "dp", None),
            P("section", "dp", None),
            P("section", "dp"),
            P("section", "dp"),
            P("section", "dp"),
            P("section", "dp"),
        ),
        check_vma=False,
    )
```

time: 1200 us -> 659 us (0.55)
  local copies, waits for them, and re-layouts: 410 us -> 162 us
  matrix products: 229 us -> 0 us
  Pallas kernels: 0 us -> 143 us
  waiting for transfers between devices: 335 us -> 202 us
  other arithmetic: 103 us -> 47.3 us
  starting transfers between devices: 66.1 us -> 90.5 us
  blocking collectives: 24.2 us -> 0 us
  between operations: 20.5 us -> 6.59 us
    dot_general x46 -> x0, matrix products: 229 us -> none  [the longest x14 72.9 us: times_transpose(): lax.dot_general(left, right, CONTRACT_COLS, preferred_element_type=jnp.fl...]
    pallas_call x0 -> x22, Pallas kernels: none -> 143 us  [the longest x20 143 us: flat_call(): pl.pallas_call(body, in_specs=specs, out_specs=[LOCAL] * len(out_shape),...]
    reshape x14 -> x4, local copies, waits for them, and re-layouts: 84.6 us -> 0.33 us  [local(): gains.append(gain_whole[:, low:low + size].reshape(1, devices * size))]
    unnamed x2 -> x0, waiting for transfers between devices: 82.6 us -> none
    transpose x5 -> x0, local copies, waits for them, and re-layouts: 48.5 us -> none  [the longest x3 33 us: unpacked(): return part.transpose(0, 2, 1, 3).reshape(devices * rows, pieces * width)]
    concatenate x17 -> x0, local copies, waits for them, and re-layouts: 42.7 us -> none  [the longest x16 41.4 us: rotate(): jnp.concatenate([first * turn_cos - second * turn_sin, second * turn_cos...]
    ppermute x14, waiting for transfers between devices: 108 us -> 65.6 us  [scatter_ring(): forward = lax.ppermute(forward, 'dp', right).astype(jnp.float32)]
    ppermute x5 -> x7, waiting for transfers between devices: 54.1 us -> 15.7 us  [one_way(): return lax.ppermute(value, 'section', [(source, 1 - source)])]
  transfers between devices with their start and end apart: 96 -> 105, of which waited for: 41 -> 41; matrix products, arithmetic and copies ran while one was open for 25% -> 18% of each run, Pallas kernels for 0% -> 13%
where the time goes in v3:
time: 659 us; the launch traced here: 650 us
  waiting for transfers between devices  202 us (31%)
  local copies, waits for them, and re-layouts  162 us (25%)
  Pallas kernels  143 us (22%)
  starting transfers between devices  90.5 us (14%)
  other arithmetic  47.3 us (7%)
  between operations  6.59 us (1%)
    pallas_call x20, Pallas kernels, flat_call(): pl.pallas_call(body, in_specs=specs, out_specs=[LOCAL] * len(out_shape),...  143 us
    unnamed x222, local copies, waits for them, and re-layouts  89.9 us
    ppermute x14, waiting for transfers between devices, scatter_ring(): forward = lax.ppermute(forward, 'dp', right).astype(jnp.float32)  65.6 us
    dynamic_update_slice x60, local copies, waits for them, and re-layouts, put(): return lax.dynamic_update_slice(whole, piece[None], (owner, offset, 0))  64.2 us
    ppermute x14, waiting for transfers between devices, gather_ring(): forward = lax.ppermute(forward, 'dp', right)  45.5 us
    ppermute x14, waiting for transfers between devices, gather_ring(): behind = lax.ppermute(behind, 'dp', left)  32.4 us
    ppermute x14, starting transfers between devices, gather_ring(): forward = lax.ppermute(forward, 'dp', right)  25.5 us
    ppermute x14, waiting for transfers between devices, scatter_ring(): behind = lax.ppermute(behind, 'dp', left).astype(jnp.float32)  23.5 us
  transfers between devices with their start and end apart: 105, of which 41 were waited for; matrix products, arithmetic and copies ran while one was open for 18% of the time, Pallas kernels for 13%

profile of v3, /device:TPU:0, one launch (start us, length us, event | category | flops | bytes accessed | tf_op | source)
XLA Modules:
  0.0 650.3 jit_solution(16172220637866524069)
XLA Ops:
  26.2 6.7 %collective-permute-done.1 = bf16[192,1024]{1,0:T(8,128)(2,1)} collective-permute-done((bf16[192,1024]{1,0:T(8,128)(2,1)}, bf16[192,1024]{1,0:T(8,128)(2,1)}, u32[]{:S(2)}, u32[]{:S(2)}) %collective-permute-start.1) | collective-permute-done | bytes 393248 | tf_op jit(solution)/shard_map/ppermute | solution.py:106
  49.4 10.7 %collective-permute-done.12 = bf16[192,1024]{1,0:T(8,128)(2,1)} collective-permute-done((bf16[192,1024]{1,0:T(8,128)(2,1)}, bf16[192,1024]{1,0:T(8,128)(2,1)}, u32[]{:S(2)}, u32[]{:S(2)}) %collective-permute-start.12) | collective-permute-done | bytes 393248 | tf_op jit(solution)/shard_map/ppermute | solution.py:106
  65.6 7.6 %collective-permute-done.15 = f32[2,144]{1,0:T(2,128)S(1)} collective-permute-done((f32[2,144]{1,0:T(2,128)S(1)}, f32[2,144]{1,0:T(2,128)S(1)}, u32[]{:S(2)}, u32[]{:S(2)}) %collective-permute-start.15) | collective-permute-done | bytes 1184 | tf_op jit(solution)/shard_map/ppermute | solution.py:59
  110.3 6.4 collective-permute-done.29
  122.7 7.1 %collective-permute-done.31 = bf16[192,1024]{1,0:T(8,128)(2,1)S(1)} collective-permute-done((bf16[192,1024]{1,0:T(8,128)(2,1)S(1)}, bf16[192,1024]{1,0:T(8,128)(2,1)S(1)}, u32[]{:S(2)}, u32[]{:S(2)}) %collective-permute-start.31) | collective-permute-done | bytes 393248 | tf_op jit(solution)/shard_map/ppermute | solution.py:107
  158.7 6.3 collective-permute-done.39
  168.3 8.3 %collective-permute-done.11 = bf16[288,1024]{1,0:T(8,128)(2,1)S(1)} collective-permute-done((bf16[288,1024]{1,0:T(8,128)(2,1)S(1)}, bf16[288,1024]{1,0:T(8,128)(2,1)S(1)}, u32[]{:S(2)}, u32[]{:S(2)}) %collective-permute-start.11) | collective-permute-done | bytes 589856 | tf_op jit(solution)/shard_map/ppermute | solution.py:107
  214.7 9.8 %collective-permute-done.58 = bf16[288,1024]{1,0:T(8,128)(2,1)S(1)} collective-permute-done((bf16[288,1024]{1,0:T(8,128)(2,1)S(1)}, bf16[288,1024]{1,0:T(8,128)(2,1)S(1)}, u32[]{:S(2)}, u32[]{:S(2)}) %collective-permute-start.58) | collective-permute-done | bytes 589856 | tf_op jit(solution)/shard_map/ppermute | solution.py:106
  231.3 6.4 copy-done
  258.4 10.4 %collective-permute-done.62 = bf16[256,1024]{1,0:T(8,128)(2,1)S(1)} collective-permute-done((bf16[256,1024]{1,0:T(8,128)(2,1)S(1)}, bf16[256,1024]{1,0:T(8,128)(2,1)S(1)}, u32[]{:S(2)}, u32[]{:S(2)}) %collective-permute-start.62) | collective-permute-done | bytes 524320 | tf_op jit(solution)/shard_map/ppermute | solution.py:26
  268.9 6.0 shard_map.249
  279.3 6.1 shard_map.253
  289.5 7.1 %copy-done.1 = bf16[16,576,1024]{2,1,0:T(8,128)(2,1)S(1)} copy-done((bf16[16,576,1024]{2,1,0:T(8,128)(2,1)S(1)}, bf16[16,576,1024]{2,1,0:T(8,128)(2,1)}, u32[]{:S(2)}) %copy-start.1) | copy-done | bytes 18874392
  318.9 7.2 %shard_map.255 = (f32[256,1024]{1,0:T(8,128)S(1)}, bf16[256,1024]{1,0:T(8,128)(2,1)S(1)}, bf16[256,3072]{1,0:T(8,128)(2,1)}, bf16[256,3072]{1,0:T(8,128)(2,1)}, f32[1,1024]{1,0:T(1,128)}) custom-call(f32[256,1024]{1,0:T(8,128)S(1)} %get-tuple-element.165.dy_ref, f32[256,1024]{1,0:T(8,128)S(1)} %copy-done.10, f32[1,1024]{1,0:T(1,128)S(1)} %reshape.225.gain_ffn_ref.gain_ref, ...), custom_call_target="tpu_custom_call" | custom-call | flops 4831838208 | bytes 28835840 | tf_op jit(solution)/shard_map/pallas_call | solution.py:187
  331.9 13.2 %shard_map.256 = (bf16[256,2048]{1,0:T(8,128)(2,1)}, bf16[256,1024]{1,0:T(8,128)(2,1)}, bf16[256,1024]{1,0:T(8,128)(2,1)}, bf16[256,1024]{1,0:T(8,128)(2,1)}, f3...) custom-call(bf16[256,1024]{1,0:T(8,128)(2,1)S(1)} %get-tuple-element.103.low_ref, ...), custom_call_target="tpu_custom_call" | custom-call | flops 5905580032 | bytes 23068672 | tf_op jit(solution)/shard_map/pallas_call | solution.py:187
  346.5 6.4 copy-done.2
  355.7 6.7 %shard_map.258 = (f32[256,1024]{1,0:T(8,128)S(1)}, bf16[256,1024]{1,0:T(8,128)(2,1)S(1)}, bf16[256,3072]{1,0:T(8,128)(2,1)}, bf16[256,3072]{1,0:T(8,128)(2,1)}, f32[1,1024]{1,0:T(1,128)}) custom-call(f32[256,1024]{1,0:T(8,128)S(1)} %copy-done.12, f32[256,1024]{1,0:T(8,128)S(1)} %copy-done.7, f32[1,1024]{1,0:T(1,128)S(1)} %reshape.225.gain_ffn_ref.gain_ref, ...), custom_call_target="tpu_custom_call" | custom-call | flops 4831838208 | bytes 28835840 | tf_op jit(solution)/shard_map/pallas_call | solution.py:187
  367.4 13.4 %shard_map.259 = (bf16[256,2048]{1,0:T(8,128)(2,1)}, bf16[256,1024]{1,0:T(8,128)(2,1)}, bf16[256,1024]{1,0:T(8,128)(2,1)}, bf16[256,1024]{1,0:T(8,128)(2,1)S(1)}...) custom-call(bf16[256,1024]{1,0:T(8,128)(2,1)S(1)} %get-tuple-element.116.low_ref, ...), custom_call_target="tpu_custom_call" | custom-call | flops 5905580032 | bytes 23068672 | tf_op jit(solution)/shard_map/pallas_call | solution.py:187
  383.3 6.4 copy-done.3
  392.5 6.1 shard_map.257
  400.9 6.1 shard_map.260
  413.0 7.6 %shard_map.262 = (bf16[8,288,1024]{2,1,0:T(8,128)(2,1)S(1)}, bf16[8,288,1024]{2,1,0:T(8,128)(2,1)}) custom-call(s32[9]{0:T(128)S(1)} %pad_add_fusion.order_ref, bf16[3072,256]{1,0:T(8,128)(2,1)S(1)} %copy-done.51, bf16[3072,256]{1,0:T(8,128)(2,1)S(1)} %copy-done.53, bf16[1024,256]{1,0:T(8,128)(2,1)S(1)} %copy-done.86, bf16[1024,256]{1,0:T(8,128)(2,1)S(1)} %copy-done.88, ...), custom_call_target="tpu_custom_call" | custom-call | flops 4831838208 | bytes 13631488 | tf_op jit(solution)/shard_map/pallas_call | solution.py:187
  433.0 8.3 %collective-permute-done.69 = bf16[288,1024]{1,0:T(8,128)(2,1)} collective-permute-done((bf16[288,1024]{1,0:T(8,128)(2,1)}, bf16[288,1024]{1,0:T(8,128)(2,1)}, u32[]{:S(2)}, u32[]{:S(2)}) %collective-permute-start.69) | collective-permute-done | bytes 589856 | tf_op jit(solution)/shard_map/ppermute | solution.py:141
  454.8 12.2 %shard_map.263 = (bf16[256,2048]{1,0:T(8,128)(2,1)S(1)}, bf16[256,1024]{1,0:T(8,128)(2,1)S(1)}, bf16[256,1024]{1,0:T(8,128)(2,1)S(1)}, bf16[256,1024]{1,0:T(8,12...) custom-call(bf16[256,1024]{1,0:T(8,128)(2,1)S(1)} %copy-done.59, ...), custom_call_target="tpu_custom_call" | custom-call | flops 5905580032 | bytes 23068672 | tf_op jit(solution)/shard_map/pallas_call | solution.py:187
  475.5 12.3 %shard_map.264 = (bf16[256,2048]{1,0:T(8,128)(2,1)S(1)}, bf16[256,1024]{1,0:T(8,128)(2,1)S(1)}, bf16[256,1024]{1,0:T(8,128)(2,1)S(1)}, bf16[256,1024]{1,0:T(8,12...) custom-call(bf16[256,1024]{1,0:T(8,128)(2,1)S(1)} %copy-done.62, ...), custom_call_target="tpu_custom_call" | custom-call | flops 5905580032 | bytes 23068672 | tf_op jit(solution)/shard_map/pallas_call | solution.py:187
  515.9 5.9 collective-permute-done.101
  523.5 6.4 collective-permute-done.97
  537.1 8.1 %collective-permute-done.98 = bf16[288,1024]{1,0:T(8,128)(2,1)S(1)} collective-permute-done((bf16[288,1024]{1,0:T(8,128)(2,1)S(1)}, bf16[288,1024]{1,0:T(8,128)(2,1)S(1)}, u32[]{:S(2)}, u32[]{:S(2)}) %collective-permute-start.98) | collective-permute-done | bytes 589856 | tf_op jit(solution)/shard_map/ppermute | solution.py:141
  552.7 9.1 %collective-permute-done.99 = bf16[288,1024]{1,0:T(8,128)(2,1)S(1)} collective-permute-done((bf16[288,1024]{1,0:T(8,128)(2,1)S(1)}, bf16[288,1024]{1,0:T(8,128)(2,1)S(1)}, u32[]{:S(2)}, u32[]{:S(2)}) %collective-permute-start.99) | collective-permute-done | bytes 589856 | tf_op jit(solution)/shard_map/ppermute | solution.py:141
  606.4 6.2 collective-permute-done.87
  617.4 8.4 %collective-permute-done.88 = bf16[192,1024]{1,0:T(8,128)(2,1)S(1)} collective-permute-done((bf16[192,1024]{1,0:T(8,128)(2,1)S(1)}, bf16[192,1024]{1,0:T(8,128)(2,1)S(1)}, u32[]{:S(2)}, u32[]{:S(2)}) %collective-permute-start.88) | collective-permute-done | bytes 393248 | tf_op jit(solution)/shard_map/ppermute | solution.py:141
  640.9 6.1 collective-permute-done.94
  (578 shorter events, 388.9 us)
Async XLA Ops:
  13.8 23.3 %collective-permute-start.18 = (bf16[384,1024]{1,0:T(8,128)(2,1)}, bf16[384,1024]{1,0:T(8,128)(2,1)}, u32[]{:S(2)}, u32[]{:S(2)}) collective-permute-start(bf16[384,1024]{1,0:T(8,128)(2,1)} %constant_dynamic-update-slice_fusion), channel_id=1, source_target_pairs={{0,1},{1,0},{2,3},{3,2},{4,5},{5,4},{6,7},{7,6},{8,9},{9,8},{10,11... | collective-permute-start | bytes 2359304 | tf_op jit(solution)/shard_map/ppermute | solution.py:109
  25.9 19.8 %collective-permute-start.20 = (bf16[192,1024]{1,0:T(8,128)(2,1)}, bf16[192,1024]{1,0:T(8,128)(2,1)S(1)}, u32[]{:S(2)}, u32[]{:S(2)}) collective-permute-start(bf16[192,1024]{1,0:T(8,128)(2,1)} %collective-permute-done.2), channel_id=1, source_target_pairs={{0,1},{1,0},{2,3},{3,2},{4,5},{5,4},{6,7},{7,6},{8,9},{9,8},{10,11... | collective-permute-start | bytes 1179656 | tf_op jit(solution)/shard_map/ppermute | solution.py:114
  34.5 62.0 %collective-permute-start.41 = (bf16[576,1024]{1,0:T(8,128)(2,1)S(1)}, bf16[576,1024]{1,0:T(8,128)(2,1)}, u32[]{:S(2)}, u32[]{:S(2)}) collective-permute-start(bf16[576,1024]{1,0:T(8,128)(2,1)S(1)} %slice_dynamic-update-slice_fusion), channel_id=1, source_target_pairs={{0,1},{1,0},{2,3},{3,2},{4,5},{5,4},{6,7},{7,6},{8,9},{9,8},{10,11... | collective-permute-start | bytes 3538952 | tf_op jit(solution)/shard_map/ppermute | solution.py:109
  35.6 53.5 %collective-permute-start.4 = (bf16[288,1024]{1,0:T(8,128)(2,1)}, bf16[288,1024]{1,0:T(8,128)(2,1)}, u32[]{:S(2)}, u32[]{:S(2)}) collective-permute-start(bf16[288,1024]{1,0:T(8,128)(2,1)} %get-tuple-element.177), channel_id=1, source_target_pairs={{0,4},{1,5},{4,8},{5,9},{8,12},{9,13},{12,14},{13,15},{14,10},{15,... | collective-permute-start | bytes 1769480 | tf_op jit(solution)/shard_map/ppermute | solution.py:106
  37.2 22.9 %collective-permute-start.12 = (bf16[192,1024]{1,0:T(8,128)(2,1)}, bf16[192,1024]{1,0:T(8,128)(2,1)}, u32[]{:S(2)}, u32[]{:S(2)}) collective-permute-start(bf16[192,1024]{1,0:T(8,128)(2,1)} %collective-permute-done.1), channel_id=1, source_target_pairs={{0,4},{1,5},{4,8},{5,9},{8,12},{9,13},{12,14},{13,15},{14,10},{15,... | collective-permute-start | bytes 1179656 | tf_op jit(solution)/shard_map/ppermute | solution.py:106
  42.6 17.8 %collective-permute-start.13 = (bf16[192,1024]{1,0:T(8,128)(2,1)}, bf16[192,1024]{1,0:T(8,128)(2,1)}, u32[]{:S(2)}, u32[]{:S(2)}) collective-permute-start(bf16[192,1024]{1,0:T(8,128)(2,1)} %collective-permute-done.3), channel_id=1, source_target_pairs={{4,0},{5,1},{8,4},{9,5},{12,8},{13,9},{14,12},{15,13},{10,14},{11,... | collective-permute-start | bytes 1179656 | tf_op jit(solution)/shard_map/ppermute | solution.py:107
  60.1 32.9 %collective-permute-start.8 = (bf16[288,1024]{1,0:T(8,128)(2,1)}, bf16[288,1024]{1,0:T(8,128)(2,1)}, u32[]{:S(2)}, u32[]{:S(2)}) collective-permute-start(bf16[288,1024]{1,0:T(8,128)(2,1)} %get-tuple-element.176), channel_id=1, source_target_pairs={{4,0},{5,1},{8,4},{9,5},{12,8},{13,9},{14,12},{15,13},{10,14},{11,... | collective-permute-start | bytes 1769480 | tf_op jit(solution)/shard_map/ppermute | solution.py:107
  89.1 19.2 %collective-permute-start.5 = (bf16[288,1024]{1,0:T(8,128)(2,1)}, bf16[288,1024]{1,0:T(8,128)(2,1)S(1)}, u32[]{:S(2)}, u32[]{:S(2)}) collective-permute-start(bf16[288,1024]{1,0:T(8,128)(2,1)} %collective-permute-done.4), channel_id=1, source_target_pairs={{0,4},{1,5},{4,8},{5,9},{8,12},{9,13},{12,14},{13,15},{14,10},{15,... | collective-permute-start | bytes 1769480 | tf_op jit(solution)/shard_map/ppermute | solution.py:106
  106.1 25.8 %collective-permute-start.9 = (bf16[288,1024]{1,0:T(8,128)(2,1)}, bf16[288,1024]{1,0:T(8,128)(2,1)S(1)}, u32[]{:S(2)}, u32[]{:S(2)}) collective-permute-start(bf16[288,1024]{1,0:T(8,128)(2,1)} %collective-permute-done.8), channel_id=1, source_target_pairs={{4,0},{5,1},{8,4},{9,5},{12,8},{13,9},{14,12},{15,13},{10,14},{11,... | collective-permute-start | bytes 1769480 | tf_op jit(solution)/shard_map/ppermute | solution.py:107
  108.3 21.5 %collective-permute-start.31 = (bf16[192,1024]{1,0:T(8,128)(2,1)S(1)}, bf16[192,1024]{1,0:T(8,128)(2,1)S(1)}, u32[]{:S(2)}, u32[]{:S(2)}) collective-permute-start(bf16[192,1024]{1,0:T(8,128)(2,1)S(1)} %collective-permute-done.27), channel_id=1, source_target_pairs={{4,0},{5,1},{8,4},{9,5},{12,8},{13,9},{14,12},{15,13},{10,14},{11,... | collective-permute-start | bytes 1179656 | tf_op jit(solution)/shard_map/ppermute | solution.py:107
  109.3 37.1 %collective-permute-start.6 = (bf16[288,1024]{1,0:T(8,128)(2,1)S(1)}, bf16[288,1024]{1,0:T(8,128)(2,1)S(1)}, u32[]{:S(2)}, u32[]{:S(2)}) collective-permute-start(bf16[288,1024]{1,0:T(8,128)(2,1)S(1)} %collective-permute-done.5), channel_id=1, source_target_pairs={{0,4},{1,5},{4,8},{5,9},{8,12},{9,13},{12,14},{13,15},{14,10},{15,... | collective-permute-start | bytes 1769480 | tf_op jit(solution)/shard_map/ppermute | solution.py:106
  119.2 18.2 %collective-permute-start.33 = (bf16[192,1024]{1,0:T(8,128)(2,1)S(1)}, bf16[192,1024]{1,0:T(8,128)(2,1)S(1)}, u32[]{:S(2)}, u32[]{:S(2)}) collective-permute-start(bf16[192,1024]{1,0:T(8,128)(2,1)S(1)} %collective-permute-done.29), channel_id=1, source_target_pairs={{0,4},{1,5},{4,8},{5,9},{8,12},{9,13},{12,14},{13,15},{14,10},{15,... | collective-permute-start | bytes 1179656 | tf_op jit(solution)/shard_map/ppermute | solution.py:106
  132.4 24.1 %collective-permute-start.10 = (bf16[288,1024]{1,0:T(8,128)(2,1)S(1)}, bf16[288,1024]{1,0:T(8,128)(2,1)S(1)}, u32[]{:S(2)}, u32[]{:S(2)}) collective-permute-start(bf16[288,1024]{1,0:T(8,128)(2,1)S(1)} %collective-permute-done.9), channel_id=1, source_target_pairs={{4,0},{5,1},{8,4},{9,5},{12,8},{13,9},{14,12},{15,13},{10,14},{11,... | collective-permute-start | bytes 1769480 | tf_op jit(solution)/shard_map/ppermute | solution.py:107
  146.3 18.6 %collective-permute-start.39 = (bf16[192,1024]{1,0:T(8,128)(2,1)S(1)}, bf16[192,1024]{1,0:T(8,128)(2,1)S(1)}, u32[]{:S(2)}, u32[]{:S(2)}) collective-permute-start(bf16[192,1024]{1,0:T(8,128)(2,1)S(1)} %collective-permute-done.35), channel_id=1, source_target_pairs={{4,0},{5,1},{8,4},{9,5},{12,8},{13,9},{14,12},{15,13},{10,14},{11,... | collective-permute-start | bytes 1179656 | tf_op jit(solution)/shard_map/ppermute | solution.py:107
  147.6 20.7 %collective-permute-start.7 = (bf16[288,1024]{1,0:T(8,128)(2,1)S(1)}, bf16[288,1024]{1,0:T(8,128)(2,1)S(1)}, u32[]{:S(2)}, u32[]{:S(2)}) collective-permute-start(bf16[288,1024]{1,0:T(8,128)(2,1)S(1)} %collective-permute-done.6), channel_id=1, source_target_pairs={{0,4},{1,5},{4,8},{5,9},{8,12},{9,13},{12,14},{13,15},{14,10},{15,... | collective-permute-start | bytes 1769480 | tf_op jit(solution)/shard_map/ppermute | solution.py:106
  156.5 22.3 %collective-permute-start.46 = (bf16[288,1024]{1,0:T(8,128)(2,1)S(1)}, bf16[288,1024]{1,0:T(8,128)(2,1)S(1)}, u32[]{:S(2)}, u32[]{:S(2)}) collective-permute-start(bf16[288,1024]{1,0:T(8,128)(2,1)S(1)} %collective-permute-done.6), channel_id=1, source_target_pairs={{0,1},{1,0},{2,3},{3,2},{4,5},{5,4},{6,7},{7,6},{8,9},{9,8},{10,11... | collective-permute-start | bytes 1769480 | tf_op jit(solution)/shard_map/ppermute | solution.py:113
  156.5 20.1 %collective-permute-start.11 = (bf16[288,1024]{1,0:T(8,128)(2,1)S(1)}, bf16[288,1024]{1,0:T(8,128)(2,1)S(1)}, u32[]{:S(2)}, u32[]{:S(2)}) collective-permute-start(bf16[288,1024]{1,0:T(8,128)(2,1)S(1)} %collective-permute-done.10), channel_id=1, source_target_pairs={{4,0},{5,1},{8,4},{9,5},{12,8},{13,9},{14,12},{15,13},{10,14},{11,... | collective-permute-start | bytes 1769480 | tf_op jit(solution)/shard_map/ppermute | solution.py:107
  178.8 18.5 %collective-permute-start.49 = (bf16[288,1024]{1,0:T(8,128)(2,1)S(1)}, bf16[288,1024]{1,0:T(8,128)(2,1)S(1)}, u32[]{:S(2)}, u32[]{:S(2)}) collective-permute-start(bf16[288,1024]{1,0:T(8,128)(2,1)S(1)} %collective-permute-done.11), channel_id=1, source_target_pairs={{0,1},{1,0},{2,3},{3,2},{4,5},{5,4},{6,7},{7,6},{8,9},{9,8},{10,11... | collective-permute-start | bytes 1769480 | tf_op jit(solution)/shard_map/ppermute | solution.py:114
  193.0 17.7 %collective-permute-start.51 = (bf16[288,1024]{1,0:T(8,128)(2,1)S(1)}, bf16[288,1024]{1,0:T(8,128)(2,1)S(1)}, u32[]{:S(2)}, u32[]{:S(2)}) collective-permute-start(bf16[288,1024]{1,0:T(8,128)(2,1)S(1)} %collective-permute-done.50), channel_id=1, source_target_pairs={{0,1},{1,0},{2,3},{3,2},{4,5},{5,4},{6,7},{7,6},{8,9},{9,8},{10,11... | collective-permute-start | bytes 1769480 | tf_op jit(solution)/shard_map/ppermute | solution.py:113
  193.0 20.0 %collective-permute-start.53 = (bf16[288,1024]{1,0:T(8,128)(2,1)S(1)}, bf16[288,1024]{1,0:T(8,128)(2,1)S(1)}, u32[]{:S(2)}, u32[]{:S(2)}) collective-permute-start(bf16[288,1024]{1,0:T(8,128)(2,1)S(1)} %collective-permute-done.52), channel_id=1, source_target_pairs={{0,1},{1,0},{2,3},{3,2},{4,5},{5,4},{6,7},{7,6},{8,9},{9,8},{10,11... | collective-permute-start | bytes 1769480 | tf_op jit(solution)/shard_map/ppermute | solution.py:114
  345.2 36.8 %collective-permute-start.65 = (bf16[256,1024]{1,0:T(8,128)(2,1)}, bf16[256,1024]{1,0:T(8,128)(2,1)}, u32[]{:S(2)}, u32[]{:S(2)}) collective-permute-start(bf16[256,1024]{1,0:T(8,128)(2,1)} %get-tuple-element.107), channel_id=1, source_target_pairs={{16,0},{17,1},{18,2},{19,3},{20,4},{21,5},{22,6},{23,7},{24,8},{25... | collective-permute-start | bytes 1572872 | tf_op jit(solution)/shard_map/ppermute | solution.py:26
  380.7 18.9 %collective-permute-start.66 = (bf16[256,1024]{1,0:T(8,128)(2,1)S(1)}, bf16[256,1024]{1,0:T(8,128)(2,1)S(1)}, u32[]{:S(2)}, u32[]{:S(2)}) collective-permute-start(bf16[256,1024]{1,0:T(8,128)(2,1)S(1)} %get-tuple-element.120), channel_id=1, source_target_pairs={{16,0},{17,1},{18,2},{19,3},{20,4},{21,5},{22,6},{23,7},{24,8},{25... | collective-permute-start | bytes 1572872 | tf_op jit(solution)/shard_map/ppermute | solution.py:26
  428.0 39.8 %collective-permute-start.63 = (bf16[1,256,1024]{2,1,0:T(8,128)(2,1)S(1)}, bf16[1,256,1024]{2,1,0:T(8,128)(2,1)}, u32[]{:S(2)}, u32[]{:S(2)}) collective-permute-start(bf16[1,256,1024]{2,1,0:T(8,128)(2,1)S(1)} %bitcast.310), channel_id=1, source_target_pairs={{16,0},{17,1},{18,2},{19,3},{20,4},{21,5},{22,6},{23,7},{24,8},{25... | collective-permute-start | bytes 1572872 | tf_op jit(solution)/shard_map/ppermute | solution.py:26
  432.6 37.5 %collective-permute-start.70 = (bf16[288,1024]{1,0:T(8,128)(2,1)S(1)}, bf16[288,1024]{1,0:T(8,128)(2,1)S(1)}, u32[]{:S(2)}, u32[]{:S(2)}) collective-permute-start(bf16[288,1024]{1,0:T(8,128)(2,1)S(1)} %fusion.28), channel_id=1, source_target_pairs={{4,0},{5,1},{8,4},{9,5},{12,8},{13,9},{14,12},{15,13},{10,14},{11,... | collective-permute-start | bytes 1769480 | tf_op jit(solution)/shard_map/ppermute | solution.py:142
  443.0 29.4 %collective-permute-start.74 = (bf16[288,1024]{1,0:T(8,128)(2,1)S(1)}, bf16[288,1024]{1,0:T(8,128)(2,1)S(1)}, u32[]{:S(2)}, u32[]{:S(2)}) collective-permute-start(bf16[288,1024]{1,0:T(8,128)(2,1)S(1)} %fusion.11), channel_id=1, source_target_pairs={{0,4},{1,5},{4,8},{5,9},{8,12},{9,13},{12,14},{13,15},{14,10},{15,... | collective-permute-start | bytes 1769480 | tf_op jit(solution)/shard_map/ppermute | solution.py:141
  471.6 21.5 %collective-permute-start.75 = (bf16[288,1024]{1,0:T(8,128)(2,1)S(1)}, bf16[288,1024]{1,0:T(8,128)(2,1)S(1)}, u32[]{:S(2)}, u32[]{:S(2)}) collective-permute-start(bf16[288,1024]{1,0:T(8,128)(2,1)S(1)} %fusion.10), channel_id=1, source_target_pairs={{4,0},{5,1},{8,4},{9,5},{12,8},{13,9},{14,12},{15,13},{10,14},{11,... | collective-permute-start | bytes 1769480 | tf_op jit(solution)/shard_map/ppermute | solution.py:142
  473.7 21.1 %collective-permute-start.95 = (bf16[288,1024]{1,0:T(8,128)(2,1)S(1)}, bf16[288,1024]{1,0:T(8,128)(2,1)S(1)}, u32[]{:S(2)}, u32[]{:S(2)}) collective-permute-start(bf16[288,1024]{1,0:T(8,128)(2,1)S(1)} %fusion.9), channel_id=1, source_target_pairs={{0,4},{1,5},{4,8},{5,9},{8,12},{9,13},{12,14},{13,15},{14,10},{15,... | collective-permute-start | bytes 1769480 | tf_op jit(solution)/shard_map/ppermute | solution.py:141
  487.9 59.3 %collective-permute-start.84 = (bf16[1,256,1024]{2,1,0:T(8,128)(2,1)S(1)}, bf16[1,256,1024]{2,1,0:T(8,128)(2,1)S(1)}, u32[]{:S(2)}, u32[]{:S(2)}) collective-permute-start(bf16[1,256,1024]{2,1,0:T(8,128)(2,1)S(1)} %bitcast.311), channel_id=1, source_target_pairs={{0,16},{1,17},{2,18},{3,19},{4,20},{5,21},{6,22},{7,23},{8,24},{9,... | collective-permute-start | bytes 1572872 | tf_op jit(solution)/shard_map/ppermute | solution.py:26
  502.0 47.8 %collective-permute-start.71 = (bf16[8,192,1024]{2,1,0:T(8,128)(2,1)S(1)}, bf16[8,192,1024]{2,1,0:T(8,128)(2,1)}, u32[]{:S(2)}, u32[]{:S(2)}) collective-permute-start(bf16[8,192,1024]{2,1,0:T(8,128)(2,1)S(1)} %get-tuple-element.149), channel_id=1, source_target_pairs={{0,1},{1,0},{2,3},{3,2},{4,5},{5,4},{6,7},{7,6},{8,9},{9,8},{10,11... | collective-permute-start | bytes 9437192 | tf_op jit(solution)/shard_map/ppermute | solution.py:130
  513.7 48.5 %collective-permute-start.76 = (bf16[8,192,1024]{2,1,0:T(8,128)(2,1)S(1)}, bf16[8,192,1024]{2,1,0:T(8,128)(2,1)S(1)}, u32[]{:S(2)}, u32[]{:S(2)}) collective-permute-start(bf16[8,192,1024]{2,1,0:T(8,128)(2,1)S(1)} %get-tuple-element.156), channel_id=1, source_target_pairs={{0,1},{1,0},{2,3},{3,2},{4,5},{5,4},{6,7},{7,6},{8,9},{9,8},{10,11... | collective-permute-start | bytes 9437192 | tf_op jit(solution)/shard_map/ppermute | solution.py:130
  549.5 31.6 %collective-permute-start.104 = (bf16[288,1024]{1,0:T(8,128)(2,1)S(1)}, bf16[288,1024]{1,0:T(8,128)(2,1)S(1)}, u32[]{:S(2)}, u32[]{:S(2)}) collective-permute-start(bf16[288,1024]{1,0:T(8,128)(2,1)S(1)} %fusion), channel_id=1, source_target_pairs={{4,0},{5,1},{8,4},{9,5},{12,8},{13,9},{14,12},{15,13},{10,14},{11,... | collective-permute-start | bytes 1769480 | tf_op jit(solution)/shard_map/ppermute | solution.py:142
  605.1 24.2 %collective-permute-start.83 = (f32[1,2]{1,0:T(1,128)S(1)}, f32[1,2]{1,0:T(1,128)S(1)}, u32[]{:S(2)}, u32[]{:S(2)}) collective-permute-start(f32[1,2]{1,0:T(1,128)S(1)} %slice.456), channel_id=1, source_target_pairs={{16,0},{17,1},{18,2},{19,3},{20,4},{21,5},{22,6},{23,7},{24,8},{25... | collective-permute-start | bytes 32 | tf_op jit(solution)/shard_map/ppermute | solution.py:26
  (179 other events, 2419.4 us)

commit v4 on v3

--- a/solution.py
+++ b/solution.py
@@ -20,6 +20,9 @@
 CONTRACT_COLS = (((1,), (1,)), ((), ()))
 RING_LEAD = 1
 FIRST_WAIT = 3
+SLOT_DEPTH = 2
+VMEM_GRANT = 10
+BLANK_SPACE = pl.ANY
 
 
 def one_way(value, source):
@@ -38,13 +41,11 @@
 def ring_routes(devices):
     chips = devices // 2
     order = list(range(0, chips, 2)) + list(range(chips - 1, 0, -2))
-    right, left = [], []
+    around = []
     for place in range(chips):
         here, there = order[place], order[(place + 1) % chips]
-        for core in range(2):
-            right.append((2 * here + core, 2 * there + core))
-            left.append((2 * there + core, 2 * here + core))
-    return right, left, [(device, device ^ 1) for device in range(devices)]
+        around += [(2 * here, 2 * there), (2 * there + 1, 2 * here + 1)]
+    return around, [(device, device ^ 1) for device in range(devices)]
 
 
 def tie(*values):
@@ -79,79 +80,93 @@
 def blank(shape, dtype):
     return pl.pallas_call(
         lambda ref: None,
-        out_specs=pl.BlockSpec(memory_space=pl.ANY),
+        out_specs=pl.BlockSpec(memory_space=BLANK_SPACE),
         out_shape=jax.ShapeDtypeStruct(shape, dtype),
     )()
 
 
-def gather_ring(shard, after=None):
+def gather_ring(packed, rows, after=None):
     devices = lax.axis_size("dp")
     chips = devices // 2
-    right, left, pair = ring_routes(devices)
+    around, pair = ring_routes(devices)
     index = lax.axis_index("dp")
     core = index % 2
     place = ring_place(index // 2, chips)
-    half = shard.shape[0] // 2
     if after is not None:
-        shard, after = tie(shard, after)
-    whole = blank((devices,) + shard.shape, shard.dtype)
+        packed, after = tie(packed, after)
+    half, model = packed.shape[1:]
+    whole = blank((devices, rows, model), packed.dtype)
+    own_low = core * (rows - half)
+    other_low = (1 - core) * (rows - half)
 
     def put(whole, piece, owner, offset):
-        return lax.dynamic_update_slice(whole, piece[None], (owner, offset, 0))
-
-    forward, behind = shard[:half], shard[half:]
+        return lax.dynamic_update_slice(whole, piece, (owner, offset, 0))
+
+    other = lax.ppermute(packed, "dp", pair)
+    mine = lax.dynamic_slice_in_dim(packed, core, 1, 0)
+    theirs = lax.dynamic_slice_in_dim(other, core, 1, 0)
+    piece = jnp.where(
+        core == 0,
+        jnp.concatenate([mine, theirs], axis=0),
+        jnp.concatenate([theirs, mine], axis=0),
+    )
     marks = []
-    other = None
     for step in range(1, chips):
-        forward = lax.ppermute(forward, "dp", right)
-        behind = lax.ppermute(behind, "dp", left)
-        if other is None:
-            other = lax.ppermute(shard, "dp", pair)
-            whole = put(whole, shard, index, 0)
-            whole = put(whole, other, index + 1 - 2 * core, 0)
-        marks.append((forward, behind))
-        forward_pair = lax.ppermute(forward, "dp", pair)
-        behind_pair = lax.ppermute(behind, "dp", pair)
-        owner = 2 * chip_at(place - step, chips)
-        whole = put(whole, forward, owner + core, 0)
-        whole = put(whole, forward_pair, owner + 1 - core, 0)
-        owner = 2 * chip_at(place + step, chips)
-        whole = put(whole, behind, owner + core, half)
-        whole = put(whole, behind_pair, owner + 1 - core, half)
+        start = piece
+        piece = lax.ppermute(piece, "dp", around)
+        if step == 1:
+            whole = put(whole, start, index - core, own_low)
+            start = lax.dynamic_slice_in_dim(other, 1 - core, 1, 0)
+            whole = put(whole, start, index + 1 - 2 * core, other_low)
+            start = lax.dynamic_slice_in_dim(packed, 1 - core, 1, 0)
+            whole = put(whole, start, index, other_low)
+        marks.append(piece)
+        swapped = lax.ppermute(piece, "dp", pair)
+        turn = (2 * core - 1) * step
+        whole = put(whole, piece, 2 * chip_at(place + turn, chips), own_low)
+        whole = put(whole, swapped, 2 * chip_at(place - turn, chips), other_low)
     return whole, marks
 
 
-def scatter_ring(forward_parts, behind_parts):
-    devices = lax.axis_size("dp")
-    chips = devices // 2
-    right, left, pair = ring_routes(devices)
-    sums = []
-    for mine, theirs in (forward_parts, behind_parts):
-        got = lax.ppermute(theirs, "dp", pair)
-        sums.append((mine, got))
-
-    def own(which, place):
-        mine, got = sums[which]
-        return mine[place].astype(jnp.float32) + got[place].astype(jnp.float32)
-
-    forward = own(0, chips - 1).astype(jnp.bfloat16)
-    behind = own(1, 1).astype(jnp.bfloat16)
-    marks = [(forward, behind)]
-    for step in range(1, chips):
-        forward = lax.ppermute(forward, "dp", right).astype(jnp.float32)
-        behind = lax.ppermute(behind, "dp", left).astype(jnp.float32)
-        forward = forward + own(0, chips - 1 - step)
-        behind = behind + own(1, (step + 1) % chips)
-        if step + 1 < chips:
-            forward = forward.astype(jnp.bfloat16)
-            behind = behind.astype(jnp.bfloat16)
-            marks.append((forward, behind))
-    return jnp.concatenate([forward, behind], axis=0), marks
-
-
-def packed(shard, width):
-    pieces = shard.shape[-1] // width
-    return [shard[:, width * i : width * (i + 1)] for i in range(pieces)]
+class ScatterRing:
+    def __init__(self, mine, theirs):
+        devices = lax.axis_size("dp")
+        self.chips = devices // 2
+        self.route, self.pair = ring_routes(devices)
+        self.mine, self.theirs, self.got = mine, theirs, None
+        early = lax.ppermute(theirs[1:2], "dp", self.pair)[0]
+        value = mine[1].astype(jnp.float32) + early.astype(jnp.float32)
+        self.value = value.astype(jnp.bfloat16)
+        self.start = self.value
+        self.step = 1
+
+    def exchange(self):
+        self.got = lax.ppermute(self.theirs, "dp", self.pair)
+
+    def advance(self, before):
+        if before is not None:
+            self.value, _ = tie(self.value, before)
+        self.step += 1
+        place = self.step % self.chips
+        value = lax.ppermute(self.value, "dp", self.route).astype(jnp.float32)
+        value = value + self.mine[place].astype(jnp.float32)
+        value = value + self.got[place].astype(jnp.float32)
+        self.value = value.astype(jnp.bfloat16) if self.step < self.chips else value
+        return self.value
+
+    def halves(self):
+        core = lax.axis_index("dp") % 2
+        own = lax.dynamic_index_in_dim(self.value, core, 0, keepdims=False)
+        other = lax.dynamic_index_in_dim(self.value, 1 - core, 0, keepdims=False)
+        other = lax.ppermute(other, "dp", self.pair)
+        return jnp.where(core == 0, own, other), jnp.where(core == 0, other, own)
+
+
+def run_slots(slots, history, depth):
+    for ring in slots:
+        if ring.step < ring.chips:
+            before = history[-depth] if len(history) >= depth else None
+            history.append(ring.advance(before))
 
 
 def beside(grad, low, pieces, rows):
@@ -180,10 +195,8 @@
 SCALARS = pl.BlockSpec(memory_space=pltpu.SMEM)
 
 
-def flat_call(body, arguments, out_shape, scratch=(), flops=0, moved=0, vmem=24, scalars=False):
-    specs = [LOCAL] * len(arguments)
-    if scalars:
-        specs[0] = SCALARS
+def flat_call(body, arguments, out_shape, scratch=(), flops=0, moved=0, vmem=VMEM_GRANT):
+    specs = [SCALARS] + [LOCAL] * (len(arguments) - 1)
     return pl.pallas_call(
         body,
         in_specs=specs,
@@ -242,16 +255,20 @@
 
 
 def attention_kernel(
-    keep, h_ref, gain_ref, gain_q_ref, gain_k_ref, gain_ffn_ref, cos_ref, sin_ref, row_ref,
-    column_ref, w_ref, hm_ref, xf_ref, *rest,
+    keep, section_ref, h_ref, came_ref, gain_ref, gain_q_ref, gain_k_ref, gain_ffn_ref, cos_ref,
+    sin_ref, row_ref, column_ref, w_ref, hm_ref, xf_ref, *rest,
 ):
     if keep:
-        xf_t_ref, xa_t_ref, o_t_ref, qkv_ref, pre_ref, o_ref = rest
+        xf_t_ref, xa_t_ref, o_t_ref, qkv_ref, pre_ref, hidden_ref, o_ref = rest
     else:
         qkv_ref, o_ref = rest
     tokens, model = h_ref.shape
     rows = w_ref.shape[1] // 6
-    hidden = h_ref[...].astype(jnp.float32)
+    hidden = h_ref[...]
+    if keep:
+        hidden = jnp.where(section_ref[0] == 0, hidden, came_ref[...])
+        hidden_ref[...] = hidden
+    hidden = hidden.astype(jnp.float32)
     scaled, _ = unit_rows(hidden)
     xa = (scaled * gain_ref[...]).astype(jnp.bfloat16)
     cosine, sine = cos_ref[...], sin_ref[...]
@@ -294,7 +311,7 @@
         o_t_ref[...] = jnp.transpose(o_ref[...])
 
 
-def attention(hidden, gains, tables, whole, keep):
+def attention(section, hidden, came, gains, tables, whole, keep):
     tokens, model = hidden.shape
     wide = QUERY_HEADS * HEAD_SIZE
     shapes = [full_shape(tokens, model), low_shape(tokens, model)]
@@ -306,12 +323,13 @@
             low_shape(wide, tokens),
             low_shape(tokens, 4 * model),
             low_shape(tokens, 3 * model),
+            low_shape(tokens, model),
         ]
     else:
         scratch = [pltpu.VMEM((tokens, 4 * model), jnp.bfloat16)] + scratch
     return flat_call(
         functools.partial(attention_kernel, keep),
-        (hidden, *gains, *tables, whole),
+        (section, hidden, came, *gains, *tables, whole),
         shapes,
         scratch=scratch,
         flops=2 * tokens * model * 6 * model + 8 * tokens * tokens * wide,
@@ -319,11 +337,11 @@
     )
 
 
-def ffn_kernel(keep, xf_ref, hm_ref, w_ref, y_ref, *rest):
+def ffn_kernel(keep, _, xf_ref, hm_ref, w_ref, *rest):
     if keep:
-        g_ref, u_ref, z_t_ref, inner = rest
+        teacher_ref, keep_ref, y_ref, g_ref, u_ref, z_t_ref, pull_ref, square_ref, inner = rest
     else:
-        (inner,) = rest
+        y_ref, inner = rest
     tokens, model = xf_ref.shape
     rows = w_ref.shape[1] // 9
     xf = xf_ref[...]
@@ -337,18 +355,25 @@
             u_ref[:, part_of(block, model)] = up.astype(jnp.bfloat16)
             z_t_ref[part_of(block, model), :] = jnp.transpose(mixed)
     total = hm_ref[...] + dot_plain(inner[...], slab(w_ref, 3 * rows, 3 * rows))
-    y_ref[...] = total.astype(jnp.bfloat16)
-
-
-def feed_forward(normed, middle, whole, keep):
+    low = total.astype(jnp.bfloat16)
+    y_ref[...] = low
+    if keep:
+        error = low.astype(jnp.float32) - teacher_ref[...]
+        pull = keep_ref[...] * error
+        pull_ref[...] = pull
+        square_ref[...] = jnp.sum(jnp.sum(pull * error, axis=0, keepdims=True), axis=1, keepdims=True)
+
+
+def feed_forward(section, normed, middle, whole, target=()):
     tokens, model = normed.shape
     width = 3 * model
     shapes = [low_shape(tokens, model)]
-    if keep:
+    if target:
         shapes += [low_shape(tokens, width), low_shape(tokens, width), low_shape(width, tokens)]
+        shapes += [full_shape(tokens, model), full_shape(1, 1)]
     return flat_call(
-        functools.partial(ffn_kernel, keep),
-        (normed, middle, whole),
+        functools.partial(ffn_kernel, bool(target)),
+        (section, normed, middle, whole, *target),
         shapes,
         scratch=[pltpu.VMEM((tokens, width), jnp.bfloat16)],
         flops=6 * tokens * width * model,
@@ -357,11 +382,14 @@
 
 
 def ffn_back_kernel(
-    dy_ref, hm_ref, gain_ref, g_ref, u_ref, w_ref, dh_ref, low_ref, dg_ref, du_ref, dgain_ref
+    section_ref, dy_ref, came_ref, hm_ref, gain_ref, g_ref, u_ref, w_ref, dh_ref, low_ref, dg_ref,
+    du_ref, dgain_ref, low_dy_ref,
 ):
     devices, rows, model = w_ref.shape
     rows = rows // 9
-    low_dy = dy_ref[...].astype(jnp.bfloat16)
+    d_result = jnp.where(section_ref[0] == 1, dy_ref[...], came_ref[...].astype(jnp.float32))
+    low_dy = d_result.astype(jnp.bfloat16)
+    low_dy_ref[...] = low_dy
     chunks = 4
     owners = devices // chunks
     chunk = 3 * model // chunks
@@ -383,23 +411,25 @@
         grad = term if grad is None else grad + term
     scaled, factor = unit_rows(hm_ref[...])
     dgain_ref[...] = jnp.sum(grad * scaled, axis=0, keepdims=True)
-    d_hidden = dy_ref[...] + norm_pull(grad, scaled, factor, gain_ref[...])
+    d_result = jnp.where(section_ref[0] == 1, dy_ref[...], came_ref[...].astype(jnp.float32))
+    d_hidden = d_result + norm_pull(grad, scaled, factor, gain_ref[...])
     dh_ref[...] = d_hidden
     low_ref[...] = d_hidden.astype(jnp.bfloat16)
 
 
-def feed_forward_back(d_result, middle, gains, gate, up, whole):
+def feed_forward_back(section, pull, came, middle, gains, gate, up, whole):
     tokens, model = middle.shape
     width = 3 * model
     return flat_call(
         ffn_back_kernel,
-        (d_result, middle, gains[3], gate, up, whole),
+        (section, pull, came, middle, gains[3], gate, up, whole),
         [
             full_shape(tokens, model),
             low_shape(tokens, model),
             low_shape(tokens, width),
             low_shape(tokens, width),
             full_shape(1, model),
+            low_shape(tokens, model),
         ],
         flops=6 * tokens * width * model,
         moved=6 * width * model + 14 * tokens * model + 8 * tokens * width,
@@ -407,8 +437,8 @@
 
 
 def attention_back_kernel(
-    low_ref, dh_ref, h_ref, qkv_ref, pre_ref, gain_ref, gain_q_ref, gain_k_ref, cos_ref, sin_ref,
-    row_ref, column_ref, w_ref, dq_ref, dk_ref, dv_ref, dx_ref, dgain_ref, dgain_q_ref,
+    _, low_ref, dh_ref, h_ref, qkv_ref, pre_ref, gain_ref, gain_q_ref, gain_k_ref, cos_ref, sin_ref,
+    row_ref, column_ref, w_ref, dq_ref, dkv_ref, dx_ref, dgain_ref, dgain_q_ref,
     dgain_k_ref, do_ref,
 ):
     tokens, model = h_ref.shape
@@ -452,31 +482,30 @@
             d_key = key_term if d_key is None else d_key + key_term
             d_value = value_term if d_value is None else d_value + value_term
             dq_ref[:, part] = through_norm(d_query, pre_ref[:, part], gain_q_ref, 0)
-        dk_ref[:, lone] = through_norm(
+        dkv_ref[:, lone] = through_norm(
             d_key * scale, pre_ref[:, part_of(QUERY_HEADS + shared)], gain_k_ref, 1
         )
-        dv_ref[:, lone] = d_value.astype(jnp.bfloat16)
+        dkv_ref[:, part_of(KEY_VALUE_HEADS + shared)] = d_value.astype(jnp.bfloat16)
     dgain_q_ref[...], dgain_k_ref[...] = gain_grads
     grad = dot_columns(dq_ref[:, part_of(0, model)], slab(w_ref, 0, rows))
     grad = grad + dot_columns(dq_ref[:, part_of(1, model)], slab(w_ref, rows, rows))
-    grad = grad + dot_columns(dk_ref[...], slab(w_ref, 4 * rows, rows))
-    grad = grad + dot_columns(dv_ref[...], slab(w_ref, 5 * rows, rows))
+    grad = grad + dot_columns(dkv_ref[:, part_of(0, model)], slab(w_ref, 4 * rows, rows))
+    grad = grad + dot_columns(dkv_ref[:, part_of(1, model)], slab(w_ref, 5 * rows, rows))
     scaled, factor = unit_rows(h_ref[...].astype(jnp.float32))
     dgain_ref[...] = jnp.sum(grad * scaled, axis=0, keepdims=True)
     d_hidden = dh_ref[...] + norm_pull(grad, scaled, factor, gain_ref[...])
     dx_ref[...] = d_hidden.astype(jnp.bfloat16)
 
 
-def attention_back(low, d_middle, hidden, qkv, pre, gains, tables, whole):
+def attention_back(section, low, d_middle, hidden, qkv, pre, gains, tables, whole):
     tokens, model = hidden.shape
     wide = QUERY_HEADS * HEAD_SIZE
     return flat_call(
         attention_back_kernel,
-        (low, d_middle, hidden, qkv, pre, *gains[:3], *tables, whole),
+        (section, low, d_middle, hidden, qkv, pre, *gains[:3], *tables, whole),
         [
             low_shape(tokens, wide),
-            low_shape(tokens, model),
-            low_shape(tokens, model),
+            low_shape(tokens, 2 * model),
             low_shape(tokens, model),
             full_shape(1, model),
             full_shape(1, HEAD_SIZE),
@@ -489,55 +518,101 @@
 
 
 def grad_kernel(plan, chips, batches, order_ref, *refs):
-    count = len(plan) * batches
-    lefts, rights = refs[:count], refs[count : 2 * count]
-    mine_ref, theirs_ref = refs[2 * count : 2 * count + 2]
-    stores = refs[2 * count + 2 :]
-    core = order_ref[chips]
-    model = mine_ref.shape[2]
-    for index, (rows, low, size, blocks, start) in enumerate(plan):
-        left, right = lefts[index * batches :][:batches], rights[index * batches :][:batches]
-        for target, side, store in (
-            (theirs_ref, 1 - core, stores[2 * index]),
-            (mine_ref, core, stores[2 * index + 1]),
-        ):
-            for t in range(chips):
-                place = pl.multiple_of((2 * order_ref[t] + side) * rows + low, 16)
+    side = order_ref[chips]
+    count = sum(1 + len(entry[4]) for entry in plan) * batches
+    target, stores = refs[count], refs[count + 1 :]
+    model = target.shape[3]
+    taken, start = 0, 0
+
+    def take():
+        nonlocal taken
+        taken += batches
+        return refs[taken - batches : taken]
+
+    for (rows, size, low, blocks, choices), store in zip(plan, stores):
+        left, rights = take(), [take() for _ in choices]
+        first = side * low
+        for t in range(chips):
+            owner = 2 * order_ref[t]
+            for core in range(2):
+                place = pl.multiple_of((owner + core) * rows + first, 16)
+                to = slice((2 * t + core) * size, (2 * t + core + 1) * size)
                 for batch in range(batches):
-                    store[batch, t * size : (t + 1) * size, :] = left[batch][pl.ds(place, size), :]
-            for block in range(blocks):
+                    store[batch, to, :] = left[batch][pl.ds(place, size), :]
+        for block in range(blocks):
+            part = part_of(block, model)
+            right = []
+            for batch in range(batches):
+                value = rights[0][batch][:, part]
+                if len(rights) > 1:
+                    value = jnp.where(side == 0, value, rights[1][batch][:, part])
+                right.append(value)
+            for half in range(2):
                 value = None
+                span = slice(half * chips * size, (half + 1) * chips * size)
                 for batch in range(batches):
-                    term = dot_plain(store[batch], right[batch][:, part_of(block, model)])
+                    term = dot_plain(store[batch, span, :], right[batch])
                     value = term if value is None else value + term
-                value = value.astype(jnp.bfloat16).reshape(chips, size, model)
-                target[:, start + block * size : start + (block + 1) * size, :] = value
+                value = value.astype(jnp.bfloat16).reshape(chips // 2, 2, size, model)
+                into = slice(start + block * size, start + (block + 1) * size)
+                target[half * chips // 2 : (half + 1) * chips // 2, :, into, :] = value
+        start += blocks * size
 
 
 def weight_grads(order, parts, model):
     batches = len(parts[0][0])
     tokens = parts[0][0][0].shape[1]
     chips = order.shape[0] - 1
-    plan, scratch, start = [], [], 0
-    for left, right, low, size in parts:
+    plan, scratch, operands, total = [], [], [], 0
+    for left, rights, size, low in parts:
         rows = left[0].shape[0] // (2 * chips)
-        blocks = right[0].shape[1] // model
-        plan.append((rows, low, size, blocks, start))
-        scratch += [pltpu.VMEM((batches, chips * size, tokens), jnp.bfloat16)] * 2
-        start += size * blocks
-    shape = low_shape(chips, start, model)
-    lefts = [array for part in parts for array in part[0]]
-    rights = [array for part in parts for array in part[1]]
-    flops = 4 * chips * start * model * tokens * batches
+        blocks = rights[0][0].shape[1] // model
+        plan.append((rows, size, low, blocks, tuple(range(len(rights)))))
+        scratch.append(pltpu.VMEM((batches, 2 * chips * size, tokens), jnp.bfloat16))
+        operands += list(left) + [array for right in rights for array in right]
+        total += size * blocks
     return flat_call(
         functools.partial(grad_kernel, tuple(plan), chips, batches),
-        (order, *lefts, *rights),
-        [shape, shape],
+        (order, *operands),
+        [low_shape(chips, 2, total, model)],
         scratch=scratch,
-        flops=flops,
-        moved=4 * chips * start * model + 8 * tokens * batches * model,
-        scalars=True,
-    )
+        flops=4 * chips * total * model * tokens * batches,
+        moved=4 * chips * total * model + 8 * tokens * batches * model,
+        vmem=14,
+    )[0]
+
+
+def pack_kernel(plan, count, *refs):
+    target, sem = refs[count], refs[count + 1]
+    model = target.shape[2]
+    copies = []
+    for half, entries in enumerate(plan):
+        low = 0
+        for source, start, rows, block in entries:
+            copies.append(
+                pltpu.make_async_copy(
+                    refs[source].at[start : start + rows, part_of(block, model)],
+                    target.at[half, low : low + rows, :],
+                    sem.at[len(copies)],
+                )
+            )
+            low += rows
+    for copy in copies:
+        copy.start()
+    for copy in copies:
+        copy.wait()
+
+
+def pack(shards, plan, model):
+    rows = sum(entry[2] for entry in plan[0])
+    return pl.pallas_call(
+        functools.partial(pack_kernel, plan, len(shards)),
+        in_specs=[pl.BlockSpec(memory_space=pl.ANY)] * len(shards),
+        out_specs=LOCAL,
+        out_shape=low_shape(2, rows, model),
+        scratch_shapes=[pltpu.SemaphoreType.DMA((len(plan[0]) + len(plan[1]),))],
+        compiler_params=pltpu.CompilerParams(vmem_limit_bytes=VMEM_GRANT << 20),
+    )(*shards)
 
 
 def local(
@@ -565,18 +640,30 @@
     rows = attn_query.shape[1]
     forward_rows = ffn_down.shape[1]
 
-    attn_shard = jnp.concatenate(
-        packed(attn_query[0], model)
-        + [attn_out[0]]
-        + packed(attn_key[0], model)
-        + packed(attn_value[0], model),
-        axis=0,
-    )
-    ffn_shard = jnp.concatenate(
-        packed(ffn_gate[0], model) + [ffn_down[0]] + packed(ffn_up[0], model), axis=0
-    )
-    attn_whole, attn_marks = gather_ring(attn_shard)
-    ffn_whole, ffn_marks = gather_ring(ffn_shard, attn_marks[min(RING_LEAD, chips - 2)])
+    cut = forward_rows // 2 if forward_rows % 32 == 0 else 2 * rows
+    attn_packed = pack(
+        (attn_query[0], attn_out[0], attn_key[0], attn_value[0]),
+        (
+            ((0, 0, rows, 0), (0, 0, rows, 1), (1, 0, rows, 0)),
+            ((1, rows, rows, 0), (2, 0, rows, 0), (3, 0, rows, 0)),
+        ),
+        model,
+    )
+    attn_whole, attn_marks = gather_ring(attn_packed, 6 * rows)
+    (ffn_gate, ffn_up, ffn_down, lengths), _ = tie(
+        (ffn_gate, ffn_up, ffn_down, lengths), attn_marks[0]
+    )
+    ffn_packed = pack(
+        (ffn_gate[0], ffn_down[0], ffn_up[0]),
+        (
+            ((0, 0, rows, 0), (0, 0, rows, 1), (0, 0, rows, 2), (1, 0, cut, 0)),
+            ((1, forward_rows - cut, cut, 0), (2, 0, rows, 0), (2, 0, rows, 1), (2, 0, rows, 2)),
+        ),
+        model,
+    )
+    ffn_whole, ffn_marks = gather_ring(
+        ffn_packed, 9 * rows, attn_marks[min(RING_LEAD, chips - 2)]
+    )
 
     gain_sizes = (norm_attn.shape[1], norm_query.shape[1], norm_key.shape[1], norm_ffn.shape[1])
     gain_shard = jnp.concatenate([norm_attn, norm_query, norm_key, norm_ffn], axis=1)
@@ -606,118 +693,117 @@
         return tie(value, marks[min(step, chips - 2)])[0]
 
     first = [inputs[batch] for batch in both]
+    where = section[None].astype(jnp.int32)
+    last = jnp.ones((1,), jnp.int32)
     carried, seen = [], []
     for batch in both:
         start = waiting(first[batch], ffn_marks, FIRST_WAIT + batch)
-        seen.append(attention(start, gains, tables[batch], attn_whole, False))
+        seen.append(attention(where, start, start, gains, tables[batch], attn_whole, False))
     for batch in both:
-        (result,) = feed_forward(seen[batch][1], seen[batch][0], ffn_whole, False)
+        (result,) = feed_forward(where, seen[batch][1], seen[batch][0], ffn_whole)
         carried.append(one_way(result, 0))
 
     kept = []
     for batch in both:
-        hidden = jnp.where(section == 0, first[batch], carried[batch])
-        mid, norm, norm_t, normalized_t, mix_t, qkv, pre = attention(
-            hidden, gains, tables[batch], attn_whole, True
+        mid, norm, norm_t, normalized_t, mix_t, qkv, pre, hidden = attention(
+            where, first[batch], carried[batch], gains, tables[batch], attn_whole, True
         )
-        result, gate, up, inner_t = feed_forward(norm, mid, ffn_whole, True)
-        kept.append((hidden, normalized_t, qkv, pre, mix_t, mid, norm_t, result, gate, up, inner_t))
-    hidden, normalized_t, qkv, pre, mixed_t, middle, normed_t, result, gate, up, inner_t = (
-        list(column) for column in zip(*kept)
-    )
-
-    cotangent, squares = [], 0.0
-    for batch in both:
-        diff = result[batch].astype(jnp.float32) - teacher[batch]
-        cotangent.append(keep[batch][:, None] * diff)
-        squares = squares + jnp.sum(cotangent[batch] * diff)
+        result, gate, up, inner_t, pull, square = feed_forward(
+            where, norm, mid, ffn_whole, (teacher[batch], keep[batch][:, None])
+        )
+        kept.append(
+            (hidden, normalized_t, qkv, pre, mix_t, mid, norm_t, result, gate, up, inner_t, pull, square)
+        )
+    (
+        hidden, normalized_t, qkv, pre, mixed_t, middle, normed_t, result, gate, up, inner_t, pull,
+        squares,
+    ) = (list(column) for column in zip(*kept))
 
     core = index % 2
     place = ring_place(index // 2, chips)
-    order = jnp.concatenate(
-        [chip_at(place + jnp.arange(chips, dtype=jnp.int32), chips), core[None]]
-    ).astype(jnp.int32)
-    cut = forward_rows // 2 if forward_rows % 32 == 0 else 2 * rows
+    away = jnp.arange(chips, dtype=jnp.int32) * (2 * core - 1)
+    order = jnp.concatenate([chip_at(place + away, chips), core[None]]).astype(jnp.int32)
+    other_order = jnp.concatenate([chip_at(place - away, chips), 1 - core[None]]).astype(jnp.int32)
 
     incoming = []
     for batch in both:
-        d_middle, d_attn, _, _, _ = feed_forward_back(
-            cotangent[batch], middle[batch], gains, gate[batch], up[batch], ffn_whole
-        )
+        d_middle, d_attn = feed_forward_back(
+            last, pull[batch], result[batch], middle[batch], gains, gate[batch], up[batch], ffn_whole
+        )[:2]
         d_hidden = attention_back(
-            d_attn, d_middle, hidden[batch], qkv[batch], pre[batch], gains, tables[batch], attn_whole
-        )[3]
+            where, d_attn, d_middle, hidden[batch], qkv[batch], pre[batch], gains, tables[batch],
+            attn_whole,
+        )[2]
         incoming.append(one_way(d_hidden, 1))
 
     d_middle, d_attn, d_gate, d_up, d_branch, gain_ffn = [], [], [], [], [], 0.0
     for batch in both:
-        d_result = jnp.where(
-            section == 1, cotangent[batch], incoming[batch].astype(jnp.float32)
+        m, a, g, u, gain, low = feed_forward_back(
+            where, pull[batch], incoming[batch], middle[batch], gains, gate[batch], up[batch],
+            ffn_whole,
         )
-        d_branch.append(d_result.astype(jnp.bfloat16))
-        m, a, g, u, gain = feed_forward_back(
-            d_result, middle[batch], gains, gate[batch], up[batch], ffn_whole
-        )
+        d_branch.append(low)
         d_middle.append(m)
         d_attn.append(a)
         d_gate.append(g)
         d_up.append(u)
         gain_ffn = gain_ffn + gain
-    forward_parts = weight_grads(
-        order, [(normed_t, d_gate, 0, rows), (inner_t, d_branch, 0, cut)], model
-    )
-    behind_parts = weight_grads(
-        order, [(inner_t, d_branch, cut, forward_rows - cut), (normed_t, d_up, 0, rows)], model
-    )
-    ffn_grad, marks = scatter_ring(forward_parts, behind_parts)
-    d_query, d_key, d_value, d_hidden = [], [], [], []
+    ffn_parts = [
+        (normed_t, (d_gate, d_up), rows, 0),
+        (inner_t, (d_branch,), cut, forward_rows - cut),
+    ]
+    theirs = weight_grads(other_order, ffn_parts, model)
+    mine = weight_grads(tie(order, theirs)[0], ffn_parts, model)
+    ffn_ring = ScatterRing(mine, theirs)
+    ffn_ring.exchange()
+    history = []
+    run_slots([ffn_ring], history, SLOT_DEPTH)
+    d_query, d_pair, d_hidden = [], [], []
     gain_attn, gain_query, gain_key = 0.0, 0.0, 0.0
     for batch in both:
-        if batch == 0:
-            value, _ = tie(d_attn[batch], (forward_parts, behind_parts))
-        else:
-            value = waiting(d_attn[batch], marks, batch - 1)
-        q, k, v, x, gain_a, gain_q, gain_k = attention_back(
-            value, d_middle[batch], hidden[batch], qkv[batch], pre[batch], gains, tables[batch],
-            attn_whole,
+        value, _ = tie(d_attn[batch], (ffn_ring.start, history[0])[batch])
+        q, kv, x, gain_a, gain_q, gain_k = attention_back(
+            where, value, d_middle[batch], hidden[batch], qkv[batch], pre[batch], gains,
+            tables[batch], attn_whole,
         )
         d_query.append(q)
-        d_key.append(k)
-        d_value.append(v)
+        d_pair.append(kv)
         d_hidden.append(x)
         gain_attn = gain_attn + gain_a
         gain_query = gain_query + gain_q
         gain_key = gain_key + gain_k
     gain_grads = (gain_attn, gain_query, gain_key, gain_ffn)
-    attn_grad, attn_marks = scatter_ring(
-        weight_grads(
-            waiting(order, marks, 1),
-            [(normalized_t, d_query, 0, rows), (mixed_t, d_attn, 0, rows)],
-            model,
-        ),
-        weight_grads(
-            waiting(order, marks, 2),
-            [
-                (mixed_t, d_attn, rows, rows),
-                (normalized_t, d_key, 0, rows),
-                (normalized_t, d_value, 0, rows),
-            ],
-            model,
-        ),
-    )
-
-    grad_gate = beside(ffn_grad, 0, 3, rows)
-    grad_down = ffn_grad[3 * rows : 3 * rows + forward_rows]
-    grad_up = beside(ffn_grad, 3 * rows + forward_rows, 3, rows)
-    grad_query = beside(attn_grad, 0, 2, rows)
-    grad_out = attn_grad[2 * rows : 4 * rows]
-    grad_key = attn_grad[4 * rows : 5 * rows]
-    grad_value = attn_grad[5 * rows :]
+    run_slots([ffn_ring], history, SLOT_DEPTH)
+    attn_parts = [
+        (normalized_t, (d_query, d_pair), rows, 0),
+        (mixed_t, (d_attn,), rows, rows),
+    ]
+    theirs = weight_grads(tie(other_order, history[1])[0], attn_parts, model)
+    mine = weight_grads(tie(order, theirs)[0], attn_parts, model)
+    run_slots([ffn_ring], history, SLOT_DEPTH)
+    attn_ring = ScatterRing(mine, theirs)
+    attn_ring.exchange()
+    tail_mark = history[-1]
+    while ffn_ring.step < chips or attn_ring.step < chips:
+        run_slots([attn_ring, ffn_ring], history, SLOT_DEPTH)
+        if attn_ring.step == 3:
+            tail_mark = history[-1]
+
+    first_half, second_half = ffn_ring.halves()
+    grad_gate = beside(first_half, 0, 3, rows)
+    grad_up = beside(second_half, 0, 3, rows)
+    grad_down = jnp.concatenate(
+        [first_half[3 * rows :], second_half[3 * rows + 2 * cut - forward_rows :]], axis=0
+    )
+    first_half, second_half = attn_ring.halves()
+    grad_query = beside(first_half, 0, 2, rows)
+    grad_key, grad_value = second_half[:rows], second_half[rows : 2 * rows]
+    grad_out = jnp.concatenate([first_half[2 * rows :], second_half[2 * rows :]], axis=0)
 
     small = jnp.concatenate(
-        [*gain_grads, jnp.stack([squares, jnp.sum(keep)])[None]], axis=1
-    )
-    small_sum = summed(waiting(small, attn_marks, 2))
+        [*gain_grads, sum(squares), jnp.sum(keep).reshape(1, 1)], axis=1
+    )
+    small_sum = summed(tie(small, tail_mark)[0])
     totals = small_sum[:, -2:]
     totals = jnp.where(section == 1, totals, one_way(totals, 1))[0]
     loss = totals[0] / (totals[1] * model)

time: 659 us -> 585 us (0.89)
  local copies, waits for them, and re-layouts: 162 us -> 94.4 us
  starting transfers between devices: 90.5 us -> 67.7 us
  waiting for transfers between devices: 202 us -> 219 us
  Pallas kernels: 143 us -> 150 us
    unnamed x222 -> x218, local copies, waits for them, and re-layouts: 89.9 us -> 30.8 us
    ppermute x90 -> x50, starting transfers between devices: 67.8 us -> 48.9 us  [the longest x14 28.3 us: gather_ring(): piece = lax.ppermute(piece, 'dp', around)]
    ppermute x90 -> x50, waiting for transfers between devices: 168 us -> 182 us  [the longest x14 93.8 us: advance(): value = lax.ppermute(self.value, 'dp', self.route).astype(jnp.float32)]
    dynamic_update_slice x60 -> x32, local copies, waits for them, and re-layouts: 64.2 us -> 55 us  [put(): return lax.dynamic_update_slice(whole, piece, (owner, offset, 0))]
    ppermute x7, waiting for transfers between devices: 15.7 us -> 8.67 us  [one_way(): return lax.ppermute(value, 'section', [(source, 1 - source)])]
    ppermute x4, waiting for transfers between devices: 6.69 us -> 13.5 us  [summed(): lax.ppermute(value, 'dp', [(low, low ^ step) for low in range(devices)])]
    convert_element_type x30 -> x14, other arithmetic: 27.3 us -> 22 us  [the longest x12 21.3 us: advance(): self.value = value.astype(jnp.bfloat16) if self.step < self.chips else value]
  transfers between devices with their start and end apart: 105 -> 65, of which waited for: 41 -> 28; matrix products, arithmetic and copies ran while one was open for 18% -> 16% of each run, Pallas kernels for 13% -> 22%
where the time goes in v4:
time: 585 us; the launch traced here: 578 us
  waiting for transfers between devices  219 us (37%)
  Pallas kernels  150 us (26%)
  local copies, waits for them, and re-layouts  94.4 us (16%)
  starting transfers between devices  67.7 us (12%)
  other arithmetic  41.1 us (7%)
  between operations  6.7 us (1%)
    pallas_call x20, Pallas kernels, flat_call(): pl.pallas_call(body, in_specs=specs, out_specs=[LOCAL] * len(out_shape),...  149 us
    ppermute x14, waiting for transfers between devices, advance(): value = lax.ppermute(self.value, 'dp', self.route).astype(jnp.float32)  93.8 us
    ppermute x14, waiting for transfers between devices, gather_ring(): piece = lax.ppermute(piece, 'dp', around)  83.9 us
    dynamic_update_slice x32, local copies, waits for them, and re-layouts, put(): return lax.dynamic_update_slice(whole, piece, (owner, offset, 0))  55 us
    unnamed x218, local copies, waits for them, and re-layouts  30.8 us
    ppermute x14, starting transfers between devices, gather_ring(): piece = lax.ppermute(piece, 'dp', around)  28.3 us
    convert_element_type x12, other arithmetic, advance(): self.value = value.astype(jnp.bfloat16) if self.step < self.chips else value  21.3 us
    ppermute x14, starting transfers between devices, advance(): value = lax.ppermute(self.value, 'dp', self.route).astype(jnp.float32)  17 us
  transfers between devices with their start and end apart: 65, of which 28 were waited for; matrix products, arithmetic and copies ran while one was open for 16% of the time, Pallas kernels for 22%

profile of v4, /device:TPU:0, one launch (start us, length us, event | category | flops | bytes accessed | tf_op | source)
XLA Modules:
  0.0 578.5 jit_solution(4636338227210779797)
XLA Ops:
  11.7 9.9 %collective-permute-done.1 = bf16[2,192,1024]{2,1,0:T(8,128)(2,1)S(1)} collective-permute-done((bf16[2,192,1024]{2,1,0:T(8,128)(2,1)S(1)}, bf16[2,192,1024]{2,1,0:T(8,128)(2,1)S(1)}, u32[]{:S(2)}, u32[]{:S(2)}) %collective-permute-start.1) | collective-permute-done | bytes 786464 | tf_op jit(solution)/shard_map/ppermute | solution.py:116
  24.4 9.3 %collective-permute-done.2 = bf16[2,192,1024]{2,1,0:T(8,128)(2,1)} collective-permute-done((bf16[2,192,1024]{2,1,0:T(8,128)(2,1)S(1)}, bf16[2,192,1024]{2,1,0:T(8,128)(2,1)}, u32[]{:S(2)}, u32[]{:S(2)}) %collective-permute-start.2) | collective-permute-done | bytes 786464 | tf_op jit(solution)/shard_map/ppermute | solution.py:116
  40.0 14.2 %collective-permute-done.4 = bf16[2,288,1024]{2,1,0:T(8,128)(2,1)} collective-permute-done((bf16[2,288,1024]{2,1,0:T(8,128)(2,1)S(1)}, bf16[2,288,1024]{2,1,0:T(8,128)(2,1)}, u32[]{:S(2)}, u32[]{:S(2)}) %collective-permute-start.4) | collective-permute-done | bytes 1179680 | tf_op jit(solution)/shard_map/ppermute | solution.py:116
  59.8 11.0 %collective-permute-done.5 = bf16[2,288,1024]{2,1,0:T(8,128)(2,1)} collective-permute-done((bf16[2,288,1024]{2,1,0:T(8,128)(2,1)}, bf16[2,288,1024]{2,1,0:T(8,128)(2,1)}, u32[]{:S(2)}, u32[]{:S(2)}) %collective-permute-start.5) | collective-permute-done | bytes 1179680 | tf_op jit(solution)/shard_map/ppermute | solution.py:116
  78.0 9.3 %collective-permute-done.6 = bf16[2,288,1024]{2,1,0:T(8,128)(2,1)} collective-permute-done((bf16[2,288,1024]{2,1,0:T(8,128)(2,1)}, bf16[2,288,1024]{2,1,0:T(8,128)(2,1)}, u32[]{:S(2)}, u32[]{:S(2)}) %collective-permute-start.6) | collective-permute-done | bytes 1179680 | tf_op jit(solution)/shard_map/ppermute | solution.py:116
  89.4 6.3 %collective-permute-done.8 = bf16[2,192,1024]{2,1,0:T(8,128)(2,1)} collective-permute-done((bf16[2,192,1024]{2,1,0:T(8,128)(2,1)}, bf16[2,192,1024]{2,1,0:T(8,128)(2,1)}, u32[]{:S(2)}, u32[]{:S(2)}) %collective-permute-start.8) | collective-permute-done | bytes 786464 | tf_op jit(solution)/shard_map/ppermute | solution.py:116
  104.6 12.2 %collective-permute-done.16 = bf16[2,192,1024]{2,1,0:T(8,128)(2,1)} collective-permute-done((bf16[2,192,1024]{2,1,0:T(8,128)(2,1)}, bf16[2,192,1024]{2,1,0:T(8,128)(2,1)}, u32[]{:S(2)}, u32[]{:S(2)}) %collective-permute-start.16) | collective-permute-done | bytes 786464 | tf_op jit(solution)/shard_map/ppermute | solution.py:116
  131.3 10.1 %collective-permute-done.11 = f32[4,144]{1,0:T(4,128)S(1)} collective-permute-done((f32[4,144]{1,0:T(4,128)S(1)}, f32[4,144]{1,0:T(4,128)S(1)}, u32[]{:S(2)}, u32[]{:S(2)}) %collective-permute-start.11) | collective-permute-done | bytes 2336 | tf_op jit(solution)/shard_map/ppermute | solution.py:60
  152.7 6.2 %collective-permute-done.20 = bf16[2,192,1024]{2,1,0:T(8,128)(2,1)} collective-permute-done((bf16[2,192,1024]{2,1,0:T(8,128)(2,1)}, bf16[2,192,1024]{2,1,0:T(8,128)(2,1)}, u32[]{:S(2)}, u32[]{:S(2)}) %collective-permute-start.20) | collective-permute-done | bytes 786464 | tf_op jit(solution)/shard_map/ppermute | solution.py:116
  220.0 6.4 %copy-done = bf16[16,576,1024]{2,1,0:T(8,128)(2,1)S(1)} copy-done((bf16[16,576,1024]{2,1,0:T(8,128)(2,1)S(1)}, bf16[16,576,1024]{2,1,0:T(8,128)(2,1)}, u32[]{:S(2)}) %copy-start) | copy-done | bytes 18874392
  235.6 5.9 %shard_map.253 = (f32[256,1024]{1,0:T(8,128)S(1)}, bf16[256,1024]{1,0:T(8,128)(2,1)S(1)}) custom-call(s32[1]{0:T(128)} %bitcast.section_ref._, bf16[256,1024]{1,0:T(8,128)(2,1)S(1)} %get-tuple-element.107.h_ref.came_ref, bf16[256,1024]{1,0:T(8,128)(2,1)S(1)} %get-tuple-element.107.h_ref.came_ref, f32[1,1024]{1,0:T(1,128)S(1)} %reshape.187.gain_ref, ...), custom_call_target="tpu_custom_call" | custom-call | flops 4294967296 | bytes 17825792 | tf_op jit(solution)/shard_map/pallas_call | solution.py:200
  241.7 6.0 %shard_map.254 = bf16[256,1024]{1,0:T(8,128)(2,1)} custom-call(s32[1]{0:T(128)} %bitcast.section_ref._, bf16[256,1024]{1,0:T(8,128)(2,1)S(1)} %get-tuple-element.108.xf_ref, f32[256,1024]{1,0:T(8,128)S(1)} %get-tuple-element.109.hm_ref, bf16[16,576,1024]{2,1,0:T(8,128)(2,1)S(1)} %bitcast.209), custom_call_target="tpu_custom_call" | custom-call | flops 4831838208 | bytes 20971520 | tf_op jit(solution)/shard_map/pallas_call | solution.py:200
  249.4 6.3 %shard_map.251 = (f32[256,1024]{1,0:T(8,128)S(1)}, bf16[256,1024]{1,0:T(8,128)(2,1)S(1)}, bf16[1024,256]{1,0:T(8,128)(2,1)S(1)}, bf16[1024,256]{1,0:T(8,128)(2,1...) custom-call(s32[1]{0:T(128)} %bitcast.section_ref._, ...), custom_call_target="tpu_custom_call" | custom-call | flops 4294967296 | bytes 17825792 | tf_op jit(solution)/shard_map/pallas_call | solution.py:200
  255.8 6.0 %shard_map.252 = (bf16[256,1024]{1,0:T(8,128)(2,1)S(1)}, bf16[256,3072]{1,0:T(8,128)(2,1)S(1)}, bf16[256,3072]{1,0:T(8,128)(2,1)S(1)}, bf16[3072,256]{1,0:T(8,12...) custom-call(s32[1]{0:T(128)} %bitcast.section_ref._, bf16[256,1024]{1,0:T(8,128)(2,1)S(1)} %get-tuple-element.104.xf_ref, ...), custom_call_target="tpu_custom_call" | custom-call | flops 4831838208 | bytes 20971520 | tf_op jit(solution)/shard_map/pallas_call | solution.py:200
  261.9 8.3 %shard_map.257 = (f32[256,1024]{1,0:T(8,128)S(1)}, bf16[256,1024]{1,0:T(8,128)(2,1)S(1)}, bf16[256,3072]{1,0:T(8,128)(2,1)}, bf16[256,3072]{1,0:T(8,128)(2,1)}, ...) custom-call(s32[1]{0:T(128)} %constant.209.clone.1.section_ref, f32[256,1024]{1,0:T(8,128)S(1)} %get-tuple-element.113.dy_ref, ...), custom_call_target="tpu_custom_call" | custom-call | flops 4831838208 | bytes 28835840 | tf_op jit(solution)/shard_map/pallas_call | solution.py:200
  270.3 13.5 %shard_map.258 = (bf16[256,2048]{1,0:T(8,128)(2,1)}, bf16[256,2048]{1,0:T(8,128)(2,1)}, bf16[256,1024]{1,0:T(8,128)(2,1)}, f32[1,1024]{1,0:T(1,128)}, f32[1,128]{1,0:T(1,128)}, /*index=5*/f32[1,128]{1,0:T(1,128)}) custom-call(s32[1]{0:T(128)} %bitcast.section_ref._, bf16[256,1024]{1,0:T(8,128)(2,1)S(1)} %get-tuple-element.116.low_ref, ...), custom_call_target="tpu_custom_call" | custom-call | flops 5905580032 | bytes 23068672 | tf_op jit(solution)/shard_map/pallas_call | solution.py:200
  287.0 6.3 %shard_map.255 = (f32[256,1024]{1,0:T(8,128)S(1)}, bf16[256,1024]{1,0:T(8,128)(2,1)S(1)}, bf16[1024,256]{1,0:T(8,128)(2,1)S(1)}, bf16[1024,256]{1,0:T(8,128)(2,1...) custom-call(s32[1]{0:T(128)} %bitcast.section_ref._, ...), custom_call_target="tpu_custom_call" | custom-call | flops 4294967296 | bytes 17825792 | tf_op jit(solution)/shard_map/pallas_call | solution.py:200
  293.4 6.0 %shard_map.256 = (bf16[256,1024]{1,0:T(8,128)(2,1)S(1)}, bf16[256,3072]{1,0:T(8,128)(2,1)S(1)}, bf16[256,3072]{1,0:T(8,128)(2,1)S(1)}, bf16[3072,256]{1,0:T(8,12...) custom-call(s32[1]{0:T(128)} %bitcast.section_ref._, bf16[256,1024]{1,0:T(8,128)(2,1)S(1)} %get-tuple-element.110.xf_ref, ...), custom_call_target="tpu_custom_call" | custom-call | flops 4831838208 | bytes 20971520 | tf_op jit(solution)/shard_map/pallas_call | solution.py:200
  300.6 8.3 %shard_map.260 = (f32[256,1024]{1,0:T(8,128)S(1)}, bf16[256,1024]{1,0:T(8,128)(2,1)S(1)}, bf16[256,3072]{1,0:T(8,128)(2,1)}, bf16[256,3072]{1,0:T(8,128)(2,1)}, ...) custom-call(s32[1]{0:T(128)} %constant.209.clone.1.section_ref, f32[256,1024]{1,0:T(8,128)S(1)} %get-tuple-element.126.dy_ref, ...), custom_call_target="tpu_custom_call" | custom-call | flops 4831838208 | bytes 28835840 | tf_op jit(solution)/shard_map/pallas_call | solution.py:200
  309.0 13.2 %shard_map.261 = (bf16[256,2048]{1,0:T(8,128)(2,1)}, bf16[256,2048]{1,0:T(8,128)(2,1)}, bf16[256,1024]{1,0:T(8,128)(2,1)S(1)}, f32[1,1024]{1,0:T(1,128)}, f32[1,128]{1,0:T(1,128)}, /*index=5*/f32[1,128]{1,0:T(1,128)}) custom-call(s32[1]{0:T(128)} %bitcast.section_ref._, bf16[256,1024]{1,0:T(8,128)(2,1)S(1)} %get-tuple-element.129.low_ref, ...), custom_call_target="tpu_custom_call" | custom-call | flops 5905580032 | bytes 23068672 | tf_op jit(solution)/shard_map/pallas_call | solution.py:200
  323.6 6.4 %shard_map.259 = (f32[256,1024]{1,0:T(8,128)S(1)}, bf16[256,1024]{1,0:T(8,128)(2,1)S(1)}, bf16[256,3072]{1,0:T(8,128)(2,1)S(1)}, bf16[256,3072]{1,0:T(8,128)(2,1...) custom-call(s32[1]{0:T(128)} %bitcast.section_ref._, f32[256,1024]{1,0:T(8,128)S(1)} %copy-done.23, ...), custom_call_target="tpu_custom_call" | custom-call | flops 4831838208 | bytes 28835840 | tf_op jit(solution)/shard_map/pallas_call | solution.py:200
  337.8 6.3 %shard_map.262 = (f32[256,1024]{1,0:T(8,128)S(1)}, bf16[256,1024]{1,0:T(8,128)(2,1)S(1)}, bf16[256,3072]{1,0:T(8,128)(2,1)S(1)}, bf16[256,3072]{1,0:T(8,128)(2,1...) custom-call(s32[1]{0:T(128)} %bitcast.section_ref._, f32[256,1024]{1,0:T(8,128)S(1)} %get-tuple-element.126.dy_ref, ...), custom_call_target="tpu_custom_call" | custom-call | flops 4831838208 | bytes 28835840 | tf_op jit(solution)/shard_map/pallas_call | solution.py:200
  348.6 5.9 %shard_map.263 = bf16[8,2,288,1024]{3,2,1,0:T(8,128)(2,1)S(1)} custom-call(s32[9]{0:T(128)S(1)} %pad_add_fusion.1.order_ref, bf16[1024,256]{1,0:T(8,128)(2,1)S(1)} %copy-done.31, bf16[1024,256]{1,0:T(8,128)(2,1)S(1)} %copy-done.35, bf16[256,3072]{1,0:T(8,128)(2,1)S(1)} %get-tuple-element.125.refs_2_, bf16[256,3072]{1,0:T(8,128)(2,1)S(1)} %get-tuple-element.135.refs_3_, ...), custom_call_target="tpu_custom_call" | custom-call | flops 4831838208 | bytes 13631488 | tf_op jit(solution)/shard_map/pallas_call | solution.py:200
  366.7 15.3 %collective-permute-done.40 = bf16[2,288,1024]{2,1,0:T(8,128)(2,1)S(1)} collective-permute-done((bf16[2,288,1024]{2,1,0:T(8,128)(2,1)S(1)}, bf16[2,288,1024]{2,1,0:T(8,128)(2,1)S(1)}, u32[]{:S(2)}, u32[]{:S(2)}) %collective-permute-start.40) | collective-permute-done | bytes 1179680 | tf_op jit(solution)/shard_map/ppermute | solution.py:151
  385.5 12.5 %shard_map.265 = (bf16[256,2048]{1,0:T(8,128)(2,1)S(1)}, bf16[256,2048]{1,0:T(8,128)(2,1)S(1)}, bf16[256,1024]{1,0:T(8,128)(2,1)S(1)}, f32[1,1024]{1,0:T(1,128)S...) custom-call(s32[1]{0:T(128)} %bitcast.section_ref._, bf16[256,1024]{1,0:T(8,128)(2,1)S(1)} %get-tuple-element.143.low_ref.refs_8_, ...), custom_call_target="tpu_custom_call" | custom-call | flops 5905580032 | bytes 23068672 | tf_op jit(solution)/shard_map/pallas_call | solution.py:200
  398.8 12.6 %shard_map.266 = (bf16[256,2048]{1,0:T(8,128)(2,1)S(1)}, bf16[256,2048]{1,0:T(8,128)(2,1)S(1)}, bf16[256,1024]{1,0:T(8,128)(2,1)S(1)}, f32[1,1024]{1,0:T(1,128)S...) custom-call(s32[1]{0:T(128)} %bitcast.section_ref._, bf16[256,1024]{1,0:T(8,128)(2,1)S(1)} %copy-done.33, ...), custom_call_target="tpu_custom_call" | custom-call | flops 5905580032 | bytes 23068672 | tf_op jit(solution)/shard_map/pallas_call | solution.py:200
  420.1 14.9 %collective-permute-done.43 = bf16[2,288,1024]{2,1,0:T(8,128)(2,1)S(1)} collective-permute-done((bf16[2,288,1024]{2,1,0:T(8,128)(2,1)S(1)}, bf16[2,288,1024]{2,1,0:T(8,128)(2,1)S(1)}, u32[]{:S(2)}, u32[]{:S(2)}) %collective-permute-start.43) | collective-permute-done | bytes 1179680 | tf_op jit(solution)/shard_map/ppermute | solution.py:151
  443.0 10.4 %collective-permute-done.44 = bf16[2,288,1024]{2,1,0:T(8,128)(2,1)S(1)} collective-permute-done((bf16[2,288,1024]{2,1,0:T(8,128)(2,1)S(1)}, bf16[2,288,1024]{2,1,0:T(8,128)(2,1)S(1)}, u32[]{:S(2)}, u32[]{:S(2)}) %collective-permute-start.44) | collective-permute-done | bytes 1179680 | tf_op jit(solution)/shard_map/ppermute | solution.py:151
  463.5 10.9 %collective-permute-done.45 = bf16[2,288,1024]{2,1,0:T(8,128)(2,1)S(1)} collective-permute-done((bf16[2,288,1024]{2,1,0:T(8,128)(2,1)S(1)}, bf16[2,288,1024]{2,1,0:T(8,128)(2,1)S(1)}, u32[]{:S(2)}, u32[]{:S(2)}) %collective-permute-start.45) | collective-permute-done | bytes 1179680 | tf_op jit(solution)/shard_map/ppermute | solution.py:151
  484.6 19.3 %collective-permute-done.56 = bf16[2,192,1024]{2,1,0:T(8,128)(2,1)S(1)} collective-permute-done((bf16[2,192,1024]{2,1,0:T(8,128)(2,1)S(1)}, bf16[2,192,1024]{2,1,0:T(8,128)(2,1)S(1)}, u32[]{:S(2)}, u32[]{:S(2)}) %collective-permute-start.56) | collective-permute-done | bytes 786464 | tf_op jit(solution)/shard_map/ppermute | solution.py:151
  520.9 9.5 %collective-permute-done.47 = f32[1,2306]{1,0:T(1,128)} collective-permute-done((f32[1,2306]{1,0:T(1,128)S(1)}, f32[1,2306]{1,0:T(1,128)}, u32[]{:S(2)}, u32[]{:S(2)}) %collective-permute-start.47) | collective-permute-done | bytes 9256 | tf_op jit(solution)/shard_map/ppermute | solution.py:75
  559.8 9.8 %collective-permute-done.62 = bf16[2,192,1024]{2,1,0:T(8,128)(2,1)S(1)} collective-permute-done((bf16[2,192,1024]{2,1,0:T(8,128)(2,1)S(1)}, bf16[2,192,1024]{2,1,0:T(8,128)(2,1)S(1)}, u32[]{:S(2)}, u32[]{:S(2)}) %collective-permute-start.62) | collective-permute-done | bytes 786464 | tf_op jit(solution)/shard_map/ppermute | solution.py:151
  (462 shorter events, 263.2 us)
Async XLA Ops:
  76.2 19.5 %collective-permute-start.8 = (bf16[2,192,1024]{2,1,0:T(8,128)(2,1)}, bf16[2,192,1024]{2,1,0:T(8,128)(2,1)}, u32[]{:S(2)}, u32[]{:S(2)}) collective-permute-start(bf16[2,192,1024]{2,1,0:T(8,128)(2,1)} %collective-permute-done.2), channel_id=1, source_target_pairs={{0,4},{5,1},{4,8},{9,5},{8,12},{13,9},{12,14},{15,13},{14,10},{11,... | collective-permute-start | bytes 2359304 | tf_op jit(solution)/shard_map/ppermute | solution.py:116
  87.3 33.8 %collective-permute-start.7 = (bf16[2,288,1024]{2,1,0:T(8,128)(2,1)}, bf16[2,288,1024]{2,1,0:T(8,128)(2,1)}, u32[]{:S(2)}, u32[]{:S(2)}) collective-permute-start(bf16[2,288,1024]{2,1,0:T(8,128)(2,1)} %collective-permute-done.6), channel_id=1, source_target_pairs={{0,4},{5,1},{4,8},{9,5},{8,12},{13,9},{12,14},{15,13},{14,10},{11,... | collective-permute-start | bytes 3538952 | tf_op jit(solution)/shard_map/ppermute | solution.py:116
  89.4 29.5 %collective-permute-start.13 = (bf16[2,192,1024]{2,1,0:T(8,128)(2,1)}, bf16[2,192,1024]{2,1,0:T(8,128)(2,1)}, u32[]{:S(2)}, u32[]{:S(2)}) collective-permute-start(bf16[2,192,1024]{2,1,0:T(8,128)(2,1)} %copy-done.94), channel_id=1, source_target_pairs={{0,1},{1,0},{2,3},{3,2},{4,5},{5,4},{6,7},{7,6},{8,9},{9,8},{10,11... | collective-permute-start | bytes 2359304 | tf_op jit(solution)/shard_map/ppermute | solution.py:124
  95.7 21.1 %collective-permute-start.16 = (bf16[2,192,1024]{2,1,0:T(8,128)(2,1)}, bf16[2,192,1024]{2,1,0:T(8,128)(2,1)}, u32[]{:S(2)}, u32[]{:S(2)}) collective-permute-start(bf16[2,192,1024]{2,1,0:T(8,128)(2,1)} %collective-permute-done.8), channel_id=1, source_target_pairs={{0,4},{5,1},{4,8},{9,5},{8,12},{13,9},{12,14},{15,13},{14,10},{11,... | collective-permute-start | bytes 2359304 | tf_op jit(solution)/shard_map/ppermute | solution.py:116
  99.4 29.8 %collective-permute-start.14 = (bf16[2,192,1024]{2,1,0:T(8,128)(2,1)}, bf16[2,192,1024]{2,1,0:T(8,128)(2,1)}, u32[]{:S(2)}, u32[]{:S(2)}) collective-permute-start(bf16[2,192,1024]{2,1,0:T(8,128)(2,1)} %collective-permute-done.2), channel_id=1, source_target_pairs={{0,1},{1,0},{2,3},{3,2},{4,5},{5,4},{6,7},{7,6},{8,9},{9,8},{10,11... | collective-permute-start | bytes 2359304 | tf_op jit(solution)/shard_map/ppermute | solution.py:124
  116.8 29.5 %collective-permute-start.18 = (bf16[2,192,1024]{2,1,0:T(8,128)(2,1)}, bf16[2,192,1024]{2,1,0:T(8,128)(2,1)}, u32[]{:S(2)}, u32[]{:S(2)}) collective-permute-start(bf16[2,192,1024]{2,1,0:T(8,128)(2,1)} %collective-permute-done.16), channel_id=1, source_target_pairs={{0,4},{5,1},{4,8},{9,5},{8,12},{13,9},{12,14},{15,13},{14,10},{11,... | collective-permute-start | bytes 2359304 | tf_op jit(solution)/shard_map/ppermute | solution.py:116
  121.1 28.8 %collective-permute-start.28 = (bf16[2,288,1024]{2,1,0:T(8,128)(2,1)}, bf16[2,288,1024]{2,1,0:T(8,128)(2,1)}, u32[]{:S(2)}, u32[]{:S(2)}) collective-permute-start(bf16[2,288,1024]{2,1,0:T(8,128)(2,1)} %collective-permute-done.7), channel_id=1, source_target_pairs={{0,4},{5,1},{4,8},{9,5},{8,12},{13,9},{12,14},{15,13},{14,10},{11,... | collective-permute-start | bytes 3538952 | tf_op jit(solution)/shard_map/ppermute | solution.py:116
  125.1 24.4 %collective-permute-start.15 = (bf16[2,192,1024]{2,1,0:T(8,128)(2,1)}, bf16[2,192,1024]{2,1,0:T(8,128)(2,1)}, u32[]{:S(2)}, u32[]{:S(2)}) collective-permute-start(bf16[2,192,1024]{2,1,0:T(8,128)(2,1)} %collective-permute-done.8), channel_id=1, source_target_pairs={{0,1},{1,0},{2,3},{3,2},{4,5},{5,4},{6,7},{7,6},{8,9},{9,8},{10,11... | collective-permute-start | bytes 2359304 | tf_op jit(solution)/shard_map/ppermute | solution.py:124
  148.8 23.4 %collective-permute-start.24 = (bf16[2,288,1024]{2,1,0:T(8,128)(2,1)}, bf16[2,288,1024]{2,1,0:T(8,128)(2,1)}, u32[]{:S(2)}, u32[]{:S(2)}) collective-permute-start(bf16[2,288,1024]{2,1,0:T(8,128)(2,1)} %collective-permute-done.4), channel_id=1, source_target_pairs={{0,1},{1,0},{2,3},{3,2},{4,5},{5,4},{6,7},{7,6},{8,9},{9,8},{10,11... | collective-permute-start | bytes 3538952 | tf_op jit(solution)/shard_map/ppermute | solution.py:124
  149.8 32.1 %collective-permute-start.30 = (bf16[2,288,1024]{2,1,0:T(8,128)(2,1)}, bf16[2,288,1024]{2,1,0:T(8,128)(2,1)S(1)}, u32[]{:S(2)}, u32[]{:S(2)}) collective-permute-start(bf16[2,288,1024]{2,1,0:T(8,128)(2,1)} %collective-permute-done.28), channel_id=1, source_target_pairs={{0,4},{5,1},{4,8},{9,5},{8,12},{13,9},{12,14},{15,13},{14,10},{11,... | collective-permute-start | bytes 3538952 | tf_op jit(solution)/shard_map/ppermute | solution.py:116
  158.9 21.0 %collective-permute-start.22 = (bf16[2,192,1024]{2,1,0:T(8,128)(2,1)}, bf16[2,192,1024]{2,1,0:T(8,128)(2,1)S(1)}, u32[]{:S(2)}, u32[]{:S(2)}) collective-permute-start(bf16[2,192,1024]{2,1,0:T(8,128)(2,1)} %collective-permute-done.20), channel_id=1, source_target_pairs={{0,4},{5,1},{4,8},{9,5},{8,12},{13,9},{12,14},{15,13},{14,10},{11,... | collective-permute-start | bytes 2359304 | tf_op jit(solution)/shard_map/ppermute | solution.py:116
  165.2 26.0 %collective-permute-start.25 = (bf16[2,288,1024]{2,1,0:T(8,128)(2,1)}, bf16[2,288,1024]{2,1,0:T(8,128)(2,1)S(1)}, u32[]{:S(2)}, u32[]{:S(2)}) collective-permute-start(bf16[2,288,1024]{2,1,0:T(8,128)(2,1)} %collective-permute-done.5), channel_id=1, source_target_pairs={{0,1},{1,0},{2,3},{3,2},{4,5},{5,4},{6,7},{7,6},{8,9},{9,8},{10,11... | collective-permute-start | bytes 3538952 | tf_op jit(solution)/shard_map/ppermute | solution.py:124
  167.2 21.8 %collective-permute-start.21 = (bf16[2,192,1024]{2,1,0:T(8,128)(2,1)}, bf16[2,192,1024]{2,1,0:T(8,128)(2,1)S(1)}, u32[]{:S(2)}, u32[]{:S(2)}) collective-permute-start(bf16[2,192,1024]{2,1,0:T(8,128)(2,1)} %collective-permute-done.20), channel_id=1, source_target_pairs={{0,1},{1,0},{2,3},{3,2},{4,5},{5,4},{6,7},{7,6},{8,9},{9,8},{10,11... | collective-permute-start | bytes 2359304 | tf_op jit(solution)/shard_map/ppermute | solution.py:124
  172.2 23.9 %collective-permute-start.26 = (bf16[2,288,1024]{2,1,0:T(8,128)(2,1)}, bf16[2,288,1024]{2,1,0:T(8,128)(2,1)S(1)}, u32[]{:S(2)}, u32[]{:S(2)}) collective-permute-start(bf16[2,288,1024]{2,1,0:T(8,128)(2,1)} %collective-permute-done.6), channel_id=1, source_target_pairs={{0,1},{1,0},{2,3},{3,2},{4,5},{5,4},{6,7},{7,6},{8,9},{9,8},{10,11... | collective-permute-start | bytes 3538952 | tf_op jit(solution)/shard_map/ppermute | solution.py:124
  190.0 20.3 %collective-permute-start.27 = (bf16[2,288,1024]{2,1,0:T(8,128)(2,1)}, bf16[2,288,1024]{2,1,0:T(8,128)(2,1)S(1)}, u32[]{:S(2)}, u32[]{:S(2)}) collective-permute-start(bf16[2,288,1024]{2,1,0:T(8,128)(2,1)} %collective-permute-done.7), channel_id=1, source_target_pairs={{0,1},{1,0},{2,3},{3,2},{4,5},{5,4},{6,7},{7,6},{8,9},{9,8},{10,11... | collective-permute-start | bytes 3538952 | tf_op jit(solution)/shard_map/ppermute | solution.py:124
  192.3 22.1 %collective-permute-start.29 = (bf16[2,288,1024]{2,1,0:T(8,128)(2,1)}, bf16[2,288,1024]{2,1,0:T(8,128)(2,1)S(1)}, u32[]{:S(2)}, u32[]{:S(2)}) collective-permute-start(bf16[2,288,1024]{2,1,0:T(8,128)(2,1)} %collective-permute-done.28), channel_id=1, source_target_pairs={{0,1},{1,0},{2,3},{3,2},{4,5},{5,4},{6,7},{7,6},{8,9},{9,8},{10,11... | collective-permute-start | bytes 3538952 | tf_op jit(solution)/shard_map/ppermute | solution.py:124
  196.0 20.7 %collective-permute-start.31 = (bf16[2,288,1024]{2,1,0:T(8,128)(2,1)S(1)}, bf16[2,288,1024]{2,1,0:T(8,128)(2,1)S(1)}, u32[]{:S(2)}, u32[]{:S(2)}) collective-permute-start(bf16[2,288,1024]{2,1,0:T(8,128)(2,1)S(1)} %collective-permute-done.30), channel_id=1, source_target_pairs={{0,1},{1,0},{2,3},{3,2},{4,5},{5,4},{6,7},{7,6},{8,9},{9,8},{10,11... | collective-permute-start | bytes 3538952 | tf_op jit(solution)/shard_map/ppermute | solution.py:124
  199.6 19.2 %collective-permute-start.33 = (bf16[2,288,1024]{2,1,0:T(8,128)(2,1)S(1)}, bf16[2,288,1024]{2,1,0:T(8,128)(2,1)S(1)}, u32[]{:S(2)}, u32[]{:S(2)}) collective-permute-start(bf16[2,288,1024]{2,1,0:T(8,128)(2,1)S(1)} %collective-permute-done.32), channel_id=1, source_target_pairs={{0,1},{1,0},{2,3},{3,2},{4,5},{5,4},{6,7},{7,6},{8,9},{9,8},{10,11... | collective-permute-start | bytes 3538952 | tf_op jit(solution)/shard_map/ppermute | solution.py:124
  247.7 37.5 %collective-permute-start.36 = (bf16[256,1024]{1,0:T(8,128)(2,1)}, bf16[256,1024]{1,0:T(8,128)(2,1)S(1)}, u32[]{:S(2)}, u32[]{:S(2)}) collective-permute-start(bf16[256,1024]{1,0:T(8,128)(2,1)} %shard_map.254), channel_id=1, source_target_pairs={{0,16},{1,17},{2,18},{3,19},{4,20},{5,21},{6,22},{7,23},{8,24},{9,... | collective-permute-start | bytes 1572872 | tf_op jit(solution)/shard_map/ppermute | solution.py:29
  283.8 39.9 %collective-permute-start.37 = (bf16[256,1024]{1,0:T(8,128)(2,1)}, bf16[256,1024]{1,0:T(8,128)(2,1)S(1)}, u32[]{:S(2)}, u32[]{:S(2)}) collective-permute-start(bf16[256,1024]{1,0:T(8,128)(2,1)} %get-tuple-element.121), channel_id=1, source_target_pairs={{16,0},{17,1},{18,2},{19,3},{20,4},{21,5},{22,6},{23,7},{24,8},{25... | collective-permute-start | bytes 1572872 | tf_op jit(solution)/shard_map/ppermute | solution.py:29
  354.5 27.6 %collective-permute-start.41 = (bf16[8,2,288,1024]{3,2,1,0:T(8,128)(2,1)S(1)}, bf16[8,2,288,1024]{3,2,1,0:T(8,128)(2,1)}, u32[]{:S(2)}, u32[]{:S(2)}) collective-permute-start(bf16[8,2,288,1024]{3,2,1,0:T(8,128)(2,1)S(1)} %shard_map.263), channel_id=1, source_target_pairs={{0,1},{1,0},{2,3},{3,2},{4,5},{5,4},{6,7},{7,6},{8,9},{9,8},{10,11... | collective-permute-start | bytes 28311560 | tf_op jit(solution)/shard_map/ppermute | solution.py:144
  384.1 28.1 %collective-permute-start.42 = (bf16[2,288,1024]{2,1,0:T(8,128)(2,1)S(1)}, bf16[2,288,1024]{2,1,0:T(8,128)(2,1)S(1)}, u32[]{:S(2)}, u32[]{:S(2)}) collective-permute-start(bf16[2,288,1024]{2,1,0:T(8,128)(2,1)S(1)} %fusion.5), channel_id=1, source_target_pairs={{0,4},{5,1},{4,8},{9,5},{8,12},{13,9},{12,14},{15,13},{14,10},{11,... | collective-permute-start | bytes 3538952 | tf_op jit(solution)/shard_map/ppermute | solution.py:151
  418.7 43.0 %collective-permute-start.54 = (bf16[8,2,192,1024]{3,2,1,0:T(8,128)(2,1)S(1)}, bf16[8,2,192,1024]{3,2,1,0:T(8,128)(2,1)S(1)}, u32[]{:S(2)}, u32[]{:S(2)}) collective-permute-start(bf16[8,2,192,1024]{3,2,1,0:T(8,128)(2,1)S(1)} %shard_map.267), channel_id=1, source_target_pairs={{0,1},{1,0},{2,3},{3,2},{4,5},{5,4},{6,7},{7,6},{8,9},{9,8},{10,11... | collective-permute-start | bytes 18874376 | tf_op jit(solution)/shard_map/ppermute | solution.py:144
  442.9 18.9 %collective-permute-start.53 = (bf16[2,192,1024]{2,1,0:T(8,128)(2,1)S(1)}, bf16[2,192,1024]{2,1,0:T(8,128)(2,1)S(1)}, u32[]{:S(2)}, u32[]{:S(2)}) collective-permute-start(bf16[2,192,1024]{2,1,0:T(8,128)(2,1)S(1)} %fusion.13), channel_id=1, source_target_pairs={{0,4},{5,1},{4,8},{9,5},{8,12},{13,9},{12,14},{15,13},{14,10},{11,... | collective-permute-start | bytes 2359304 | tf_op jit(solution)/shard_map/ppermute | solution.py:151
  455.3 19.0 %collective-permute-start.45 = (bf16[2,288,1024]{2,1,0:T(8,128)(2,1)S(1)}, bf16[2,288,1024]{2,1,0:T(8,128)(2,1)S(1)}, u32[]{:S(2)}, u32[]{:S(2)}) collective-permute-start(bf16[2,288,1024]{2,1,0:T(8,128)(2,1)S(1)} %fusion.2), channel_id=1, source_target_pairs={{0,4},{5,1},{4,8},{9,5},{8,12},{13,9},{12,14},{15,13},{14,10},{11,... | collective-permute-start | bytes 3538952 | tf_op jit(solution)/shard_map/ppermute | solution.py:151
  462.2 20.6 %collective-permute-start.55 = (bf16[2,192,1024]{2,1,0:T(8,128)(2,1)S(1)}, bf16[2,192,1024]{2,1,0:T(8,128)(2,1)S(1)}, u32[]{:S(2)}, u32[]{:S(2)}) collective-permute-start(bf16[2,192,1024]{2,1,0:T(8,128)(2,1)S(1)} %fusion.11), channel_id=1, source_target_pairs={{0,4},{5,1},{4,8},{9,5},{8,12},{13,9},{12,14},{15,13},{14,10},{11,... | collective-permute-start | bytes 2359304 | tf_op jit(solution)/shard_map/ppermute | solution.py:151
  476.4 30.1 %collective-permute-start.59 = (bf16[2,288,1024]{2,1,0:T(8,128)(2,1)S(1)}, bf16[2,288,1024]{2,1,0:T(8,128)(2,1)S(1)}, u32[]{:S(2)}, u32[]{:S(2)}) collective-permute-start(bf16[2,288,1024]{2,1,0:T(8,128)(2,1)S(1)} %fusion.1), channel_id=1, source_target_pairs={{0,4},{5,1},{4,8},{9,5},{8,12},{13,9},{12,14},{15,13},{14,10},{11,... | collective-permute-start | bytes 3538952 | tf_op jit(solution)/shard_map/ppermute | solution.py:151
  483.2 20.6 %collective-permute-start.56 = (bf16[2,192,1024]{2,1,0:T(8,128)(2,1)S(1)}, bf16[2,192,1024]{2,1,0:T(8,128)(2,1)S(1)}, u32[]{:S(2)}, u32[]{:S(2)}) collective-permute-start(bf16[2,192,1024]{2,1,0:T(8,128)(2,1)S(1)} %fusion.10), channel_id=1, source_target_pairs={{0,4},{5,1},{4,8},{9,5},{8,12},{13,9},{12,14},{15,13},{14,10},{11,... | collective-permute-start | bytes 2359304 | tf_op jit(solution)/shard_map/ppermute | solution.py:151
  509.5 28.8 %collective-permute-start.60 = (bf16[2,288,1024]{2,1,0:T(8,128)(2,1)}, bf16[2,288,1024]{2,1,0:T(8,128)(2,1)S(1)}, u32[]{:S(2)}, u32[]{:S(2)}) collective-permute-start(bf16[2,288,1024]{2,1,0:T(8,128)(2,1)} %fusion), channel_id=1, source_target_pairs={{0,4},{5,1},{4,8},{9,5},{8,12},{13,9},{12,14},{15,13},{14,10},{11,... | collective-permute-start | bytes 3538952 | tf_op jit(solution)/shard_map/ppermute | solution.py:151
  509.6 21.6 %collective-permute-start.35 = (bf16[1,256,1024]{2,1,0:T(8,128)(2,1)S(1)}, bf16[1,256,1024]{2,1,0:T(8,128)(2,1)}, u32[]{:S(2)}, u32[]{:S(2)}) collective-permute-start(bf16[1,256,1024]{2,1,0:T(8,128)(2,1)S(1)} %bitcast.212), channel_id=1, source_target_pairs={{16,0},{17,1},{18,2},{19,3},{20,4},{21,5},{22,6},{23,7},{24,8},{25... | collective-permute-start | bytes 1572872 | tf_op jit(solution)/shard_map/ppermute | solution.py:29
  519.5 21.2 %collective-permute-start.58 = (bf16[2,192,1024]{2,1,0:T(8,128)(2,1)S(1)}, bf16[2,192,1024]{2,1,0:T(8,128)(2,1)}, u32[]{:S(2)}, u32[]{:S(2)}) collective-permute-start(bf16[2,192,1024]{2,1,0:T(8,128)(2,1)S(1)} %fusion.8), channel_id=1, source_target_pairs={{0,4},{5,1},{4,8},{9,5},{8,12},{13,9},{12,14},{15,13},{14,10},{11,... | collective-permute-start | bytes 2359304 | tf_op jit(solution)/shard_map/ppermute | solution.py:151
  540.7 18.5 %collective-permute-start.64 = (f32[288,1024]{1,0:T(8,128)S(1)}, f32[288,1024]{1,0:T(8,128)S(1)}, u32[]{:S(2)}, u32[]{:S(2)}) collective-permute-start(f32[288,1024]{1,0:T(8,128)S(1)} %dynamic-slice_bitcast_fusion), channel_id=1, source_target_pairs={{0,1},{1,0},{2,3},{3,2},{4,5},{5,4},{6,7},{7,6},{8,9},{9,8},{10,11... | collective-permute-start | bytes 3538952 | tf_op jit(solution)/shard_map/ppermute | solution.py:161
  (142 other events, 2478.9 us)

commit v5 on v4

--- a/solution.py
+++ b/solution.py
@@ -18,11 +18,8 @@
 NEGATIVE = -1e30
 CONTRACT_ROWS = (((0,), (0,)), ((), ()))
 CONTRACT_COLS = (((1,), (1,)), ((), ()))
-RING_LEAD = 1
-FIRST_WAIT = 3
-SLOT_DEPTH = 2
+SMALL_LAST = True
 VMEM_GRANT = 10
-BLANK_SPACE = pl.ANY
 
 
 def one_way(value, source):
@@ -48,84 +45,66 @@
     return around, [(device, device ^ 1) for device in range(devices)]
 
 
-def tie(*values):
-    return lax.optimization_barrier(values)
-
-
-def spread(value):
+def cycles(value):
     devices = lax.axis_size("dp")
     index = lax.axis_index("dp")
-    step = 1
-    while step < devices:
-        other = lax.ppermute(value, "dp", [(low, low ^ step) for low in range(devices)])
-        later = (index // step) % 2 == 1
-        value = jnp.where(
-            later,
-            jnp.concatenate([other, value], axis=0),
-            jnp.concatenate([value, other], axis=0),
+    width = 1
+    while width < devices:
+        base = min(4, devices // width)
+        got = [value]
+        for turn in range(1, base):
+            route = []
+            for low in range(devices):
+                digit = low // width % base
+                route.append((low, low + ((digit + turn) % base - digit) * width))
+            got.append(lax.ppermute(value, "dp", route))
+        value = yield got, index // width % base
+        width *= base
+
+
+def joined(got, digit):
+    base, size = len(got), got[0].shape[0]
+    turned = [got[-place % base] for place in range(base)] * 2
+    start = (base - digit) % base * size
+    return lax.dynamic_slice_in_dim(jnp.concatenate(turned, axis=0), start, base * size, 0)
+
+
+class GatherRing:
+    def __init__(self, packed):
+        devices = lax.axis_size("dp")
+        self.chips = devices // 2
+        self.route, self.pair = ring_routes(devices)
+        self.packed = packed
+        self.other = lax.ppermute(packed, "dp", self.pair)
+        core = lax.axis_index("dp") % 2
+        self.pieces = [self.stack(core)]
+        self.others = [self.stack(1 - core)]
+        self.step = 1
+
+    def stack(self, which):
+        core = lax.axis_index("dp") % 2
+        first = lax.dynamic_slice_in_dim(self.packed, which, 1, 0)
+        second = lax.dynamic_slice_in_dim(self.other, which, 1, 0)
+        return jnp.where(
+            core == 0,
+            jnp.concatenate([first, second], axis=0),
+            jnp.concatenate([second, first], axis=0),
         )
-        step *= 2
-    return value
-
-
-def summed(value):
-    devices = lax.axis_size("dp")
-    step = 1
-    while step < devices:
-        value = value + lax.ppermute(value, "dp", [(low, low ^ step) for low in range(devices)])
-        step *= 2
-    return value
-
-
-def blank(shape, dtype):
-    return pl.pallas_call(
-        lambda ref: None,
-        out_specs=pl.BlockSpec(memory_space=BLANK_SPACE),
-        out_shape=jax.ShapeDtypeStruct(shape, dtype),
-    )()
-
-
-def gather_ring(packed, rows, after=None):
-    devices = lax.axis_size("dp")
-    chips = devices // 2
-    around, pair = ring_routes(devices)
-    index = lax.axis_index("dp")
-    core = index % 2
-    place = ring_place(index // 2, chips)
-    if after is not None:
-        packed, after = tie(packed, after)
-    half, model = packed.shape[1:]
-    whole = blank((devices, rows, model), packed.dtype)
-    own_low = core * (rows - half)
-    other_low = (1 - core) * (rows - half)
-
-    def put(whole, piece, owner, offset):
-        return lax.dynamic_update_slice(whole, piece, (owner, offset, 0))
-
-    other = lax.ppermute(packed, "dp", pair)
-    mine = lax.dynamic_slice_in_dim(packed, core, 1, 0)
-    theirs = lax.dynamic_slice_in_dim(other, core, 1, 0)
-    piece = jnp.where(
-        core == 0,
-        jnp.concatenate([mine, theirs], axis=0),
-        jnp.concatenate([theirs, mine], axis=0),
-    )
-    marks = []
-    for step in range(1, chips):
-        start = piece
-        piece = lax.ppermute(piece, "dp", around)
-        if step == 1:
-            whole = put(whole, start, index - core, own_low)
-            start = lax.dynamic_slice_in_dim(other, 1 - core, 1, 0)
-            whole = put(whole, start, index + 1 - 2 * core, other_low)
-            start = lax.dynamic_slice_in_dim(packed, 1 - core, 1, 0)
-            whole = put(whole, start, index, other_low)
-        marks.append(piece)
-        swapped = lax.ppermute(piece, "dp", pair)
-        turn = (2 * core - 1) * step
-        whole = put(whole, piece, 2 * chip_at(place + turn, chips), own_low)
-        whole = put(whole, swapped, 2 * chip_at(place - turn, chips), other_low)
-    return whole, marks
+
+    def advance(self, *before):
+        value = self.pieces[-1]
+        if before:
+            value = self.pieces[-1] = hold(value, *before)
+        self.pieces.append(lax.ppermute(value, "dp", self.route))
+        self.swap(value)
+        self.step += 1
+        if self.step == self.chips:
+            self.swap(self.pieces[-1])
+        return self.pieces[-1]
+
+    def swap(self, value):
+        if len(self.pieces) > 2 or self.step == self.chips:
+            self.others.append(lax.ppermute(value, "dp", self.pair))
 
 
 class ScatterRing:
@@ -133,19 +112,15 @@
         devices = lax.axis_size("dp")
         self.chips = devices // 2
         self.route, self.pair = ring_routes(devices)
-        self.mine, self.theirs, self.got = mine, theirs, None
-        early = lax.ppermute(theirs[1:2], "dp", self.pair)[0]
-        value = mine[1].astype(jnp.float32) + early.astype(jnp.float32)
+        self.mine = mine
+        self.got = lax.ppermute(theirs, "dp", self.pair)
+        value = mine[1].astype(jnp.float32) + self.got[1].astype(jnp.float32)
         self.value = value.astype(jnp.bfloat16)
-        self.start = self.value
         self.step = 1
 
-    def exchange(self):
-        self.got = lax.ppermute(self.theirs, "dp", self.pair)
-
-    def advance(self, before):
-        if before is not None:
-            self.value, _ = tie(self.value, before)
+    def advance(self, *before):
+        if before:
+            self.value = hold(self.value, *before)
         self.step += 1
         place = self.step % self.chips
         value = lax.ppermute(self.value, "dp", self.route).astype(jnp.float32)
@@ -162,13 +137,6 @@
         return jnp.where(core == 0, own, other), jnp.where(core == 0, other, own)
 
 
-def run_slots(slots, history, depth):
-    for ring in slots:
-        if ring.step < ring.chips:
-            before = history[-depth] if len(history) >= depth else None
-            history.append(ring.advance(before))
-
-
 def beside(grad, low, pieces, rows):
     return jnp.concatenate(
         [grad[low + rows * i : low + rows * (i + 1)] for i in range(pieces)], axis=1
@@ -193,12 +161,28 @@
 
 LOCAL = pl.BlockSpec(memory_space=pltpu.VMEM)
 SCALARS = pl.BlockSpec(memory_space=pltpu.SMEM)
-
-
-def flat_call(body, arguments, out_shape, scratch=(), flops=0, moved=0, vmem=VMEM_GRANT):
-    specs = [SCALARS] + [LOCAL] * (len(arguments) - 1)
+ANYWHERE = pl.BlockSpec(memory_space=pl.ANY)
+
+
+def hold(value, *after):
     return pl.pallas_call(
-        body,
+        lambda *refs: None,
+        in_specs=[ANYWHERE] * (1 + len(after)),
+        out_specs=ANYWHERE,
+        out_shape=jax.ShapeDtypeStruct(value.shape, value.dtype),
+        input_output_aliases={0: 0},
+    )(value, *after)
+
+
+def flat_call(body, arguments, out_shape, scratch=(), flops=0, moved=0, vmem=VMEM_GRANT, after=()):
+    specs = [SCALARS] + [LOCAL] * (len(arguments) - 1) + [ANYWHERE] * len(after)
+    count = len(arguments)
+
+    def run(*refs):
+        body(*refs[:count], *refs[count + len(after) :])
+
+    return pl.pallas_call(
+        run,
         in_specs=specs,
         out_specs=[LOCAL] * len(out_shape),
         out_shape=out_shape,
@@ -207,7 +191,7 @@
         cost_estimate=pl.CostEstimate(
             flops=int(flops), bytes_accessed=int(moved), transcendentals=0
         ),
-    )(*arguments)
+    )(*arguments, *after)
 
 
 def low_shape(*shape):
@@ -497,7 +481,7 @@
     dx_ref[...] = d_hidden.astype(jnp.bfloat16)
 
 
-def attention_back(section, low, d_middle, hidden, qkv, pre, gains, tables, whole):
+def attention_back(section, low, d_middle, hidden, qkv, pre, gains, tables, whole, after=()):
     tokens, model = hidden.shape
     wide = QUERY_HEADS * HEAD_SIZE
     return flat_call(
@@ -514,76 +498,79 @@
         scratch=[pltpu.VMEM((tokens, wide), jnp.bfloat16)],
         flops=2 * tokens * model * 6 * model + 20 * tokens * tokens * wide,
         moved=12 * model * model + 40 * tokens * model,
+        after=after,
     )
 
 
 def grad_kernel(plan, chips, batches, order_ref, *refs):
-    side = order_ref[chips]
-    count = sum(1 + len(entry[4]) for entry in plan) * batches
-    target, stores = refs[count], refs[count + 1 :]
-    model = target.shape[3]
-    taken, start = 0, 0
-
-    def take():
-        nonlocal taken
-        taken += batches
-        return refs[taken - batches : taken]
-
-    for (rows, size, low, blocks, choices), store in zip(plan, stores):
-        left, rights = take(), [take() for _ in choices]
-        first = side * low
-        for t in range(chips):
-            owner = 2 * order_ref[t]
-            for core in range(2):
-                place = pl.multiple_of((owner + core) * rows + first, 16)
-                to = slice((2 * t + core) * size, (2 * t + core + 1) * size)
+    count = sum(1 + len(entry[5]) for entry in plan) * batches
+    targets, stores = refs[count : count + 2], refs[count + 2 :]
+    model = targets[0].shape[3]
+    for target, base in ((targets[0], 0), (targets[1], chips + 1)):
+        side = order_ref[base + chips]
+        taken, start = 0, 0
+        for (rows, size, low, least, blocks, choices), store in zip(plan, stores):
+            left = refs[taken : taken + batches]
+            taken += batches
+            rights = []
+            for _ in choices:
+                rights.append(refs[taken : taken + batches])
+                taken += batches
+            first = least + side * low
+            for t in range(chips):
+                owner = 2 * order_ref[base + t]
+                for core in range(2):
+                    place = pl.multiple_of((owner + core) * rows + first, 16)
+                    to = slice((2 * t + core) * size, (2 * t + core + 1) * size)
+                    for batch in range(batches):
+                        store[batch, to, :] = left[batch][pl.ds(place, size), :]
+            for block in range(blocks):
+                part = part_of(block, model)
+                right = []
                 for batch in range(batches):
-                    store[batch, to, :] = left[batch][pl.ds(place, size), :]
-        for block in range(blocks):
-            part = part_of(block, model)
-            right = []
-            for batch in range(batches):
-                value = rights[0][batch][:, part]
-                if len(rights) > 1:
-                    value = jnp.where(side == 0, value, rights[1][batch][:, part])
-                right.append(value)
-            for half in range(2):
-                value = None
-                span = slice(half * chips * size, (half + 1) * chips * size)
-                for batch in range(batches):
-                    term = dot_plain(store[batch, span, :], right[batch])
-                    value = term if value is None else value + term
-                value = value.astype(jnp.bfloat16).reshape(chips // 2, 2, size, model)
-                into = slice(start + block * size, start + (block + 1) * size)
-                target[half * chips // 2 : (half + 1) * chips // 2, :, into, :] = value
-        start += blocks * size
-
-
-def weight_grads(order, parts, model):
+                    value = rights[0][batch][:, part]
+                    if len(rights) > 1:
+                        value = jnp.where(side == 0, value, rights[1][batch][:, part])
+                    right.append(value)
+                for half in range(2):
+                    value = None
+                    span = slice(half * chips * size, (half + 1) * chips * size)
+                    for batch in range(batches):
+                        term = dot_plain(store[batch, span, :], right[batch])
+                        value = term if value is None else value + term
+                    value = value.astype(jnp.bfloat16).reshape(chips // 2, 2, size, model)
+                    into = slice(start + block * size, start + (block + 1) * size)
+                    target[half * chips // 2 : (half + 1) * chips // 2, :, into, :] = value
+            start += blocks * size
+
+
+def weight_grads(orders, parts, model, after=()):
     batches = len(parts[0][0])
     tokens = parts[0][0][0].shape[1]
-    chips = order.shape[0] - 1
+    chips = orders.shape[0] // 2 - 1
     plan, scratch, operands, total = [], [], [], 0
-    for left, rights, size, low in parts:
+    for left, rights, size, low, least in parts:
         rows = left[0].shape[0] // (2 * chips)
         blocks = rights[0][0].shape[1] // model
-        plan.append((rows, size, low, blocks, tuple(range(len(rights)))))
+        plan.append((rows, size, low, least, blocks, tuple(range(len(rights)))))
         scratch.append(pltpu.VMEM((batches, 2 * chips * size, tokens), jnp.bfloat16))
         operands += list(left) + [array for right in rights for array in right]
         total += size * blocks
+    shape = low_shape(chips, 2, total, model)
     return flat_call(
         functools.partial(grad_kernel, tuple(plan), chips, batches),
-        (order, *operands),
-        [low_shape(chips, 2, total, model)],
+        (orders, *operands),
+        [shape, shape],
         scratch=scratch,
-        flops=4 * chips * total * model * tokens * batches,
-        moved=4 * chips * total * model + 8 * tokens * batches * model,
+        flops=8 * chips * total * model * tokens * batches,
+        moved=8 * chips * total * model + 8 * tokens * batches * model,
         vmem=14,
-    )[0]
-
-
-def pack_kernel(plan, count, *refs):
-    target, sem = refs[count], refs[count + 1]
+        after=after,
+    )
+
+
+def pack_kernel(plan, *refs):
+    target, sem = refs[-2:]
     model = target.shape[2]
     copies = []
     for half, entries in enumerate(plan):
@@ -603,16 +590,55 @@
         copy.wait()
 
 
-def pack(shards, plan, model):
+def pack(shards, plan, model, after=()):
     rows = sum(entry[2] for entry in plan[0])
     return pl.pallas_call(
-        functools.partial(pack_kernel, plan, len(shards)),
-        in_specs=[pl.BlockSpec(memory_space=pl.ANY)] * len(shards),
+        functools.partial(pack_kernel, plan),
+        in_specs=[ANYWHERE] * (len(shards) + len(after)),
         out_specs=LOCAL,
         out_shape=low_shape(2, rows, model),
         scratch_shapes=[pltpu.SemaphoreType.DMA((len(plan[0]) + len(plan[1]),))],
         compiler_params=pltpu.CompilerParams(vmem_limit_bytes=VMEM_GRANT << 20),
-    )(*shards)
+    )(*shards, *after)
+
+
+def assemble_kernel(chips, plan, order_ref, *refs):
+    target, sem = refs[-2:]
+    copies = []
+    for group, (low, rows, start, further) in enumerate(plan):
+        for turn in range(2):
+            base = turn * (chips + 1)
+            place = pl.multiple_of(start + order_ref[base + chips] * further, 16)
+            for t in range(chips):
+                piece = refs[(2 * group + turn) * chips + t]
+                copies.append(
+                    pltpu.make_async_copy(
+                        piece.at[:, low : low + rows, :],
+                        target.at[pl.ds(2 * order_ref[base + t], 2), pl.ds(place, rows), :],
+                        sem.at[len(copies)],
+                    )
+                )
+    for copy in copies:
+        copy.start()
+    for copy in copies:
+        copy.wait()
+
+
+def assemble(orders, sources, rows):
+    chips = sources[0][0].chips
+    pieces = [piece for source in sources for piece in source[0].pieces + source[0].others]
+    model = pieces[0].shape[2]
+    return pl.pallas_call(
+        functools.partial(assemble_kernel, chips, tuple(source[1:] for source in sources)),
+        in_specs=[SCALARS] + [ANYWHERE] * len(pieces),
+        out_specs=LOCAL,
+        out_shape=low_shape(2 * chips, rows, model),
+        scratch_shapes=[pltpu.SemaphoreType.DMA((len(pieces),))],
+        compiler_params=pltpu.CompilerParams(vmem_limit_bytes=VMEM_GRANT << 20),
+        cost_estimate=pl.CostEstimate(
+            flops=0, bytes_accessed=8 * chips * rows * model, transcendentals=0
+        ),
+    )(orders, *pieces)
 
 
 def local(
@@ -641,6 +667,15 @@
     forward_rows = ffn_down.shape[1]
 
     cut = forward_rows // 2 if forward_rows % 32 == 0 else 2 * rows
+    core = index % 2
+    place = ring_place(index // 2, chips)
+    away = jnp.arange(chips, dtype=jnp.int32) * (2 * core - 1)
+    order = jnp.concatenate([chip_at(place + away, chips), core[None]]).astype(jnp.int32)
+    other_order = jnp.concatenate([chip_at(place - away, chips), 1 - core[None]]).astype(jnp.int32)
+    orders = jnp.concatenate([order, other_order])
+    gain_sizes = (norm_attn.shape[1], norm_query.shape[1], norm_key.shape[1], norm_ffn.shape[1])
+    gain_shard = jnp.concatenate([norm_attn, norm_query, norm_key, norm_ffn], axis=1)
+    moved = cut // 2
     attn_packed = pack(
         (attn_query[0], attn_out[0], attn_key[0], attn_value[0]),
         (
@@ -649,31 +684,19 @@
         ),
         model,
     )
-    attn_whole, attn_marks = gather_ring(attn_packed, 6 * rows)
-    (ffn_gate, ffn_up, ffn_down, lengths), _ = tie(
-        (ffn_gate, ffn_up, ffn_down, lengths), attn_marks[0]
-    )
     ffn_packed = pack(
         (ffn_gate[0], ffn_down[0], ffn_up[0]),
         (
             ((0, 0, rows, 0), (0, 0, rows, 1), (0, 0, rows, 2), (1, 0, cut, 0)),
-            ((1, forward_rows - cut, cut, 0), (2, 0, rows, 0), (2, 0, rows, 1), (2, 0, rows, 2)),
+            (
+                (1, forward_rows - cut, cut, 0),
+                (2, 0, rows, 0),
+                (2, 0, rows, 1),
+                (2, 0, rows, 2),
+            ),
         ),
         model,
     )
-    ffn_whole, ffn_marks = gather_ring(
-        ffn_packed, 9 * rows, attn_marks[min(RING_LEAD, chips - 2)]
-    )
-
-    gain_sizes = (norm_attn.shape[1], norm_query.shape[1], norm_key.shape[1], norm_ffn.shape[1])
-    gain_shard = jnp.concatenate([norm_attn, norm_query, norm_key, norm_ffn], axis=1)
-    gain_shard, _ = tie(gain_shard.astype(jnp.float32), attn_marks[min(2, chips - 2)])
-    gain_whole = spread(gain_shard)
-    gains, low = [], 0
-    for size in gain_sizes:
-        gains.append(gain_whole[:, low : low + size].reshape(1, devices * size))
-        low += size
-
     segments, places = jax.vmap(layout)(lengths[:, 0, :])
     keep = (segments < slots - 1).astype(jnp.float32)
     tables = []
@@ -687,18 +710,46 @@
                 segments[batch].reshape(1, 1, TOKENS_PER_SHARD),
             )
         )
+    keep_columns = [keep[batch][:, None] for batch in range(batches)]
+    early = [array for table in tables for array in table] + keep_columns + [orders]
+    attn_ring = GatherRing(attn_packed)
+    ffn_ring = GatherRing(ffn_packed)
+    gain_rounds = cycles(gain_shard.astype(jnp.float32))
+    got, digit = next(gain_rounds)
+    attn_ring.advance()
+    ffn_ring.advance()
+    attn_ring.advance(*early)
+    ffn_ring.advance(attn_ring.others[0], ffn_ring.others[0])
+    while True:
+        gain_whole = joined(got, digit)
+        attn_ring.advance(gain_whole)
+        ffn_ring.advance()
+        try:
+            got, digit = gain_rounds.send(gain_whole)
+        except StopIteration:
+            break
+    gains, low = [], 0
+    for size in gain_sizes:
+        gains.append(gain_whole[:, low : low + size].reshape(1, devices * size))
+        low += size
+
+    attn_ring.advance(*gains)
+    while ffn_ring.step < chips:
+        ffn_ring.advance()
+        if attn_ring.step < chips:
+            attn_ring.advance()
+    half = 3 * rows + cut
+    ffn_low = 9 * rows - half
+    attn_whole = assemble(orders, [(attn_ring, 0, 3 * rows, 0, 3 * rows)], 6 * rows)
+    ffn_whole = assemble(orders, [(ffn_ring, 0, half, 0, ffn_low)], 9 * rows)
     both = range(batches)
-
-    def waiting(value, marks, step):
-        return tie(value, marks[min(step, chips - 2)])[0]
 
     first = [inputs[batch] for batch in both]
     where = section[None].astype(jnp.int32)
     last = jnp.ones((1,), jnp.int32)
     carried, seen = [], []
     for batch in both:
-        start = waiting(first[batch], ffn_marks, FIRST_WAIT + batch)
-        seen.append(attention(where, start, start, gains, tables[batch], attn_whole, False))
+        seen.append(attention(where, first[batch], first[batch], gains, tables[batch], attn_whole, False))
     for batch in both:
         (result,) = feed_forward(where, seen[batch][1], seen[batch][0], ffn_whole)
         carried.append(one_way(result, 0))
@@ -709,7 +760,7 @@
             where, first[batch], carried[batch], gains, tables[batch], attn_whole, True
         )
         result, gate, up, inner_t, pull, square = feed_forward(
-            where, norm, mid, ffn_whole, (teacher[batch], keep[batch][:, None])
+            where, norm, mid, ffn_whole, (teacher[batch], keep_columns[batch])
         )
         kept.append(
             (hidden, normalized_t, qkv, pre, mix_t, mid, norm_t, result, gate, up, inner_t, pull, square)
@@ -718,12 +769,6 @@
         hidden, normalized_t, qkv, pre, mixed_t, middle, normed_t, result, gate, up, inner_t, pull,
         squares,
     ) = (list(column) for column in zip(*kept))
-
-    core = index % 2
-    place = ring_place(index // 2, chips)
-    away = jnp.arange(chips, dtype=jnp.int32) * (2 * core - 1)
-    order = jnp.concatenate([chip_at(place + away, chips), core[None]]).astype(jnp.int32)
-    other_order = jnp.concatenate([chip_at(place - away, chips), 1 - core[None]]).astype(jnp.int32)
 
     incoming = []
     for batch in both:
@@ -749,22 +794,19 @@
         d_up.append(u)
         gain_ffn = gain_ffn + gain
     ffn_parts = [
-        (normed_t, (d_gate, d_up), rows, 0),
-        (inner_t, (d_branch,), cut, forward_rows - cut),
+        (normed_t, (d_gate, d_up), rows, 0, 0),
+        (inner_t, (d_branch,), cut - moved, forward_rows - cut + moved, 0),
     ]
-    theirs = weight_grads(other_order, ffn_parts, model)
-    mine = weight_grads(tie(order, theirs)[0], ffn_parts, model)
-    ffn_ring = ScatterRing(mine, theirs)
-    ffn_ring.exchange()
-    history = []
-    run_slots([ffn_ring], history, SLOT_DEPTH)
+    their_orders = jnp.concatenate([other_order, order])
     d_query, d_pair, d_hidden = [], [], []
     gain_attn, gain_query, gain_key = 0.0, 0.0, 0.0
     for batch in both:
-        value, _ = tie(d_attn[batch], (ffn_ring.start, history[0])[batch])
+        if batch + 1 == batches:
+            theirs, mine = weight_grads(their_orders, ffn_parts, model, tuple(d_query))
+            ffn_ring = ScatterRing(mine, theirs)
         q, kv, x, gain_a, gain_q, gain_k = attention_back(
-            where, value, d_middle[batch], hidden[batch], qkv[batch], pre[batch], gains,
-            tables[batch], attn_whole,
+            where, d_attn[batch], d_middle[batch], hidden[batch], qkv[batch], pre[batch], gains,
+            tables[batch], attn_whole, (mine,) if batch + 1 == batches else (),
         )
         d_query.append(q)
         d_pair.append(kv)
@@ -773,37 +815,50 @@
         gain_query = gain_query + gain_q
         gain_key = gain_key + gain_k
     gain_grads = (gain_attn, gain_query, gain_key, gain_ffn)
-    run_slots([ffn_ring], history, SLOT_DEPTH)
     attn_parts = [
-        (normalized_t, (d_query, d_pair), rows, 0),
-        (mixed_t, (d_attn,), rows, rows),
+        (normalized_t, (d_query, d_pair), rows, 0, 0),
+        (mixed_t, (d_attn,), rows, rows, 0),
+        (inner_t, (d_branch,), moved, forward_rows - 2 * cut + moved, cut - moved),
     ]
-    theirs = weight_grads(tie(other_order, history[1])[0], attn_parts, model)
-    mine = weight_grads(tie(order, theirs)[0], attn_parts, model)
-    run_slots([ffn_ring], history, SLOT_DEPTH)
+    theirs, mine = weight_grads(their_orders, attn_parts, model, (ffn_ring.value,))
     attn_ring = ScatterRing(mine, theirs)
-    attn_ring.exchange()
-    tail_mark = history[-1]
-    while ffn_ring.step < chips or attn_ring.step < chips:
-        run_slots([attn_ring, ffn_ring], history, SLOT_DEPTH)
-        if attn_ring.step == 3:
-            tail_mark = history[-1]
-
-    first_half, second_half = ffn_ring.halves()
-    grad_gate = beside(first_half, 0, 3, rows)
-    grad_up = beside(second_half, 0, 3, rows)
+    small = jnp.concatenate([*gain_grads, sum(squares), jnp.sum(keep).reshape(1, 1)], axis=1)
+    small_rounds = cycles(small)
+    got, _ = next(small_rounds)
+    waits = []
+    while ffn_ring.step < chips:
+        ffn_ring.advance(*waits)
+        attn_ring.advance()
+        waits = []
+        if ffn_ring.step % 2 == 1 and got is not None:
+            small = sum(got)
+            waits = [small]
+            try:
+                got, _ = small_rounds.send(small)
+            except StopIteration:
+                got = None
+    while got is not None:
+        small = sum(got)
+        try:
+            got, _ = small_rounds.send(small)
+        except StopIteration:
+            got = None
+
+    ffn_first, ffn_second = ffn_ring.halves()
+    attn_first, attn_second = attn_ring.halves()
+    grad_gate = beside(ffn_first, 0, 3, rows)
+    grad_up = beside(ffn_second, 0, 3, rows)
+    grad_query = beside(attn_first, 0, 2, rows)
+    grad_key, grad_value = attn_second[:rows], attn_second[rows : 2 * rows]
+    grad_out = jnp.concatenate(
+        [attn_first[2 * rows : 3 * rows], attn_second[2 * rows : 3 * rows]], axis=0
+    )
+    again = 3 * rows + max(0, 2 * cut - forward_rows)
     grad_down = jnp.concatenate(
-        [first_half[3 * rows :], second_half[3 * rows + 2 * cut - forward_rows :]], axis=0
-    )
-    first_half, second_half = attn_ring.halves()
-    grad_query = beside(first_half, 0, 2, rows)
-    grad_key, grad_value = second_half[:rows], second_half[rows : 2 * rows]
-    grad_out = jnp.concatenate([first_half[2 * rows :], second_half[2 * rows :]], axis=0)
-
-    small = jnp.concatenate(
-        [*gain_grads, sum(squares), jnp.sum(keep).reshape(1, 1)], axis=1
-    )
-    small_sum = summed(tie(small, tail_mark)[0])
+        [ffn_first[3 * rows :], attn_first[3 * rows :], attn_second[again:], ffn_second[3 * rows :]],
+        axis=0,
+    )
+    small_sum = small
     totals = small_sum[:, -2:]
     totals = jnp.where(section == 1, totals, one_way(totals, 1))[0]
     loss = totals[0] / (totals[1] * model)

time: 585 us -> 572 us (0.978)
  other arithmetic: 41.1 us -> 56.8 us
  local copies, waits for them, and re-layouts: 94.4 us -> 79.6 us
  starting transfers between devices: 67.7 us -> 57.6 us
  waiting for transfers between devices: 219 us -> 209 us
    dynamic_update_slice x32 -> x0, local copies, waits for them, and re-layouts: 55 us -> none  [put(): return lax.dynamic_update_slice(whole, piece, (owner, offset, 0))]
    unnamed x218 -> x230, local copies, waits for them, and re-layouts: 30.8 us -> 55.7 us
    ppermute x14, starting transfers between devices: 17 us -> 3.5 us  [advance(): value = lax.ppermute(self.value, 'dp', self.route).astype(jnp.float32)]
    convert_element_type x12, other arithmetic: 21.3 us -> 30.6 us  [advance(): self.value = value.astype(jnp.bfloat16) if self.step < self.chips else value]
    ppermute x7, waiting for transfers between devices: 8.67 us -> 1.01 us  [one_way(): return lax.ppermute(value, 'section', [(source, 1 - source)])]
    pallas_call x24 -> x29, Pallas kernels: 150 us -> 155 us  [the longest x18 146 us: flat_call(): pl.pallas_call(run, in_specs=specs, out_specs=[LOCAL] * len(out_shape), o...]
    ppermute x42 -> x44, starting transfers between devices: 38 us -> 38.5 us  [the longest x14 19.2 us: advance(): self.pieces.append(lax.ppermute(value, 'dp', self.route))]
    ppermute x42 -> x44, waiting for transfers between devices: 116 us -> 116 us  [the longest x14 79.9 us: advance(): self.pieces.append(lax.ppermute(value, 'dp', self.route))]
  transfers between devices with their start and end apart: 65 -> 67, of which waited for: 28 -> 27; matrix products, arithmetic and copies ran while one was open for 16% -> 13% of each run, Pallas kernels for 22% -> 21%
where the time goes in v5:
time: 572 us; the launch traced here: 565 us
  waiting for transfers between devices  209 us (37%)
  Pallas kernels  155 us (27%)
  local copies, waits for them, and re-layouts  79.6 us (14%)
  starting transfers between devices  57.6 us (10%)
  other arithmetic  56.8 us (10%)
  between operations  6.29 us (1%)
    pallas_call x18, Pallas kernels, flat_call(): pl.pallas_call(run, in_specs=specs, out_specs=[LOCAL] * len(out_shape), o...  146 us
    ppermute x14, waiting for transfers between devices, advance(): value = lax.ppermute(self.value, 'dp', self.route).astype(jnp.float32)  92 us
    ppermute x14, waiting for transfers between devices, advance(): self.pieces.append(lax.ppermute(value, 'dp', self.route))  79.9 us
    unnamed x230, local copies, waits for them, and re-layouts  55.7 us
    ppermute x12, waiting for transfers between devices, cycles(): got.append(lax.ppermute(value, 'dp', route))  35.3 us
    convert_element_type x12, other arithmetic, advance(): self.value = value.astype(jnp.bfloat16) if self.step < self.chips else value  30.6 us
    ppermute x14, starting transfers between devices, advance(): self.pieces.append(lax.ppermute(value, 'dp', self.route))  19.2 us
    ppermute x7, starting transfers between devices, one_way(): return lax.ppermute(value, 'section', [(source, 1 - source)])  15.5 us
  transfers between devices with their start and end apart: 67, of which 27 were waited for; matrix products, arithmetic and copies ran while one was open for 13% of the time, Pallas kernels for 21%

profile of v5, /device:TPU:0, one launch (start us, length us, event | category | flops | bytes accessed | tf_op | source)
XLA Modules:
  0.0 564.9 jit_solution(15804867050453145321)
XLA Ops:
  16.7 10.2 %collective-permute-done.22.refs_0_ = bf16[2,288,1024]{2,1,0:T(8,128)(2,1)S(1)} collective-permute-done((bf16[2,288,1024]{2,1,0:T(8,128)(2,1)S(1)}, bf16[2,288,1024]{2,1,0:T(8,128)(2,1)S(1)}, u32[]{:S(2)}, u32[]{:S(2)}) %collective-permute-start.22) | collective-permute-done | bytes 1179680 | tf_op jit(solution)/shard_map/ppermute | solution.py:98
  34.0 10.5 %collective-permute-done.23.refs_2_ = bf16[2,288,1024]{2,1,0:T(8,128)(2,1)} collective-permute-done((bf16[2,288,1024]{2,1,0:T(8,128)(2,1)}, bf16[2,288,1024]{2,1,0:T(8,128)(2,1)}, u32[]{:S(2)}, u32[]{:S(2)}) %collective-permute-start.23) | collective-permute-done | bytes 1179680 | tf_op jit(solution)/shard_map/ppermute | solution.py:98
  60.3 13.7 %collective-permute-done.1 = f32[1,144]{1,0:T(1,128)S(1)} collective-permute-done((f32[1,144]{1,0:T(1,128)S(1)}, f32[1,144]{1,0:T(1,128)S(1)}, u32[]{:S(2)}, u32[]{:S(2)}) %collective-permute-start.1) | collective-permute-done | bytes 608 | tf_op jit(solution)/shard_map/ppermute | solution.py:60
  84.6 14.8 %collective-permute-done.5 = f32[4,144]{1,0:T(4,128)S(1)} collective-permute-done((f32[4,144]{1,0:T(4,128)}, f32[4,144]{1,0:T(4,128)S(1)}, u32[]{:S(2)}, u32[]{:S(2)}) %collective-permute-start.5) | collective-permute-done | bytes 2336 | tf_op jit(solution)/shard_map/ppermute | solution.py:60
  108.4 8.0 %collective-permute-done.10.refs_0_ = bf16[2,192,1024]{2,1,0:T(8,128)(2,1)} collective-permute-done((bf16[2,192,1024]{2,1,0:T(8,128)(2,1)}, bf16[2,192,1024]{2,1,0:T(8,128)(2,1)}, u32[]{:S(2)}, u32[]{:S(2)}) %collective-permute-start.10) | collective-permute-done | bytes 786464 | tf_op jit(solution)/shard_map/ppermute | solution.py:98
  117.1 20.3 %collective-permute-done.11.refs_5_ = bf16[2,192,1024]{2,1,0:T(8,128)(2,1)S(1)} collective-permute-done((bf16[2,192,1024]{2,1,0:T(8,128)(2,1)}, bf16[2,192,1024]{2,1,0:T(8,128)(2,1)S(1)}, u32[]{:S(2)}, u32[]{:S(2)}) %collective-permute-start.11) | collective-permute-done | bytes 786464 | tf_op jit(solution)/shard_map/ppermute | solution.py:98
  141.2 8.2 %collective-permute-done.12.refs_6_ = bf16[2,192,1024]{2,1,0:T(8,128)(2,1)S(1)} collective-permute-done((bf16[2,192,1024]{2,1,0:T(8,128)(2,1)S(1)}, bf16[2,192,1024]{2,1,0:T(8,128)(2,1)S(1)}, u32[]{:S(2)}, u32[]{:S(2)}) %collective-permute-start.12) | collective-permute-done | bytes 786464 | tf_op jit(solution)/shard_map/ppermute | solution.py:98
  150.5 11.6 %collective-permute-done.27.refs_6_ = bf16[2,288,1024]{2,1,0:T(8,128)(2,1)} collective-permute-done((bf16[2,288,1024]{2,1,0:T(8,128)(2,1)}, bf16[2,288,1024]{2,1,0:T(8,128)(2,1)}, u32[]{:S(2)}, u32[]{:S(2)}) %collective-permute-start.27) | collective-permute-done | bytes 1179680 | tf_op jit(solution)/shard_map/ppermute | solution.py:98
  176.1 7.1 %collective-permute-done.28.refs_7_ = bf16[2,288,1024]{2,1,0:T(8,128)(2,1)} collective-permute-done((bf16[2,288,1024]{2,1,0:T(8,128)(2,1)}, bf16[2,288,1024]{2,1,0:T(8,128)(2,1)}, u32[]{:S(2)}, u32[]{:S(2)}) %collective-permute-start.28) | collective-permute-done | bytes 1179680 | tf_op jit(solution)/shard_map/ppermute | solution.py:98
  201.3 5.9 %shard_map.254.refs_3_.refs_7_ = bf16[16,576,1024]{2,1,0:T(8,128)(2,1)S(1)} custom-call(s32[18]{0:T(128)S(1)} %copy-done.56, bf16[2,288,1024]{2,1,0:T(8,128)(2,1)S(1)} %maximum_select_fusion.refs_0_, bf16[2,288,1024]{2,1,0:T(8,128)(2,1)S(1)} %copy-done.8, bf16[2,288,1024]{2,1,0:T(8,128)(2,1)} %collective-permute-done.23.refs_2_, ...), custom_call_target="tpu_custom_call" | custom-call | bytes 37748736 | tf_op jit(solution)/shard_map/pallas_call | solution.py:631
  233.1 6.0 %shard_map.256 = (f32[256,1024]{1,0:T(8,128)S(1)}, bf16[256,1024]{1,0:T(8,128)(2,1)S(1)}, bf16[1024,256]{1,0:T(8,128)(2,1)S(1)}, bf16[1024,256]{1,0:T(8,128)(2,1...) custom-call(s32[1]{0:T(128)} %bitcast.refs_0_, ...), custom_call_target="tpu_custom_call" | custom-call | flops 4294967296 | bytes 17825792 | tf_op jit(solution)/shard_map/pallas_call | solution.py:184
  239.1 5.9 %shard_map.257 = (bf16[256,1024]{1,0:T(8,128)(2,1)S(1)}, bf16[256,3072]{1,0:T(8,128)(2,1)S(1)}, bf16[256,3072]{1,0:T(8,128)(2,1)S(1)}, bf16[3072,256]{1,0:T(8,12...) custom-call(s32[1]{0:T(128)} %bitcast.refs_0_, bf16[256,1024]{1,0:T(8,128)(2,1)S(1)} %get-tuple-element.82.refs_1_, ...), custom_call_target="tpu_custom_call" | custom-call | flops 4831838208 | bytes 20971520 | tf_op jit(solution)/shard_map/pallas_call | solution.py:184
  246.2 8.1 %shard_map.262 = (f32[256,1024]{1,0:T(8,128)S(1)}, bf16[256,1024]{1,0:T(8,128)(2,1)S(1)}, bf16[256,3072]{1,0:T(8,128)(2,1)}, bf16[256,3072]{1,0:T(8,128)(2,1)}, ...) custom-call(s32[1]{0:T(128)} %constant.155.clone.1.refs_0_, f32[256,1024]{1,0:T(8,128)S(1)} %get-tuple-element.90.refs_1_, ...), custom_call_target="tpu_custom_call" | custom-call | flops 4831838208 | bytes 28835840 | tf_op jit(solution)/shard_map/pallas_call | solution.py:184
  254.4 13.1 %shard_map.263 = (bf16[256,2048]{1,0:T(8,128)(2,1)}, bf16[256,2048]{1,0:T(8,128)(2,1)}, bf16[256,1024]{1,0:T(8,128)(2,1)}, f32[1,1024]{1,0:T(1,128)}, f32[1,128]{1,0:T(1,128)}, /*index=5*/f32[1,128]{1,0:T(1,128)}) custom-call(s32[1]{0:T(128)} %bitcast.refs_0_, bf16[256,1024]{1,0:T(8,128)(2,1)S(1)} %get-tuple-element.93.refs_1_, ...), custom_call_target="tpu_custom_call" | custom-call | flops 5905580032 | bytes 23068672 | tf_op jit(solution)/shard_map/pallas_call | solution.py:184
  273.3 5.9 %shard_map.260 = (f32[256,1024]{1,0:T(8,128)S(1)}, bf16[256,1024]{1,0:T(8,128)(2,1)S(1)}, bf16[1024,256]{1,0:T(8,128)(2,1)S(1)}, bf16[1024,256]{1,0:T(8,128)(2,1...) custom-call(s32[1]{0:T(128)} %bitcast.refs_0_, ...), custom_call_target="tpu_custom_call" | custom-call | flops 4294967296 | bytes 17825792 | tf_op jit(solution)/shard_map/pallas_call | solution.py:184
  287.9 8.1 %shard_map.266 = (f32[256,1024]{1,0:T(8,128)S(1)}, bf16[256,1024]{1,0:T(8,128)(2,1)S(1)}, bf16[256,3072]{1,0:T(8,128)(2,1)}, bf16[256,3072]{1,0:T(8,128)(2,1)}, ...) custom-call(s32[1]{0:T(128)} %constant.155.clone.1.refs_0_, f32[256,1024]{1,0:T(8,128)S(1)} %get-tuple-element.102.refs_1_, ...), custom_call_target="tpu_custom_call" | custom-call | flops 4831838208 | bytes 28835840 | tf_op jit(solution)/shard_map/pallas_call | solution.py:184
  296.0 13.1 %shard_map.267 = (bf16[256,2048]{1,0:T(8,128)(2,1)}, bf16[256,2048]{1,0:T(8,128)(2,1)}, bf16[256,1024]{1,0:T(8,128)(2,1)}, f32[1,1024]{1,0:T(1,128)}, f32[1,128]{1,0:T(1,128)}, /*index=5*/f32[1,128]{1,0:T(1,128)}) custom-call(s32[1]{0:T(128)} %bitcast.refs_0_, bf16[256,1024]{1,0:T(8,128)(2,1)S(1)} %get-tuple-element.105.refs_1_, ...), custom_call_target="tpu_custom_call" | custom-call | flops 5905580032 | bytes 23068672 | tf_op jit(solution)/shard_map/pallas_call | solution.py:184
  310.6 6.1 %shard_map.264 = (f32[256,1024]{1,0:T(8,128)S(1)}, bf16[256,1024]{1,0:T(8,128)(2,1)S(1)}, bf16[256,3072]{1,0:T(8,128)(2,1)S(1)}, bf16[256,3072]{1,0:T(8,128)(2,1...) custom-call(s32[1]{0:T(128)} %bitcast.refs_0_, f32[256,1024]{1,0:T(8,128)S(1)} %get-tuple-element.90.refs_1_, ...), custom_call_target="tpu_custom_call" | custom-call | flops 4831838208 | bytes 28835840 | tf_op jit(solution)/shard_map/pallas_call | solution.py:184
  323.5 12.6 %shard_map.265 = (bf16[256,2048]{1,0:T(8,128)(2,1)S(1)}, bf16[256,2048]{1,0:T(8,128)(2,1)S(1)}, bf16[256,1024]{1,0:T(8,128)(2,1)S(1)}, f32[1,1024]{1,0:T(1,128)S...) custom-call(s32[1]{0:T(128)} %bitcast.refs_0_, bf16[256,1024]{1,0:T(8,128)(2,1)S(1)} %get-tuple-element.99.refs_1_.refs_9_, ...), custom_call_target="tpu_custom_call" | custom-call | flops 5905580032 | bytes 23068672 | tf_op jit(solution)/shard_map/pallas_call | solution.py:184
  338.1 6.2 %shard_map.268 = (f32[256,1024]{1,0:T(8,128)S(1)}, bf16[256,1024]{1,0:T(8,128)(2,1)S(1)}, bf16[256,3072]{1,0:T(8,128)(2,1)S(1)}, bf16[256,3072]{1,0:T(8,128)(2,1...) custom-call(s32[1]{0:T(128)} %bitcast.refs_0_, f32[256,1024]{1,0:T(8,128)S(1)} %get-tuple-element.102.refs_1_, ...), custom_call_target="tpu_custom_call" | custom-call | flops 4831838208 | bytes 28835840 | tf_op jit(solution)/shard_map/pallas_call | solution.py:184
  350.0 9.1 %shard_map.269 = (bf16[8,2,240,1024]{3,2,1,0:T(8,128)(2,1)S(1)}, bf16[8,2,240,1024]{3,2,1,0:T(8,128)(2,1)S(1)}) custom-call(s32[18]{0:T(128)S(1)} %get-tuple-element.198.refs_0_, bf16[1024,256]{1,0:T(8,128)(2,1)S(1)} %copy-done.87, bf16[1024,256]{1,0:T(8,128)(2,1)S(1)} %copy-done.93, bf16[256,3072]{1,0:T(8,128)(2,1)S(1)} %copy-done.67, ...), custom_call_target="tpu_custom_call" | custom-call | flops 8053063680 | bytes 19922944 | tf_op jit(solution)/shard_map/pallas_call | solution.py:184
  359.5 12.5 %shard_map.270 = (bf16[256,2048]{1,0:T(8,128)(2,1)S(1)}, bf16[256,2048]{1,0:T(8,128)(2,1)S(1)}, bf16[256,1024]{1,0:T(8,128)(2,1)S(1)}, f32[1,1024]{1,0:T(1,128)S...) custom-call(s32[1]{0:T(128)} %bitcast.refs_0_, bf16[256,1024]{1,0:T(8,128)(2,1)S(1)} %get-tuple-element.111.refs_1_.refs_10_, ...), custom_call_target="tpu_custom_call" | custom-call | flops 5905580032 | bytes 23068672 | tf_op jit(solution)/shard_map/pallas_call | solution.py:184
  375.4 11.7 %shard_map.271 = (bf16[8,2,240,1024]{3,2,1,0:T(8,128)(2,1)}, bf16[8,2,240,1024]{3,2,1,0:T(8,128)(2,1)S(1)}) custom-call(s32[18]{0:T(128)S(1)} %get-tuple-element.198.refs_0_, bf16[1024,256]{1,0:T(8,128)(2,1)S(1)} %copy-done.85, bf16[1024,256]{1,0:T(8,128)(2,1)S(1)} %copy-done.89, bf16[256,2048]{1,0:T(8,128)(2,1)S(1)} %copy-done.95, ...), custom_call_target="tpu_custom_call" | custom-call | flops 8053063680 | bytes 19922944 | tf_op jit(solution)/shard_map/pallas_call | solution.py:184
  390.5 14.1 %collective-permute-done.59 = bf16[2,240,1024]{2,1,0:T(8,128)(2,1)S(1)} collective-permute-done((bf16[2,240,1024]{2,1,0:T(8,128)(2,1)S(1)}, bf16[2,240,1024]{2,1,0:T(8,128)(2,1)S(1)}, u32[]{:S(2)}, u32[]{:S(2)}) %collective-permute-start.59) | collective-permute-done | bytes 983072 | tf_op jit(solution)/shard_map/ppermute | solution.py:126
  426.0 6.7 %collective-permute-done.51 = bf16[2,240,1024]{2,1,0:T(8,128)(2,1)} collective-permute-done((bf16[2,240,1024]{2,1,0:T(8,128)(2,1)S(1)}, bf16[2,240,1024]{2,1,0:T(8,128)(2,1)}, u32[]{:S(2)}, u32[]{:S(2)}) %collective-permute-start.51) | collective-permute-done | bytes 983072 | tf_op jit(solution)/shard_map/ppermute | solution.py:126
  445.3 8.4 %collective-permute-done.52 = bf16[2,240,1024]{2,1,0:T(8,128)(2,1)S(1)} collective-permute-done((bf16[2,240,1024]{2,1,0:T(8,128)(2,1)S(1)}, bf16[2,240,1024]{2,1,0:T(8,128)(2,1)S(1)}, u32[]{:S(2)}, u32[]{:S(2)}) %collective-permute-start.52) | collective-permute-done | bytes 983072 | tf_op jit(solution)/shard_map/ppermute | solution.py:126
  456.5 7.7 %collective-permute-done.62 = bf16[2,240,1024]{2,1,0:T(8,128)(2,1)S(1)} collective-permute-done((bf16[2,240,1024]{2,1,0:T(8,128)(2,1)S(1)}, bf16[2,240,1024]{2,1,0:T(8,128)(2,1)S(1)}, u32[]{:S(2)}, u32[]{:S(2)}) %collective-permute-start.62) | collective-permute-done | bytes 983072 | tf_op jit(solution)/shard_map/ppermute | solution.py:126
  467.5 7.3 %collective-permute-done.53 = bf16[2,240,1024]{2,1,0:T(8,128)(2,1)} collective-permute-done((bf16[2,240,1024]{2,1,0:T(8,128)(2,1)S(1)}, bf16[2,240,1024]{2,1,0:T(8,128)(2,1)}, u32[]{:S(2)}, u32[]{:S(2)}) %collective-permute-start.53) | collective-permute-done | bytes 983072 | tf_op jit(solution)/shard_map/ppermute | solution.py:126
  477.5 7.8 %collective-permute-done.63 = bf16[2,240,1024]{2,1,0:T(8,128)(2,1)S(1)} collective-permute-done((bf16[2,240,1024]{2,1,0:T(8,128)(2,1)}, bf16[2,240,1024]{2,1,0:T(8,128)(2,1)S(1)}, u32[]{:S(2)}, u32[]{:S(2)}) %collective-permute-start.63) | collective-permute-done | bytes 983072 | tf_op jit(solution)/shard_map/ppermute | solution.py:126
  487.6 8.2 %collective-permute-done.54 = bf16[2,240,1024]{2,1,0:T(8,128)(2,1)S(1)} collective-permute-done((bf16[2,240,1024]{2,1,0:T(8,128)(2,1)S(1)}, bf16[2,240,1024]{2,1,0:T(8,128)(2,1)S(1)}, u32[]{:S(2)}, u32[]{:S(2)}) %collective-permute-start.54) | collective-permute-done | bytes 983072 | tf_op jit(solution)/shard_map/ppermute | solution.py:126
  498.2 8.2 %collective-permute-done.64 = bf16[2,240,1024]{2,1,0:T(8,128)(2,1)S(1)} collective-permute-done((bf16[2,240,1024]{2,1,0:T(8,128)(2,1)S(1)}, bf16[2,240,1024]{2,1,0:T(8,128)(2,1)S(1)}, u32[]{:S(2)}, u32[]{:S(2)}) %collective-permute-start.64) | collective-permute-done | bytes 983072 | tf_op jit(solution)/shard_map/ppermute | solution.py:126
  545.8 9.0 %collective-permute-done.57 = bf16[2,240,1024]{2,1,0:T(8,128)(2,1)S(1)} collective-permute-done((bf16[2,240,1024]{2,1,0:T(8,128)(2,1)S(1)}, bf16[2,240,1024]{2,1,0:T(8,128)(2,1)S(1)}, u32[]{:S(2)}, u32[]{:S(2)}) %collective-permute-start.57) | collective-permute-done | bytes 983072 | tf_op jit(solution)/shard_map/ppermute | solution.py:126
  (450 shorter events, 252.5 us)
Async XLA Ops:
  31.4 22.6 %collective-permute-start.7 = (bf16[2,192,1024]{2,1,0:T(8,128)(2,1)S(1)}, bf16[2,192,1024]{2,1,0:T(8,128)(2,1)S(1)}, u32[]{:S(2)}, u32[]{:S(2)}) collective-permute-start(bf16[2,192,1024]{2,1,0:T(8,128)(2,1)S(1)} %maximum_select_fusion.2.refs_0_), channel_id=1, source_target_pairs={{0,4},{5,1},{4,8},{9,5},{8,12},{13,9},{12,14},{15,13},{14,10},{11,... | collective-permute-start | bytes 2359304 | tf_op jit(solution)/shard_map/ppermute | solution.py:98
  44.5 32.4 %collective-permute-start.24 = (bf16[2,288,1024]{2,1,0:T(8,128)(2,1)}, bf16[2,288,1024]{2,1,0:T(8,128)(2,1)}, u32[]{:S(2)}, u32[]{:S(2)}) collective-permute-start(bf16[2,288,1024]{2,1,0:T(8,128)(2,1)} %collective-permute-done.23.refs_2_), channel_id=1, source_target_pairs={{0,4},{5,1},{4,8},{9,5},{8,12},{13,9},{12,14},{15,13},{14,10},{11,... | collective-permute-start | bytes 3538952 | tf_op jit(solution)/shard_map/ppermute | solution.py:98
  54.9 19.7 %collective-permute-start.8 = (bf16[2,192,1024]{2,1,0:T(8,128)(2,1)}, bf16[2,192,1024]{2,1,0:T(8,128)(2,1)S(1)}, u32[]{:S(2)}, u32[]{:S(2)}) collective-permute-start(bf16[2,192,1024]{2,1,0:T(8,128)(2,1)} %shard_map.246.refs_1_), channel_id=1, source_target_pairs={{0,4},{5,1},{4,8},{9,5},{8,12},{13,9},{12,14},{15,13},{14,10},{11,... | collective-permute-start | bytes 2359304 | tf_op jit(solution)/shard_map/ppermute | solution.py:98
  75.5 26.0 %collective-permute-start.9 = (bf16[2,192,1024]{2,1,0:T(8,128)(2,1)}, bf16[2,192,1024]{2,1,0:T(8,128)(2,1)}, u32[]{:S(2)}, u32[]{:S(2)}) collective-permute-start(bf16[2,192,1024]{2,1,0:T(8,128)(2,1)} %shard_map.247.refs_2_), channel_id=1, source_target_pairs={{0,4},{5,1},{4,8},{9,5},{8,12},{13,9},{12,14},{15,13},{14,10},{11,... | collective-permute-start | bytes 2359304 | tf_op jit(solution)/shard_map/ppermute | solution.py:98
  76.9 27.1 %collective-permute-start.25 = (bf16[2,288,1024]{2,1,0:T(8,128)(2,1)}, bf16[2,288,1024]{2,1,0:T(8,128)(2,1)}, u32[]{:S(2)}, u32[]{:S(2)}) collective-permute-start(bf16[2,288,1024]{2,1,0:T(8,128)(2,1)} %collective-permute-done.24.refs_3_), channel_id=1, source_target_pairs={{0,4},{5,1},{4,8},{9,5},{8,12},{13,9},{12,14},{15,13},{14,10},{11,... | collective-permute-start | bytes 3538952 | tf_op jit(solution)/shard_map/ppermute | solution.py:98
  78.4 21.0 %collective-permute-start.5 = (f32[4,144]{1,0:T(4,128)}, f32[4,144]{1,0:T(4,128)S(1)}, u32[]{:S(2)}, u32[]{:S(2)}) collective-permute-start(f32[4,144]{1,0:T(4,128)} %constant_dynamic-slice_fusion.14.refs_1_), channel_id=1, source_target_pairs={{0,4},{1,5},{2,6},{3,7},{4,8},{5,9},{6,10},{7,11},{8,12},{9,13},{1... | collective-permute-start | bytes 6920 | tf_op jit(solution)/shard_map/ppermute | solution.py:60
  80.0 19.4 %collective-permute-start.4 = (f32[4,144]{1,0:T(4,128)}, f32[4,144]{1,0:T(4,128)S(1)}, u32[]{:S(2)}, u32[]{:S(2)}) collective-permute-start(f32[4,144]{1,0:T(4,128)} %constant_dynamic-slice_fusion.14.refs_1_), channel_id=1, source_target_pairs={{0,8},{1,9},{2,10},{3,11},{4,12},{5,13},{6,14},{7,15},{8,0},{9,1},... | collective-permute-start | bytes 6920 | tf_op jit(solution)/shard_map/ppermute | solution.py:60
  104.0 33.4 %collective-permute-start.26 = (bf16[2,288,1024]{2,1,0:T(8,128)(2,1)}, bf16[2,288,1024]{2,1,0:T(8,128)(2,1)}, u32[]{:S(2)}, u32[]{:S(2)}) collective-permute-start(bf16[2,288,1024]{2,1,0:T(8,128)(2,1)} %collective-permute-done.25.refs_4_), channel_id=1, source_target_pairs={{0,4},{5,1},{4,8},{9,5},{8,12},{13,9},{12,14},{15,13},{14,10},{11,... | collective-permute-start | bytes 3538952 | tf_op jit(solution)/shard_map/ppermute | solution.py:98
  116.4 21.0 %collective-permute-start.11 = (bf16[2,192,1024]{2,1,0:T(8,128)(2,1)}, bf16[2,192,1024]{2,1,0:T(8,128)(2,1)S(1)}, u32[]{:S(2)}, u32[]{:S(2)}) collective-permute-start(bf16[2,192,1024]{2,1,0:T(8,128)(2,1)} %shard_map.249.refs_4_), channel_id=1, source_target_pairs={{0,4},{5,1},{4,8},{9,5},{8,12},{13,9},{12,14},{15,13},{14,10},{11,... | collective-permute-start | bytes 2359304 | tf_op jit(solution)/shard_map/ppermute | solution.py:98
  116.4 32.9 %collective-permute-start.29 = (bf16[2,288,1024]{2,1,0:T(8,128)(2,1)S(1)}, bf16[2,288,1024]{2,1,0:T(8,128)(2,1)S(1)}, u32[]{:S(2)}, u32[]{:S(2)}) collective-permute-start(bf16[2,288,1024]{2,1,0:T(8,128)(2,1)S(1)} %copy-done.8), channel_id=1, source_target_pairs={{0,1},{1,0},{2,3},{3,2},{4,5},{5,4},{6,7},{7,6},{8,9},{9,8},{10,11... | collective-permute-start | bytes 3538952 | tf_op jit(solution)/shard_map/ppermute | solution.py:107
  116.5 22.4 %collective-permute-start.14 = (bf16[2,192,1024]{2,1,0:T(8,128)(2,1)}, bf16[2,192,1024]{2,1,0:T(8,128)(2,1)S(1)}, u32[]{:S(2)}, u32[]{:S(2)}) collective-permute-start(bf16[2,192,1024]{2,1,0:T(8,128)(2,1)} %shard_map.246.refs_1_), channel_id=1, source_target_pairs={{0,1},{1,0},{2,3},{3,2},{4,5},{5,4},{6,7},{7,6},{8,9},{9,8},{10,11... | collective-permute-start | bytes 2359304 | tf_op jit(solution)/shard_map/ppermute | solution.py:107
  117.0 22.8 %collective-permute-start.15 = (bf16[2,192,1024]{2,1,0:T(8,128)(2,1)}, bf16[2,192,1024]{2,1,0:T(8,128)(2,1)S(1)}, u32[]{:S(2)}, u32[]{:S(2)}) collective-permute-start(bf16[2,192,1024]{2,1,0:T(8,128)(2,1)} %shard_map.247.refs_2_), channel_id=1, source_target_pairs={{0,1},{1,0},{2,3},{3,2},{4,5},{5,4},{6,7},{7,6},{8,9},{9,8},{10,11... | collective-permute-start | bytes 2359304 | tf_op jit(solution)/shard_map/ppermute | solution.py:107
  137.4 24.7 %collective-permute-start.27 = (bf16[2,288,1024]{2,1,0:T(8,128)(2,1)}, bf16[2,288,1024]{2,1,0:T(8,128)(2,1)}, u32[]{:S(2)}, u32[]{:S(2)}) collective-permute-start(bf16[2,288,1024]{2,1,0:T(8,128)(2,1)} %collective-permute-done.26.refs_5_), channel_id=1, source_target_pairs={{0,4},{5,1},{4,8},{9,5},{8,12},{13,9},{12,14},{15,13},{14,10},{11,... | collective-permute-start | bytes 3538952 | tf_op jit(solution)/shard_map/ppermute | solution.py:98
  139.8 22.5 %collective-permute-start.16 = (bf16[2,192,1024]{2,1,0:T(8,128)(2,1)}, bf16[2,192,1024]{2,1,0:T(8,128)(2,1)S(1)}, u32[]{:S(2)}, u32[]{:S(2)}) collective-permute-start(bf16[2,192,1024]{2,1,0:T(8,128)(2,1)} %shard_map.248.refs_3_), channel_id=1, source_target_pairs={{0,1},{1,0},{2,3},{3,2},{4,5},{5,4},{6,7},{7,6},{8,9},{9,8},{10,11... | collective-permute-start | bytes 2359304 | tf_op jit(solution)/shard_map/ppermute | solution.py:107
  140.7 23.5 %collective-permute-start.17 = (bf16[2,192,1024]{2,1,0:T(8,128)(2,1)}, bf16[2,192,1024]{2,1,0:T(8,128)(2,1)S(1)}, u32[]{:S(2)}, u32[]{:S(2)}) collective-permute-start(bf16[2,192,1024]{2,1,0:T(8,128)(2,1)} %shard_map.249.refs_4_), channel_id=1, source_target_pairs={{0,1},{1,0},{2,3},{3,2},{4,5},{5,4},{6,7},{7,6},{8,9},{9,8},{10,11... | collective-permute-start | bytes 2359304 | tf_op jit(solution)/shard_map/ppermute | solution.py:107
  149.4 21.1 %collective-permute-start.13 = (bf16[2,192,1024]{2,1,0:T(8,128)(2,1)S(1)}, bf16[2,192,1024]{2,1,0:T(8,128)(2,1)S(1)}, u32[]{:S(2)}, u32[]{:S(2)}) collective-permute-start(bf16[2,192,1024]{2,1,0:T(8,128)(2,1)S(1)} %collective-permute-done.12.refs_6_), channel_id=1, source_target_pairs={{0,4},{5,1},{4,8},{9,5},{8,12},{13,9},{12,14},{15,13},{14,10},{11,... | collective-permute-start | bytes 2359304 | tf_op jit(solution)/shard_map/ppermute | solution.py:98
  150.5 20.9 %collective-permute-start.30 = (bf16[2,288,1024]{2,1,0:T(8,128)(2,1)}, bf16[2,288,1024]{2,1,0:T(8,128)(2,1)S(1)}, u32[]{:S(2)}, u32[]{:S(2)}) collective-permute-start(bf16[2,288,1024]{2,1,0:T(8,128)(2,1)} %collective-permute-done.23.refs_2_), channel_id=1, source_target_pairs={{0,1},{1,0},{2,3},{3,2},{4,5},{5,4},{6,7},{7,6},{8,9},{9,8},{10,11... | collective-permute-start | bytes 3538952 | tf_op jit(solution)/shard_map/ppermute | solution.py:107
  162.1 21.1 %collective-permute-start.28 = (bf16[2,288,1024]{2,1,0:T(8,128)(2,1)}, bf16[2,288,1024]{2,1,0:T(8,128)(2,1)}, u32[]{:S(2)}, u32[]{:S(2)}) collective-permute-start(bf16[2,288,1024]{2,1,0:T(8,128)(2,1)} %collective-permute-done.27.refs_6_), channel_id=1, source_target_pairs={{0,4},{5,1},{4,8},{9,5},{8,12},{13,9},{12,14},{15,13},{14,10},{11,... | collective-permute-start | bytes 3538952 | tf_op jit(solution)/shard_map/ppermute | solution.py:98
  172.3 28.8 %collective-permute-start.31 = (bf16[2,288,1024]{2,1,0:T(8,128)(2,1)}, bf16[2,288,1024]{2,1,0:T(8,128)(2,1)}, u32[]{:S(2)}, u32[]{:S(2)}) collective-permute-start(bf16[2,288,1024]{2,1,0:T(8,128)(2,1)} %collective-permute-done.24.refs_3_), channel_id=1, source_target_pairs={{0,1},{1,0},{2,3},{3,2},{4,5},{5,4},{6,7},{7,6},{8,9},{9,8},{10,11... | collective-permute-start | bytes 3538952 | tf_op jit(solution)/shard_map/ppermute | solution.py:107
  173.8 27.4 %collective-permute-start.32 = (bf16[2,288,1024]{2,1,0:T(8,128)(2,1)}, bf16[2,288,1024]{2,1,0:T(8,128)(2,1)}, u32[]{:S(2)}, u32[]{:S(2)}) collective-permute-start(bf16[2,288,1024]{2,1,0:T(8,128)(2,1)} %collective-permute-done.25.refs_4_), channel_id=1, source_target_pairs={{0,1},{1,0},{2,3},{3,2},{4,5},{5,4},{6,7},{7,6},{8,9},{9,8},{10,11... | collective-permute-start | bytes 3538952 | tf_op jit(solution)/shard_map/ppermute | solution.py:107
  174.7 26.5 %collective-permute-start.33 = (bf16[2,288,1024]{2,1,0:T(8,128)(2,1)}, bf16[2,288,1024]{2,1,0:T(8,128)(2,1)}, u32[]{:S(2)}, u32[]{:S(2)}) collective-permute-start(bf16[2,288,1024]{2,1,0:T(8,128)(2,1)} %collective-permute-done.26.refs_5_), channel_id=1, source_target_pairs={{0,1},{1,0},{2,3},{3,2},{4,5},{5,4},{6,7},{7,6},{8,9},{9,8},{10,11... | collective-permute-start | bytes 3538952 | tf_op jit(solution)/shard_map/ppermute | solution.py:107
  176.1 25.1 %collective-permute-start.34 = (bf16[2,288,1024]{2,1,0:T(8,128)(2,1)}, bf16[2,288,1024]{2,1,0:T(8,128)(2,1)}, u32[]{:S(2)}, u32[]{:S(2)}) collective-permute-start(bf16[2,288,1024]{2,1,0:T(8,128)(2,1)} %collective-permute-done.27.refs_6_), channel_id=1, source_target_pairs={{0,1},{1,0},{2,3},{3,2},{4,5},{5,4},{6,7},{7,6},{8,9},{9,8},{10,11... | collective-permute-start | bytes 3538952 | tf_op jit(solution)/shard_map/ppermute | solution.py:107
  212.3 20.8 %collective-permute-start.36 = (bf16[256,1024]{1,0:T(8,128)(2,1)S(1)}, bf16[256,1024]{1,0:T(8,128)(2,1)S(1)}, u32[]{:S(2)}, u32[]{:S(2)}) collective-permute-start(bf16[256,1024]{1,0:T(8,128)(2,1)S(1)} %shard_map.255), channel_id=1, source_target_pairs={{0,16},{1,17},{2,18},{3,19},{4,20},{5,21},{6,22},{7,23},{8,24},{9,... | collective-permute-start | bytes 1572872 | tf_op jit(solution)/shard_map/ppermute | solution.py:26
  231.4 37.3 %collective-permute-start.38 = (bf16[256,1024]{1,0:T(8,128)(2,1)S(1)}, bf16[256,1024]{1,0:T(8,128)(2,1)S(1)}, u32[]{:S(2)}, u32[]{:S(2)}) collective-permute-start(bf16[256,1024]{1,0:T(8,128)(2,1)S(1)} %shard_map.259), channel_id=1, source_target_pairs={{0,16},{1,17},{2,18},{3,19},{4,20},{5,21},{6,22},{7,23},{8,24},{9,... | collective-permute-start | bytes 1572872 | tf_op jit(solution)/shard_map/ppermute | solution.py:26
  267.5 43.1 %collective-permute-start.39 = (bf16[256,1024]{1,0:T(8,128)(2,1)}, bf16[256,1024]{1,0:T(8,128)(2,1)S(1)}, u32[]{:S(2)}, u32[]{:S(2)}) collective-permute-start(bf16[256,1024]{1,0:T(8,128)(2,1)} %get-tuple-element.98), channel_id=1, source_target_pairs={{16,0},{17,1},{18,2},{19,3},{20,4},{21,5},{22,6},{23,7},{24,8},{25... | collective-permute-start | bytes 1572872 | tf_op jit(solution)/shard_map/ppermute | solution.py:26
  309.2 28.9 %collective-permute-start.40 = (bf16[256,1024]{1,0:T(8,128)(2,1)}, bf16[256,1024]{1,0:T(8,128)(2,1)S(1)}, u32[]{:S(2)}, u32[]{:S(2)}) collective-permute-start(bf16[256,1024]{1,0:T(8,128)(2,1)} %get-tuple-element.110), channel_id=1, source_target_pairs={{16,0},{17,1},{18,2},{19,3},{20,4},{21,5},{22,6},{23,7},{24,8},{25... | collective-permute-start | bytes 1572872 | tf_op jit(solution)/shard_map/ppermute | solution.py:26
  390.2 22.8 %collective-permute-start.50 = (bf16[8,2,240,1024]{3,2,1,0:T(8,128)(2,1)}, bf16[8,2,240,1024]{3,2,1,0:T(8,128)(2,1)}, u32[]{:S(2)}, u32[]{:S(2)}) collective-permute-start(bf16[8,2,240,1024]{3,2,1,0:T(8,128)(2,1)} %get-tuple-element.145), channel_id=1, source_target_pairs={{0,1},{1,0},{2,3},{3,2},{4,5},{5,4},{6,7},{7,6},{8,9},{9,8},{10,11... | collective-permute-start | bytes 23592968 | tf_op jit(solution)/shard_map/ppermute | solution.py:116
  435.2 20.7 %collective-permute-start.46 = (f32[1,2306]{1,0:T(1,128)S(1)}, f32[1,2306]{1,0:T(1,128)S(1)}, u32[]{:S(2)}, u32[]{:S(2)}) collective-permute-start(f32[1,2306]{1,0:T(1,128)S(1)} %copy-done.100), channel_id=1, source_target_pairs={{0,12},{1,13},{2,14},{3,15},{4,0},{5,1},{6,2},{7,3},{8,4},{9,5},{1... | collective-permute-start | bytes 27680 | tf_op jit(solution)/shard_map/ppermute | solution.py:60
  455.8 19.1 %collective-permute-start.53 = (bf16[2,240,1024]{2,1,0:T(8,128)(2,1)S(1)}, bf16[2,240,1024]{2,1,0:T(8,128)(2,1)}, u32[]{:S(2)}, u32[]{:S(2)}) collective-permute-start(bf16[2,240,1024]{2,1,0:T(8,128)(2,1)S(1)} %fusion.10), channel_id=1, source_target_pairs={{0,4},{5,1},{4,8},{9,5},{8,12},{13,9},{12,14},{15,13},{14,10},{11,... | collective-permute-start | bytes 2949128 | tf_op jit(solution)/shard_map/ppermute | solution.py:126
  487.4 19.0 %collective-permute-start.64 = (bf16[2,240,1024]{2,1,0:T(8,128)(2,1)S(1)}, bf16[2,240,1024]{2,1,0:T(8,128)(2,1)S(1)}, u32[]{:S(2)}, u32[]{:S(2)}) collective-permute-start(bf16[2,240,1024]{2,1,0:T(8,128)(2,1)S(1)} %fusion.1), channel_id=1, source_target_pairs={{0,4},{5,1},{4,8},{9,5},{8,12},{13,9},{12,14},{15,13},{14,10},{11,... | collective-permute-start | bytes 2949128 | tf_op jit(solution)/shard_map/ppermute | solution.py:126
  509.4 21.5 %collective-permute-start.65 = (bf16[2,240,1024]{2,1,0:T(8,128)(2,1)}, bf16[2,240,1024]{2,1,0:T(8,128)(2,1)S(1)}, u32[]{:S(2)}, u32[]{:S(2)}) collective-permute-start(bf16[2,240,1024]{2,1,0:T(8,128)(2,1)} %fusion), channel_id=1, source_target_pairs={{0,4},{5,1},{4,8},{9,5},{8,12},{13,9},{12,14},{15,13},{14,10},{11,... | collective-permute-start | bytes 2949128 | tf_op jit(solution)/shard_map/ppermute | solution.py:126
  520.1 24.5 %collective-permute-start.48 = (bf16[1,256,1024]{2,1,0:T(8,128)(2,1)S(1)}, bf16[1,256,1024]{2,1,0:T(8,128)(2,1)S(1)}, u32[]{:S(2)}, u32[]{:S(2)}) collective-permute-start(bf16[1,256,1024]{2,1,0:T(8,128)(2,1)S(1)} %bitcast.194), channel_id=1, source_target_pairs={{0,16},{1,17},{2,18},{3,19},{4,20},{5,21},{6,22},{7,23},{8,24},{9,... | collective-permute-start | bytes 1572872 | tf_op jit(solution)/shard_map/ppermute | solution.py:26
  (150 other events, 1226.2 us)

commit v6 on v5

--- a/solution.py
+++ b/solution.py
@@ -18,8 +18,10 @@
 NEGATIVE = -1e30
 CONTRACT_ROWS = (((0,), (0,)), ((), ()))
 CONTRACT_COLS = (((1,), (1,)), ((), ()))
+GAIN_ROWS = 16
+HOLD_FLOPS = 4400000000
 SMALL_LAST = True
-VMEM_GRANT = 10
+VMEM_GRANT = 8
 
 
 def one_way(value, source):
@@ -62,15 +64,9 @@
         width *= base
 
 
-def joined(got, digit):
-    base, size = len(got), got[0].shape[0]
-    turned = [got[-place % base] for place in range(base)] * 2
-    start = (base - digit) % base * size
-    return lax.dynamic_slice_in_dim(jnp.concatenate(turned, axis=0), start, base * size, 0)
-
-
 class GatherRing:
-    def __init__(self, packed):
+    def __init__(self, packed, paced=False):
+        self.paced = paced
         devices = lax.axis_size("dp")
         self.chips = devices // 2
         self.route, self.pair = ring_routes(devices)
@@ -93,7 +89,7 @@
 
     def advance(self, *before):
         value = self.pieces[-1]
-        if before:
+        if before or self.paced and self.step > 1:
             value = self.pieces[-1] = hold(value, *before)
         self.pieces.append(lax.ppermute(value, "dp", self.route))
         self.swap(value)
@@ -171,6 +167,7 @@
         out_specs=ANYWHERE,
         out_shape=jax.ShapeDtypeStruct(value.shape, value.dtype),
         input_output_aliases={0: 0},
+        cost_estimate=pl.CostEstimate(flops=HOLD_FLOPS, bytes_accessed=0, transcendentals=0),
     )(value, *after)
 
 
@@ -675,12 +672,14 @@
     orders = jnp.concatenate([order, other_order])
     gain_sizes = (norm_attn.shape[1], norm_query.shape[1], norm_key.shape[1], norm_ffn.shape[1])
     gain_shard = jnp.concatenate([norm_attn, norm_query, norm_key, norm_ffn], axis=1)
+    gain_count = gain_shard.shape[1]
+    gain_shard = jnp.pad(gain_shard, ((0, GAIN_ROWS - 1), (0, model - gain_count)))
     moved = cut // 2
     attn_packed = pack(
-        (attn_query[0], attn_out[0], attn_key[0], attn_value[0]),
+        (attn_query[0], attn_out[0], attn_key[0], attn_value[0], gain_shard),
         (
-            ((0, 0, rows, 0), (0, 0, rows, 1), (1, 0, rows, 0)),
-            ((1, rows, rows, 0), (2, 0, rows, 0), (3, 0, rows, 0)),
+            ((0, 0, rows, 0), (0, 0, rows, 1), (1, 0, rows, 0), (4, 0, GAIN_ROWS, 0)),
+            ((1, rows, rows, 0), (2, 0, rows, 0), (3, 0, rows, 0), (4, 0, GAIN_ROWS, 0)),
         ),
         model,
     )
@@ -711,40 +710,34 @@
             )
         )
     keep_columns = [keep[batch][:, None] for batch in range(batches)]
-    early = [array for table in tables for array in table] + keep_columns + [orders]
-    attn_ring = GatherRing(attn_packed)
+    first = [inputs[batch] for batch in range(batches)]
+    target = [teacher[batch] for batch in range(batches)]
+    early = [array for table in tables for array in table] + keep_columns + first + target + [orders]
+    attn_ring = GatherRing(attn_packed, True)
     ffn_ring = GatherRing(ffn_packed)
-    gain_rounds = cycles(gain_shard.astype(jnp.float32))
-    got, digit = next(gain_rounds)
     attn_ring.advance()
     ffn_ring.advance()
     attn_ring.advance(*early)
     ffn_ring.advance(attn_ring.others[0], ffn_ring.others[0])
-    while True:
-        gain_whole = joined(got, digit)
-        attn_ring.advance(gain_whole)
+    while ffn_ring.step < chips:
+        attn_ring.advance()
         ffn_ring.advance()
-        try:
-            got, digit = gain_rounds.send(gain_whole)
-        except StopIteration:
-            break
+    carried_gains = jnp.stack([piece[:, 3 * rows, :gain_count] for piece in attn_ring.pieces])
+    chip = jnp.arange(chips, dtype=jnp.int32)
+    found = lax.rem((2 * core - 1) * (ring_place(chip, chips) - place) + chips, chips)
+    gain_whole = jnp.take(carried_gains, found, axis=0).reshape(devices, gain_count)
+    gain_whole = gain_whole.astype(jnp.float32)
     gains, low = [], 0
     for size in gain_sizes:
         gains.append(gain_whole[:, low : low + size].reshape(1, devices * size))
         low += size
 
-    attn_ring.advance(*gains)
-    while ffn_ring.step < chips:
-        ffn_ring.advance()
-        if attn_ring.step < chips:
-            attn_ring.advance()
     half = 3 * rows + cut
     ffn_low = 9 * rows - half
     attn_whole = assemble(orders, [(attn_ring, 0, 3 * rows, 0, 3 * rows)], 6 * rows)
     ffn_whole = assemble(orders, [(ffn_ring, 0, half, 0, ffn_low)], 9 * rows)
     both = range(batches)
 
-    first = [inputs[batch] for batch in both]
     where = section[None].astype(jnp.int32)
     last = jnp.ones((1,), jnp.int32)
     carried, seen = [], []
@@ -760,7 +753,7 @@
             where, first[batch], carried[batch], gains, tables[batch], attn_whole, True
         )
         result, gate, up, inner_t, pull, square = feed_forward(
-            where, norm, mid, ffn_whole, (teacher[batch], keep_columns[batch])
+            where, norm, mid, ffn_whole, (target[batch], keep_columns[batch])
         )
         kept.append(
             (hidden, normalized_t, qkv, pre, mix_t, mid, norm_t, result, gate, up, inner_t, pull, square)

time: 572 us -> 550 us (0.962)
  waiting for transfers between devices: 209 us -> 183 us
  starting transfers between devices: 57.6 us -> 77.6 us
  local copies, waits for them, and re-layouts: 79.6 us -> 62.4 us
    ppermute x12 -> x6, waiting for transfers between devices: 35.3 us -> 6.09 us  [cycles(): got.append(lax.ppermute(value, 'dp', route))]
    ppermute x14, waiting for transfers between devices: 79.9 us -> 101 us  [advance(): self.pieces.append(lax.ppermute(value, 'dp', self.route))]
    ppermute x14, starting transfers between devices: 3.5 us -> 22.3 us  [advance(): value = lax.ppermute(self.value, 'dp', self.route).astype(jnp.float32)]
    unnamed x230 -> x205, local copies, waits for them, and re-layouts: 55.7 us -> 38.4 us
    ppermute x14, waiting for transfers between devices: 92 us -> 75.7 us  [advance(): value = lax.ppermute(self.value, 'dp', self.route).astype(jnp.float32)]
    ppermute x14, starting transfers between devices: 19.2 us -> 29.8 us  [advance(): self.pieces.append(lax.ppermute(value, 'dp', self.route))]
    ppermute x12 -> x6, starting transfers between devices: 15.1 us -> 5.53 us  [cycles(): got.append(lax.ppermute(value, 'dp', route))]
  transfers between devices with their start and end apart: 67 -> 61, of which waited for: 27 -> 28; matrix products, arithmetic and copies ran while one was open for 13% -> 13% of each run, Pallas kernels for 21% -> 22%
where the time goes in v6:
time: 550 us; the launch traced here: 543 us
  waiting for transfers between devices  183 us (33%)
  Pallas kernels  157 us (29%)
  starting transfers between devices  77.6 us (14%)
  local copies, waits for them, and re-layouts  62.4 us (11%)
  other arithmetic  56.7 us (10%)
  between operations  6.26 us (1%)
    pallas_call x18, Pallas kernels, flat_call(): pl.pallas_call(run, in_specs=specs, out_specs=[LOCAL] * len(out_shape), o...  146 us
    ppermute x14, waiting for transfers between devices, advance(): self.pieces.append(lax.ppermute(value, 'dp', self.route))  101 us
    ppermute x14, waiting for transfers between devices, advance(): value = lax.ppermute(self.value, 'dp', self.route).astype(jnp.float32)  75.7 us
    unnamed x205, local copies, waits for them, and re-layouts  38.4 us
    convert_element_type x12, other arithmetic, advance(): self.value = value.astype(jnp.bfloat16) if self.step < self.chips else value  30 us
    ppermute x14, starting transfers between devices, advance(): self.pieces.append(lax.ppermute(value, 'dp', self.route))  29.8 us
    ppermute x14, starting transfers between devices, advance(): value = lax.ppermute(self.value, 'dp', self.route).astype(jnp.float32)  22.3 us
    ppermute x7, starting transfers between devices, one_way(): return lax.ppermute(value, 'section', [(source, 1 - source)])  16 us
  transfers between devices with their start and end apart: 61, of which 28 were waited for; matrix products, arithmetic and copies ran while one was open for 13% of the time, Pallas kernels for 22%

profile of v6, /device:TPU:0, one launch (start us, length us, event | category | flops | bytes accessed | tf_op | source)
XLA Modules:
  0.0 543.5 jit_solution(2805651320510050763)
XLA Ops:
  35.2 6.8 %collective-permute-done.16.refs_0_ = bf16[2,288,1024]{2,1,0:T(8,128)(2,1)S(1)} collective-permute-done((bf16[2,288,1024]{2,1,0:T(8,128)(2,1)S(1)}, bf16[2,288,1024]{2,1,0:T(8,128)(2,1)S(1)}, u32[]{:S(2)}, u32[]{:S(2)}) %collective-permute-start.16) | collective-permute-done | bytes 1179680 | tf_op jit(solution)/shard_map/ppermute | solution.py:94
  45.1 6.1 %collective-permute-done.2.refs_0_ = bf16[2,208,1024]{2,1,0:T(8,128)(2,1)} collective-permute-done((bf16[2,208,1024]{2,1,0:T(8,128)(2,1)}, bf16[2,208,1024]{2,1,0:T(8,128)(2,1)}, u32[]{:S(2)}, u32[]{:S(2)}) %collective-permute-start.2) | collective-permute-done | bytes 852000 | tf_op jit(solution)/shard_map/ppermute | solution.py:94
  53.3 10.5 %collective-permute-done.17.refs_2_ = bf16[2,288,1024]{2,1,0:T(8,128)(2,1)S(1)} collective-permute-done((bf16[2,288,1024]{2,1,0:T(8,128)(2,1)}, bf16[2,288,1024]{2,1,0:T(8,128)(2,1)S(1)}, u32[]{:S(2)}, u32[]{:S(2)}) %collective-permute-start.17) | collective-permute-done | bytes 1179680 | tf_op jit(solution)/shard_map/ppermute | solution.py:94
  65.8 7.2 %collective-permute-done.3.refs_0_ = bf16[2,208,1024]{2,1,0:T(8,128)(2,1)} collective-permute-done((bf16[2,208,1024]{2,1,0:T(8,128)(2,1)}, bf16[2,208,1024]{2,1,0:T(8,128)(2,1)}, u32[]{:S(2)}, u32[]{:S(2)}) %collective-permute-start.3) | collective-permute-done | bytes 852000 | tf_op jit(solution)/shard_map/ppermute | solution.py:94
  75.1 10.6 %collective-permute-done.18.refs_3_ = bf16[2,288,1024]{2,1,0:T(8,128)(2,1)} collective-permute-done((bf16[2,288,1024]{2,1,0:T(8,128)(2,1)S(1)}, bf16[2,288,1024]{2,1,0:T(8,128)(2,1)}, u32[]{:S(2)}, u32[]{:S(2)}) %collective-permute-start.18) | collective-permute-done | bytes 1179680 | tf_op jit(solution)/shard_map/ppermute | solution.py:94
  87.7 7.1 %collective-permute-done.4.refs_0_ = bf16[2,208,1024]{2,1,0:T(8,128)(2,1)} collective-permute-done((bf16[2,208,1024]{2,1,0:T(8,128)(2,1)}, bf16[2,208,1024]{2,1,0:T(8,128)(2,1)}, u32[]{:S(2)}, u32[]{:S(2)}) %collective-permute-start.4) | collective-permute-done | bytes 852000 | tf_op jit(solution)/shard_map/ppermute | solution.py:94
  96.8 10.5 %collective-permute-done.19.refs_4_ = bf16[2,288,1024]{2,1,0:T(8,128)(2,1)S(1)} collective-permute-done((bf16[2,288,1024]{2,1,0:T(8,128)(2,1)}, bf16[2,288,1024]{2,1,0:T(8,128)(2,1)S(1)}, u32[]{:S(2)}, u32[]{:S(2)}) %collective-permute-start.19) | collective-permute-done | bytes 1179680 | tf_op jit(solution)/shard_map/ppermute | solution.py:94
  109.4 7.2 %collective-permute-done.5.refs_0_ = bf16[2,208,1024]{2,1,0:T(8,128)(2,1)} collective-permute-done((bf16[2,208,1024]{2,1,0:T(8,128)(2,1)}, bf16[2,208,1024]{2,1,0:T(8,128)(2,1)}, u32[]{:S(2)}, u32[]{:S(2)}) %collective-permute-start.5) | collective-permute-done | bytes 852000 | tf_op jit(solution)/shard_map/ppermute | solution.py:94
  119.1 10.0 %collective-permute-done.20.refs_5_ = bf16[2,288,1024]{2,1,0:T(8,128)(2,1)} collective-permute-done((bf16[2,288,1024]{2,1,0:T(8,128)(2,1)S(1)}, bf16[2,288,1024]{2,1,0:T(8,128)(2,1)}, u32[]{:S(2)}, u32[]{:S(2)}) %collective-permute-start.20) | collective-permute-done | bytes 1179680 | tf_op jit(solution)/shard_map/ppermute | solution.py:94
  131.5 6.8 %collective-permute-done.6.refs_0_ = bf16[2,208,1024]{2,1,0:T(8,128)(2,1)} collective-permute-done((bf16[2,208,1024]{2,1,0:T(8,128)(2,1)}, bf16[2,208,1024]{2,1,0:T(8,128)(2,1)}, u32[]{:S(2)}, u32[]{:S(2)}) %collective-permute-start.6) | collective-permute-done | bytes 852000 | tf_op jit(solution)/shard_map/ppermute | solution.py:94
  141.7 9.3 %collective-permute-done.21.refs_6_ = bf16[2,288,1024]{2,1,0:T(8,128)(2,1)} collective-permute-done((bf16[2,288,1024]{2,1,0:T(8,128)(2,1)}, bf16[2,288,1024]{2,1,0:T(8,128)(2,1)}, u32[]{:S(2)}, u32[]{:S(2)}) %collective-permute-start.21) | collective-permute-done | bytes 1179680 | tf_op jit(solution)/shard_map/ppermute | solution.py:94
  190.4 6.0 %shard_map.256.refs_3_.refs_7_ = bf16[16,576,1024]{2,1,0:T(8,128)(2,1)S(1)} custom-call(s32[18]{0:T(128)S(1)} %copy-done.44, bf16[2,288,1024]{2,1,0:T(8,128)(2,1)S(1)} %maximum_select_fusion.refs_0_, bf16[2,288,1024]{2,1,0:T(8,128)(2,1)S(1)} %copy-done.14, bf16[2,288,1024]{2,1,0:T(8,128)(2,1)S(1)} %copy-done.10, ...), custom_call_target="tpu_custom_call" | custom-call | bytes 37748736 | tf_op jit(solution)/shard_map/pallas_call | solution.py:628
  223.1 6.1 %shard_map.258 = (f32[256,1024]{1,0:T(8,128)S(1)}, bf16[256,1024]{1,0:T(8,128)(2,1)S(1)}, bf16[1024,256]{1,0:T(8,128)(2,1)S(1)}, bf16[1024,256]{1,0:T(8,128)(2,1...) custom-call(s32[1]{0:T(128)} %bitcast.refs_0_, ...), custom_call_target="tpu_custom_call" | custom-call | flops 4294967296 | bytes 17825792 | tf_op jit(solution)/shard_map/pallas_call | solution.py:181
  235.2 8.1 %shard_map.264 = (f32[256,1024]{1,0:T(8,128)S(1)}, bf16[256,1024]{1,0:T(8,128)(2,1)S(1)}, bf16[256,3072]{1,0:T(8,128)(2,1)}, bf16[256,3072]{1,0:T(8,128)(2,1)}, ...) custom-call(s32[1]{0:T(128)} %constant.161.clone.1.refs_0_, f32[256,1024]{1,0:T(8,128)S(1)} %get-tuple-element.90.refs_1_, ...), custom_call_target="tpu_custom_call" | custom-call | flops 4831838208 | bytes 28835840 | tf_op jit(solution)/shard_map/pallas_call | solution.py:181
  243.4 13.0 %shard_map.265 = (bf16[256,2048]{1,0:T(8,128)(2,1)}, bf16[256,2048]{1,0:T(8,128)(2,1)}, bf16[256,1024]{1,0:T(8,128)(2,1)S(1)}, f32[1,1024]{1,0:T(1,128)}, f32[1,128]{1,0:T(1,128)}, /*index=5*/f32[1,128]{1,0:T(1,128)}) custom-call(s32[1]{0:T(128)} %bitcast.refs_0_, bf16[256,1024]{1,0:T(8,128)(2,1)S(1)} %get-tuple-element.93.refs_1_, ...), custom_call_target="tpu_custom_call" | custom-call | flops 5905580032 | bytes 23068672 | tf_op jit(solution)/shard_map/pallas_call | solution.py:181
  262.3 6.1 %shard_map.262 = (f32[256,1024]{1,0:T(8,128)S(1)}, bf16[256,1024]{1,0:T(8,128)(2,1)S(1)}, bf16[1024,256]{1,0:T(8,128)(2,1)S(1)}, bf16[1024,256]{1,0:T(8,128)(2,1...) custom-call(s32[1]{0:T(128)} %bitcast.refs_0_, ...), custom_call_target="tpu_custom_call" | custom-call | flops 4294967296 | bytes 17825792 | tf_op jit(solution)/shard_map/pallas_call | solution.py:181
  275.3 8.1 %shard_map.268 = (f32[256,1024]{1,0:T(8,128)S(1)}, bf16[256,1024]{1,0:T(8,128)(2,1)S(1)}, bf16[256,3072]{1,0:T(8,128)(2,1)}, bf16[256,3072]{1,0:T(8,128)(2,1)}, ...) custom-call(s32[1]{0:T(128)} %constant.161.clone.1.refs_0_, f32[256,1024]{1,0:T(8,128)S(1)} %get-tuple-element.102.refs_1_, ...), custom_call_target="tpu_custom_call" | custom-call | flops 4831838208 | bytes 28835840 | tf_op jit(solution)/shard_map/pallas_call | solution.py:181
  283.5 13.1 %shard_map.269 = (bf16[256,2048]{1,0:T(8,128)(2,1)}, bf16[256,2048]{1,0:T(8,128)(2,1)}, bf16[256,1024]{1,0:T(8,128)(2,1)S(1)}, f32[1,1024]{1,0:T(1,128)}, f32[1,128]{1,0:T(1,128)}, /*index=5*/f32[1,128]{1,0:T(1,128)}) custom-call(s32[1]{0:T(128)} %bitcast.refs_0_, bf16[256,1024]{1,0:T(8,128)(2,1)S(1)} %get-tuple-element.105.refs_1_, ...), custom_call_target="tpu_custom_call" | custom-call | flops 5905580032 | bytes 23068672 | tf_op jit(solution)/shard_map/pallas_call | solution.py:181
  298.0 6.2 %shard_map.266 = (f32[256,1024]{1,0:T(8,128)S(1)}, bf16[256,1024]{1,0:T(8,128)(2,1)S(1)}, bf16[256,3072]{1,0:T(8,128)(2,1)S(1)}, bf16[256,3072]{1,0:T(8,128)(2,1...) custom-call(s32[1]{0:T(128)} %bitcast.refs_0_, f32[256,1024]{1,0:T(8,128)S(1)} %get-tuple-element.90.refs_1_, ...), custom_call_target="tpu_custom_call" | custom-call | flops 4831838208 | bytes 28835840 | tf_op jit(solution)/shard_map/pallas_call | solution.py:181
  310.0 12.7 %shard_map.267 = (bf16[256,2048]{1,0:T(8,128)(2,1)S(1)}, bf16[256,2048]{1,0:T(8,128)(2,1)S(1)}, bf16[256,1024]{1,0:T(8,128)(2,1)S(1)}, f32[1,1024]{1,0:T(1,128)S...) custom-call(s32[1]{0:T(128)} %bitcast.refs_0_, bf16[256,1024]{1,0:T(8,128)(2,1)S(1)} %get-tuple-element.99.refs_1_.refs_9_, ...), custom_call_target="tpu_custom_call" | custom-call | flops 5905580032 | bytes 23068672 | tf_op jit(solution)/shard_map/pallas_call | solution.py:181
  323.7 6.2 %shard_map.270 = (f32[256,1024]{1,0:T(8,128)S(1)}, bf16[256,1024]{1,0:T(8,128)(2,1)S(1)}, bf16[256,3072]{1,0:T(8,128)(2,1)S(1)}, bf16[256,3072]{1,0:T(8,128)(2,1...) custom-call(s32[1]{0:T(128)} %bitcast.refs_0_, f32[256,1024]{1,0:T(8,128)S(1)} %get-tuple-element.102.refs_1_, ...), custom_call_target="tpu_custom_call" | custom-call | flops 4831838208 | bytes 28835840 | tf_op jit(solution)/shard_map/pallas_call | solution.py:181
  330.0 9.1 %shard_map.271 = (bf16[8,2,240,1024]{3,2,1,0:T(8,128)(2,1)S(1)}, bf16[8,2,240,1024]{3,2,1,0:T(8,128)(2,1)S(1)}) custom-call(s32[18]{0:T(128)S(1)} %get-tuple-element.198.refs_0_, bf16[1024,256]{1,0:T(8,128)(2,1)S(1)} %copy-done.74, bf16[1024,256]{1,0:T(8,128)(2,1)S(1)} %copy-done.80, bf16[256,3072]{1,0:T(8,128)(2,1)S(1)} %copy-done.54, ...), custom_call_target="tpu_custom_call" | custom-call | flops 8053063680 | bytes 19922944 | tf_op jit(solution)/shard_map/pallas_call | solution.py:181
  339.4 12.5 %shard_map.272 = (bf16[256,2048]{1,0:T(8,128)(2,1)S(1)}, bf16[256,2048]{1,0:T(8,128)(2,1)S(1)}, bf16[256,1024]{1,0:T(8,128)(2,1)S(1)}, f32[1,1024]{1,0:T(1,128)S...) custom-call(s32[1]{0:T(128)} %bitcast.refs_0_, bf16[256,1024]{1,0:T(8,128)(2,1)S(1)} %get-tuple-element.111.refs_1_.refs_10_, ...), custom_call_target="tpu_custom_call" | custom-call | flops 5905580032 | bytes 23068672 | tf_op jit(solution)/shard_map/pallas_call | solution.py:181
  354.2 11.6 %shard_map.273 = (bf16[8,2,240,1024]{3,2,1,0:T(8,128)(2,1)}, bf16[8,2,240,1024]{3,2,1,0:T(8,128)(2,1)S(1)}) custom-call(s32[18]{0:T(128)S(1)} %get-tuple-element.198.refs_0_, bf16[1024,256]{1,0:T(8,128)(2,1)S(1)} %copy-done.72, bf16[1024,256]{1,0:T(8,128)(2,1)S(1)} %copy-done.76, bf16[256,2048]{1,0:T(8,128)(2,1)S(1)} %get-tuple-element.123.refs_11_.refs_3_, ...), custom_call_target="tpu_custom_call" | custom-call | flops 8053063680 | bytes 19922944 | tf_op jit(solution)/shard_map/pallas_call | solution.py:181
  370.8 12.5 %collective-permute-done.53 = bf16[2,240,1024]{2,1,0:T(8,128)(2,1)S(1)} collective-permute-done((bf16[2,240,1024]{2,1,0:T(8,128)(2,1)S(1)}, bf16[2,240,1024]{2,1,0:T(8,128)(2,1)S(1)}, u32[]{:S(2)}, u32[]{:S(2)}) %collective-permute-start.53) | collective-permute-done | bytes 983072 | tf_op jit(solution)/shard_map/ppermute | solution.py:122
  394.7 6.1 %collective-permute-done.36 = f32[1,2306]{1,0:T(1,128)S(1)} collective-permute-done((f32[1,2306]{1,0:T(1,128)S(1)}, f32[1,2306]{1,0:T(1,128)S(1)}, u32[]{:S(2)}, u32[]{:S(2)}) %collective-permute-start.36) | collective-permute-done | bytes 9256 | tf_op jit(solution)/shard_map/ppermute | solution.py:62
  425.5 6.9 %collective-permute-done.46 = bf16[2,240,1024]{2,1,0:T(8,128)(2,1)S(1)} collective-permute-done((bf16[2,240,1024]{2,1,0:T(8,128)(2,1)S(1)}, bf16[2,240,1024]{2,1,0:T(8,128)(2,1)S(1)}, u32[]{:S(2)}, u32[]{:S(2)}) %collective-permute-start.46) | collective-permute-done | bytes 983072 | tf_op jit(solution)/shard_map/ppermute | solution.py:122
  436.6 6.3 %collective-permute-done.56 = bf16[2,240,1024]{2,1,0:T(8,128)(2,1)S(1)} collective-permute-done((bf16[2,240,1024]{2,1,0:T(8,128)(2,1)S(1)}, bf16[2,240,1024]{2,1,0:T(8,128)(2,1)S(1)}, u32[]{:S(2)}, u32[]{:S(2)}) %collective-permute-start.56) | collective-permute-done | bytes 983072 | tf_op jit(solution)/shard_map/ppermute | solution.py:122
  457.4 6.6 %collective-permute-done.57 = bf16[2,240,1024]{2,1,0:T(8,128)(2,1)S(1)} collective-permute-done((bf16[2,240,1024]{2,1,0:T(8,128)(2,1)}, bf16[2,240,1024]{2,1,0:T(8,128)(2,1)S(1)}, u32[]{:S(2)}, u32[]{:S(2)}) %collective-permute-start.57) | collective-permute-done | bytes 983072 | tf_op jit(solution)/shard_map/ppermute | solution.py:122
  467.9 6.6 %collective-permute-done.48 = bf16[2,240,1024]{2,1,0:T(8,128)(2,1)S(1)} collective-permute-done((bf16[2,240,1024]{2,1,0:T(8,128)(2,1)S(1)}, bf16[2,240,1024]{2,1,0:T(8,128)(2,1)S(1)}, u32[]{:S(2)}, u32[]{:S(2)}) %collective-permute-start.48) | collective-permute-done | bytes 983072 | tf_op jit(solution)/shard_map/ppermute | solution.py:122
  478.4 6.6 %collective-permute-done.58 = bf16[2,240,1024]{2,1,0:T(8,128)(2,1)S(1)} collective-permute-done((bf16[2,240,1024]{2,1,0:T(8,128)(2,1)S(1)}, bf16[2,240,1024]{2,1,0:T(8,128)(2,1)S(1)}, u32[]{:S(2)}, u32[]{:S(2)}) %collective-permute-start.58) | collective-permute-done | bytes 983072 | tf_op jit(solution)/shard_map/ppermute | solution.py:122
  526.0 7.2 %collective-permute-done.51 = bf16[2,240,1024]{2,1,0:T(8,128)(2,1)S(1)} collective-permute-done((bf16[2,240,1024]{2,1,0:T(8,128)(2,1)S(1)}, bf16[2,240,1024]{2,1,0:T(8,128)(2,1)S(1)}, u32[]{:S(2)}, u32[]{:S(2)}) %collective-permute-start.51) | collective-permute-done | bytes 983072 | tf_op jit(solution)/shard_map/ppermute | solution.py:122
  (428 shorter events, 267.6 us)
Async XLA Ops:
  20.8 21.2 %collective-permute-start.16 = (bf16[2,288,1024]{2,1,0:T(8,128)(2,1)S(1)}, bf16[2,288,1024]{2,1,0:T(8,128)(2,1)S(1)}, u32[]{:S(2)}, u32[]{:S(2)}) collective-permute-start(bf16[2,288,1024]{2,1,0:T(8,128)(2,1)S(1)} %maximum_select_fusion.refs_0_), channel_id=1, source_target_pairs={{0,4},{5,1},{4,8},{9,5},{8,12},{13,9},{12,14},{15,13},{14,10},{11,... | collective-permute-start | bytes 3538952 | tf_op jit(solution)/shard_map/ppermute | solution.py:94
  29.5 21.8 %collective-permute-start.2 = (bf16[2,208,1024]{2,1,0:T(8,128)(2,1)}, bf16[2,208,1024]{2,1,0:T(8,128)(2,1)}, u32[]{:S(2)}, u32[]{:S(2)}) collective-permute-start(bf16[2,208,1024]{2,1,0:T(8,128)(2,1)} %shard_map.246.refs_1_), channel_id=1, source_target_pairs={{0,4},{5,1},{4,8},{9,5},{8,12},{13,9},{12,14},{15,13},{14,10},{11,... | collective-permute-start | bytes 2555912 | tf_op jit(solution)/shard_map/ppermute | solution.py:94
  43.0 20.7 %collective-permute-start.17 = (bf16[2,288,1024]{2,1,0:T(8,128)(2,1)}, bf16[2,288,1024]{2,1,0:T(8,128)(2,1)S(1)}, u32[]{:S(2)}, u32[]{:S(2)}) collective-permute-start(bf16[2,288,1024]{2,1,0:T(8,128)(2,1)} %shard_map.255.refs_1_), channel_id=1, source_target_pairs={{0,4},{5,1},{4,8},{9,5},{8,12},{13,9},{12,14},{15,13},{14,10},{11,... | collective-permute-start | bytes 3538952 | tf_op jit(solution)/shard_map/ppermute | solution.py:94
  51.2 21.8 %collective-permute-start.3 = (bf16[2,208,1024]{2,1,0:T(8,128)(2,1)}, bf16[2,208,1024]{2,1,0:T(8,128)(2,1)}, u32[]{:S(2)}, u32[]{:S(2)}) collective-permute-start(bf16[2,208,1024]{2,1,0:T(8,128)(2,1)} %shard_map.247.refs_2_), channel_id=1, source_target_pairs={{0,4},{5,1},{4,8},{9,5},{8,12},{13,9},{12,14},{15,13},{14,10},{11,... | collective-permute-start | bytes 2555912 | tf_op jit(solution)/shard_map/ppermute | solution.py:94
  63.8 21.9 %collective-permute-start.18 = (bf16[2,288,1024]{2,1,0:T(8,128)(2,1)S(1)}, bf16[2,288,1024]{2,1,0:T(8,128)(2,1)}, u32[]{:S(2)}, u32[]{:S(2)}) collective-permute-start(bf16[2,288,1024]{2,1,0:T(8,128)(2,1)S(1)} %collective-permute-done.17.refs_2_), channel_id=1, source_target_pairs={{0,4},{5,1},{4,8},{9,5},{8,12},{13,9},{12,14},{15,13},{14,10},{11,... | collective-permute-start | bytes 3538952 | tf_op jit(solution)/shard_map/ppermute | solution.py:94
  73.0 21.8 %collective-permute-start.4 = (bf16[2,208,1024]{2,1,0:T(8,128)(2,1)}, bf16[2,208,1024]{2,1,0:T(8,128)(2,1)}, u32[]{:S(2)}, u32[]{:S(2)}) collective-permute-start(bf16[2,208,1024]{2,1,0:T(8,128)(2,1)} %shard_map.248.refs_3_), channel_id=1, source_target_pairs={{0,4},{5,1},{4,8},{9,5},{8,12},{13,9},{12,14},{15,13},{14,10},{11,... | collective-permute-start | bytes 2555912 | tf_op jit(solution)/shard_map/ppermute | solution.py:94
  85.6 21.7 %collective-permute-start.19 = (bf16[2,288,1024]{2,1,0:T(8,128)(2,1)}, bf16[2,288,1024]{2,1,0:T(8,128)(2,1)S(1)}, u32[]{:S(2)}, u32[]{:S(2)}) collective-permute-start(bf16[2,288,1024]{2,1,0:T(8,128)(2,1)} %collective-permute-done.18.refs_3_), channel_id=1, source_target_pairs={{0,4},{5,1},{4,8},{9,5},{8,12},{13,9},{12,14},{15,13},{14,10},{11,... | collective-permute-start | bytes 3538952 | tf_op jit(solution)/shard_map/ppermute | solution.py:94
  94.8 21.8 %collective-permute-start.5 = (bf16[2,208,1024]{2,1,0:T(8,128)(2,1)}, bf16[2,208,1024]{2,1,0:T(8,128)(2,1)}, u32[]{:S(2)}, u32[]{:S(2)}) collective-permute-start(bf16[2,208,1024]{2,1,0:T(8,128)(2,1)} %shard_map.249.refs_4_), channel_id=1, source_target_pairs={{0,4},{5,1},{4,8},{9,5},{8,12},{13,9},{12,14},{15,13},{14,10},{11,... | collective-permute-start | bytes 2555912 | tf_op jit(solution)/shard_map/ppermute | solution.py:94
  107.3 21.9 %collective-permute-start.20 = (bf16[2,288,1024]{2,1,0:T(8,128)(2,1)S(1)}, bf16[2,288,1024]{2,1,0:T(8,128)(2,1)}, u32[]{:S(2)}, u32[]{:S(2)}) collective-permute-start(bf16[2,288,1024]{2,1,0:T(8,128)(2,1)S(1)} %collective-permute-done.19.refs_4_), channel_id=1, source_target_pairs={{0,4},{5,1},{4,8},{9,5},{8,12},{13,9},{12,14},{15,13},{14,10},{11,... | collective-permute-start | bytes 3538952 | tf_op jit(solution)/shard_map/ppermute | solution.py:94
  116.5 21.8 %collective-permute-start.6 = (bf16[2,208,1024]{2,1,0:T(8,128)(2,1)}, bf16[2,208,1024]{2,1,0:T(8,128)(2,1)}, u32[]{:S(2)}, u32[]{:S(2)}) collective-permute-start(bf16[2,208,1024]{2,1,0:T(8,128)(2,1)} %shard_map.250.refs_5_), channel_id=1, source_target_pairs={{0,4},{5,1},{4,8},{9,5},{8,12},{13,9},{12,14},{15,13},{14,10},{11,... | collective-permute-start | bytes 2555912 | tf_op jit(solution)/shard_map/ppermute | solution.py:94
  118.6 19.7 %collective-permute-start.8 = (bf16[2,208,1024]{2,1,0:T(8,128)(2,1)}, bf16[2,208,1024]{2,1,0:T(8,128)(2,1)}, u32[]{:S(2)}, u32[]{:S(2)}) collective-permute-start(bf16[2,208,1024]{2,1,0:T(8,128)(2,1)} %shard_map.246.refs_1_), channel_id=1, source_target_pairs={{0,1},{1,0},{2,3},{3,2},{4,5},{5,4},{6,7},{7,6},{8,9},{9,8},{10,11... | collective-permute-start | bytes 2555912 | tf_op jit(solution)/shard_map/ppermute | solution.py:103
  118.6 20.2 %collective-permute-start.9 = (bf16[2,208,1024]{2,1,0:T(8,128)(2,1)}, bf16[2,208,1024]{2,1,0:T(8,128)(2,1)}, u32[]{:S(2)}, u32[]{:S(2)}) collective-permute-start(bf16[2,208,1024]{2,1,0:T(8,128)(2,1)} %shard_map.247.refs_2_), channel_id=1, source_target_pairs={{0,1},{1,0},{2,3},{3,2},{4,5},{5,4},{6,7},{7,6},{8,9},{9,8},{10,11... | collective-permute-start | bytes 2555912 | tf_op jit(solution)/shard_map/ppermute | solution.py:103
  129.2 21.8 %collective-permute-start.21 = (bf16[2,288,1024]{2,1,0:T(8,128)(2,1)}, bf16[2,288,1024]{2,1,0:T(8,128)(2,1)}, u32[]{:S(2)}, u32[]{:S(2)}) collective-permute-start(bf16[2,288,1024]{2,1,0:T(8,128)(2,1)} %collective-permute-done.20.refs_5_), channel_id=1, source_target_pairs={{0,4},{5,1},{4,8},{9,5},{8,12},{13,9},{12,14},{15,13},{14,10},{11,... | collective-permute-start | bytes 3538952 | tf_op jit(solution)/shard_map/ppermute | solution.py:94
  131.4 23.2 %collective-permute-start.23 = (bf16[2,288,1024]{2,1,0:T(8,128)(2,1)}, bf16[2,288,1024]{2,1,0:T(8,128)(2,1)}, u32[]{:S(2)}, u32[]{:S(2)}) collective-permute-start(bf16[2,288,1024]{2,1,0:T(8,128)(2,1)} %shard_map.255.refs_1_), channel_id=1, source_target_pairs={{0,1},{1,0},{2,3},{3,2},{4,5},{5,4},{6,7},{7,6},{8,9},{9,8},{10,11... | collective-permute-start | bytes 3538952 | tf_op jit(solution)/shard_map/ppermute | solution.py:103
  138.8 21.1 %collective-permute-start.7 = (bf16[2,208,1024]{2,1,0:T(8,128)(2,1)}, bf16[2,208,1024]{2,1,0:T(8,128)(2,1)S(1)}, u32[]{:S(2)}, u32[]{:S(2)}) collective-permute-start(bf16[2,208,1024]{2,1,0:T(8,128)(2,1)} %shard_map.251.refs_6_), channel_id=1, source_target_pairs={{0,4},{5,1},{4,8},{9,5},{8,12},{13,9},{12,14},{15,13},{14,10},{11,... | collective-permute-start | bytes 2555912 | tf_op jit(solution)/shard_map/ppermute | solution.py:94
  150.9 21.8 %collective-permute-start.22 = (bf16[2,288,1024]{2,1,0:T(8,128)(2,1)}, bf16[2,288,1024]{2,1,0:T(8,128)(2,1)}, u32[]{:S(2)}, u32[]{:S(2)}) collective-permute-start(bf16[2,288,1024]{2,1,0:T(8,128)(2,1)} %collective-permute-done.21.refs_6_), channel_id=1, source_target_pairs={{0,4},{5,1},{4,8},{9,5},{8,12},{13,9},{12,14},{15,13},{14,10},{11,... | collective-permute-start | bytes 3538952 | tf_op jit(solution)/shard_map/ppermute | solution.py:94
  163.9 26.4 %collective-permute-start.25 = (bf16[2,288,1024]{2,1,0:T(8,128)(2,1)}, bf16[2,288,1024]{2,1,0:T(8,128)(2,1)}, u32[]{:S(2)}, u32[]{:S(2)}) collective-permute-start(bf16[2,288,1024]{2,1,0:T(8,128)(2,1)} %collective-permute-done.18.refs_3_), channel_id=1, source_target_pairs={{0,1},{1,0},{2,3},{3,2},{4,5},{5,4},{6,7},{7,6},{8,9},{9,8},{10,11... | collective-permute-start | bytes 3538952 | tf_op jit(solution)/shard_map/ppermute | solution.py:103
  165.4 25.0 %collective-permute-start.26 = (bf16[2,288,1024]{2,1,0:T(8,128)(2,1)}, bf16[2,288,1024]{2,1,0:T(8,128)(2,1)}, u32[]{:S(2)}, u32[]{:S(2)}) collective-permute-start(bf16[2,288,1024]{2,1,0:T(8,128)(2,1)} %copy-done.11), channel_id=1, source_target_pairs={{0,1},{1,0},{2,3},{3,2},{4,5},{5,4},{6,7},{7,6},{8,9},{9,8},{10,11... | collective-permute-start | bytes 3538952 | tf_op jit(solution)/shard_map/ppermute | solution.py:103
  166.3 24.1 %collective-permute-start.27 = (bf16[2,288,1024]{2,1,0:T(8,128)(2,1)}, bf16[2,288,1024]{2,1,0:T(8,128)(2,1)}, u32[]{:S(2)}, u32[]{:S(2)}) collective-permute-start(bf16[2,288,1024]{2,1,0:T(8,128)(2,1)} %collective-permute-done.20.refs_5_), channel_id=1, source_target_pairs={{0,1},{1,0},{2,3},{3,2},{4,5},{5,4},{6,7},{7,6},{8,9},{9,8},{10,11... | collective-permute-start | bytes 3538952 | tf_op jit(solution)/shard_map/ppermute | solution.py:103
  167.7 22.7 %collective-permute-start.28 = (bf16[2,288,1024]{2,1,0:T(8,128)(2,1)}, bf16[2,288,1024]{2,1,0:T(8,128)(2,1)}, u32[]{:S(2)}, u32[]{:S(2)}) collective-permute-start(bf16[2,288,1024]{2,1,0:T(8,128)(2,1)} %collective-permute-done.21.refs_6_), channel_id=1, source_target_pairs={{0,1},{1,0},{2,3},{3,2},{4,5},{5,4},{6,7},{7,6},{8,9},{9,8},{10,11... | collective-permute-start | bytes 3538952 | tf_op jit(solution)/shard_map/ppermute | solution.py:103
  201.6 21.5 %collective-permute-start.30 = (bf16[256,1024]{1,0:T(8,128)(2,1)S(1)}, bf16[256,1024]{1,0:T(8,128)(2,1)S(1)}, u32[]{:S(2)}, u32[]{:S(2)}) collective-permute-start(bf16[256,1024]{1,0:T(8,128)(2,1)S(1)} %shard_map.257), channel_id=1, source_target_pairs={{0,16},{1,17},{2,18},{3,19},{4,20},{5,21},{6,22},{7,23},{8,24},{9,... | collective-permute-start | bytes 1572872 | tf_op jit(solution)/shard_map/ppermute | solution.py:28
  221.4 36.3 %collective-permute-start.32 = (bf16[256,1024]{1,0:T(8,128)(2,1)S(1)}, bf16[256,1024]{1,0:T(8,128)(2,1)S(1)}, u32[]{:S(2)}, u32[]{:S(2)}) collective-permute-start(bf16[256,1024]{1,0:T(8,128)(2,1)S(1)} %shard_map.261), channel_id=1, source_target_pairs={{0,16},{1,17},{2,18},{3,19},{4,20},{5,21},{6,22},{7,23},{8,24},{9,... | collective-permute-start | bytes 1572872 | tf_op jit(solution)/shard_map/ppermute | solution.py:28
  256.4 41.6 %collective-permute-start.33 = (bf16[256,1024]{1,0:T(8,128)(2,1)S(1)}, bf16[256,1024]{1,0:T(8,128)(2,1)S(1)}, u32[]{:S(2)}, u32[]{:S(2)}) collective-permute-start(bf16[256,1024]{1,0:T(8,128)(2,1)S(1)} %get-tuple-element.98), channel_id=1, source_target_pairs={{16,0},{17,1},{18,2},{19,3},{20,4},{21,5},{22,6},{23,7},{24,8},{25... | collective-permute-start | bytes 1572872 | tf_op jit(solution)/shard_map/ppermute | solution.py:28
  296.6 27.1 %collective-permute-start.34 = (bf16[256,1024]{1,0:T(8,128)(2,1)S(1)}, bf16[256,1024]{1,0:T(8,128)(2,1)S(1)}, u32[]{:S(2)}, u32[]{:S(2)}) collective-permute-start(bf16[256,1024]{1,0:T(8,128)(2,1)S(1)} %get-tuple-element.110), channel_id=1, source_target_pairs={{16,0},{17,1},{18,2},{19,3},{20,4},{21,5},{22,6},{23,7},{24,8},{25... | collective-permute-start | bytes 1572872 | tf_op jit(solution)/shard_map/ppermute | solution.py:28
  368.9 22.3 %collective-permute-start.44 = (bf16[8,2,240,1024]{3,2,1,0:T(8,128)(2,1)}, bf16[8,2,240,1024]{3,2,1,0:T(8,128)(2,1)}, u32[]{:S(2)}, u32[]{:S(2)}) collective-permute-start(bf16[8,2,240,1024]{3,2,1,0:T(8,128)(2,1)} %get-tuple-element.145), channel_id=1, source_target_pairs={{0,1},{1,0},{2,3},{3,2},{4,5},{5,4},{6,7},{7,6},{8,9},{9,8},{10,11... | collective-permute-start | bytes 23592968 | tf_op jit(solution)/shard_map/ppermute | solution.py:112
  413.4 19.0 %collective-permute-start.46 = (bf16[2,240,1024]{2,1,0:T(8,128)(2,1)S(1)}, bf16[2,240,1024]{2,1,0:T(8,128)(2,1)S(1)}, u32[]{:S(2)}, u32[]{:S(2)}) collective-permute-start(bf16[2,240,1024]{2,1,0:T(8,128)(2,1)S(1)} %fusion.11), channel_id=1, source_target_pairs={{0,4},{5,1},{4,8},{9,5},{8,12},{13,9},{12,14},{15,13},{14,10},{11,... | collective-permute-start | bytes 2949128 | tf_op jit(solution)/shard_map/ppermute | solution.py:122
  414.6 21.4 %collective-permute-start.40 = (f32[1,2306]{1,0:T(1,128)S(1)}, f32[1,2306]{1,0:T(1,128)S(1)}, u32[]{:S(2)}, u32[]{:S(2)}) collective-permute-start(f32[1,2306]{1,0:T(1,128)S(1)} %copy-done.86), channel_id=1, source_target_pairs={{0,12},{1,13},{2,14},{3,15},{4,0},{5,1},{6,2},{7,3},{8,4},{9,5},{1... | collective-permute-start | bytes 27680 | tf_op jit(solution)/shard_map/ppermute | solution.py:62
  423.9 19.0 %collective-permute-start.56 = (bf16[2,240,1024]{2,1,0:T(8,128)(2,1)S(1)}, bf16[2,240,1024]{2,1,0:T(8,128)(2,1)S(1)}, u32[]{:S(2)}, u32[]{:S(2)}) collective-permute-start(bf16[2,240,1024]{2,1,0:T(8,128)(2,1)S(1)} %fusion.3), channel_id=1, source_target_pairs={{0,4},{5,1},{4,8},{9,5},{8,12},{13,9},{12,14},{15,13},{14,10},{11,... | collective-permute-start | bytes 2949128 | tf_op jit(solution)/shard_map/ppermute | solution.py:122
  455.5 19.0 %collective-permute-start.48 = (bf16[2,240,1024]{2,1,0:T(8,128)(2,1)S(1)}, bf16[2,240,1024]{2,1,0:T(8,128)(2,1)S(1)}, u32[]{:S(2)}, u32[]{:S(2)}) collective-permute-start(bf16[2,240,1024]{2,1,0:T(8,128)(2,1)S(1)} %fusion.9), channel_id=1, source_target_pairs={{0,4},{5,1},{4,8},{9,5},{8,12},{13,9},{12,14},{15,13},{14,10},{11,... | collective-permute-start | bytes 2949128 | tf_op jit(solution)/shard_map/ppermute | solution.py:122
  476.6 19.0 %collective-permute-start.49 = (bf16[2,240,1024]{2,1,0:T(8,128)(2,1)S(1)}, bf16[2,240,1024]{2,1,0:T(8,128)(2,1)S(1)}, u32[]{:S(2)}, u32[]{:S(2)}) collective-permute-start(bf16[2,240,1024]{2,1,0:T(8,128)(2,1)S(1)} %fusion.8), channel_id=1, source_target_pairs={{0,4},{5,1},{4,8},{9,5},{8,12},{13,9},{12,14},{15,13},{14,10},{11,... | collective-permute-start | bytes 2949128 | tf_op jit(solution)/shard_map/ppermute | solution.py:122
  488.1 22.1 %collective-permute-start.59 = (bf16[2,240,1024]{2,1,0:T(8,128)(2,1)}, bf16[2,240,1024]{2,1,0:T(8,128)(2,1)S(1)}, u32[]{:S(2)}, u32[]{:S(2)}) collective-permute-start(bf16[2,240,1024]{2,1,0:T(8,128)(2,1)} %fusion), channel_id=1, source_target_pairs={{0,4},{5,1},{4,8},{9,5},{8,12},{13,9},{12,14},{15,13},{14,10},{11,... | collective-permute-start | bytes 2949128 | tf_op jit(solution)/shard_map/ppermute | solution.py:122
  500.4 24.4 %collective-permute-start.42 = (bf16[1,256,1024]{2,1,0:T(8,128)(2,1)S(1)}, bf16[1,256,1024]{2,1,0:T(8,128)(2,1)S(1)}, u32[]{:S(2)}, u32[]{:S(2)}) collective-permute-start(bf16[1,256,1024]{2,1,0:T(8,128)(2,1)S(1)} %bitcast.212), channel_id=1, source_target_pairs={{0,16},{1,17},{2,18},{3,19},{4,20},{5,21},{6,22},{7,23},{8,24},{9,... | collective-permute-start | bytes 1572872 | tf_op jit(solution)/shard_map/ppermute | solution.py:28
  (128 other events, 1152.6 us)

commit v7 on v6

--- a/solution.py
+++ b/solution.py
@@ -820,8 +820,8 @@
     got, _ = next(small_rounds)
     waits = []
     while ffn_ring.step < chips:
-        ffn_ring.advance(*waits)
-        attn_ring.advance()
+        ffn_ring.advance()
+        attn_ring.advance(*waits)
         waits = []
         if ffn_ring.step % 2 == 1 and got is not None:
             small = sum(got)

time: 550 us -> 544 us (0.989)
    ppermute x6, waiting for transfers between devices: 6.09 us -> 0.02 us  [cycles(): got.append(lax.ppermute(value, 'dp', route))]
    ppermute x14, waiting for transfers between devices: 75.7 us -> 81.4 us  [advance(): value = lax.ppermute(self.value, 'dp', self.route).astype(jnp.float32)]
    unnamed x205 -> x199, local copies, waits for them, and re-layouts: 38.4 us -> 35.6 us
where the time goes in v7:
time: 544 us; the launch traced here: 538 us
  waiting for transfers between devices  183 us (34%)
  Pallas kernels  155 us (28%)
  starting transfers between devices  77.3 us (14%)
  local copies, waits for them, and re-layouts  59.4 us (11%)
  other arithmetic  57.2 us (11%)
  between operations  6.23 us (1%)
    pallas_call x18, Pallas kernels, flat_call(): pl.pallas_call(run, in_specs=specs, out_specs=[LOCAL] * len(out_shape), o...  144 us
    ppermute x14, waiting for transfers between devices, advance(): self.pieces.append(lax.ppermute(value, 'dp', self.route))  101 us
    ppermute x14, waiting for transfers between devices, advance(): value = lax.ppermute(self.value, 'dp', self.route).astype(jnp.float32)  81.4 us
    unnamed x199, local copies, waits for them, and re-layouts  35.6 us
    convert_element_type x12, other arithmetic, advance(): self.value = value.astype(jnp.bfloat16) if self.step < self.chips else value  30.9 us
    ppermute x14, starting transfers between devices, advance(): self.pieces.append(lax.ppermute(value, 'dp', self.route))  29.8 us
    ppermute x14, starting transfers between devices, advance(): value = lax.ppermute(self.value, 'dp', self.route).astype(jnp.float32)  22 us
    ppermute x7, starting transfers between devices, one_way(): return lax.ppermute(value, 'section', [(source, 1 - source)])  15.9 us
  transfers between devices with their start and end apart: 61, of which 28 were waited for; matrix products, arithmetic and copies ran while one was open for 13% of the time, Pallas kernels for 22%

profile of v7, /device:TPU:0, one launch (start us, length us, event | category | flops | bytes accessed | tf_op | source)
XLA Modules:
  0.0 537.7 jit_solution(5268877833083798841)
XLA Ops:
  35.1 6.8 %collective-permute-done.16.refs_0_ = bf16[2,288,1024]{2,1,0:T(8,128)(2,1)S(1)} collective-permute-done((bf16[2,288,1024]{2,1,0:T(8,128)(2,1)S(1)}, bf16[2,288,1024]{2,1,0:T(8,128)(2,1)S(1)}, u32[]{:S(2)}, u32[]{:S(2)}) %collective-permute-start.16) | collective-permute-done | bytes 1179680 | tf_op jit(solution)/shard_map/ppermute | solution.py:94
  45.0 6.1 %collective-permute-done.2.refs_0_ = bf16[2,208,1024]{2,1,0:T(8,128)(2,1)} collective-permute-done((bf16[2,208,1024]{2,1,0:T(8,128)(2,1)}, bf16[2,208,1024]{2,1,0:T(8,128)(2,1)}, u32[]{:S(2)}, u32[]{:S(2)}) %collective-permute-start.2) | collective-permute-done | bytes 852000 | tf_op jit(solution)/shard_map/ppermute | solution.py:94
  53.2 10.5 %collective-permute-done.17.refs_2_ = bf16[2,288,1024]{2,1,0:T(8,128)(2,1)S(1)} collective-permute-done((bf16[2,288,1024]{2,1,0:T(8,128)(2,1)}, bf16[2,288,1024]{2,1,0:T(8,128)(2,1)S(1)}, u32[]{:S(2)}, u32[]{:S(2)}) %collective-permute-start.17) | collective-permute-done | bytes 1179680 | tf_op jit(solution)/shard_map/ppermute | solution.py:94
  65.8 7.2 %collective-permute-done.3.refs_0_ = bf16[2,208,1024]{2,1,0:T(8,128)(2,1)} collective-permute-done((bf16[2,208,1024]{2,1,0:T(8,128)(2,1)}, bf16[2,208,1024]{2,1,0:T(8,128)(2,1)}, u32[]{:S(2)}, u32[]{:S(2)}) %collective-permute-start.3) | collective-permute-done | bytes 852000 | tf_op jit(solution)/shard_map/ppermute | solution.py:94
  75.0 10.6 %collective-permute-done.18.refs_3_ = bf16[2,288,1024]{2,1,0:T(8,128)(2,1)} collective-permute-done((bf16[2,288,1024]{2,1,0:T(8,128)(2,1)S(1)}, bf16[2,288,1024]{2,1,0:T(8,128)(2,1)}, u32[]{:S(2)}, u32[]{:S(2)}) %collective-permute-start.18) | collective-permute-done | bytes 1179680 | tf_op jit(solution)/shard_map/ppermute | solution.py:94
  87.6 7.1 %collective-permute-done.4.refs_0_ = bf16[2,208,1024]{2,1,0:T(8,128)(2,1)} collective-permute-done((bf16[2,208,1024]{2,1,0:T(8,128)(2,1)}, bf16[2,208,1024]{2,1,0:T(8,128)(2,1)}, u32[]{:S(2)}, u32[]{:S(2)}) %collective-permute-start.4) | collective-permute-done | bytes 852000 | tf_op jit(solution)/shard_map/ppermute | solution.py:94
  96.8 10.5 %collective-permute-done.19.refs_4_ = bf16[2,288,1024]{2,1,0:T(8,128)(2,1)S(1)} collective-permute-done((bf16[2,288,1024]{2,1,0:T(8,128)(2,1)}, bf16[2,288,1024]{2,1,0:T(8,128)(2,1)S(1)}, u32[]{:S(2)}, u32[]{:S(2)}) %collective-permute-start.19) | collective-permute-done | bytes 1179680 | tf_op jit(solution)/shard_map/ppermute | solution.py:94
  109.3 7.2 %collective-permute-done.5.refs_0_ = bf16[2,208,1024]{2,1,0:T(8,128)(2,1)} collective-permute-done((bf16[2,208,1024]{2,1,0:T(8,128)(2,1)}, bf16[2,208,1024]{2,1,0:T(8,128)(2,1)}, u32[]{:S(2)}, u32[]{:S(2)}) %collective-permute-start.5) | collective-permute-done | bytes 852000 | tf_op jit(solution)/shard_map/ppermute | solution.py:94
  119.0 10.0 %collective-permute-done.20.refs_5_ = bf16[2,288,1024]{2,1,0:T(8,128)(2,1)} collective-permute-done((bf16[2,288,1024]{2,1,0:T(8,128)(2,1)S(1)}, bf16[2,288,1024]{2,1,0:T(8,128)(2,1)}, u32[]{:S(2)}, u32[]{:S(2)}) %collective-permute-start.20) | collective-permute-done | bytes 1179680 | tf_op jit(solution)/shard_map/ppermute | solution.py:94
  131.4 6.8 %collective-permute-done.6.refs_0_ = bf16[2,208,1024]{2,1,0:T(8,128)(2,1)} collective-permute-done((bf16[2,208,1024]{2,1,0:T(8,128)(2,1)}, bf16[2,208,1024]{2,1,0:T(8,128)(2,1)}, u32[]{:S(2)}, u32[]{:S(2)}) %collective-permute-start.6) | collective-permute-done | bytes 852000 | tf_op jit(solution)/shard_map/ppermute | solution.py:94
  141.6 9.3 %collective-permute-done.21.refs_6_ = bf16[2,288,1024]{2,1,0:T(8,128)(2,1)} collective-permute-done((bf16[2,288,1024]{2,1,0:T(8,128)(2,1)}, bf16[2,288,1024]{2,1,0:T(8,128)(2,1)}, u32[]{:S(2)}, u32[]{:S(2)}) %collective-permute-start.21) | collective-permute-done | bytes 1179680 | tf_op jit(solution)/shard_map/ppermute | solution.py:94
  223.0 6.1 %shard_map.258 = (f32[256,1024]{1,0:T(8,128)S(1)}, bf16[256,1024]{1,0:T(8,128)(2,1)S(1)}, bf16[1024,256]{1,0:T(8,128)(2,1)S(1)}, bf16[1024,256]{1,0:T(8,128)(2,1...) custom-call(s32[1]{0:T(128)} %bitcast.refs_0_, ...), custom_call_target="tpu_custom_call" | custom-call | flops 4294967296 | bytes 17825792 | tf_op jit(solution)/shard_map/pallas_call | solution.py:181
  235.1 8.1 %shard_map.264 = (f32[256,1024]{1,0:T(8,128)S(1)}, bf16[256,1024]{1,0:T(8,128)(2,1)S(1)}, bf16[256,3072]{1,0:T(8,128)(2,1)}, bf16[256,3072]{1,0:T(8,128)(2,1)}, ...) custom-call(s32[1]{0:T(128)} %constant.161.clone.1.refs_0_, f32[256,1024]{1,0:T(8,128)S(1)} %get-tuple-element.90.refs_1_, ...), custom_call_target="tpu_custom_call" | custom-call | flops 4831838208 | bytes 28835840 | tf_op jit(solution)/shard_map/pallas_call | solution.py:181
  243.3 13.0 %shard_map.265 = (bf16[256,2048]{1,0:T(8,128)(2,1)}, bf16[256,2048]{1,0:T(8,128)(2,1)}, bf16[256,1024]{1,0:T(8,128)(2,1)S(1)}, f32[1,1024]{1,0:T(1,128)}, f32[1,128]{1,0:T(1,128)}, /*index=5*/f32[1,128]{1,0:T(1,128)}) custom-call(s32[1]{0:T(128)} %bitcast.refs_0_, bf16[256,1024]{1,0:T(8,128)(2,1)S(1)} %get-tuple-element.93.refs_1_, ...), custom_call_target="tpu_custom_call" | custom-call | flops 5905580032 | bytes 23068672 | tf_op jit(solution)/shard_map/pallas_call | solution.py:181
  262.2 6.1 %shard_map.262 = (f32[256,1024]{1,0:T(8,128)S(1)}, bf16[256,1024]{1,0:T(8,128)(2,1)S(1)}, bf16[1024,256]{1,0:T(8,128)(2,1)S(1)}, bf16[1024,256]{1,0:T(8,128)(2,1...) custom-call(s32[1]{0:T(128)} %bitcast.refs_0_, ...), custom_call_target="tpu_custom_call" | custom-call | flops 4294967296 | bytes 17825792 | tf_op jit(solution)/shard_map/pallas_call | solution.py:181
  275.3 8.1 %shard_map.268 = (f32[256,1024]{1,0:T(8,128)S(1)}, bf16[256,1024]{1,0:T(8,128)(2,1)S(1)}, bf16[256,3072]{1,0:T(8,128)(2,1)}, bf16[256,3072]{1,0:T(8,128)(2,1)}, ...) custom-call(s32[1]{0:T(128)} %constant.161.clone.1.refs_0_, f32[256,1024]{1,0:T(8,128)S(1)} %get-tuple-element.102.refs_1_, ...), custom_call_target="tpu_custom_call" | custom-call | flops 4831838208 | bytes 28835840 | tf_op jit(solution)/shard_map/pallas_call | solution.py:181
  283.4 13.1 %shard_map.269 = (bf16[256,2048]{1,0:T(8,128)(2,1)}, bf16[256,2048]{1,0:T(8,128)(2,1)}, bf16[256,1024]{1,0:T(8,128)(2,1)S(1)}, f32[1,1024]{1,0:T(1,128)}, f32[1,128]{1,0:T(1,128)}, /*index=5*/f32[1,128]{1,0:T(1,128)}) custom-call(s32[1]{0:T(128)} %bitcast.refs_0_, bf16[256,1024]{1,0:T(8,128)(2,1)S(1)} %get-tuple-element.105.refs_1_, ...), custom_call_target="tpu_custom_call" | custom-call | flops 5905580032 | bytes 23068672 | tf_op jit(solution)/shard_map/pallas_call | solution.py:181
  298.0 6.2 %shard_map.266 = (f32[256,1024]{1,0:T(8,128)S(1)}, bf16[256,1024]{1,0:T(8,128)(2,1)S(1)}, bf16[256,3072]{1,0:T(8,128)(2,1)S(1)}, bf16[256,3072]{1,0:T(8,128)(2,1...) custom-call(s32[1]{0:T(128)} %bitcast.refs_0_, f32[256,1024]{1,0:T(8,128)S(1)} %get-tuple-element.90.refs_1_, ...), custom_call_target="tpu_custom_call" | custom-call | flops 4831838208 | bytes 28835840 | tf_op jit(solution)/shard_map/pallas_call | solution.py:181
  310.3 12.7 %shard_map.267 = (bf16[256,2048]{1,0:T(8,128)(2,1)S(1)}, bf16[256,2048]{1,0:T(8,128)(2,1)S(1)}, bf16[256,1024]{1,0:T(8,128)(2,1)S(1)}, f32[1,1024]{1,0:T(1,128)S...) custom-call(s32[1]{0:T(128)} %bitcast.refs_0_, bf16[256,1024]{1,0:T(8,128)(2,1)S(1)} %get-tuple-element.99.refs_1_.refs_9_, ...), custom_call_target="tpu_custom_call" | custom-call | flops 5905580032 | bytes 23068672 | tf_op jit(solution)/shard_map/pallas_call | solution.py:181
  324.0 6.1 %shard_map.270 = (f32[256,1024]{1,0:T(8,128)S(1)}, bf16[256,1024]{1,0:T(8,128)(2,1)S(1)}, bf16[256,3072]{1,0:T(8,128)(2,1)S(1)}, bf16[256,3072]{1,0:T(8,128)(2,1...) custom-call(s32[1]{0:T(128)} %bitcast.refs_0_, f32[256,1024]{1,0:T(8,128)S(1)} %get-tuple-element.102.refs_1_, ...), custom_call_target="tpu_custom_call" | custom-call | flops 4831838208 | bytes 28835840 | tf_op jit(solution)/shard_map/pallas_call | solution.py:181
  330.2 9.1 %shard_map.271 = (bf16[8,2,240,1024]{3,2,1,0:T(8,128)(2,1)S(1)}, bf16[8,2,240,1024]{3,2,1,0:T(8,128)(2,1)S(1)}) custom-call(s32[18]{0:T(128)S(1)} %get-tuple-element.198.refs_0_, bf16[1024,256]{1,0:T(8,128)(2,1)S(1)} %copy-done.70, bf16[1024,256]{1,0:T(8,128)(2,1)S(1)} %copy-done.76, bf16[256,3072]{1,0:T(8,128)(2,1)S(1)} %copy-done.54, ...), custom_call_target="tpu_custom_call" | custom-call | flops 8053063680 | bytes 19922944 | tf_op jit(solution)/shard_map/pallas_call | solution.py:181
  339.7 12.5 %shard_map.272 = (bf16[256,2048]{1,0:T(8,128)(2,1)S(1)}, bf16[256,2048]{1,0:T(8,128)(2,1)S(1)}, bf16[256,1024]{1,0:T(8,128)(2,1)S(1)}, f32[1,1024]{1,0:T(1,128)S...) custom-call(s32[1]{0:T(128)} %bitcast.refs_0_, bf16[256,1024]{1,0:T(8,128)(2,1)S(1)} %get-tuple-element.111.refs_1_.refs_10_, ...), custom_call_target="tpu_custom_call" | custom-call | flops 5905580032 | bytes 23068672 | tf_op jit(solution)/shard_map/pallas_call | solution.py:181
  354.2 8.9 %shard_map.273 = (bf16[8,2,240,1024]{3,2,1,0:T(8,128)(2,1)S(1)}, bf16[8,2,240,1024]{3,2,1,0:T(8,128)(2,1)S(1)}) custom-call(s32[18]{0:T(128)S(1)} %get-tuple-element.198.refs_0_, bf16[1024,256]{1,0:T(8,128)(2,1)S(1)} %copy-done.68, bf16[1024,256]{1,0:T(8,128)(2,1)S(1)} %copy-done.72, bf16[256,2048]{1,0:T(8,128)(2,1)S(1)} %get-tuple-element.123.refs_11_.refs_3_, ...), custom_call_target="tpu_custom_call" | custom-call | flops 8053063680 | bytes 19922944 | tf_op jit(solution)/shard_map/pallas_call | solution.py:181
  365.0 12.5 %collective-permute-done.53 = bf16[2,240,1024]{2,1,0:T(8,128)(2,1)S(1)} collective-permute-done((bf16[2,240,1024]{2,1,0:T(8,128)(2,1)S(1)}, bf16[2,240,1024]{2,1,0:T(8,128)(2,1)S(1)}, u32[]{:S(2)}, u32[]{:S(2)}) %collective-permute-start.53) | collective-permute-done | bytes 983072 | tf_op jit(solution)/shard_map/ppermute | solution.py:122
  388.8 6.2 %collective-permute-done.54 = bf16[2,240,1024]{2,1,0:T(8,128)(2,1)} collective-permute-done((bf16[2,240,1024]{2,1,0:T(8,128)(2,1)}, bf16[2,240,1024]{2,1,0:T(8,128)(2,1)}, u32[]{:S(2)}, u32[]{:S(2)}) %collective-permute-start.54) | collective-permute-done | bytes 983072 | tf_op jit(solution)/shard_map/ppermute | solution.py:122
  398.7 6.7 %collective-permute-done.45 = bf16[2,240,1024]{2,1,0:T(8,128)(2,1)} collective-permute-done((bf16[2,240,1024]{2,1,0:T(8,128)(2,1)}, bf16[2,240,1024]{2,1,0:T(8,128)(2,1)}, u32[]{:S(2)}, u32[]{:S(2)}) %collective-permute-start.45) | collective-permute-done | bytes 983072 | tf_op jit(solution)/shard_map/ppermute | solution.py:122
  409.9 6.2 %collective-permute-done.55 = bf16[2,240,1024]{2,1,0:T(8,128)(2,1)S(1)} collective-permute-done((bf16[2,240,1024]{2,1,0:T(8,128)(2,1)S(1)}, bf16[2,240,1024]{2,1,0:T(8,128)(2,1)S(1)}, u32[]{:S(2)}, u32[]{:S(2)}) %collective-permute-start.55) | collective-permute-done | bytes 983072 | tf_op jit(solution)/shard_map/ppermute | solution.py:122
  419.4 7.2 %collective-permute-done.46 = bf16[2,240,1024]{2,1,0:T(8,128)(2,1)S(1)} collective-permute-done((bf16[2,240,1024]{2,1,0:T(8,128)(2,1)S(1)}, bf16[2,240,1024]{2,1,0:T(8,128)(2,1)S(1)}, u32[]{:S(2)}, u32[]{:S(2)}) %collective-permute-start.46) | collective-permute-done | bytes 983072 | tf_op jit(solution)/shard_map/ppermute | solution.py:122
  441.2 6.5 %collective-permute-done.47 = bf16[2,240,1024]{2,1,0:T(8,128)(2,1)S(1)} collective-permute-done((bf16[2,240,1024]{2,1,0:T(8,128)(2,1)}, bf16[2,240,1024]{2,1,0:T(8,128)(2,1)S(1)}, u32[]{:S(2)}, u32[]{:S(2)}) %collective-permute-start.47) | collective-permute-done | bytes 983072 | tf_op jit(solution)/shard_map/ppermute | solution.py:122
  451.9 6.3 %collective-permute-done.57 = bf16[2,240,1024]{2,1,0:T(8,128)(2,1)S(1)} collective-permute-done((bf16[2,240,1024]{2,1,0:T(8,128)(2,1)S(1)}, bf16[2,240,1024]{2,1,0:T(8,128)(2,1)S(1)}, u32[]{:S(2)}, u32[]{:S(2)}) %collective-permute-start.57) | collective-permute-done | bytes 983072 | tf_op jit(solution)/shard_map/ppermute | solution.py:122
  462.2 6.6 %collective-permute-done.48 = bf16[2,240,1024]{2,1,0:T(8,128)(2,1)S(1)} collective-permute-done((bf16[2,240,1024]{2,1,0:T(8,128)(2,1)S(1)}, bf16[2,240,1024]{2,1,0:T(8,128)(2,1)S(1)}, u32[]{:S(2)}, u32[]{:S(2)}) %collective-permute-start.48) | collective-permute-done | bytes 983072 | tf_op jit(solution)/shard_map/ppermute | solution.py:122
  520.3 7.2 %collective-permute-done.51 = bf16[2,240,1024]{2,1,0:T(8,128)(2,1)S(1)} collective-permute-done((bf16[2,240,1024]{2,1,0:T(8,128)(2,1)S(1)}, bf16[2,240,1024]{2,1,0:T(8,128)(2,1)S(1)}, u32[]{:S(2)}, u32[]{:S(2)}) %collective-permute-start.51) | collective-permute-done | bytes 983072 | tf_op jit(solution)/shard_map/ppermute | solution.py:122
  (422 shorter events, 263.9 us)
Async XLA Ops:
  20.7 21.2 %collective-permute-start.16 = (bf16[2,288,1024]{2,1,0:T(8,128)(2,1)S(1)}, bf16[2,288,1024]{2,1,0:T(8,128)(2,1)S(1)}, u32[]{:S(2)}, u32[]{:S(2)}) collective-permute-start(bf16[2,288,1024]{2,1,0:T(8,128)(2,1)S(1)} %maximum_select_fusion.refs_0_), channel_id=1, source_target_pairs={{0,4},{5,1},{4,8},{9,5},{8,12},{13,9},{12,14},{15,13},{14,10},{11,... | collective-permute-start | bytes 3538952 | tf_op jit(solution)/shard_map/ppermute | solution.py:94
  29.4 21.8 %collective-permute-start.2 = (bf16[2,208,1024]{2,1,0:T(8,128)(2,1)}, bf16[2,208,1024]{2,1,0:T(8,128)(2,1)}, u32[]{:S(2)}, u32[]{:S(2)}) collective-permute-start(bf16[2,208,1024]{2,1,0:T(8,128)(2,1)} %shard_map.246.refs_1_), channel_id=1, source_target_pairs={{0,4},{5,1},{4,8},{9,5},{8,12},{13,9},{12,14},{15,13},{14,10},{11,... | collective-permute-start | bytes 2555912 | tf_op jit(solution)/shard_map/ppermute | solution.py:94
  43.0 20.7 %collective-permute-start.17 = (bf16[2,288,1024]{2,1,0:T(8,128)(2,1)}, bf16[2,288,1024]{2,1,0:T(8,128)(2,1)S(1)}, u32[]{:S(2)}, u32[]{:S(2)}) collective-permute-start(bf16[2,288,1024]{2,1,0:T(8,128)(2,1)} %shard_map.255.refs_1_), channel_id=1, source_target_pairs={{0,4},{5,1},{4,8},{9,5},{8,12},{13,9},{12,14},{15,13},{14,10},{11,... | collective-permute-start | bytes 3538952 | tf_op jit(solution)/shard_map/ppermute | solution.py:94
  51.1 21.8 %collective-permute-start.3 = (bf16[2,208,1024]{2,1,0:T(8,128)(2,1)}, bf16[2,208,1024]{2,1,0:T(8,128)(2,1)}, u32[]{:S(2)}, u32[]{:S(2)}) collective-permute-start(bf16[2,208,1024]{2,1,0:T(8,128)(2,1)} %shard_map.247.refs_2_), channel_id=1, source_target_pairs={{0,4},{5,1},{4,8},{9,5},{8,12},{13,9},{12,14},{15,13},{14,10},{11,... | collective-permute-start | bytes 2555912 | tf_op jit(solution)/shard_map/ppermute | solution.py:94
  63.7 21.9 %collective-permute-start.18 = (bf16[2,288,1024]{2,1,0:T(8,128)(2,1)S(1)}, bf16[2,288,1024]{2,1,0:T(8,128)(2,1)}, u32[]{:S(2)}, u32[]{:S(2)}) collective-permute-start(bf16[2,288,1024]{2,1,0:T(8,128)(2,1)S(1)} %collective-permute-done.17.refs_2_), channel_id=1, source_target_pairs={{0,4},{5,1},{4,8},{9,5},{8,12},{13,9},{12,14},{15,13},{14,10},{11,... | collective-permute-start | bytes 3538952 | tf_op jit(solution)/shard_map/ppermute | solution.py:94
  72.9 21.8 %collective-permute-start.4 = (bf16[2,208,1024]{2,1,0:T(8,128)(2,1)}, bf16[2,208,1024]{2,1,0:T(8,128)(2,1)}, u32[]{:S(2)}, u32[]{:S(2)}) collective-permute-start(bf16[2,208,1024]{2,1,0:T(8,128)(2,1)} %shard_map.248.refs_3_), channel_id=1, source_target_pairs={{0,4},{5,1},{4,8},{9,5},{8,12},{13,9},{12,14},{15,13},{14,10},{11,... | collective-permute-start | bytes 2555912 | tf_op jit(solution)/shard_map/ppermute | solution.py:94
  85.6 21.7 %collective-permute-start.19 = (bf16[2,288,1024]{2,1,0:T(8,128)(2,1)}, bf16[2,288,1024]{2,1,0:T(8,128)(2,1)S(1)}, u32[]{:S(2)}, u32[]{:S(2)}) collective-permute-start(bf16[2,288,1024]{2,1,0:T(8,128)(2,1)} %collective-permute-done.18.refs_3_), channel_id=1, source_target_pairs={{0,4},{5,1},{4,8},{9,5},{8,12},{13,9},{12,14},{15,13},{14,10},{11,... | collective-permute-start | bytes 3538952 | tf_op jit(solution)/shard_map/ppermute | solution.py:94
  94.7 21.8 %collective-permute-start.5 = (bf16[2,208,1024]{2,1,0:T(8,128)(2,1)}, bf16[2,208,1024]{2,1,0:T(8,128)(2,1)}, u32[]{:S(2)}, u32[]{:S(2)}) collective-permute-start(bf16[2,208,1024]{2,1,0:T(8,128)(2,1)} %shard_map.249.refs_4_), channel_id=1, source_target_pairs={{0,4},{5,1},{4,8},{9,5},{8,12},{13,9},{12,14},{15,13},{14,10},{11,... | collective-permute-start | bytes 2555912 | tf_op jit(solution)/shard_map/ppermute | solution.py:94
  107.2 21.9 %collective-permute-start.20 = (bf16[2,288,1024]{2,1,0:T(8,128)(2,1)S(1)}, bf16[2,288,1024]{2,1,0:T(8,128)(2,1)}, u32[]{:S(2)}, u32[]{:S(2)}) collective-permute-start(bf16[2,288,1024]{2,1,0:T(8,128)(2,1)S(1)} %collective-permute-done.19.refs_4_), channel_id=1, source_target_pairs={{0,4},{5,1},{4,8},{9,5},{8,12},{13,9},{12,14},{15,13},{14,10},{11,... | collective-permute-start | bytes 3538952 | tf_op jit(solution)/shard_map/ppermute | solution.py:94
  116.5 21.8 %collective-permute-start.6 = (bf16[2,208,1024]{2,1,0:T(8,128)(2,1)}, bf16[2,208,1024]{2,1,0:T(8,128)(2,1)}, u32[]{:S(2)}, u32[]{:S(2)}) collective-permute-start(bf16[2,208,1024]{2,1,0:T(8,128)(2,1)} %shard_map.250.refs_5_), channel_id=1, source_target_pairs={{0,4},{5,1},{4,8},{9,5},{8,12},{13,9},{12,14},{15,13},{14,10},{11,... | collective-permute-start | bytes 2555912 | tf_op jit(solution)/shard_map/ppermute | solution.py:94
  118.5 19.7 %collective-permute-start.8 = (bf16[2,208,1024]{2,1,0:T(8,128)(2,1)}, bf16[2,208,1024]{2,1,0:T(8,128)(2,1)}, u32[]{:S(2)}, u32[]{:S(2)}) collective-permute-start(bf16[2,208,1024]{2,1,0:T(8,128)(2,1)} %shard_map.246.refs_1_), channel_id=1, source_target_pairs={{0,1},{1,0},{2,3},{3,2},{4,5},{5,4},{6,7},{7,6},{8,9},{9,8},{10,11... | collective-permute-start | bytes 2555912 | tf_op jit(solution)/shard_map/ppermute | solution.py:103
  118.5 20.2 %collective-permute-start.9 = (bf16[2,208,1024]{2,1,0:T(8,128)(2,1)}, bf16[2,208,1024]{2,1,0:T(8,128)(2,1)}, u32[]{:S(2)}, u32[]{:S(2)}) collective-permute-start(bf16[2,208,1024]{2,1,0:T(8,128)(2,1)} %shard_map.247.refs_2_), channel_id=1, source_target_pairs={{0,1},{1,0},{2,3},{3,2},{4,5},{5,4},{6,7},{7,6},{8,9},{9,8},{10,11... | collective-permute-start | bytes 2555912 | tf_op jit(solution)/shard_map/ppermute | solution.py:103
  129.1 21.8 %collective-permute-start.21 = (bf16[2,288,1024]{2,1,0:T(8,128)(2,1)}, bf16[2,288,1024]{2,1,0:T(8,128)(2,1)}, u32[]{:S(2)}, u32[]{:S(2)}) collective-permute-start(bf16[2,288,1024]{2,1,0:T(8,128)(2,1)} %collective-permute-done.20.refs_5_), channel_id=1, source_target_pairs={{0,4},{5,1},{4,8},{9,5},{8,12},{13,9},{12,14},{15,13},{14,10},{11,... | collective-permute-start | bytes 3538952 | tf_op jit(solution)/shard_map/ppermute | solution.py:94
  131.4 23.2 %collective-permute-start.23 = (bf16[2,288,1024]{2,1,0:T(8,128)(2,1)}, bf16[2,288,1024]{2,1,0:T(8,128)(2,1)}, u32[]{:S(2)}, u32[]{:S(2)}) collective-permute-start(bf16[2,288,1024]{2,1,0:T(8,128)(2,1)} %shard_map.255.refs_1_), channel_id=1, source_target_pairs={{0,1},{1,0},{2,3},{3,2},{4,5},{5,4},{6,7},{7,6},{8,9},{9,8},{10,11... | collective-permute-start | bytes 3538952 | tf_op jit(solution)/shard_map/ppermute | solution.py:103
  138.7 21.1 %collective-permute-start.7 = (bf16[2,208,1024]{2,1,0:T(8,128)(2,1)}, bf16[2,208,1024]{2,1,0:T(8,128)(2,1)S(1)}, u32[]{:S(2)}, u32[]{:S(2)}) collective-permute-start(bf16[2,208,1024]{2,1,0:T(8,128)(2,1)} %shard_map.251.refs_6_), channel_id=1, source_target_pairs={{0,4},{5,1},{4,8},{9,5},{8,12},{13,9},{12,14},{15,13},{14,10},{11,... | collective-permute-start | bytes 2555912 | tf_op jit(solution)/shard_map/ppermute | solution.py:94
  150.9 21.8 %collective-permute-start.22 = (bf16[2,288,1024]{2,1,0:T(8,128)(2,1)}, bf16[2,288,1024]{2,1,0:T(8,128)(2,1)}, u32[]{:S(2)}, u32[]{:S(2)}) collective-permute-start(bf16[2,288,1024]{2,1,0:T(8,128)(2,1)} %collective-permute-done.21.refs_6_), channel_id=1, source_target_pairs={{0,4},{5,1},{4,8},{9,5},{8,12},{13,9},{12,14},{15,13},{14,10},{11,... | collective-permute-start | bytes 3538952 | tf_op jit(solution)/shard_map/ppermute | solution.py:94
  163.9 26.4 %collective-permute-start.25 = (bf16[2,288,1024]{2,1,0:T(8,128)(2,1)}, bf16[2,288,1024]{2,1,0:T(8,128)(2,1)}, u32[]{:S(2)}, u32[]{:S(2)}) collective-permute-start(bf16[2,288,1024]{2,1,0:T(8,128)(2,1)} %collective-permute-done.18.refs_3_), channel_id=1, source_target_pairs={{0,1},{1,0},{2,3},{3,2},{4,5},{5,4},{6,7},{7,6},{8,9},{9,8},{10,11... | collective-permute-start | bytes 3538952 | tf_op jit(solution)/shard_map/ppermute | solution.py:103
  165.4 24.9 %collective-permute-start.26 = (bf16[2,288,1024]{2,1,0:T(8,128)(2,1)}, bf16[2,288,1024]{2,1,0:T(8,128)(2,1)}, u32[]{:S(2)}, u32[]{:S(2)}) collective-permute-start(bf16[2,288,1024]{2,1,0:T(8,128)(2,1)} %copy-done.11), channel_id=1, source_target_pairs={{0,1},{1,0},{2,3},{3,2},{4,5},{5,4},{6,7},{7,6},{8,9},{9,8},{10,11... | collective-permute-start | bytes 3538952 | tf_op jit(solution)/shard_map/ppermute | solution.py:103
  166.3 24.0 %collective-permute-start.27 = (bf16[2,288,1024]{2,1,0:T(8,128)(2,1)}, bf16[2,288,1024]{2,1,0:T(8,128)(2,1)}, u32[]{:S(2)}, u32[]{:S(2)}) collective-permute-start(bf16[2,288,1024]{2,1,0:T(8,128)(2,1)} %collective-permute-done.20.refs_5_), channel_id=1, source_target_pairs={{0,1},{1,0},{2,3},{3,2},{4,5},{5,4},{6,7},{7,6},{8,9},{9,8},{10,11... | collective-permute-start | bytes 3538952 | tf_op jit(solution)/shard_map/ppermute | solution.py:103
  167.7 22.6 %collective-permute-start.28 = (bf16[2,288,1024]{2,1,0:T(8,128)(2,1)}, bf16[2,288,1024]{2,1,0:T(8,128)(2,1)}, u32[]{:S(2)}, u32[]{:S(2)}) collective-permute-start(bf16[2,288,1024]{2,1,0:T(8,128)(2,1)} %collective-permute-done.21.refs_6_), channel_id=1, source_target_pairs={{0,1},{1,0},{2,3},{3,2},{4,5},{5,4},{6,7},{7,6},{8,9},{9,8},{10,11... | collective-permute-start | bytes 3538952 | tf_op jit(solution)/shard_map/ppermute | solution.py:103
  201.5 21.5 %collective-permute-start.30 = (bf16[256,1024]{1,0:T(8,128)(2,1)S(1)}, bf16[256,1024]{1,0:T(8,128)(2,1)S(1)}, u32[]{:S(2)}, u32[]{:S(2)}) collective-permute-start(bf16[256,1024]{1,0:T(8,128)(2,1)S(1)} %shard_map.257), channel_id=1, source_target_pairs={{0,16},{1,17},{2,18},{3,19},{4,20},{5,21},{6,22},{7,23},{8,24},{9,... | collective-permute-start | bytes 1572872 | tf_op jit(solution)/shard_map/ppermute | solution.py:28
  221.3 36.3 %collective-permute-start.32 = (bf16[256,1024]{1,0:T(8,128)(2,1)S(1)}, bf16[256,1024]{1,0:T(8,128)(2,1)S(1)}, u32[]{:S(2)}, u32[]{:S(2)}) collective-permute-start(bf16[256,1024]{1,0:T(8,128)(2,1)S(1)} %shard_map.261), channel_id=1, source_target_pairs={{0,16},{1,17},{2,18},{3,19},{4,20},{5,21},{6,22},{7,23},{8,24},{9,... | collective-permute-start | bytes 1572872 | tf_op jit(solution)/shard_map/ppermute | solution.py:28
  256.3 41.6 %collective-permute-start.33 = (bf16[256,1024]{1,0:T(8,128)(2,1)S(1)}, bf16[256,1024]{1,0:T(8,128)(2,1)S(1)}, u32[]{:S(2)}, u32[]{:S(2)}) collective-permute-start(bf16[256,1024]{1,0:T(8,128)(2,1)S(1)} %get-tuple-element.98), channel_id=1, source_target_pairs={{16,0},{17,1},{18,2},{19,3},{20,4},{21,5},{22,6},{23,7},{24,8},{25... | collective-permute-start | bytes 1572872 | tf_op jit(solution)/shard_map/ppermute | solution.py:28
  296.5 27.4 %collective-permute-start.34 = (bf16[256,1024]{1,0:T(8,128)(2,1)S(1)}, bf16[256,1024]{1,0:T(8,128)(2,1)S(1)}, u32[]{:S(2)}, u32[]{:S(2)}) collective-permute-start(bf16[256,1024]{1,0:T(8,128)(2,1)S(1)} %get-tuple-element.110), channel_id=1, source_target_pairs={{16,0},{17,1},{18,2},{19,3},{20,4},{21,5},{22,6},{23,7},{24,8},{25... | collective-permute-start | bytes 1572872 | tf_op jit(solution)/shard_map/ppermute | solution.py:28
  383.5 21.9 %collective-permute-start.45 = (bf16[2,240,1024]{2,1,0:T(8,128)(2,1)}, bf16[2,240,1024]{2,1,0:T(8,128)(2,1)}, u32[]{:S(2)}, u32[]{:S(2)}) collective-permute-start(bf16[2,240,1024]{2,1,0:T(8,128)(2,1)} %fusion.13), channel_id=1, source_target_pairs={{0,4},{5,1},{4,8},{9,5},{8,12},{13,9},{12,14},{15,13},{14,10},{11,... | collective-permute-start | bytes 2949128 | tf_op jit(solution)/shard_map/ppermute | solution.py:122
  387.8 21.4 %collective-permute-start.37 = (f32[1,2306]{1,0:T(1,128)S(1)}, f32[1,2306]{1,0:T(1,128)S(1)}, u32[]{:S(2)}, u32[]{:S(2)}) collective-permute-start(f32[1,2306]{1,0:T(1,128)S(1)} %concatenate.82), channel_id=1, source_target_pairs={{0,3},{1,0},{2,1},{3,2},{4,7},{5,4},{6,5},{7,6},{8,11},{9,8},{10,9... | collective-permute-start | bytes 27680 | tf_op jit(solution)/shard_map/ppermute | solution.py:62
  388.1 21.2 %collective-permute-start.36 = (f32[1,2306]{1,0:T(1,128)S(1)}, f32[1,2306]{1,0:T(1,128)S(1)}, u32[]{:S(2)}, u32[]{:S(2)}) collective-permute-start(f32[1,2306]{1,0:T(1,128)S(1)} %concatenate.82), channel_id=1, source_target_pairs={{0,2},{1,3},{2,0},{3,1},{4,6},{5,7},{6,4},{7,5},{8,10},{9,11},{10,... | collective-permute-start | bytes 27680 | tf_op jit(solution)/shard_map/ppermute | solution.py:62
  388.6 20.7 %collective-permute-start.35 = (f32[1,2306]{1,0:T(1,128)S(1)}, f32[1,2306]{1,0:T(1,128)S(1)}, u32[]{:S(2)}, u32[]{:S(2)}) collective-permute-start(f32[1,2306]{1,0:T(1,128)S(1)} %concatenate.82), channel_id=1, source_target_pairs={{0,1},{1,2},{2,3},{3,0},{4,5},{5,6},{6,7},{7,4},{8,9},{9,10},{10,1... | collective-permute-start | bytes 27680 | tf_op jit(solution)/shard_map/ppermute | solution.py:62
  418.2 19.1 %collective-permute-start.56 = (bf16[2,240,1024]{2,1,0:T(8,128)(2,1)S(1)}, bf16[2,240,1024]{2,1,0:T(8,128)(2,1)}, u32[]{:S(2)}, u32[]{:S(2)}) collective-permute-start(bf16[2,240,1024]{2,1,0:T(8,128)(2,1)S(1)} %fusion.3), channel_id=1, source_target_pairs={{0,4},{5,1},{4,8},{9,5},{8,12},{13,9},{12,14},{15,13},{14,10},{11,... | collective-permute-start | bytes 2949128 | tf_op jit(solution)/shard_map/ppermute | solution.py:122
  430.8 20.5 %collective-permute-start.40 = (f32[1,2306]{1,0:T(1,128)S(1)}, f32[1,2306]{1,0:T(1,128)S(1)}, u32[]{:S(2)}, u32[]{:S(2)}) collective-permute-start(f32[1,2306]{1,0:T(1,128)S(1)} %copy-done.83), channel_id=1, source_target_pairs={{0,12},{1,13},{2,14},{3,15},{4,0},{5,1},{6,2},{7,3},{8,4},{9,5},{1... | collective-permute-start | bytes 27680 | tf_op jit(solution)/shard_map/ppermute | solution.py:62
  482.7 21.7 %collective-permute-start.59 = (bf16[2,240,1024]{2,1,0:T(8,128)(2,1)}, bf16[2,240,1024]{2,1,0:T(8,128)(2,1)S(1)}, u32[]{:S(2)}, u32[]{:S(2)}) collective-permute-start(bf16[2,240,1024]{2,1,0:T(8,128)(2,1)} %fusion), channel_id=1, source_target_pairs={{0,4},{5,1},{4,8},{9,5},{8,12},{13,9},{12,14},{15,13},{14,10},{11,... | collective-permute-start | bytes 2949128 | tf_op jit(solution)/shard_map/ppermute | solution.py:122
  494.7 24.4 %collective-permute-start.42 = (bf16[1,256,1024]{2,1,0:T(8,128)(2,1)S(1)}, bf16[1,256,1024]{2,1,0:T(8,128)(2,1)S(1)}, u32[]{:S(2)}, u32[]{:S(2)}) collective-permute-start(bf16[1,256,1024]{2,1,0:T(8,128)(2,1)S(1)} %bitcast.212), channel_id=1, source_target_pairs={{0,16},{1,17},{2,18},{3,19},{4,20},{5,21},{6,22},{7,23},{8,24},{9,... | collective-permute-start | bytes 1572872 | tf_op jit(solution)/shard_map/ppermute | solution.py:28
  (125 other events, 1101.9 us)

commit v8 on v7

--- a/solution.py
+++ b/solution.py
@@ -21,7 +21,7 @@
 GAIN_ROWS = 16
 HOLD_FLOPS = 4400000000
 SMALL_LAST = True
-VMEM_GRANT = 8
+VMEM_GRANT = 9
 
 
 def one_way(value, source):

time: 544 us -> 542 us (level)
    unnamed x199 -> x201, local copies, waits for them, and re-layouts: 35.6 us -> 33.4 us
where the time goes in v8:
time: 542 us; the launch traced here: 536 us
  waiting for transfers between devices  184 us (34%)
  Pallas kernels  155 us (29%)
  starting transfers between devices  77.5 us (14%)
  local copies, waits for them, and re-layouts  57.3 us (11%)
  other arithmetic  55.8 us (10%)
  between operations  6.29 us (1%)
    pallas_call x18, Pallas kernels, flat_call(): pl.pallas_call(run, in_specs=specs, out_specs=[LOCAL] * len(out_shape), o...  143 us
    ppermute x14, waiting for transfers between devices, advance(): self.pieces.append(lax.ppermute(value, 'dp', self.route))  101 us
    ppermute x14, waiting for transfers between devices, advance(): value = lax.ppermute(self.value, 'dp', self.route).astype(jnp.float32)  82.7 us
    unnamed x201, local copies, waits for them, and re-layouts  33.4 us
    convert_element_type x12, other arithmetic, advance(): self.value = value.astype(jnp.bfloat16) if self.step < self.chips else value  30.2 us
    ppermute x14, starting transfers between devices, advance(): self.pieces.append(lax.ppermute(value, 'dp', self.route))  29.8 us
    ppermute x14, starting transfers between devices, advance(): value = lax.ppermute(self.value, 'dp', self.route).astype(jnp.float32)  22.1 us
    ppermute x7, starting transfers between devices, one_way(): return lax.ppermute(value, 'section', [(source, 1 - source)])  16 us
  transfers between devices with their start and end apart: 61, of which 28 were waited for; matrix products, arithmetic and copies ran while one was open for 13% of the time, Pallas kernels for 22%

profile of v8, /device:TPU:0, one launch (start us, length us, event | category | flops | bytes accessed | tf_op | source)
XLA Modules:
  0.0 535.5 jit_solution(14898766956614005884)
XLA Ops:
  35.2 6.8 %collective-permute-done.16.refs_0_ = bf16[2,288,1024]{2,1,0:T(8,128)(2,1)S(1)} collective-permute-done((bf16[2,288,1024]{2,1,0:T(8,128)(2,1)S(1)}, bf16[2,288,1024]{2,1,0:T(8,128)(2,1)S(1)}, u32[]{:S(2)}, u32[]{:S(2)}) %collective-permute-start.16) | collective-permute-done | bytes 1179680 | tf_op jit(solution)/shard_map/ppermute | solution.py:94
  45.1 6.1 %collective-permute-done.2.refs_0_ = bf16[2,208,1024]{2,1,0:T(8,128)(2,1)} collective-permute-done((bf16[2,208,1024]{2,1,0:T(8,128)(2,1)}, bf16[2,208,1024]{2,1,0:T(8,128)(2,1)}, u32[]{:S(2)}, u32[]{:S(2)}) %collective-permute-start.2) | collective-permute-done | bytes 852000 | tf_op jit(solution)/shard_map/ppermute | solution.py:94
  53.3 10.5 %collective-permute-done.17.refs_2_ = bf16[2,288,1024]{2,1,0:T(8,128)(2,1)S(1)} collective-permute-done((bf16[2,288,1024]{2,1,0:T(8,128)(2,1)}, bf16[2,288,1024]{2,1,0:T(8,128)(2,1)S(1)}, u32[]{:S(2)}, u32[]{:S(2)}) %collective-permute-start.17) | collective-permute-done | bytes 1179680 | tf_op jit(solution)/shard_map/ppermute | solution.py:94
  65.8 7.2 %collective-permute-done.3.refs_0_ = bf16[2,208,1024]{2,1,0:T(8,128)(2,1)} collective-permute-done((bf16[2,208,1024]{2,1,0:T(8,128)(2,1)}, bf16[2,208,1024]{2,1,0:T(8,128)(2,1)}, u32[]{:S(2)}, u32[]{:S(2)}) %collective-permute-start.3) | collective-permute-done | bytes 852000 | tf_op jit(solution)/shard_map/ppermute | solution.py:94
  75.1 10.6 %collective-permute-done.18.refs_3_ = bf16[2,288,1024]{2,1,0:T(8,128)(2,1)} collective-permute-done((bf16[2,288,1024]{2,1,0:T(8,128)(2,1)S(1)}, bf16[2,288,1024]{2,1,0:T(8,128)(2,1)}, u32[]{:S(2)}, u32[]{:S(2)}) %collective-permute-start.18) | collective-permute-done | bytes 1179680 | tf_op jit(solution)/shard_map/ppermute | solution.py:94
  87.7 7.1 %collective-permute-done.4.refs_0_ = bf16[2,208,1024]{2,1,0:T(8,128)(2,1)} collective-permute-done((bf16[2,208,1024]{2,1,0:T(8,128)(2,1)}, bf16[2,208,1024]{2,1,0:T(8,128)(2,1)}, u32[]{:S(2)}, u32[]{:S(2)}) %collective-permute-start.4) | collective-permute-done | bytes 852000 | tf_op jit(solution)/shard_map/ppermute | solution.py:94
  96.8 10.5 %collective-permute-done.19.refs_4_ = bf16[2,288,1024]{2,1,0:T(8,128)(2,1)S(1)} collective-permute-done((bf16[2,288,1024]{2,1,0:T(8,128)(2,1)}, bf16[2,288,1024]{2,1,0:T(8,128)(2,1)S(1)}, u32[]{:S(2)}, u32[]{:S(2)}) %collective-permute-start.19) | collective-permute-done | bytes 1179680 | tf_op jit(solution)/shard_map/ppermute | solution.py:94
  109.4 7.2 %collective-permute-done.5.refs_0_ = bf16[2,208,1024]{2,1,0:T(8,128)(2,1)} collective-permute-done((bf16[2,208,1024]{2,1,0:T(8,128)(2,1)}, bf16[2,208,1024]{2,1,0:T(8,128)(2,1)}, u32[]{:S(2)}, u32[]{:S(2)}) %collective-permute-start.5) | collective-permute-done | bytes 852000 | tf_op jit(solution)/shard_map/ppermute | solution.py:94
  119.1 10.0 %collective-permute-done.20.refs_5_ = bf16[2,288,1024]{2,1,0:T(8,128)(2,1)} collective-permute-done((bf16[2,288,1024]{2,1,0:T(8,128)(2,1)S(1)}, bf16[2,288,1024]{2,1,0:T(8,128)(2,1)}, u32[]{:S(2)}, u32[]{:S(2)}) %collective-permute-start.20) | collective-permute-done | bytes 1179680 | tf_op jit(solution)/shard_map/ppermute | solution.py:94
  131.5 6.8 %collective-permute-done.6.refs_0_ = bf16[2,208,1024]{2,1,0:T(8,128)(2,1)} collective-permute-done((bf16[2,208,1024]{2,1,0:T(8,128)(2,1)}, bf16[2,208,1024]{2,1,0:T(8,128)(2,1)}, u32[]{:S(2)}, u32[]{:S(2)}) %collective-permute-start.6) | collective-permute-done | bytes 852000 | tf_op jit(solution)/shard_map/ppermute | solution.py:94
  141.6 9.3 %collective-permute-done.21.refs_6_ = bf16[2,288,1024]{2,1,0:T(8,128)(2,1)} collective-permute-done((bf16[2,288,1024]{2,1,0:T(8,128)(2,1)}, bf16[2,288,1024]{2,1,0:T(8,128)(2,1)}, u32[]{:S(2)}, u32[]{:S(2)}) %collective-permute-start.21) | collective-permute-done | bytes 1179680 | tf_op jit(solution)/shard_map/ppermute | solution.py:94
  223.0 6.0 %shard_map.258 = (f32[256,1024]{1,0:T(8,128)S(1)}, bf16[256,1024]{1,0:T(8,128)(2,1)S(1)}, bf16[1024,256]{1,0:T(8,128)(2,1)S(1)}, bf16[1024,256]{1,0:T(8,128)(2,1...) custom-call(s32[1]{0:T(128)} %bitcast.refs_0_, ...), custom_call_target="tpu_custom_call" | custom-call | flops 4294967296 | bytes 17825792 | tf_op jit(solution)/shard_map/pallas_call | solution.py:181
  235.1 8.1 %shard_map.264 = (f32[256,1024]{1,0:T(8,128)S(1)}, bf16[256,1024]{1,0:T(8,128)(2,1)S(1)}, bf16[256,3072]{1,0:T(8,128)(2,1)}, bf16[256,3072]{1,0:T(8,128)(2,1)}, ...) custom-call(s32[1]{0:T(128)} %constant.161.clone.1.refs_0_, f32[256,1024]{1,0:T(8,128)S(1)} %get-tuple-element.90.refs_1_, ...), custom_call_target="tpu_custom_call" | custom-call | flops 4831838208 | bytes 28835840 | tf_op jit(solution)/shard_map/pallas_call | solution.py:181
  243.3 13.0 %shard_map.265 = (bf16[256,2048]{1,0:T(8,128)(2,1)}, bf16[256,2048]{1,0:T(8,128)(2,1)}, bf16[256,1024]{1,0:T(8,128)(2,1)S(1)}, f32[1,1024]{1,0:T(1,128)}, f32[1,128]{1,0:T(1,128)}, /*index=5*/f32[1,128]{1,0:T(1,128)}) custom-call(s32[1]{0:T(128)} %bitcast.refs_0_, bf16[256,1024]{1,0:T(8,128)(2,1)S(1)} %get-tuple-element.93.refs_1_, ...), custom_call_target="tpu_custom_call" | custom-call | flops 5905580032 | bytes 23068672 | tf_op jit(solution)/shard_map/pallas_call | solution.py:181
  262.1 6.1 %shard_map.262 = (f32[256,1024]{1,0:T(8,128)S(1)}, bf16[256,1024]{1,0:T(8,128)(2,1)S(1)}, bf16[1024,256]{1,0:T(8,128)(2,1)S(1)}, bf16[1024,256]{1,0:T(8,128)(2,1...) custom-call(s32[1]{0:T(128)} %bitcast.refs_0_, ...), custom_call_target="tpu_custom_call" | custom-call | flops 4294967296 | bytes 17825792 | tf_op jit(solution)/shard_map/pallas_call | solution.py:181
  274.2 8.1 %shard_map.268 = (f32[256,1024]{1,0:T(8,128)S(1)}, bf16[256,1024]{1,0:T(8,128)(2,1)S(1)}, bf16[256,3072]{1,0:T(8,128)(2,1)}, bf16[256,3072]{1,0:T(8,128)(2,1)}, ...) custom-call(s32[1]{0:T(128)} %constant.161.clone.1.refs_0_, f32[256,1024]{1,0:T(8,128)S(1)} %get-tuple-element.102.refs_1_, ...), custom_call_target="tpu_custom_call" | custom-call | flops 4831838208 | bytes 28835840 | tf_op jit(solution)/shard_map/pallas_call | solution.py:181
  282.4 13.1 %shard_map.269 = (bf16[256,2048]{1,0:T(8,128)(2,1)}, bf16[256,2048]{1,0:T(8,128)(2,1)}, bf16[256,1024]{1,0:T(8,128)(2,1)S(1)}, f32[1,1024]{1,0:T(1,128)}, f32[1,128]{1,0:T(1,128)}, /*index=5*/f32[1,128]{1,0:T(1,128)}) custom-call(s32[1]{0:T(128)} %bitcast.refs_0_, bf16[256,1024]{1,0:T(8,128)(2,1)S(1)} %get-tuple-element.105.refs_1_, ...), custom_call_target="tpu_custom_call" | custom-call | flops 5905580032 | bytes 23068672 | tf_op jit(solution)/shard_map/pallas_call | solution.py:181
  296.9 6.2 %shard_map.266 = (f32[256,1024]{1,0:T(8,128)S(1)}, bf16[256,1024]{1,0:T(8,128)(2,1)S(1)}, bf16[256,3072]{1,0:T(8,128)(2,1)S(1)}, bf16[256,3072]{1,0:T(8,128)(2,1...) custom-call(s32[1]{0:T(128)} %bitcast.refs_0_, f32[256,1024]{1,0:T(8,128)S(1)} %get-tuple-element.90.refs_1_, ...), custom_call_target="tpu_custom_call" | custom-call | flops 4831838208 | bytes 28835840 | tf_op jit(solution)/shard_map/pallas_call | solution.py:181
  308.9 12.6 %shard_map.267 = (bf16[256,2048]{1,0:T(8,128)(2,1)S(1)}, bf16[256,2048]{1,0:T(8,128)(2,1)S(1)}, bf16[256,1024]{1,0:T(8,128)(2,1)S(1)}, f32[1,1024]{1,0:T(1,128)S...) custom-call(s32[1]{0:T(128)} %bitcast.refs_0_, bf16[256,1024]{1,0:T(8,128)(2,1)S(1)} %get-tuple-element.99.refs_1_.refs_9_, ...), custom_call_target="tpu_custom_call" | custom-call | flops 5905580032 | bytes 23068672 | tf_op jit(solution)/shard_map/pallas_call | solution.py:181
  321.6 6.2 %shard_map.270 = (f32[256,1024]{1,0:T(8,128)S(1)}, bf16[256,1024]{1,0:T(8,128)(2,1)S(1)}, bf16[256,3072]{1,0:T(8,128)(2,1)S(1)}, bf16[256,3072]{1,0:T(8,128)(2,1...) custom-call(s32[1]{0:T(128)} %bitcast.refs_0_, f32[256,1024]{1,0:T(8,128)S(1)} %get-tuple-element.102.refs_1_, ...), custom_call_target="tpu_custom_call" | custom-call | flops 4831838208 | bytes 28835840 | tf_op jit(solution)/shard_map/pallas_call | solution.py:181
  327.8 9.1 %shard_map.271 = (bf16[8,2,240,1024]{3,2,1,0:T(8,128)(2,1)S(1)}, bf16[8,2,240,1024]{3,2,1,0:T(8,128)(2,1)S(1)}) custom-call(s32[18]{0:T(128)S(1)} %get-tuple-element.198.refs_0_, bf16[1024,256]{1,0:T(8,128)(2,1)S(1)} %copy-done.73, bf16[1024,256]{1,0:T(8,128)(2,1)S(1)} %copy-done.79, bf16[256,3072]{1,0:T(8,128)(2,1)S(1)} %copy-done.53, ...), custom_call_target="tpu_custom_call" | custom-call | flops 8053063680 | bytes 19922944 | tf_op jit(solution)/shard_map/pallas_call | solution.py:181
  337.3 12.5 %shard_map.272 = (bf16[256,2048]{1,0:T(8,128)(2,1)S(1)}, bf16[256,2048]{1,0:T(8,128)(2,1)S(1)}, bf16[256,1024]{1,0:T(8,128)(2,1)S(1)}, f32[1,1024]{1,0:T(1,128)S...) custom-call(s32[1]{0:T(128)} %bitcast.refs_0_, bf16[256,1024]{1,0:T(8,128)(2,1)S(1)} %get-tuple-element.111.refs_1_.refs_10_, ...), custom_call_target="tpu_custom_call" | custom-call | flops 5905580032 | bytes 23068672 | tf_op jit(solution)/shard_map/pallas_call | solution.py:181
  352.0 8.9 %shard_map.273 = (bf16[8,2,240,1024]{3,2,1,0:T(8,128)(2,1)S(1)}, bf16[8,2,240,1024]{3,2,1,0:T(8,128)(2,1)S(1)}) custom-call(s32[18]{0:T(128)S(1)} %get-tuple-element.198.refs_0_, bf16[1024,256]{1,0:T(8,128)(2,1)S(1)} %copy-done.71, bf16[1024,256]{1,0:T(8,128)(2,1)S(1)} %copy-done.75, bf16[256,2048]{1,0:T(8,128)(2,1)S(1)} %get-tuple-element.123.refs_11_.refs_3_, ...), custom_call_target="tpu_custom_call" | custom-call | flops 8053063680 | bytes 19922944 | tf_op jit(solution)/shard_map/pallas_call | solution.py:181
  362.9 12.5 %collective-permute-done.53 = bf16[2,240,1024]{2,1,0:T(8,128)(2,1)S(1)} collective-permute-done((bf16[2,240,1024]{2,1,0:T(8,128)(2,1)S(1)}, bf16[2,240,1024]{2,1,0:T(8,128)(2,1)S(1)}, u32[]{:S(2)}, u32[]{:S(2)}) %collective-permute-start.53) | collective-permute-done | bytes 983072 | tf_op jit(solution)/shard_map/ppermute | solution.py:122
  385.9 6.9 %collective-permute-done.54 = bf16[2,240,1024]{2,1,0:T(8,128)(2,1)} collective-permute-done((bf16[2,240,1024]{2,1,0:T(8,128)(2,1)}, bf16[2,240,1024]{2,1,0:T(8,128)(2,1)}, u32[]{:S(2)}, u32[]{:S(2)}) %collective-permute-start.54) | collective-permute-done | bytes 983072 | tf_op jit(solution)/shard_map/ppermute | solution.py:122
  396.5 6.7 %collective-permute-done.45 = bf16[2,240,1024]{2,1,0:T(8,128)(2,1)} collective-permute-done((bf16[2,240,1024]{2,1,0:T(8,128)(2,1)S(1)}, bf16[2,240,1024]{2,1,0:T(8,128)(2,1)}, u32[]{:S(2)}, u32[]{:S(2)}) %collective-permute-start.45) | collective-permute-done | bytes 983072 | tf_op jit(solution)/shard_map/ppermute | solution.py:122
  407.7 6.2 %collective-permute-done.55 = bf16[2,240,1024]{2,1,0:T(8,128)(2,1)S(1)} collective-permute-done((bf16[2,240,1024]{2,1,0:T(8,128)(2,1)S(1)}, bf16[2,240,1024]{2,1,0:T(8,128)(2,1)S(1)}, u32[]{:S(2)}, u32[]{:S(2)}) %collective-permute-start.55) | collective-permute-done | bytes 983072 | tf_op jit(solution)/shard_map/ppermute | solution.py:122
  417.2 7.2 %collective-permute-done.46 = bf16[2,240,1024]{2,1,0:T(8,128)(2,1)S(1)} collective-permute-done((bf16[2,240,1024]{2,1,0:T(8,128)(2,1)S(1)}, bf16[2,240,1024]{2,1,0:T(8,128)(2,1)S(1)}, u32[]{:S(2)}, u32[]{:S(2)}) %collective-permute-start.46) | collective-permute-done | bytes 983072 | tf_op jit(solution)/shard_map/ppermute | solution.py:122
  438.6 6.9 %collective-permute-done.47 = bf16[2,240,1024]{2,1,0:T(8,128)(2,1)S(1)} collective-permute-done((bf16[2,240,1024]{2,1,0:T(8,128)(2,1)}, bf16[2,240,1024]{2,1,0:T(8,128)(2,1)S(1)}, u32[]{:S(2)}, u32[]{:S(2)}) %collective-permute-start.47) | collective-permute-done | bytes 983072 | tf_op jit(solution)/shard_map/ppermute | solution.py:122
  449.8 6.3 %collective-permute-done.57 = bf16[2,240,1024]{2,1,0:T(8,128)(2,1)S(1)} collective-permute-done((bf16[2,240,1024]{2,1,0:T(8,128)(2,1)S(1)}, bf16[2,240,1024]{2,1,0:T(8,128)(2,1)S(1)}, u32[]{:S(2)}, u32[]{:S(2)}) %collective-permute-start.57) | collective-permute-done | bytes 983072 | tf_op jit(solution)/shard_map/ppermute | solution.py:122
  460.0 6.6 %collective-permute-done.48 = bf16[2,240,1024]{2,1,0:T(8,128)(2,1)S(1)} collective-permute-done((bf16[2,240,1024]{2,1,0:T(8,128)(2,1)S(1)}, bf16[2,240,1024]{2,1,0:T(8,128)(2,1)S(1)}, u32[]{:S(2)}, u32[]{:S(2)}) %collective-permute-start.48) | collective-permute-done | bytes 983072 | tf_op jit(solution)/shard_map/ppermute | solution.py:122
  518.1 7.2 %collective-permute-done.51 = bf16[2,240,1024]{2,1,0:T(8,128)(2,1)S(1)} collective-permute-done((bf16[2,240,1024]{2,1,0:T(8,128)(2,1)S(1)}, bf16[2,240,1024]{2,1,0:T(8,128)(2,1)S(1)}, u32[]{:S(2)}, u32[]{:S(2)}) %collective-permute-start.51) | collective-permute-done | bytes 983072 | tf_op jit(solution)/shard_map/ppermute | solution.py:122
  (424 shorter events, 260.7 us)
Async XLA Ops:
  20.7 21.2 %collective-permute-start.16 = (bf16[2,288,1024]{2,1,0:T(8,128)(2,1)S(1)}, bf16[2,288,1024]{2,1,0:T(8,128)(2,1)S(1)}, u32[]{:S(2)}, u32[]{:S(2)}) collective-permute-start(bf16[2,288,1024]{2,1,0:T(8,128)(2,1)S(1)} %maximum_select_fusion.refs_0_), channel_id=1, source_target_pairs={{0,4},{5,1},{4,8},{9,5},{8,12},{13,9},{12,14},{15,13},{14,10},{11,... | collective-permute-start | bytes 3538952 | tf_op jit(solution)/shard_map/ppermute | solution.py:94
  29.4 21.8 %collective-permute-start.2 = (bf16[2,208,1024]{2,1,0:T(8,128)(2,1)}, bf16[2,208,1024]{2,1,0:T(8,128)(2,1)}, u32[]{:S(2)}, u32[]{:S(2)}) collective-permute-start(bf16[2,208,1024]{2,1,0:T(8,128)(2,1)} %shard_map.246.refs_1_), channel_id=1, source_target_pairs={{0,4},{5,1},{4,8},{9,5},{8,12},{13,9},{12,14},{15,13},{14,10},{11,... | collective-permute-start | bytes 2555912 | tf_op jit(solution)/shard_map/ppermute | solution.py:94
  43.0 20.7 %collective-permute-start.17 = (bf16[2,288,1024]{2,1,0:T(8,128)(2,1)}, bf16[2,288,1024]{2,1,0:T(8,128)(2,1)S(1)}, u32[]{:S(2)}, u32[]{:S(2)}) collective-permute-start(bf16[2,288,1024]{2,1,0:T(8,128)(2,1)} %shard_map.255.refs_1_), channel_id=1, source_target_pairs={{0,4},{5,1},{4,8},{9,5},{8,12},{13,9},{12,14},{15,13},{14,10},{11,... | collective-permute-start | bytes 3538952 | tf_op jit(solution)/shard_map/ppermute | solution.py:94
  51.2 21.8 %collective-permute-start.3 = (bf16[2,208,1024]{2,1,0:T(8,128)(2,1)}, bf16[2,208,1024]{2,1,0:T(8,128)(2,1)}, u32[]{:S(2)}, u32[]{:S(2)}) collective-permute-start(bf16[2,208,1024]{2,1,0:T(8,128)(2,1)} %shard_map.247.refs_2_), channel_id=1, source_target_pairs={{0,4},{5,1},{4,8},{9,5},{8,12},{13,9},{12,14},{15,13},{14,10},{11,... | collective-permute-start | bytes 2555912 | tf_op jit(solution)/shard_map/ppermute | solution.py:94
  63.7 21.9 %collective-permute-start.18 = (bf16[2,288,1024]{2,1,0:T(8,128)(2,1)S(1)}, bf16[2,288,1024]{2,1,0:T(8,128)(2,1)}, u32[]{:S(2)}, u32[]{:S(2)}) collective-permute-start(bf16[2,288,1024]{2,1,0:T(8,128)(2,1)S(1)} %collective-permute-done.17.refs_2_), channel_id=1, source_target_pairs={{0,4},{5,1},{4,8},{9,5},{8,12},{13,9},{12,14},{15,13},{14,10},{11,... | collective-permute-start | bytes 3538952 | tf_op jit(solution)/shard_map/ppermute | solution.py:94
  73.0 21.8 %collective-permute-start.4 = (bf16[2,208,1024]{2,1,0:T(8,128)(2,1)}, bf16[2,208,1024]{2,1,0:T(8,128)(2,1)}, u32[]{:S(2)}, u32[]{:S(2)}) collective-permute-start(bf16[2,208,1024]{2,1,0:T(8,128)(2,1)} %shard_map.248.refs_3_), channel_id=1, source_target_pairs={{0,4},{5,1},{4,8},{9,5},{8,12},{13,9},{12,14},{15,13},{14,10},{11,... | collective-permute-start | bytes 2555912 | tf_op jit(solution)/shard_map/ppermute | solution.py:94
  85.6 21.7 %collective-permute-start.19 = (bf16[2,288,1024]{2,1,0:T(8,128)(2,1)}, bf16[2,288,1024]{2,1,0:T(8,128)(2,1)S(1)}, u32[]{:S(2)}, u32[]{:S(2)}) collective-permute-start(bf16[2,288,1024]{2,1,0:T(8,128)(2,1)} %collective-permute-done.18.refs_3_), channel_id=1, source_target_pairs={{0,4},{5,1},{4,8},{9,5},{8,12},{13,9},{12,14},{15,13},{14,10},{11,... | collective-permute-start | bytes 3538952 | tf_op jit(solution)/shard_map/ppermute | solution.py:94
  94.7 21.8 %collective-permute-start.5 = (bf16[2,208,1024]{2,1,0:T(8,128)(2,1)}, bf16[2,208,1024]{2,1,0:T(8,128)(2,1)}, u32[]{:S(2)}, u32[]{:S(2)}) collective-permute-start(bf16[2,208,1024]{2,1,0:T(8,128)(2,1)} %shard_map.249.refs_4_), channel_id=1, source_target_pairs={{0,4},{5,1},{4,8},{9,5},{8,12},{13,9},{12,14},{15,13},{14,10},{11,... | collective-permute-start | bytes 2555912 | tf_op jit(solution)/shard_map/ppermute | solution.py:94
  107.3 21.9 %collective-permute-start.20 = (bf16[2,288,1024]{2,1,0:T(8,128)(2,1)S(1)}, bf16[2,288,1024]{2,1,0:T(8,128)(2,1)}, u32[]{:S(2)}, u32[]{:S(2)}) collective-permute-start(bf16[2,288,1024]{2,1,0:T(8,128)(2,1)S(1)} %collective-permute-done.19.refs_4_), channel_id=1, source_target_pairs={{0,4},{5,1},{4,8},{9,5},{8,12},{13,9},{12,14},{15,13},{14,10},{11,... | collective-permute-start | bytes 3538952 | tf_op jit(solution)/shard_map/ppermute | solution.py:94
  116.5 21.8 %collective-permute-start.6 = (bf16[2,208,1024]{2,1,0:T(8,128)(2,1)}, bf16[2,208,1024]{2,1,0:T(8,128)(2,1)}, u32[]{:S(2)}, u32[]{:S(2)}) collective-permute-start(bf16[2,208,1024]{2,1,0:T(8,128)(2,1)} %shard_map.250.refs_5_), channel_id=1, source_target_pairs={{0,4},{5,1},{4,8},{9,5},{8,12},{13,9},{12,14},{15,13},{14,10},{11,... | collective-permute-start | bytes 2555912 | tf_op jit(solution)/shard_map/ppermute | solution.py:94
  118.6 19.7 %collective-permute-start.8 = (bf16[2,208,1024]{2,1,0:T(8,128)(2,1)}, bf16[2,208,1024]{2,1,0:T(8,128)(2,1)}, u32[]{:S(2)}, u32[]{:S(2)}) collective-permute-start(bf16[2,208,1024]{2,1,0:T(8,128)(2,1)} %shard_map.246.refs_1_), channel_id=1, source_target_pairs={{0,1},{1,0},{2,3},{3,2},{4,5},{5,4},{6,7},{7,6},{8,9},{9,8},{10,11... | collective-permute-start | bytes 2555912 | tf_op jit(solution)/shard_map/ppermute | solution.py:103
  118.6 20.2 %collective-permute-start.9 = (bf16[2,208,1024]{2,1,0:T(8,128)(2,1)}, bf16[2,208,1024]{2,1,0:T(8,128)(2,1)}, u32[]{:S(2)}, u32[]{:S(2)}) collective-permute-start(bf16[2,208,1024]{2,1,0:T(8,128)(2,1)} %shard_map.247.refs_2_), channel_id=1, source_target_pairs={{0,1},{1,0},{2,3},{3,2},{4,5},{5,4},{6,7},{7,6},{8,9},{9,8},{10,11... | collective-permute-start | bytes 2555912 | tf_op jit(solution)/shard_map/ppermute | solution.py:103
  129.1 21.8 %collective-permute-start.21 = (bf16[2,288,1024]{2,1,0:T(8,128)(2,1)}, bf16[2,288,1024]{2,1,0:T(8,128)(2,1)}, u32[]{:S(2)}, u32[]{:S(2)}) collective-permute-start(bf16[2,288,1024]{2,1,0:T(8,128)(2,1)} %collective-permute-done.20.refs_5_), channel_id=1, source_target_pairs={{0,4},{5,1},{4,8},{9,5},{8,12},{13,9},{12,14},{15,13},{14,10},{11,... | collective-permute-start | bytes 3538952 | tf_op jit(solution)/shard_map/ppermute | solution.py:94
  131.4 23.2 %collective-permute-start.23 = (bf16[2,288,1024]{2,1,0:T(8,128)(2,1)}, bf16[2,288,1024]{2,1,0:T(8,128)(2,1)}, u32[]{:S(2)}, u32[]{:S(2)}) collective-permute-start(bf16[2,288,1024]{2,1,0:T(8,128)(2,1)} %shard_map.255.refs_1_), channel_id=1, source_target_pairs={{0,1},{1,0},{2,3},{3,2},{4,5},{5,4},{6,7},{7,6},{8,9},{9,8},{10,11... | collective-permute-start | bytes 3538952 | tf_op jit(solution)/shard_map/ppermute | solution.py:103
  138.8 21.1 %collective-permute-start.7 = (bf16[2,208,1024]{2,1,0:T(8,128)(2,1)}, bf16[2,208,1024]{2,1,0:T(8,128)(2,1)S(1)}, u32[]{:S(2)}, u32[]{:S(2)}) collective-permute-start(bf16[2,208,1024]{2,1,0:T(8,128)(2,1)} %shard_map.251.refs_6_), channel_id=1, source_target_pairs={{0,4},{5,1},{4,8},{9,5},{8,12},{13,9},{12,14},{15,13},{14,10},{11,... | collective-permute-start | bytes 2555912 | tf_op jit(solution)/shard_map/ppermute | solution.py:94
  150.9 21.8 %collective-permute-start.22 = (bf16[2,288,1024]{2,1,0:T(8,128)(2,1)}, bf16[2,288,1024]{2,1,0:T(8,128)(2,1)}, u32[]{:S(2)}, u32[]{:S(2)}) collective-permute-start(bf16[2,288,1024]{2,1,0:T(8,128)(2,1)} %collective-permute-done.21.refs_6_), channel_id=1, source_target_pairs={{0,4},{5,1},{4,8},{9,5},{8,12},{13,9},{12,14},{15,13},{14,10},{11,... | collective-permute-start | bytes 3538952 | tf_op jit(solution)/shard_map/ppermute | solution.py:94
  163.9 26.4 %collective-permute-start.25 = (bf16[2,288,1024]{2,1,0:T(8,128)(2,1)}, bf16[2,288,1024]{2,1,0:T(8,128)(2,1)}, u32[]{:S(2)}, u32[]{:S(2)}) collective-permute-start(bf16[2,288,1024]{2,1,0:T(8,128)(2,1)} %collective-permute-done.18.refs_3_), channel_id=1, source_target_pairs={{0,1},{1,0},{2,3},{3,2},{4,5},{5,4},{6,7},{7,6},{8,9},{9,8},{10,11... | collective-permute-start | bytes 3538952 | tf_op jit(solution)/shard_map/ppermute | solution.py:103
  165.4 25.0 %collective-permute-start.26 = (bf16[2,288,1024]{2,1,0:T(8,128)(2,1)}, bf16[2,288,1024]{2,1,0:T(8,128)(2,1)}, u32[]{:S(2)}, u32[]{:S(2)}) collective-permute-start(bf16[2,288,1024]{2,1,0:T(8,128)(2,1)} %copy-done.11), channel_id=1, source_target_pairs={{0,1},{1,0},{2,3},{3,2},{4,5},{5,4},{6,7},{7,6},{8,9},{9,8},{10,11... | collective-permute-start | bytes 3538952 | tf_op jit(solution)/shard_map/ppermute | solution.py:103
  166.3 24.1 %collective-permute-start.27 = (bf16[2,288,1024]{2,1,0:T(8,128)(2,1)}, bf16[2,288,1024]{2,1,0:T(8,128)(2,1)}, u32[]{:S(2)}, u32[]{:S(2)}) collective-permute-start(bf16[2,288,1024]{2,1,0:T(8,128)(2,1)} %collective-permute-done.20.refs_5_), channel_id=1, source_target_pairs={{0,1},{1,0},{2,3},{3,2},{4,5},{5,4},{6,7},{7,6},{8,9},{9,8},{10,11... | collective-permute-start | bytes 3538952 | tf_op jit(solution)/shard_map/ppermute | solution.py:103
  167.7 22.6 %collective-permute-start.28 = (bf16[2,288,1024]{2,1,0:T(8,128)(2,1)}, bf16[2,288,1024]{2,1,0:T(8,128)(2,1)}, u32[]{:S(2)}, u32[]{:S(2)}) collective-permute-start(bf16[2,288,1024]{2,1,0:T(8,128)(2,1)} %collective-permute-done.21.refs_6_), channel_id=1, source_target_pairs={{0,1},{1,0},{2,3},{3,2},{4,5},{5,4},{6,7},{7,6},{8,9},{9,8},{10,11... | collective-permute-start | bytes 3538952 | tf_op jit(solution)/shard_map/ppermute | solution.py:103
  201.5 21.5 %collective-permute-start.30 = (bf16[256,1024]{1,0:T(8,128)(2,1)S(1)}, bf16[256,1024]{1,0:T(8,128)(2,1)S(1)}, u32[]{:S(2)}, u32[]{:S(2)}) collective-permute-start(bf16[256,1024]{1,0:T(8,128)(2,1)S(1)} %shard_map.257), channel_id=1, source_target_pairs={{0,16},{1,17},{2,18},{3,19},{4,20},{5,21},{6,22},{7,23},{8,24},{9,... | collective-permute-start | bytes 1572872 | tf_op jit(solution)/shard_map/ppermute | solution.py:28
  221.4 36.2 %collective-permute-start.32 = (bf16[256,1024]{1,0:T(8,128)(2,1)S(1)}, bf16[256,1024]{1,0:T(8,128)(2,1)S(1)}, u32[]{:S(2)}, u32[]{:S(2)}) collective-permute-start(bf16[256,1024]{1,0:T(8,128)(2,1)S(1)} %shard_map.261), channel_id=1, source_target_pairs={{0,16},{1,17},{2,18},{3,19},{4,20},{5,21},{6,22},{7,23},{8,24},{9,... | collective-permute-start | bytes 1572872 | tf_op jit(solution)/shard_map/ppermute | solution.py:28
  256.3 40.7 %collective-permute-start.33 = (bf16[256,1024]{1,0:T(8,128)(2,1)S(1)}, bf16[256,1024]{1,0:T(8,128)(2,1)S(1)}, u32[]{:S(2)}, u32[]{:S(2)}) collective-permute-start(bf16[256,1024]{1,0:T(8,128)(2,1)S(1)} %get-tuple-element.98), channel_id=1, source_target_pairs={{16,0},{17,1},{18,2},{19,3},{20,4},{21,5},{22,6},{23,7},{24,8},{25... | collective-permute-start | bytes 1572872 | tf_op jit(solution)/shard_map/ppermute | solution.py:28
  295.5 26.0 %collective-permute-start.34 = (bf16[256,1024]{1,0:T(8,128)(2,1)S(1)}, bf16[256,1024]{1,0:T(8,128)(2,1)S(1)}, u32[]{:S(2)}, u32[]{:S(2)}) collective-permute-start(bf16[256,1024]{1,0:T(8,128)(2,1)S(1)} %get-tuple-element.110), channel_id=1, source_target_pairs={{16,0},{17,1},{18,2},{19,3},{20,4},{21,5},{22,6},{23,7},{24,8},{25... | collective-permute-start | bytes 1572872 | tf_op jit(solution)/shard_map/ppermute | solution.py:28
  380.1 23.2 %collective-permute-start.45 = (bf16[2,240,1024]{2,1,0:T(8,128)(2,1)S(1)}, bf16[2,240,1024]{2,1,0:T(8,128)(2,1)}, u32[]{:S(2)}, u32[]{:S(2)}) collective-permute-start(bf16[2,240,1024]{2,1,0:T(8,128)(2,1)S(1)} %fusion.13), channel_id=1, source_target_pairs={{0,4},{5,1},{4,8},{9,5},{8,12},{13,9},{12,14},{15,13},{14,10},{11,... | collective-permute-start | bytes 2949128 | tf_op jit(solution)/shard_map/ppermute | solution.py:122
  384.9 22.2 %collective-permute-start.37 = (f32[1,2306]{1,0:T(1,128)S(1)}, f32[1,2306]{1,0:T(1,128)S(1)}, u32[]{:S(2)}, u32[]{:S(2)}) collective-permute-start(f32[1,2306]{1,0:T(1,128)S(1)} %concatenate.82), channel_id=1, source_target_pairs={{0,3},{1,0},{2,1},{3,2},{4,7},{5,4},{6,5},{7,6},{8,11},{9,8},{10,9... | collective-permute-start | bytes 27680 | tf_op jit(solution)/shard_map/ppermute | solution.py:62
  385.2 21.9 %collective-permute-start.36 = (f32[1,2306]{1,0:T(1,128)S(1)}, f32[1,2306]{1,0:T(1,128)S(1)}, u32[]{:S(2)}, u32[]{:S(2)}) collective-permute-start(f32[1,2306]{1,0:T(1,128)S(1)} %concatenate.82), channel_id=1, source_target_pairs={{0,2},{1,3},{2,0},{3,1},{4,6},{5,7},{6,4},{7,5},{8,10},{9,11},{10,... | collective-permute-start | bytes 27680 | tf_op jit(solution)/shard_map/ppermute | solution.py:62
  385.7 21.4 %collective-permute-start.35 = (f32[1,2306]{1,0:T(1,128)S(1)}, f32[1,2306]{1,0:T(1,128)S(1)}, u32[]{:S(2)}, u32[]{:S(2)}) collective-permute-start(f32[1,2306]{1,0:T(1,128)S(1)} %concatenate.82), channel_id=1, source_target_pairs={{0,1},{1,2},{2,3},{3,0},{4,5},{5,6},{6,7},{7,4},{8,9},{9,10},{10,1... | collective-permute-start | bytes 27680 | tf_op jit(solution)/shard_map/ppermute | solution.py:62
  428.6 20.5 %collective-permute-start.40 = (f32[1,2306]{1,0:T(1,128)S(1)}, f32[1,2306]{1,0:T(1,128)S(1)}, u32[]{:S(2)}, u32[]{:S(2)}) collective-permute-start(f32[1,2306]{1,0:T(1,128)S(1)} %copy-done.84), channel_id=1, source_target_pairs={{0,12},{1,13},{2,14},{3,15},{4,0},{5,1},{6,2},{7,3},{8,4},{9,5},{1... | collective-permute-start | bytes 27680 | tf_op jit(solution)/shard_map/ppermute | solution.py:62
  437.1 19.0 %collective-permute-start.57 = (bf16[2,240,1024]{2,1,0:T(8,128)(2,1)S(1)}, bf16[2,240,1024]{2,1,0:T(8,128)(2,1)S(1)}, u32[]{:S(2)}, u32[]{:S(2)}) collective-permute-start(bf16[2,240,1024]{2,1,0:T(8,128)(2,1)S(1)} %fusion.2), channel_id=1, source_target_pairs={{0,4},{5,1},{4,8},{9,5},{8,12},{13,9},{12,14},{15,13},{14,10},{11,... | collective-permute-start | bytes 2949128 | tf_op jit(solution)/shard_map/ppermute | solution.py:122
  480.2 22.1 %collective-permute-start.59 = (bf16[2,240,1024]{2,1,0:T(8,128)(2,1)}, bf16[2,240,1024]{2,1,0:T(8,128)(2,1)S(1)}, u32[]{:S(2)}, u32[]{:S(2)}) collective-permute-start(bf16[2,240,1024]{2,1,0:T(8,128)(2,1)} %fusion), channel_id=1, source_target_pairs={{0,4},{5,1},{4,8},{9,5},{8,12},{13,9},{12,14},{15,13},{14,10},{11,... | collective-permute-start | bytes 2949128 | tf_op jit(solution)/shard_map/ppermute | solution.py:122
  492.5 24.5 %collective-permute-start.42 = (bf16[1,256,1024]{2,1,0:T(8,128)(2,1)S(1)}, bf16[1,256,1024]{2,1,0:T(8,128)(2,1)S(1)}, u32[]{:S(2)}, u32[]{:S(2)}) collective-permute-start(bf16[1,256,1024]{2,1,0:T(8,128)(2,1)S(1)} %bitcast.212), channel_id=1, source_target_pairs={{0,16},{1,17},{2,18},{3,19},{4,20},{5,21},{6,22},{7,23},{8,24},{9,... | collective-permute-start | bytes 1572872 | tf_op jit(solution)/shard_map/ppermute | solution.py:28
  (126 other events, 1120.1 us)
